TPU v7x, 32 devices: a whole 2x2x4 slice. The times are simulated.
32 devices in a mesh: wide: 8 (over z, x), grid: 4 (over y, core).
Axes of the slice: x: 2, y: 2, z: 4, core: 2. Of those that a mesh axis runs over, the one named last changes fastest.
Arguments:
- tokens: bfloat16 [4096, 2048], P('wide', 'grid'), may hold values from -6 to 6
- segment_ids: int32 [4096], replicated, may hold values from 0 to 3, never falling along the last dimension, each value on 1 to 2000 neighbouring positions
- attention_routes: int32 [4096, 2], P('wide'), may hold values from 0 to 3, all different within a row; in each aligned block of 512 rows (0 to 511, 512 to 1023, ...) at most 320 rows name the same one
- expert_routes: int32 [4096, 2], P('wide'), may hold values from 0 to 3, all different within a row; in each aligned block of 512 rows (0 to 511, 512 to 1023, ...) at most 320 rows name the same one
- attention_gain: bfloat16 [2048], P('wide'), may hold values from 0.099609375 to 1.8984375
- attention_kv: bfloat16 [2048, 16, 2, 128], P('wide', 'grid'), may hold values from -0.125 to 0.125
- attention_query: bfloat16 [4, 2048, 16, 128], P(None, 'wide', 'grid'), may hold values from -0.125 to 0.125
- attention_out: bfloat16 [4, 16, 128, 2048], P(None, 'grid', None, 'wide'), may hold values from -1 to 1
- attention_router: bfloat16 [2048, 4], P('wide'), may hold values from -0.09375 to 0.09375
- feedforward_gain: bfloat16 [2048], P('wide'), may hold values from 0.099609375 to 1.8984375
- feedforward_router: bfloat16 [2048, 4], P('wide'), may hold values from -0.09375 to 0.09375
- expert_gate_up: bfloat16 [4, 2048, 2, 5632], P(None, 'wide', None, 'grid'), may hold values from -0.125 to 0.125
- expert_down: bfloat16 [4, 5632, 2048], P(None, 'grid', 'wide'), may hold values from -0.078125 to 0.078125
- output_grad: bfloat16 [4096, 2048], P('wide', 'grid'), may hold values from -6 to 6
Outputs:
- layer_output: bfloat16 [4096, 2048], P('wide', 'grid')
- input_grad: bfloat16 [4096, 2048], P('wide', 'grid')
- attention_gain_grad: float32 [2048], P('wide')
- attention_kv_grad: float32 [2048, 16, 2, 128], P('wide', 'grid')
- attention_query_grad: float32 [4, 2048, 16, 128], P(None, 'wide', 'grid')
- attention_out_grad: float32 [4, 16, 128, 2048], P(None, 'grid', None, 'wide')
- attention_router_grad: float32 [2048, 4], P('wide')
- feedforward_gain_grad: float32 [2048], P('wide')
- feedforward_router_grad: float32 [2048, 4], P('wide')
- expert_gate_up_grad: float32 [4, 2048, 2, 5632], P(None, 'wide', None, 'grid')
- expert_down_grad: float32 [4, 5632, 2048], P(None, 'grid', 'wide')
Inputs may be any that keep to these rules, and one draw needn't show every extreme that they name: `segment_ids`: segment numbers never fall along the tokens; every document holds 1 to 2000 tokens and one holds exactly 2000. `attention_routes`: each token names two different experts; in the rows of one index of wide no expert is named by more than 320 tokens, and in every draw some expert is named by exactly 320 tokens of one such block. `expert_routes`: each token names two different experts; in the rows of one index of wide no expert is named by more than 320 tokens, and in every draw some expert is named by exactly 320 tokens of one such block.
All inputs are finite; a program needn't handle non-finite values.
Results may differ from a plain program's by a relative error of at most 0.028.
Values may be sent and summed in bfloat16 or wider, within the bound.
A program may use at most 512 MiB of HBM per device.

v0:
```python
import math

import jax
import jax.numpy as jnp
from jax import lax
from jax.sharding import PartitionSpec as P

LENGTH = 4096
CAP = 320
REACH = 4


EPSILON = 1e-05
ROPE_BASE = 10000.0
NEGATIVE = -1e30


def passed_along(array, axis, by):
    count = lax.axis_size(axis)
    pairs = [(i, i + by) for i in range(count) if 0 <= i + by < count]
    return lax.ppermute(array, axis, pairs)


def rope_tables(positions, table_width):
    half_width = table_width // 2
    frequency = ROPE_BASE ** (-jnp.arange(half_width, dtype=jnp.float32) / half_width)
    angles = positions.astype(jnp.float32)[:, None] * frequency[None, :]
    return (jnp.cos(angles), jnp.sin(angles))


def rotate(values, cosine, sine_table):
    half_width = values.shape[-1] // 2
    leading = values[..., :half_width]
    trailing = values[..., half_width:]
    return jnp.concatenate(
        [leading * cosine - trailing * sine_table, trailing * cosine + leading * sine_table],
        axis=-1,
    )


def slot_plan(routes, experts, capacity):
    pair_experts = routes.reshape(-1)
    pair_count = pair_experts.shape[0]
    onehot = (pair_experts[:, None] == jnp.arange(experts, dtype=jnp.int32)[None, :]).astype(
        jnp.int32
    )
    before = jnp.cumsum(onehot, axis=0) - onehot
    slot_rank = jnp.sum(before * onehot, axis=1)
    slot_place = pair_experts * capacity + slot_rank
    source = (
        jnp.zeros((experts * capacity,), jnp.int32)
        .at[slot_place]
        .set(jnp.arange(pair_count, dtype=jnp.int32))
    )
    filled = jnp.zeros((experts * capacity,), jnp.int32).at[slot_place].set(1)
    return (slot_place, source, filled)


def pair_slots(pair_rows, slot_map):
    picked = pair_rows[slot_map[1]]
    return jnp.where(slot_map[2][:, None] > 0, picked, jnp.zeros_like(picked))


def token_slots(token_rows, slot_map):
    picked = token_rows[slot_map[1] // 2]
    return jnp.where(slot_map[2][:, None] > 0, picked, jnp.zeros_like(picked))


def slot_pairs(slot_rows, slot_map):
    return slot_rows[slot_map[0]]


def route_gates(hidden, router, routes):
    logits = jnp.dot(hidden, router, preferred_element_type=jnp.float32)
    choose = (
        routes[:, :, None] == jnp.arange(router.shape[1], dtype=jnp.int32)[None, None, :]
    ).astype(jnp.float32)
    picked = jnp.sum(choose * logits[:, None, :], axis=-1)
    return (jax.nn.softmax(picked, axis=-1), choose)


def logits_grad(gate_values, grad_gates, choose):
    grad_picked = gate_values * (
        grad_gates - jnp.sum(gate_values * grad_gates, axis=-1, keepdims=True)
    )
    return jnp.sum(choose * grad_picked[:, :, None], axis=1)


def norm_back(grad_hidden, normed, inverse, gain_row):
    grad_normed = grad_hidden * gain_row
    return inverse * (grad_normed - normed * jnp.mean(grad_normed * normed, axis=-1, keepdims=True))


def contract_first(left_matrix, right_matrix):
    return lax.dot_general(
        left_matrix, right_matrix, (((0,), (0,)), ((), ())), preferred_element_type=jnp.float32
    )


def contract_last(left_matrix, right_matrix):
    return lax.dot_general(
        left_matrix, right_matrix, (((1,), (1,)), ((), ())), preferred_element_type=jnp.float32
    )


def swiglu_back(gate_pre, up_pre, grad_hidden):
    sigmoid_gate = jax.nn.sigmoid(gate_pre)
    silu_gate = gate_pre * sigmoid_gate
    grad_gate = grad_hidden * up_pre * sigmoid_gate * (1.0 + gate_pre * (1.0 - sigmoid_gate))
    grad_up = grad_hidden * silu_gate
    return (
        jnp.stack([grad_gate, grad_up], axis=1).astype(jnp.bfloat16).reshape(gate_pre.shape[0], -1)
    )


def per_device(
    tokens,
    segment_ids,
    attention_routes,
    expert_routes,
    attention_gain,
    attention_kv,
    attention_query,
    attention_out,
    attention_router,
    feedforward_gain,
    feedforward_router,
    expert_gate_up,
    expert_down,
    output_grad,
):
    row_count = tokens.shape[0]
    wide_count = lax.axis_size("wide")
    wide_index = lax.axis_index("wide")
    grid_index = lax.axis_index("grid")
    feature_slice = tokens.shape[1]
    seq_length = min(LENGTH, row_count * wide_count)
    head_local = attention_kv.shape[1]
    head_width = attention_kv.shape[3]
    expert_count = attention_query.shape[0]
    score_scaling = 1.0 / math.sqrt(head_width)
    block_rows = min(512, row_count)
    block_count = row_count // block_rows
    inputs = lax.all_gather(tokens, "grid", axis=1, tiled=True).astype(jnp.float32)
    model_width = inputs.shape[1]
    norm_first, router_first, norm_second, router_second, kv_weight, query_weight, out_weight = (
        lax.all_gather(attention_gain, "wide", axis=0, tiled=True),
        lax.all_gather(attention_router, "wide", axis=0, tiled=True),
        lax.all_gather(feedforward_gain, "wide", axis=0, tiled=True),
        lax.all_gather(feedforward_router, "wide", axis=0, tiled=True),
        lax.all_gather(attention_kv, "wide", axis=0, tiled=True),
        lax.all_gather(attention_query, "wide", axis=1, tiled=True),
        lax.all_gather(attention_out, "wide", axis=3, tiled=True),
    )
    gain_first = norm_first.astype(jnp.float32)
    gain_second = norm_second.astype(jnp.float32)
    inverse_first = lax.rsqrt(jnp.mean(inputs * inputs, axis=-1, keepdims=True) + EPSILON)
    normed_first = inputs * inverse_first
    hidden_first = (normed_first * gain_first).astype(jnp.bfloat16)
    global_position = wide_index * row_count + jnp.arange(row_count, dtype=jnp.int32)
    cosine, sine_table = rope_tables(global_position % seq_length, head_width)
    gates_first, choose_first = route_gates(hidden_first, router_first, attention_routes)
    kv_flat = jnp.dot(
        hidden_first, kv_weight.reshape(model_width, -1), preferred_element_type=jnp.float32
    )
    kv_rows = kv_flat.reshape(row_count, head_local, 2, head_width)
    key_local = rotate(kv_rows[:, :, 0], cosine[:, None, :], sine_table[:, None, :]).astype(
        jnp.bfloat16
    )
    value_local = kv_rows[:, :, 1].astype(jnp.bfloat16)
    kv_local = jnp.stack([key_local, value_local], axis=2)
    plan_first = slot_plan(attention_routes, expert_count, CAP)
    slot_inputs = token_slots(hidden_first, plan_first).reshape(expert_count, CAP, model_width)
    query_slots = jnp.einsum(
        "ecm,emf->ecf",
        slot_inputs,
        query_weight.reshape(expert_count, model_width, -1),
        preferred_element_type=jnp.float32,
    )
    query_pre = slot_pairs(query_slots.reshape(expert_count * CAP, -1), plan_first).reshape(
        row_count, 2, head_local, head_width
    )
    queries = rotate(query_pre, cosine[:, None, None, :], sine_table[:, None, None, :]).astype(
        jnp.bfloat16
    )
    earlier = []
    for offset in range(REACH, 0, -1):
        earlier.append(passed_along(kv_local, "wide", offset))
    kv_all = jnp.concatenate(earlier + [kv_local], axis=0)
    gathered_keys = kv_all[:, :, 0]
    gathered_values = kv_all[:, :, 1]
    padded_segment = jnp.concatenate([jnp.full((REACH * row_count,), -1, jnp.int32), segment_ids])
    key_segment = lax.dynamic_slice_in_dim(
        padded_segment, wide_index * row_count, (REACH + 1) * row_count, 0
    )
    key_position = (wide_index - REACH) * row_count + jnp.arange(
        (REACH + 1) * row_count, dtype=jnp.int32
    )
    query_segment = lax.dynamic_slice_in_dim(segment_ids, wide_index * row_count, row_count, 0)

    def block_scores(query_block_rows, block_position, block_segment):
        allowed = (
            (key_segment[None, :] == block_segment[:, None])
            & (key_position[None, :] <= block_position[:, None])
            & (
                jnp.floor_divide(key_position, seq_length)[None, :]
                == jnp.floor_divide(block_position, seq_length)[:, None]
            )
        )
        score_matrix = (
            jnp.einsum(
                "jfeu,geu->fejg",
                query_block_rows,
                gathered_keys,
                preferred_element_type=jnp.float32,
            )
            * score_scaling
        )
        return jnp.where(allowed[None, None], score_matrix, NEGATIVE)

    def forward_block(carried, pieces):
        query_block_rows, block_position, block_segment = pieces
        score_matrix = block_scores(query_block_rows, block_position, block_segment)
        largest = jnp.max(score_matrix, axis=-1, keepdims=True)
        weights = jnp.exp(score_matrix - largest)
        totals = jnp.sum(weights, axis=-1, keepdims=True)
        attention_probabilities = (weights / totals).astype(jnp.bfloat16)
        attended_output = jnp.einsum(
            "jegf,feq->gjeq",
            attention_probabilities,
            gathered_values,
            preferred_element_type=jnp.float32,
        )
        return (carried, (attended_output, (largest + jnp.log(totals))[..., 0]))

    query_blocks = queries.reshape(block_count, block_rows, 2, head_local, head_width)
    position_blocks = global_position.reshape(block_count, block_rows)
    segment_blocks = query_segment.reshape(block_count, block_rows)
    attended_blocks, logsum = lax.scan(
        forward_block, 0, (query_blocks, position_blocks, segment_blocks)
    )[1]
    attended_low = attended_blocks.reshape(row_count, 2, head_local * head_width).astype(
        jnp.bfloat16
    )
    out_inputs = pair_slots(attended_low.reshape(2 * row_count, -1), plan_first).reshape(
        expert_count, CAP, -1
    )
    branch_slots = jnp.einsum(
        "ecf,efm->ecm",
        out_inputs,
        out_weight.reshape(expert_count, -1, model_width),
        preferred_element_type=jnp.float32,
    )
    branch_first = slot_pairs(
        branch_slots.reshape(expert_count * CAP, model_width), plan_first
    ).reshape(row_count, 2, model_width)
    mixed_first = jnp.sum(gates_first[:, :, None] * branch_first, axis=1)
    residual = inputs + lax.psum(mixed_first.astype(jnp.bfloat16), "grid").astype(jnp.float32)
    inverse_second = lax.rsqrt(jnp.mean(residual * residual, axis=-1, keepdims=True) + EPSILON)
    normed_second = residual * inverse_second
    hidden_second = (normed_second * gain_second).astype(jnp.bfloat16)
    gates_second, choose_second = route_gates(hidden_second, router_second, expert_routes)
    plan_second = slot_plan(expert_routes, expert_count, CAP)
    expert_inputs = token_slots(hidden_second, plan_second).reshape(expert_count, CAP, model_width)
    grad_out = lax.all_gather(output_grad, "grid", axis=1, tiled=True).astype(jnp.float32)
    grad_branch_second = (gates_second[:, :, None] * grad_out[:, None, :]).astype(jnp.bfloat16)
    grad_slots_second = pair_slots(
        grad_branch_second.reshape(2 * row_count, -1), plan_second
    ).reshape(expert_count, CAP, model_width)

    def expert_forward(carried, pieces):
        gate_up_piece, down_piece, slot_rows = pieces
        gate_up_full, down_full = (
            lax.all_gather(gate_up_piece, "wide", axis=0, tiled=True),
            lax.all_gather(down_piece, "wide", axis=1, tiled=True),
        )
        gate_up = jnp.dot(
            slot_rows, gate_up_full.reshape(model_width, -1), preferred_element_type=jnp.float32
        ).reshape(slot_rows.shape[0], 2, -1)
        hidden = (jax.nn.silu(gate_up[:, 0]) * gate_up[:, 1]).astype(jnp.bfloat16)
        result = jnp.dot(hidden, down_full, preferred_element_type=jnp.float32)
        return (carried, (result, gate_up))

    forward_scan = lax.scan(expert_forward, 0, (expert_gate_up, expert_down, expert_inputs))[1]
    expert_result = forward_scan[0]
    gate_up_kept = forward_scan[1]
    branch_second = slot_pairs(
        expert_result.reshape(expert_count * CAP, model_width), plan_second
    ).reshape(row_count, 2, model_width)
    mixed_second = jnp.sum(gates_second[:, :, None] * branch_second, axis=1)
    added = lax.psum_scatter(
        mixed_second.astype(jnp.bfloat16), "grid", scatter_dimension=1, tiled=True
    ).astype(jnp.float32)
    own_residual = lax.dynamic_slice_in_dim(residual, grid_index * feature_slice, feature_slice, 1)
    layer_output = (own_residual + added).astype(jnp.bfloat16)
    grad_gate_part_second = jnp.sum(grad_out[:, None, :] * branch_second, axis=-1)

    def expert_backward(carried, pieces):
        gate_up_piece, down_piece, slot_rows, gate_up, grad_result = pieces
        gate_up_full, down_full = (
            lax.all_gather(gate_up_piece, "wide", axis=0, tiled=True),
            lax.all_gather(down_piece, "wide", axis=1, tiled=True),
        )
        gate_pre = gate_up[:, 0]
        up_pre = gate_up[:, 1]
        hidden_low = (jax.nn.silu(gate_pre) * up_pre).astype(jnp.bfloat16)
        grad_hidden = contract_last(grad_result, down_full)
        grad_down = contract_first(hidden_low, grad_result)
        grad_gate_up = swiglu_back(gate_pre, up_pre, grad_hidden)
        grad_weight = contract_first(slot_rows, grad_gate_up).reshape(model_width, 2, -1)
        grad_rows = contract_last(grad_gate_up, gate_up_full.reshape(model_width, -1))
        grad_weight_part, grad_down_part = (
            lax.psum_scatter(
                grad_weight.astype(jnp.bfloat16), "wide", scatter_dimension=0, tiled=True
            ).astype(jnp.float32),
            lax.psum_scatter(
                grad_down.astype(jnp.bfloat16), "wide", scatter_dimension=1, tiled=True
            ).astype(jnp.float32),
        )
        return (carried, (grad_weight_part, grad_down_part, grad_rows))

    weight_items = (expert_gate_up, expert_down)
    back_scan = lax.scan(
        expert_backward, 0, weight_items + (expert_inputs, gate_up_kept, grad_slots_second)
    )[1]
    expert_gate_up_grad = back_scan[0]
    expert_down_grad = back_scan[1]
    grad_slot_rows = back_scan[2]
    grad_hidden_second = (
        slot_pairs(grad_slot_rows.reshape(expert_count * CAP, model_width), plan_second)
        .reshape(row_count, 2, model_width)
        .sum(axis=1)
    )
    grad_hidden_second, grad_gate_second = (
        lax.psum(grad_hidden_second.astype(jnp.bfloat16), "grid").astype(jnp.float32),
        lax.psum(grad_gate_part_second.astype(jnp.bfloat16), "grid").astype(jnp.float32),
    )
    grad_logits_second = logits_grad(gates_second, grad_gate_second, choose_second)
    grad_router_second = jnp.dot(
        hidden_second.astype(jnp.float32).T, grad_logits_second, precision=lax.Precision.HIGHEST
    )
    grad_hidden_second = grad_hidden_second + jnp.dot(
        grad_logits_second, router_second.astype(jnp.float32).T, precision=lax.Precision.HIGHEST
    )
    grad_gain_second = jnp.sum(grad_hidden_second * normed_second, axis=0)
    grad_residual = grad_out + norm_back(
        grad_hidden_second, normed_second, inverse_second, gain_second
    )
    kv_back, query_back, out_back = (
        lax.all_gather(attention_kv, "wide", axis=0, tiled=True),
        lax.all_gather(attention_query, "wide", axis=1, tiled=True),
        lax.all_gather(attention_out, "wide", axis=3, tiled=True),
    )
    grad_branch_first = (gates_first[:, :, None] * grad_residual[:, None, :]).astype(jnp.bfloat16)
    grad_gate_part_first = jnp.sum(grad_residual[:, None, :] * branch_first, axis=-1)
    grad_out_slots = pair_slots(grad_branch_first.reshape(2 * row_count, -1), plan_first).reshape(
        expert_count, CAP, model_width
    )
    out_matrix = out_back.reshape(expert_count, -1, model_width)
    grad_out_weight = jnp.einsum(
        "ecf,ecm->efm", out_inputs, grad_out_slots, preferred_element_type=jnp.float32
    )
    grad_attended_slots = jnp.einsum(
        "ecm,efm->ecf", grad_out_slots, out_matrix, preferred_element_type=jnp.float32
    )
    grad_attended = slot_pairs(
        grad_attended_slots.reshape(expert_count * CAP, -1), plan_first
    ).astype(jnp.bfloat16)
    grad_attended_blocks = grad_attended.reshape(block_count, block_rows, 2, head_local, head_width)

    def backward_block(carried, pieces):
        query_block_rows, block_position, block_segment, block_gradient, block_logsum = pieces
        score_matrix = block_scores(query_block_rows, block_position, block_segment)
        attention_probabilities = jnp.exp(score_matrix - block_logsum[..., None])
        probabilities_reduced = attention_probabilities.astype(jnp.bfloat16)
        grad_values = carried[1] + jnp.einsum(
            "wipn,pwio->nio",
            probabilities_reduced,
            block_gradient,
            preferred_element_type=jnp.float32,
        )
        grad_chances = jnp.einsum(
            "jfeu,geu->fejg", block_gradient, gathered_values, preferred_element_type=jnp.float32
        )
        score_gradient = (
            attention_probabilities
            * (
                grad_chances
                - jnp.sum(attention_probabilities * grad_chances, axis=-1, keepdims=True)
            )
        ).astype(jnp.bfloat16)
        grad_query = (
            jnp.einsum(
                "jegf,feq->gjeq", score_gradient, gathered_keys, preferred_element_type=jnp.float32
            )
            * score_scaling
        )
        grad_keys = (
            carried[0]
            + jnp.einsum(
                "wipn,pwio->nio",
                score_gradient,
                query_block_rows,
                preferred_element_type=jnp.float32,
            )
            * score_scaling
        )
        return ((grad_keys, grad_values), grad_query)

    zero_keys = jnp.zeros(gathered_keys.shape, jnp.float32)
    (grad_keys, grad_values), grad_query = lax.scan(
        backward_block,
        (zero_keys, zero_keys),
        (query_blocks, position_blocks, segment_blocks, grad_attended_blocks, logsum),
    )
    grad_kv_all = jnp.stack([grad_keys, grad_values], axis=2)
    grad_kv = grad_kv_all[REACH * row_count :]
    for offset in range(REACH, 0, -1):
        begin_row = (REACH - offset) * row_count
        grad_kv = grad_kv + passed_along(
            grad_kv_all[begin_row : begin_row + row_count].astype(jnp.bfloat16), "wide", -offset
        ).astype(jnp.float32)
    grad_key_pre = rotate(grad_kv[:, :, 0], cosine[:, None, :], -sine_table[:, None, :])
    grad_kv_low = (
        jnp.stack([grad_key_pre, grad_kv[:, :, 1]], axis=2)
        .astype(jnp.bfloat16)
        .reshape(row_count, -1)
    )
    grad_query_pre = rotate(
        grad_query.reshape(row_count, 2, head_local, head_width),
        cosine[:, None, None, :],
        -sine_table[:, None, None, :],
    ).astype(jnp.bfloat16)
    grad_query_slots = pair_slots(grad_query_pre.reshape(2 * row_count, -1), plan_first).reshape(
        expert_count, CAP, -1
    )
    grad_query_weight = jnp.einsum(
        "ecm,ecf->emf", slot_inputs, grad_query_slots, preferred_element_type=jnp.float32
    )
    grad_input_slots = jnp.einsum(
        "ecf,emf->ecm",
        grad_query_slots,
        query_back.reshape(expert_count, model_width, -1),
        preferred_element_type=jnp.float32,
    )
    grad_hidden_first = (
        slot_pairs(grad_input_slots.reshape(expert_count * CAP, model_width), plan_first)
        .reshape(row_count, 2, model_width)
        .sum(axis=1)
    )
    grad_kv_weight = contract_first(hidden_first, grad_kv_low)
    grad_hidden_first = grad_hidden_first + contract_last(
        grad_kv_low, kv_back.reshape(model_width, -1)
    )
    grad_hidden_first, grad_gate_first = (
        lax.psum(grad_hidden_first.astype(jnp.bfloat16), "grid").astype(jnp.float32),
        lax.psum(grad_gate_part_first.astype(jnp.bfloat16), "grid").astype(jnp.float32),
    )
    grad_logits_first = logits_grad(gates_first, grad_gate_first, choose_first)
    grad_router_first = jnp.dot(
        hidden_first.astype(jnp.float32).T, grad_logits_first, precision=lax.Precision.HIGHEST
    )
    grad_hidden_first = grad_hidden_first + jnp.dot(
        grad_logits_first, router_first.astype(jnp.float32).T, precision=lax.Precision.HIGHEST
    )
    grad_gain_first = jnp.sum(grad_hidden_first * normed_first, axis=0)
    grad_inputs = grad_residual + norm_back(
        grad_hidden_first, normed_first, inverse_first, gain_first
    )
    input_grad = lax.dynamic_slice_in_dim(
        grad_inputs, grid_index * feature_slice, feature_slice, 1
    ).astype(jnp.bfloat16)
    summed = (
        lax.psum_scatter(
            grad_gain_first.astype(jnp.bfloat16), "wide", scatter_dimension=0, tiled=True
        ).astype(jnp.float32),
        lax.psum_scatter(
            grad_kv_weight.reshape(model_width, head_local, 2, head_width).astype(jnp.bfloat16),
            "wide",
            scatter_dimension=0,
            tiled=True,
        ).astype(jnp.float32),
        lax.psum_scatter(
            grad_query_weight.reshape(expert_count, model_width, head_local, head_width).astype(
                jnp.bfloat16
            ),
            "wide",
            scatter_dimension=1,
            tiled=True,
        ).astype(jnp.float32),
        lax.psum_scatter(
            grad_out_weight.reshape(expert_count, head_local, head_width, model_width).astype(
                jnp.bfloat16
            ),
            "wide",
            scatter_dimension=3,
            tiled=True,
        ).astype(jnp.float32),
        lax.psum_scatter(
            grad_router_first.astype(jnp.bfloat16), "wide", scatter_dimension=0, tiled=True
        ).astype(jnp.float32),
        lax.psum_scatter(
            grad_gain_second.astype(jnp.bfloat16), "wide", scatter_dimension=0, tiled=True
        ).astype(jnp.float32),
        lax.psum_scatter(
            grad_router_second.astype(jnp.bfloat16), "wide", scatter_dimension=0, tiled=True
        ).astype(jnp.float32),
    )
    return (
        layer_output,
        input_grad,
        summed[0],
        summed[1],
        summed[2],
        summed[3],
        summed[4],
        summed[5],
        summed[6],
        expert_gate_up_grad,
        expert_down_grad,
    )


def solution(mesh):
    in_specs = (
        P("wide", "grid"),
        P(),
        P("wide", None),
        P("wide", None),
        P("wide"),
        P("wide", "grid", None, None),
        P(None, "wide", "grid", None),
        P(None, "grid", None, "wide"),
        P("wide", None),
        P("wide"),
        P("wide", None),
        P(None, "wide", None, "grid"),
        P(None, "grid", "wide"),
        P("wide", "grid"),
    )
    out_specs = (
        P("wide", "grid"),
        P("wide", "grid"),
        P("wide"),
        P("wide", "grid", None, None),
        P(None, "wide", "grid", None),
        P(None, "grid", None, "wide"),
        P("wide", None),
        P("wide"),
        P("wide", None),
        P(None, "wide", None, "grid"),
        P(None, "grid", "wide"),
    )
    return jax.shard_map(
        per_device, mesh=mesh, in_specs=in_specs, out_specs=out_specs, check_vma=False
    )
```

profile of v0, /device:TPU:0, one launch (start us, length us, event | category | flops | bytes accessed | tf_op | source)
XLA Modules:
  0.0 5017.6 jit_solution(7606003074359579268)
XLA Ops:
  13.0 22.2 all-gather.4
  64.5 46.6 all-gather.26.cloned.1.call-done
  137.1 219.7 %all_gather.44 = bf16[2048,4]{0,1:T(4,128)(2,1)S(1)} all-gather(bf16[256,4]{0,1:T(4,128)(2,1)} %param.26), channel_id=1, replica_groups=mesh['wide'=8,'grid'=4] {'wide'}, dimensions={0}, use_global_device_ids=true | all-gather | bytes 18432 | tf_op jit(solution)/shard_map/all_gather | solution.py:148
  386.6 13.3 reshape.733
  416.4 20.6 fusion.145
  437.0 16.4 fusion.53
  453.4 18.2 fusion.84
  486.3 12.9 gather_fusion.3
  509.8 15.0 multiply_reduce_fusion.3
  529.4 46.4 all-gather.5
  576.8 26.0 all_gather.49
  612.1 10.9 mul.497
  646.5 13.6 gather_fusion.6
  674.1 1068.6 %while.4 = (s32[]{:T(128)}, f32[4,320,2048]{2,1,0:T(8,128)}, f32[4,320,2,1408]{3,2,1,0:T(2,128)}, bf16[4,320,2048]{2,1,0:T(8,128)(2,1)}, bf16[4,256,2,1408]{3,2,...) while((s32[]{:T(128)}, f32[4,320,2048]{2,1,0:T(8,128)}, f32[4,320,2,1408]{3,2,1,0:T(2,128)}, ...), condition=%wide.region_23.24_spmd, body=%wide.region_22.23_spmd.sunk | while | flops 5539184640 | bytes 157483216 | solution.py:284
  680.1 159.8 %all-gather.36.cloned.1.call-done = bf16[1,2048,2,1408]{3,2,0,1:T(2,128)(2,1)} async-done(((bf16[1,256,2,1408]{3,2,0,1:T(2,128)(2,1)}), bf16[1,2048,2,1408]{3,2,0,1:T(2,128)(2,1)}) %all-gather.36.cloned.1.call-update) | async-done | bytes 11534352 | tf_op jit(solution)/shard_map/while/body/eval_jaxpr/all_gather | solution.py:274
  874.6 59.9 %all-gather.34.cloned.1.call-done = bf16[1,1408,2048]{2,1,0:T(8,128)(2,1)} async-done(((bf16[1,1408,256]{2,1,0:T(8,128)(2,1)}), bf16[1,1408,2048]{2,1,0:T(8,128)(2,1)}) %all-gather.34.cloned.1.call-update) | async-done | bytes 5767184 | tf_op jit(solution)/shard_map/while/body/eval_jaxpr/all_gather | solution.py:275
  947.0 160.1 %all-gather.36.cloned.1.call-done = bf16[1,2048,2,1408]{3,2,0,1:T(2,128)(2,1)} async-done(((bf16[1,256,2,1408]{3,2,0,1:T(2,128)(2,1)}), bf16[1,2048,2,1408]{3,2,0,1:T(2,128)(2,1)}) %all-gather.36.cloned.1.call-update) | async-done | bytes 11534352 | tf_op jit(solution)/shard_map/while/body/eval_jaxpr/all_gather | solution.py:274
  1141.9 59.7 %all-gather.34.cloned.1.call-done = bf16[1,1408,2048]{2,1,0:T(8,128)(2,1)} async-done(((bf16[1,1408,256]{2,1,0:T(8,128)(2,1)}), bf16[1,1408,2048]{2,1,0:T(8,128)(2,1)}) %all-gather.34.cloned.1.call-update) | async-done | bytes 5767184 | tf_op jit(solution)/shard_map/while/body/eval_jaxpr/all_gather | solution.py:275
  1214.1 160.1 %all-gather.36.cloned.1.call-done = bf16[1,2048,2,1408]{3,2,0,1:T(2,128)(2,1)} async-done(((bf16[1,256,2,1408]{3,2,0,1:T(2,128)(2,1)}), bf16[1,2048,2,1408]{3,2,0,1:T(2,128)(2,1)}) %all-gather.36.cloned.1.call-update) | async-done | bytes 11534352 | tf_op jit(solution)/shard_map/while/body/eval_jaxpr/all_gather | solution.py:274
  1408.9 59.8 %all-gather.34.cloned.1.call-done = bf16[1,1408,2048]{2,1,0:T(8,128)(2,1)} async-done(((bf16[1,1408,256]{2,1,0:T(8,128)(2,1)}), bf16[1,1408,2048]{2,1,0:T(8,128)(2,1)}) %all-gather.34.cloned.1.call-update) | async-done | bytes 5767184 | tf_op jit(solution)/shard_map/while/body/eval_jaxpr/all_gather | solution.py:275
  1481.2 160.1 %all-gather.36.cloned.1.call-done = bf16[1,2048,2,1408]{3,2,0,1:T(2,128)(2,1)} async-done(((bf16[1,256,2,1408]{3,2,0,1:T(2,128)(2,1)}), bf16[1,2048,2,1408]{3,2,0,1:T(2,128)(2,1)}) %all-gather.36.cloned.1.call-update) | async-done | bytes 11534352 | tf_op jit(solution)/shard_map/while/body/eval_jaxpr/all_gather | solution.py:274
  1676.1 59.8 %all-gather.34.cloned.1.call-done = bf16[1,1408,2048]{2,1,0:T(8,128)(2,1)} async-done(((bf16[1,1408,256]{2,1,0:T(8,128)(2,1)}), bf16[1,1408,2048]{2,1,0:T(8,128)(2,1)}) %all-gather.34.cloned.1.call-update) | async-done | bytes 5767184 | tf_op jit(solution)/shard_map/while/body/eval_jaxpr/all_gather | solution.py:275
  1742.7 13.0 gather_fusion.5
  1771.5 2301.3 %while.5 = (s32[]{:T(128)}, f32[4,256,2,1408]{3,2,1,0:T(2,128)}, f32[4,1408,256]{2,1,0:T(8,128)}, f32[4,320,2048]{2,1,0:T(8,128)}, bf16[4,320,2048]{2,1,0:T(8,12...) while((s32[]{:T(128)}, f32[4,256,2,1408]{3,2,1,0:T(2,128)}, ...), condition=%wide.region_29.30_spmd, body=%wide.region_26.29_spmd.sunk | while | flops 11093057536 | bytes 218857776 | solution.py:323
  1790.0 76.8 %all-gather.38.cloned.1.call-done = bf16[1,1408,2048]{2,1,0:T(8,128)(2,1)} async-done(((bf16[1,1408,256]{2,1,0:T(8,128)(2,1)}), bf16[1,1408,2048]{2,1,0:T(8,128)(2,1)}) %all-gather.38.cloned.1.call-update) | async-done | bytes 5767184 | tf_op jit(solution)/shard_map/while/body/eval_jaxpr/all_gather | solution.py:302
  1884.2 95.2 %reduce-scatter.30.cloned.1.call-done = bf16[1408,256]{1,0:T(8,128)(2,1)} async-done(((bf16[1408,2048]{1,0:T(8,128)(2,1)}), bf16[1408,256]{1,0:T(8,128)(2,1)}) %reduce-scatter.30.cloned.1.call-update) | async-done | bytes 720912 | tf_op jit(solution)/shard_map/while/body/eval_jaxpr/reduce_scatter | solution.py:316
  1981.7 164.0 %all-gather.40.cloned.1.call-done = bf16[1,2048,2,1408]{3,1,2,0:T(8,128)(2,1)} async-done(((bf16[1,256,2,1408]{3,1,2,0:T(8,128)(2,1)}), bf16[1,2048,2,1408]{3,1,2,0:T(8,128)(2,1)}) %all-gather.40.cloned.1.call-update) | async-done | bytes 11534352 | tf_op jit(solution)/shard_map/while/body/eval_jaxpr/all_gather | solution.py:301
  2154.5 186.0 %reduce-scatter.28.cloned.1.call-done = bf16[256,2,1408]{2,0,1:T(8,128)(2,1)} async-done(((bf16[2048,2,1408]{2,0,1:T(8,128)(2,1)}), bf16[256,2,1408]{2,0,1:T(8,128)(2,1)}) %reduce-scatter.28.cloned.1.call-update) | async-done | bytes 1441808 | tf_op jit(solution)/shard_map/while/body/eval_jaxpr/reduce_scatter | solution.py:313
  2364.0 78.2 %all-gather.38.cloned.1.call-done = bf16[1,1408,2048]{2,1,0:T(8,128)(2,1)} async-done(((bf16[1,1408,256]{2,1,0:T(8,128)(2,1)}), bf16[1,1408,2048]{2,1,0:T(8,128)(2,1)}) %all-gather.38.cloned.1.call-update) | async-done | bytes 5767184 | tf_op jit(solution)/shard_map/while/body/eval_jaxpr/all_gather | solution.py:302
  2459.5 95.2 %reduce-scatter.30.cloned.1.call-done = bf16[1408,256]{1,0:T(8,128)(2,1)} async-done(((bf16[1408,2048]{1,0:T(8,128)(2,1)}), bf16[1408,256]{1,0:T(8,128)(2,1)}) %reduce-scatter.30.cloned.1.call-update) | async-done | bytes 720912 | tf_op jit(solution)/shard_map/while/body/eval_jaxpr/reduce_scatter | solution.py:316
  2557.1 164.2 %all-gather.40.cloned.1.call-done = bf16[1,2048,2,1408]{3,1,2,0:T(8,128)(2,1)} async-done(((bf16[1,256,2,1408]{3,1,2,0:T(8,128)(2,1)}), bf16[1,2048,2,1408]{3,1,2,0:T(8,128)(2,1)}) %all-gather.40.cloned.1.call-update) | async-done | bytes 11534352 | tf_op jit(solution)/shard_map/while/body/eval_jaxpr/all_gather | solution.py:301
  2729.9 186.2 %reduce-scatter.28.cloned.1.call-done = bf16[256,2,1408]{2,0,1:T(8,128)(2,1)} async-done(((bf16[2048,2,1408]{2,0,1:T(8,128)(2,1)}), bf16[256,2,1408]{2,0,1:T(8,128)(2,1)}) %reduce-scatter.28.cloned.1.call-update) | async-done | bytes 1441808 | tf_op jit(solution)/shard_map/while/body/eval_jaxpr/reduce_scatter | solution.py:313
  2939.7 78.2 %all-gather.38.cloned.1.call-done = bf16[1,1408,2048]{2,1,0:T(8,128)(2,1)} async-done(((bf16[1,1408,256]{2,1,0:T(8,128)(2,1)}), bf16[1,1408,2048]{2,1,0:T(8,128)(2,1)}) %all-gather.38.cloned.1.call-update) | async-done | bytes 5767184 | tf_op jit(solution)/shard_map/while/body/eval_jaxpr/all_gather | solution.py:302
  3035.2 95.2 %reduce-scatter.30.cloned.1.call-done = bf16[1408,256]{1,0:T(8,128)(2,1)} async-done(((bf16[1408,2048]{1,0:T(8,128)(2,1)}), bf16[1408,256]{1,0:T(8,128)(2,1)}) %reduce-scatter.30.cloned.1.call-update) | async-done | bytes 720912 | tf_op jit(solution)/shard_map/while/body/eval_jaxpr/reduce_scatter | solution.py:316
  3132.7 164.2 %all-gather.40.cloned.1.call-done = bf16[1,2048,2,1408]{3,1,2,0:T(8,128)(2,1)} async-done(((bf16[1,256,2,1408]{3,1,2,0:T(8,128)(2,1)}), bf16[1,2048,2,1408]{3,1,2,0:T(8,128)(2,1)}) %all-gather.40.cloned.1.call-update) | async-done | bytes 11534352 | tf_op jit(solution)/shard_map/while/body/eval_jaxpr/all_gather | solution.py:301
  3305.6 186.1 %reduce-scatter.28.cloned.1.call-done = bf16[256,2,1408]{2,0,1:T(8,128)(2,1)} async-done(((bf16[2048,2,1408]{2,0,1:T(8,128)(2,1)}), bf16[256,2,1408]{2,0,1:T(8,128)(2,1)}) %reduce-scatter.28.cloned.1.call-update) | async-done | bytes 1441808 | tf_op jit(solution)/shard_map/while/body/eval_jaxpr/reduce_scatter | solution.py:313
  3515.2 77.9 %all-gather.38.cloned.1.call-done = bf16[1,1408,2048]{2,1,0:T(8,128)(2,1)} async-done(((bf16[1,1408,256]{2,1,0:T(8,128)(2,1)}), bf16[1,1408,2048]{2,1,0:T(8,128)(2,1)}) %all-gather.38.cloned.1.call-update) | async-done | bytes 5767184 | tf_op jit(solution)/shard_map/while/body/eval_jaxpr/all_gather | solution.py:302
  3610.4 95.4 %reduce-scatter.30.cloned.1.call-done = bf16[1408,256]{1,0:T(8,128)(2,1)} async-done(((bf16[1408,2048]{1,0:T(8,128)(2,1)}), bf16[1408,256]{1,0:T(8,128)(2,1)}) %reduce-scatter.30.cloned.1.call-update) | async-done | bytes 720912 | tf_op jit(solution)/shard_map/while/body/eval_jaxpr/reduce_scatter | solution.py:316
  3708.1 164.2 %all-gather.40.cloned.1.call-done = bf16[1,2048,2,1408]{3,1,2,0:T(8,128)(2,1)} async-done(((bf16[1,256,2,1408]{3,1,2,0:T(8,128)(2,1)}), bf16[1,2048,2,1408]{3,1,2,0:T(8,128)(2,1)}) %all-gather.40.cloned.1.call-update) | async-done | bytes 11534352 | tf_op jit(solution)/shard_map/while/body/eval_jaxpr/all_gather | solution.py:301
  3881.0 186.1 %reduce-scatter.28.cloned.1.call-done = bf16[256,2,1408]{2,0,1:T(8,128)(2,1)} async-done(((bf16[2048,2,1408]{2,0,1:T(8,128)(2,1)}), bf16[256,2,1408]{2,0,1:T(8,128)(2,1)}) %reduce-scatter.28.cloned.1.call-update) | async-done | bytes 1441808 | tf_op jit(solution)/shard_map/while/body/eval_jaxpr/reduce_scatter | solution.py:313
  4072.9 12.9 gather_fusion.7
  4085.8 10.6 reshape.743
  4096.4 12.8 reduce_sum.235
  4109.4 19.4 multiply_reduce_fusion.1
  4138.0 22.0 all-reduce.10.cloned.1.call-done
  4186.9 10.9 mul.511
  4203.7 13.6 gather_fusion.8
  4230.5 28.0 fusion.50
  4258.5 33.7 fusion.52
  4292.2 12.3 multiply_bitcast_fusion
  4304.5 12.4 fusion.60
  4317.0 17.6 fusion.61
  4359.8 11.7 fusion.86
  4372.4 12.9 gather_fusion.11
  4385.3 10.7 reshape.746
  4397.0 13.4 reduce_sum.241
  4410.7 82.4 %collective-permute-done.4 = bf16[512,4,2,128]{0,3,1,2:T(8,128)(2,1)} collective-permute-done((bf16[512,4,2,128]{0,3,1,2:T(8,128)(2,1)}, bf16[512,4,2,128]{0,3,1,2:T(8,128)(2,1)}, u32[]{:S(2)}, u32[]{:S(2)}) %collective-permute-start.4) | collective-permute-done | bytes 1048608 | tf_op jit(solution)/shard_map/ppermute | solution.py:21
  4518.1 14.7 copy.241
  4532.8 14.6 reshape.904
  4564.1 12.9 all-reduce.12.cloned.1.call-done
  4583.5 21.6 all-reduce.3
  4614.2 89.1 %reduce-scatter.18.cloned.1.call-done = bf16[256,4,2,128]{3,0,2,1:T(8,128)(2,1)} async-done(((bf16[2048,4,2,128]{3,0,2,1:T(8,128)(2,1)}), bf16[256,4,2,128]{3,0,2,1:T(8,128)(2,1)}) %reduce-scatter.18.cloned.1.call-update) | async-done | bytes 524304 | tf_op jit(solution)/shard_map/reduce_scatter | solution.py:477
  4705.9 150.2 %reduce-scatter.22.cloned.1.call-done = bf16[256,2048]{1,0:T(8,128)(2,1)} async-done(((bf16[2048,2048]{1,0:T(8,128)(2,1)}), bf16[256,2048]{1,0:T(8,128)(2,1)}) %reduce-scatter.22.cloned.1.call-update) | async-done | bytes 1048592
  4859.4 148.7 %reduce-scatter.20.cloned.1.call-done = bf16[4,4,128,256]{3,2,1,0:T(8,128)(2,1)} async-done(((bf16[4,4,128,2048]{3,2,1,0:T(8,128)(2,1)}), bf16[4,4,128,256]{3,2,1,0:T(8,128)(2,1)}) %reduce-scatter.20.cloned.1.call-update) | async-done | bytes 1048592 | tf_op jit(solution)/shard_map/reduce_scatter | solution.py:491
  (528 shorter events, 743.5 us)
Async XLA Ops:
  7.2 41.4 copy-start.67
  7.2 51.1 %all-gather.24.cloned.1.call-start = ((), (), s32[]{:S(2)}) async-start(), calls=%async_computation.8 | async-start | bytes 2621440 | tf_op jit(solution)/shard_map/all_gather | solution.py:144
  8.0 103.2 %all-gather.26.cloned.1.call-start = ((), (), s32[]{:S(2)}) async-start(), calls=%async_computation.9 | async-start | bytes 4718592 | tf_op jit(solution)/shard_map/all_gather | solution.py:151
  9.9 376.6 %all-gather.28.cloned.1.call-start = ((), (), s32[]{:S(2)}) async-start(), calls=%async_computation.10 | async-start | bytes 9437184 | tf_op jit(solution)/shard_map/all_gather | solution.py:152
  10.7 466.0 %all-gather.30.cloned.1.call-start = ((), (), s32[]{:S(2)}) async-start(), calls=%async_computation.11 | async-start | bytes 9437184 | tf_op jit(solution)/shard_map/all_gather | solution.py:153
  11.3 592.3 %all-gather.32.cloned.1.call-start = ((), (), s32[]{:S(2)}) async-start(), calls=%async_computation.14 | async-start | bytes 2621440 | tf_op jit(solution)/shard_map/all_gather | solution.py:265
  11.8 616.0 %all-reduce.8.cloned.1.call-start = ((), (), s32[]{:S(2)}) async-start(), calls=%async_computation.12 | async-start | bytes 4194304 | tf_op jit(solution)/shard_map/psum | solution.py:258
  48.6 437.6 %copy-start.40 = (s32[1024]{0:T(1024)}, s32[1024]{0:T(1024)S(1)}, u32[]{:S(2)}) copy-start(s32[1024]{0:T(1024)S(1)} %get-tuple-element.363) | copy-start | bytes 12292
  54.9 81.2 %copy-start.23 = (f32[512,64]{0,1:T(8,128)}, f32[512,64]{0,1:T(8,128)S(1)}, u32[]{:S(2)}) copy-start(f32[512,64]{0,1:T(8,128)S(1)} %get-tuple-element.352) | copy-start | bytes 393220
  64.5 300.8 %copy-start = (bf16[512,2048]{1,0:T(8,128)(2,1)}, bf16[512,2048]{1,0:T(8,128)(2,1)S(1)}, u32[]{:S(2)}) copy-start(bf16[512,2048]{1,0:T(8,128)(2,1)S(1)} %get-tuple-element.339) | copy-start | bytes 6291460
  123.6 243.3 %collective-permute-start = (bf16[512,4,2,128]{0,3,2,1:T(8,128)(2,1)}, bf16[512,4,2,128]{0,3,2,1:T(8,128)(2,1)}, u32[]{:S(2)}, u32[]{:S(2)}) collective-permute-start(bf16[512,4,2,128]{0,3,2,1:T(8,128)(2,1)} %pad_maximum_fusion.1), channel_id=1, source_target_pairs={{0,16},{4,20},{8,24},{12,28},{1,17},{5,21},{9,25},{13,29},{2,18},{... | collective-permute-start | bytes 3145736 | tf_op jit(solution)/shard_map/ppermute | solution.py:21
  128.3 240.9 %collective-permute-start.1 = (bf16[512,4,2,128]{0,3,2,1:T(8,128)(2,1)}, bf16[512,4,2,128]{0,3,2,1:T(8,128)(2,1)}, u32[]{:S(2)}, u32[]{:S(2)}) collective-permute-start(bf16[512,4,2,128]{0,3,2,1:T(8,128)(2,1)} %pad_maximum_fusion.1), channel_id=1, source_target_pairs={{0,12},{4,16},{8,20},{12,24},{16,28},{1,13},{5,17},{9,21},{13,25},... | collective-permute-start | bytes 3145736 | tf_op jit(solution)/shard_map/ppermute | solution.py:21
  132.4 340.1 %copy-start.36 = (s32[2048]{0:T(1024)}, s32[2048]{0:T(1024)S(1)}, u32[]{:S(2)}) copy-start(s32[2048]{0:T(1024)S(1)} %get-tuple-element.361) | copy-start | bytes 24580
  132.4 239.1 %collective-permute-start.2 = (bf16[512,4,2,128]{0,3,2,1:T(8,128)(2,1)}, bf16[512,4,2,128]{0,3,2,1:T(8,128)(2,1)}, u32[]{:S(2)}, u32[]{:S(2)}) collective-permute-start(bf16[512,4,2,128]{0,3,2,1:T(8,128)(2,1)} %pad_maximum_fusion.1), channel_id=1, source_target_pairs={{0,8},{4,12},{8,16},{12,20},{16,24},{20,28},{1,9},{5,13},{9,17},{1... | collective-permute-start | bytes 3145736 | tf_op jit(solution)/shard_map/ppermute | solution.py:21
  136.3 279.2 %copy-start.20 = (f32[512,64]{1,0:T(8,128)}, f32[512,64]{1,0:T(8,128)S(1)}, u32[]{:S(2)}) copy-start(f32[512,64]{1,0:T(8,128)S(1)} %copy.189) | copy-start | bytes 393220
  137.1 339.6 %copy-start.38 = (pred[4,320]{1,0:T(4,128)(4,1)}, pred[4,320]{1,0:T(4,128)(4,1)S(1)}, u32[]{:S(2)}) copy-start(pred[4,320]{1,0:T(4,128)(4,1)S(1)} %broadcast_in_dim.211) | copy-start | bytes 3844
  363.0 20.1 collective-permute-start.3
  509.8 66.2 %copy-start.25 = (f32[512,64]{0,1:T(8,128)S(1)}, f32[512,64]{0,1:T(8,128)}, u32[]{:S(2)}) copy-start(f32[512,64]{0,1:T(8,128)} %get-tuple-element.350) | copy-start | bytes 393220
  509.8 67.0 %copy-start.76 = (bf16[256,4]{0,1:T(4,128)(2,1)S(1)}, bf16[256,4]{0,1:T(4,128)(2,1)}, u32[]{:S(2)}) copy-start(bf16[256,4]{0,1:T(4,128)(2,1)} %param.28) | copy-start | bytes 6148
  509.8 93.0 %copy-start.60 = (s32[1280]{0:T(1024)S(1)}, s32[1280]{0:T(1024)}, u32[]{:S(2)}) copy-start(s32[1280]{0:T(1024)} %get-tuple-element.347) | copy-start | bytes 15364
  575.8 54.6 %copy-start.42 = (f32[8,1,256]{2,1,0:T(1,128)}, f32[8,1,256]{2,1,0:T(1,128)S(1)}, u32[]{:S(2)}) copy-start(f32[8,1,256]{2,1,0:T(1,128)S(1)} %convert_element_type.294) | copy-start | bytes 24580
  674.1 1068.6 %copy-start.57 = (s32[1024]{0:T(1024)S(1)}, s32[1024]{0:T(1024)}, u32[]{:S(2)}) copy-start(s32[1024]{0:T(1024)} %get-tuple-element.362) | copy-start | bytes 12292
  674.5 165.4 %all-gather.36.cloned.1.call-start = ((), (), s32[]{:S(2)}) async-start(), calls=%async_computation.23 | async-start | bytes 12976128 | tf_op jit(solution)/shard_map/while/body/eval_jaxpr/all_gather | solution.py:274
  678.0 256.5 %all-gather.34.cloned.1.call-start = ((), (), s32[]{:S(2)}) async-start(), calls=%async_computation.22 | async-start | bytes 6488064 | tf_op jit(solution)/shard_map/while/body/eval_jaxpr/all_gather | solution.py:275
  941.5 165.7 %all-gather.36.cloned.1.call-start = ((), (), s32[]{:S(2)}) async-start(), calls=%async_computation.23 | async-start | bytes 12976128 | tf_op jit(solution)/shard_map/while/body/eval_jaxpr/all_gather | solution.py:274
  944.9 256.7 %all-gather.34.cloned.1.call-start = ((), (), s32[]{:S(2)}) async-start(), calls=%async_computation.22 | async-start | bytes 6488064 | tf_op jit(solution)/shard_map/while/body/eval_jaxpr/all_gather | solution.py:275
  1208.6 165.7 %all-gather.36.cloned.1.call-start = ((), (), s32[]{:S(2)}) async-start(), calls=%async_computation.23 | async-start | bytes 12976128 | tf_op jit(solution)/shard_map/while/body/eval_jaxpr/all_gather | solution.py:274
  1212.0 256.7 %all-gather.34.cloned.1.call-start = ((), (), s32[]{:S(2)}) async-start(), calls=%async_computation.22 | async-start | bytes 6488064 | tf_op jit(solution)/shard_map/while/body/eval_jaxpr/all_gather | solution.py:275
  1475.7 165.7 %all-gather.36.cloned.1.call-start = ((), (), s32[]{:S(2)}) async-start(), calls=%async_computation.23 | async-start | bytes 12976128 | tf_op jit(solution)/shard_map/while/body/eval_jaxpr/all_gather | solution.py:274
  1479.1 256.7 %all-gather.34.cloned.1.call-start = ((), (), s32[]{:S(2)}) async-start(), calls=%async_computation.22 | async-start | bytes 6488064 | tf_op jit(solution)/shard_map/while/body/eval_jaxpr/all_gather | solution.py:275
  1771.5 2301.3 %copy-start.58 = (s32[1024]{0:T(1024)S(1)}, s32[1024]{0:T(1024)}, u32[]{:S(2)}) copy-start(s32[1024]{0:T(1024)} %get-tuple-element.362) | copy-start | bytes 12292
  1771.7 95.2 %all-gather.38.cloned.1.call-start = ((), (), s32[]{:S(2)}) async-start(), calls=%async_computation.24 | async-start | bytes 6488064 | tf_op jit(solution)/shard_map/while/body/eval_jaxpr/all_gather | solution.py:302
  1773.8 205.6 %reduce-scatter.30.cloned.1.call-start = ((), (), s32[]{:S(2)}) async-start(), calls=%async_computation.26 | async-start | bytes 6488064 | tf_op jit(solution)/shard_map/while/body/eval_jaxpr/reduce_scatter | solution.py:316
  1786.3 359.4 %all-gather.40.cloned.1.call-start = ((), (), s32[]{:S(2)}) async-start(), calls=%async_computation.27 | async-start | bytes 12976128 | tf_op jit(solution)/shard_map/while/body/eval_jaxpr/all_gather | solution.py:301
  1790.0 550.5 %reduce-scatter.28.cloned.1.call-start = ((), (), s32[]{:S(2)}) async-start(), calls=%async_computation.25 | async-start | bytes 12976128 | tf_op jit(solution)/shard_map/while/body/eval_jaxpr/reduce_scatter | solution.py:313
  2345.8 96.4 %all-gather.38.cloned.1.call-start = ((), (), s32[]{:S(2)}) async-start(), calls=%async_computation.24 | async-start | bytes 6488064 | tf_op jit(solution)/shard_map/while/body/eval_jaxpr/all_gather | solution.py:302
  2347.9 206.9 %reduce-scatter.30.cloned.1.call-start = ((), (), s32[]{:S(2)}) async-start(), calls=%async_computation.26 | async-start | bytes 6488064 | tf_op jit(solution)/shard_map/while/body/eval_jaxpr/reduce_scatter | solution.py:316
  2360.3 360.9 %all-gather.40.cloned.1.call-start = ((), (), s32[]{:S(2)}) async-start(), calls=%async_computation.27 | async-start | bytes 12976128 | tf_op jit(solution)/shard_map/while/body/eval_jaxpr/all_gather | solution.py:301
  2364.0 552.2 %reduce-scatter.28.cloned.1.call-start = ((), (), s32[]{:S(2)}) async-start(), calls=%async_computation.25 | async-start | bytes 12976128 | tf_op jit(solution)/shard_map/while/body/eval_jaxpr/reduce_scatter | solution.py:313
  2921.5 96.4 %all-gather.38.cloned.1.call-start = ((), (), s32[]{:S(2)}) async-start(), calls=%async_computation.24 | async-start | bytes 6488064 | tf_op jit(solution)/shard_map/while/body/eval_jaxpr/all_gather | solution.py:302
  2923.6 206.9 %reduce-scatter.30.cloned.1.call-start = ((), (), s32[]{:S(2)}) async-start(), calls=%async_computation.26 | async-start | bytes 6488064 | tf_op jit(solution)/shard_map/while/body/eval_jaxpr/reduce_scatter | solution.py:316
  2936.0 360.9 %all-gather.40.cloned.1.call-start = ((), (), s32[]{:S(2)}) async-start(), calls=%async_computation.27 | async-start | bytes 12976128 | tf_op jit(solution)/shard_map/while/body/eval_jaxpr/all_gather | solution.py:301
  2939.7 552.0 %reduce-scatter.28.cloned.1.call-start = ((), (), s32[]{:S(2)}) async-start(), calls=%async_computation.25 | async-start | bytes 12976128 | tf_op jit(solution)/shard_map/while/body/eval_jaxpr/reduce_scatter | solution.py:313
  3497.0 96.1 %all-gather.38.cloned.1.call-start = ((), (), s32[]{:S(2)}) async-start(), calls=%async_computation.24 | async-start | bytes 6488064 | tf_op jit(solution)/shard_map/while/body/eval_jaxpr/all_gather | solution.py:302
  3499.1 206.7 %reduce-scatter.30.cloned.1.call-start = ((), (), s32[]{:S(2)}) async-start(), calls=%async_computation.26 | async-start | bytes 6488064 | tf_op jit(solution)/shard_map/while/body/eval_jaxpr/reduce_scatter | solution.py:316
  3511.5 360.8 %all-gather.40.cloned.1.call-start = ((), (), s32[]{:S(2)}) async-start(), calls=%async_computation.27 | async-start | bytes 12976128 | tf_op jit(solution)/shard_map/while/body/eval_jaxpr/all_gather | solution.py:301
  3515.2 551.9 %reduce-scatter.28.cloned.1.call-start = ((), (), s32[]{:S(2)}) async-start(), calls=%async_computation.25 | async-start | bytes 12976128 | tf_op jit(solution)/shard_map/while/body/eval_jaxpr/reduce_scatter | solution.py:313
  4072.8 87.2 %all-reduce.10.cloned.1.call-start = ((), (), s32[]{:S(2)}) async-start(), calls=%async_computation.15 | async-start | bytes 4194304 | tf_op jit(solution)/shard_map/psum | solution.py:335
  4109.3 50.7 %copy-start.43 = (f32[8,1,256]{2,1,0:T(1,128)S(1)}, f32[8,1,256]{2,1,0:T(1,128)}, u32[]{:S(2)}) copy-start(f32[8,1,256]{2,1,0:T(1,128)} %copy-done.42) | copy-start | bytes 24580
  4109.3 50.7 %copy-start.47 = (bf16[2048,4]{0,1:T(4,128)(2,1)S(1)}, bf16[2048,4]{0,1:T(4,128)(2,1)}, u32[]{:S(2)}) copy-start(bf16[2048,4]{0,1:T(4,128)(2,1)} %copy-done.46) | copy-start | bytes 49156
  4109.3 50.7 %copy-start.69 = (f32[512]{0:T(512)S(1)}, f32[512]{0:T(512)}, u32[]{:S(2)}) copy-start(f32[512]{0:T(512)} %copy-done.68) | copy-start | bytes 6148
  4109.3 451.8 %reduce-scatter.26.cloned.1.call-start = ((), (), s32[]{:S(2)}) async-start(), calls=%async_computation.21 | async-start | bytes 589824
  4137.9 424.7 %reduce-scatter.24.cloned.1.call-start = ((), (), s32[]{:S(2)}) async-start(), calls=%async_computation.20 | async-start | bytes 589824
  4347.6 63.0 %collective-permute-start.7 = (bf16[512,4,2,128]{0,3,1,2:T(8,128)(2,1)}, bf16[512,4,2,128]{0,3,1,2:T(8,128)(2,1)}, u32[]{:S(2)}, u32[]{:S(2)}) collective-permute-start(bf16[512,4,2,128]{0,3,1,2:T(8,128)(2,1)} %get-tuple-element.329), channel_id=1, source_target_pairs={{4,0},{8,4},{12,8},{16,12},{20,16},{24,20},{28,24},{5,1},{9,5},{13... | collective-permute-start | bytes 3145736 | tf_op jit(solution)/shard_map/ppermute | solution.py:21
  4348.9 61.8 %collective-permute-start.6 = (bf16[512,4,2,128]{0,3,1,2:T(8,128)(2,1)}, bf16[512,4,2,128]{0,3,1,2:T(8,128)(2,1)}, u32[]{:S(2)}, u32[]{:S(2)}) collective-permute-start(bf16[512,4,2,128]{0,3,1,2:T(8,128)(2,1)} %get-tuple-element.330), channel_id=1, source_target_pairs={{8,0},{12,4},{16,8},{20,12},{24,16},{28,20},{9,1},{13,5},{17,9},{2... | collective-permute-start | bytes 3145736 | tf_op jit(solution)/shard_map/ppermute | solution.py:21
  4350.2 60.5 %collective-permute-start.5 = (bf16[512,4,2,128]{0,3,1,2:T(8,128)(2,1)}, bf16[512,4,2,128]{0,3,1,2:T(8,128)(2,1)}, u32[]{:S(2)}, u32[]{:S(2)}) collective-permute-start(bf16[512,4,2,128]{0,3,1,2:T(8,128)(2,1)} %get-tuple-element.331), channel_id=1, source_target_pairs={{12,0},{16,4},{20,8},{24,12},{28,16},{13,1},{17,5},{21,9},{25,13},... | collective-permute-start | bytes 3145736 | tf_op jit(solution)/shard_map/ppermute | solution.py:21
  4351.5 141.6 %collective-permute-start.4 = (bf16[512,4,2,128]{0,3,1,2:T(8,128)(2,1)}, bf16[512,4,2,128]{0,3,1,2:T(8,128)(2,1)}, u32[]{:S(2)}, u32[]{:S(2)}) collective-permute-start(bf16[512,4,2,128]{0,3,1,2:T(8,128)(2,1)} %get-tuple-element.328), channel_id=1, source_target_pairs={{16,0},{20,4},{24,8},{28,12},{17,1},{21,5},{25,9},{29,13},{18,2},{... | collective-permute-start | bytes 3145736 | tf_op jit(solution)/shard_map/ppermute | solution.py:21
  4410.4 86.6 %copy-start.24 = (f32[512,64]{0,1:T(8,128)S(1)}, f32[512,64]{0,1:T(8,128)}, u32[]{:S(2)}) copy-start(f32[512,64]{0,1:T(8,128)} %copy-done.23) | copy-start | bytes 393220
  4410.4 166.6 %all-reduce.12.cloned.1.call-start = ((), (), s32[]{:S(2)}) async-start(), calls=%async_computation.16 | async-start | bytes 4194304 | tf_op jit(solution)/shard_map/psum | solution.py:456
  4410.6 86.4 %copy-start.26 = (f32[512,64]{0,1:T(8,128)S(1)}, f32[512,64]{0,1:T(8,128)}, u32[]{:S(2)}) copy-start(f32[512,64]{0,1:T(8,128)} %get-tuple-element.350) | copy-start | bytes 393220
  4503.3 108.6 %reduce-scatter.16.cloned.1.call-start = ((), (), s32[]{:S(2)}) async-start(), calls=%async_computation.13 | async-start | bytes 2621440 | tf_op jit(solution)/shard_map/reduce_scatter | solution.py:291
  4504.0 199.3 %reduce-scatter.18.cloned.1.call-start = ((), (), s32[]{:S(2)}) async-start(), calls=%async_computation.17 | async-start | bytes 4718592 | tf_op jit(solution)/shard_map/reduce_scatter | solution.py:477
  4509.2 346.8 %reduce-scatter.22.cloned.1.call-start = ((), (), s32[]{:S(2)}) async-start(), calls=%async_computation.19 | async-start | bytes 9437184
  4547.4 460.7 %reduce-scatter.20.cloned.1.call-start = ((), (), s32[]{:S(2)}) async-start(), calls=%async_computation.18 | async-start | bytes 9437184 | tf_op jit(solution)/shard_map/reduce_scatter | solution.py:491
  (70 other events, 763.4 us)
Sparse Core Ops, SparseCore 0:
  9.6 25.2 all-gather.23
  37.7 73.3 all-gather.25
  113.3 182.1 all-gather.27
  297.4 171.9 all-gather.29
  470.8 20.9 all-gather.31
  525.0 83.0 all-reduce.7
  678.3 161.5 all-gather.35
  842.8 91.7 all-gather.33
  945.3 161.8 all-gather.35
  1109.8 91.7 all-gather.33
  1212.4 161.8 all-gather.35
  1376.9 91.7 all-gather.33
  1479.5 161.8 all-gather.35
  1644.0 91.7 all-gather.33
  1775.0 91.7 all-gather.37
  1870.8 108.5 reduce-scatter.29
  1982.2 163.4 all-gather.39
  2149.6 190.8 reduce-scatter.27
  2349.5 92.6 all-gather.37
  2446.2 108.5 reduce-scatter.29
  2557.8 163.4 all-gather.39
  2725.3 190.8 reduce-scatter.27
  2925.2 92.6 all-gather.37
  3021.8 108.5 reduce-scatter.29
  3133.4 163.4 all-gather.39
  3300.8 190.8 reduce-scatter.27
  3500.4 92.6 all-gather.37
  3597.2 108.5 reduce-scatter.29
  3708.8 163.4 all-gather.39
  3876.1 190.8 reduce-scatter.27
  4109.3 50.5 all-reduce.9
  4163.3 61.9 reduce-scatter.25
  4410.5 113.1 reduce-scatter.23
  4526.7 50.3 all-reduce.11
  4580.3 31.4 reduce-scatter.15
  4615.3 87.9 reduce-scatter.17
  4707.2 148.7 reduce-scatter.21
  4859.7 148.3 reduce-scatter.19
where the time goes:
time: 5030 us; the launch traced here: 5020 us
  waiting for transfers between devices  3540 us (70%)
  local copies, waits for them, and re-layouts  497 us (10%)
  matrix products  385 us (8%)
  blocking collectives  349 us (7%)
  other arithmetic  210 us (4%)
    reduce_scatter x4, waiting for transfers between devices, expert_backward(): lax.psum_scatter(grad_weight.astype(jnp.bfloat16), 'wide', scatter_dimens...  744 us
    all_gather x4, waiting for transfers between devices, expert_backward(): lax.all_gather(gate_up_piece, 'wide', axis=0, tiled=True)  657 us
    all_gather x4, waiting for transfers between devices, expert_forward(): lax.all_gather(gate_up_piece, 'wide', axis=0, tiled=True)  640 us
    reduce_scatter x4, waiting for transfers between devices, expert_backward(): lax.psum_scatter(grad_down.astype(jnp.bfloat16), 'wide', scatter_dimensio...  381 us
    all_gather x4, waiting for transfers between devices, expert_backward(): lax.all_gather(down_piece, 'wide', axis=1, tiled=True)  311 us
    all_gather x4, waiting for transfers between devices, expert_forward(): lax.all_gather(down_piece, 'wide', axis=1, tiled=True)  239 us
    all_gather x1, blocking collectives, per_device(): lax.all_gather(attention_router, 'wide', axis=0, tiled=True)  220 us
    unnamed x17, waiting for transfers between devices  153 us
  transfers between devices with their start and end apart: 46, of which 33 were waited for; matrix products, arithmetic and copies ran while one was open for 18% of the time, Pallas kernels for 0%

commit v1 on v0

v1 whole, which is shorter than its diff:
```python
import functools
import math

import jax
import jax.numpy as jnp
from jax import lax
from jax.experimental import pallas as pl
from jax.experimental.pallas import tpu as pltpu
from jax.sharding import Mesh, PartitionSpec as P

CAP = 320
PLANES = 4
HALVES = 2
BLOCKS = PLANES * HALVES
EPSILON = 1e-05
ROPE_BASE = 10000.0
NEGATIVE = -1e30
BF16 = jnp.bfloat16
F32 = jnp.float32
PLACES = ("z", "x")
VMEM_BYTES = 56 * 1024 * 1024


def rope_tables(positions, table_width):
    half_width = table_width // 2
    frequency = ROPE_BASE ** (-jnp.arange(half_width, dtype=F32) / half_width)
    angles = positions.astype(F32)[:, None] * frequency[None, :]
    return (jnp.cos(angles), jnp.sin(angles))


def rotate(values, cosine, sine_table):
    half_width = values.shape[-1] // 2
    leading = values[..., :half_width]
    trailing = values[..., half_width:]
    return jnp.concatenate(
        [leading * cosine - trailing * sine_table, trailing * cosine + leading * sine_table],
        axis=-1,
    )


def dot(left, right):
    return jnp.dot(left, right, preferred_element_type=F32)


def contract_first(left, right):
    return lax.dot_general(left, right, (((0,), (0,)), ((), ())), preferred_element_type=F32)


def contract_last(left, right):
    return lax.dot_general(left, right, (((1,), (1,)), ((), ())), preferred_element_type=F32)


def exact(left, right):
    return jnp.dot(left, right, precision=lax.Precision.HIGHEST)


def first_of(position_ref, index):
    return position_ref[index]


def attention_scores(q, k_ref, low_bound, high_bound, tile, tile_rows, scaling):
    rows = pl.ds(pl.multiple_of(tile * tile_rows, tile_rows), tile_rows)
    keys = k_ref[rows, :]
    scores = contract_last(q, keys) * scaling
    column = tile * tile_rows + lax.broadcasted_iota(jnp.int32, scores.shape, 1)
    allowed = (column >= low_bound) & (column <= high_bound)
    return rows, keys, scores, allowed


def attention_forward_kernel(
    begin_ref, q_ref, k_ref, v_ref, rank_ref, low_ref, high_ref, out_ref, lse_ref, *, scaling
):
    block = pl.program_id(1)
    cap, width = out_ref.shape
    tile_rows = q_ref.shape[0]
    pick = (lax.broadcasted_iota(jnp.int32, (cap, tile_rows), 0) == rank_ref[0]).astype(BF16)
    q = dot(pick, q_ref[...]).astype(BF16)
    low_bound, high_bound = low_ref[...], high_ref[...]

    def step(tile, carried):
        largest, total, summed = carried
        rows, _, scores, allowed = attention_scores(
            q, k_ref, low_bound, high_bound, tile, tile_rows, scaling
        )
        scores = jnp.where(allowed, scores, NEGATIVE)
        new_largest = jnp.maximum(largest, jnp.max(scores, axis=1, keepdims=True))
        weights = jnp.where(allowed, jnp.exp(scores - new_largest), 0.0)
        shrink = jnp.exp(largest - new_largest)
        return (
            new_largest,
            total * shrink + jnp.sum(weights, axis=1, keepdims=True),
            summed * shrink + dot(weights.astype(BF16), v_ref[rows, :]),
        )

    largest, total, summed = lax.fori_loop(
        begin_ref[block],
        block + 1,
        step,
        (jnp.full((cap, 1), NEGATIVE, F32), jnp.zeros((cap, 1), F32), jnp.zeros((cap, width), F32)),
    )
    out_ref[...] = (summed / total).astype(BF16)
    lse_ref[0] = largest + jnp.log(total)


def attention_backward_kernel(
    begin_ref, q_ref, k_ref, v_ref, rank_ref, low_ref, high_ref, out_ref, lse_ref, grad_ref,
    dq_ref, dk_ref, dv_ref, *, scaling
):
    block = pl.program_id(1)
    cap, width = out_ref.shape
    tile_rows = q_ref.shape[0]
    pick = (lax.broadcasted_iota(jnp.int32, (cap, tile_rows), 0) == rank_ref[0]).astype(BF16)
    q = dot(pick, q_ref[...]).astype(BF16)
    low_bound, high_bound = low_ref[...], high_ref[...]
    grad = grad_ref[...]
    delta = jnp.sum(grad.astype(F32) * out_ref[...].astype(F32), axis=1, keepdims=True)
    lse = lse_ref[0]

    @pl.when(block == 0)
    def _():
        dk_ref[...] = jnp.zeros_like(dk_ref)
        dv_ref[...] = jnp.zeros_like(dv_ref)

    def step(tile, dq):
        rows, keys, scores, allowed = attention_scores(
            q, k_ref, low_bound, high_bound, tile, tile_rows, scaling
        )
        chances = jnp.where(allowed, jnp.exp(scores - lse), 0.0)
        dv_ref[rows, :] += contract_first(chances.astype(BF16), grad)
        grad_chances = contract_last(grad, v_ref[rows, :])
        grad_scores = (chances * (grad_chances - delta)).astype(BF16)
        dk_ref[rows, :] += contract_first(grad_scores, q) * scaling
        return dq + dot(grad_scores, keys)

    dq = lax.fori_loop(begin_ref[block], block + 1, step, jnp.zeros((cap, width), F32))
    dq_ref[...] = dq * scaling


def attention_specs(row_count, token_count, width):
    return dict(
        q=pl.BlockSpec((row_count, width), lambda h, b, s: (b, h)),
        k=pl.BlockSpec((token_count, width), lambda h, b, s: (0, h)),
        rank=pl.BlockSpec((1, 1, row_count), lambda h, b, s: (b, 0, 0)),
        bound=pl.BlockSpec((CAP, 1), lambda h, b, s: (b, 0)),
        slots=pl.BlockSpec((CAP, width), lambda h, b, s: (b, h)),
        lse=pl.BlockSpec((1, CAP, 1), lambda h, b, s: (h, b, 0)),
    )


def attention_forward(begin, q, k, v, rank, low_bound, high_bound, width):
    token_count, heads = q.shape[0], q.shape[1] // width
    row_count = token_count // BLOCKS
    s = attention_specs(row_count, token_count, width)
    return pl.pallas_call(
        functools.partial(attention_forward_kernel, scaling=1.0 / math.sqrt(width)),
        grid_spec=pltpu.PrefetchScalarGridSpec(
            num_scalar_prefetch=1,
            grid=(heads, BLOCKS),
            in_specs=[s["q"], s["k"], s["k"], s["rank"], s["bound"], s["bound"]],
            out_specs=[s["slots"], s["lse"]],
        ),
        out_shape=[
            jax.ShapeDtypeStruct((BLOCKS * CAP, heads * width), BF16),
            jax.ShapeDtypeStruct((heads, BLOCKS * CAP, 1), F32),
        ],
        compiler_params=pltpu.CompilerParams(vmem_limit_bytes=VMEM_BYTES),
        cost_estimate=pl.CostEstimate(
            flops=10_000_000_000, bytes_accessed=8_000_000, transcendentals=8_000_000
        ),
        name="attention_forward",
    )(begin, q, k, v, rank, low_bound, high_bound)


def attention_backward(begin, q, k, v, rank, low_bound, high_bound, out, lse, grad, width):
    token_count, heads = q.shape[0], q.shape[1] // width
    row_count = token_count // BLOCKS
    s = attention_specs(row_count, token_count, width)
    return pl.pallas_call(
        functools.partial(attention_backward_kernel, scaling=1.0 / math.sqrt(width)),
        grid_spec=pltpu.PrefetchScalarGridSpec(
            num_scalar_prefetch=1,
            grid=(heads, BLOCKS),
            in_specs=[
                s["q"], s["k"], s["k"], s["rank"], s["bound"], s["bound"],
                s["slots"], s["lse"], s["slots"],
            ],
            out_specs=[s["slots"], s["k"], s["k"]],
        ),
        out_shape=[
            jax.ShapeDtypeStruct((BLOCKS * CAP, heads * width), F32),
            jax.ShapeDtypeStruct((token_count, heads * width), F32),
            jax.ShapeDtypeStruct((token_count, heads * width), F32),
        ],
        compiler_params=pltpu.CompilerParams(vmem_limit_bytes=VMEM_BYTES),
        cost_estimate=pl.CostEstimate(
            flops=20_000_000_000, bytes_accessed=16_000_000, transcendentals=8_000_000
        ),
        name="attention_backward",
    )(begin, q, k, v, rank, low_bound, high_bound, out, lse, grad)


def exchanged(pieces):
    return lax.all_to_all(pieces, PLACES, 0, 0, tiled=True)


def spread_weights(pieces):
    return lax.all_gather(exchanged(pieces), "t", axis=0, tiled=False)


def return_gradients(pieces):
    return exchanged(lax.psum_scatter(pieces, "t", scatter_dimension=0, tiled=False))


def to_plane(slots):
    arrived = lax.all_to_all(slots, "z", 0, 0, tiled=True)
    gathered = lax.all_gather(arrived, ("x", "grid"), axis=0, tiled=False)
    planes, cap, width = arrived.shape
    gathered = gathered.reshape(HALVES, -1, planes, cap, width)
    return gathered.transpose(2, 0, 3, 1, 4).reshape(BLOCKS * cap, -1)


def from_plane(partial, grid_count):
    pieces = partial.reshape(PLANES, HALVES, CAP, grid_count, -1).transpose(1, 3, 0, 2, 4)
    pieces = pieces.reshape((HALVES * grid_count,) + pieces.shape[2:])
    summed = lax.psum_scatter(pieces, ("x", "grid"), scatter_dimension=0, tiled=False)
    return lax.all_to_all(summed, "z", 0, 0, tiled=True)


def grid_sum(values):
    shape = values.shape
    return lax.all_gather(values.reshape(-1, 128), "grid", axis=0).sum(axis=0).reshape(shape)


def ranks(member):
    counted = member.astype(jnp.int32)
    before = jnp.cumsum(counted, axis=-1) - counted
    return jnp.where(member, before, -1)


def picks(rank):
    return jnp.arange(CAP, dtype=jnp.int32)[:, None] == rank[..., None, :]


def routed(routes):
    return routes[:, None, :] == jnp.arange(PLANES, dtype=jnp.int32)[None, :, None]


def route_gates(logits, member):
    shown = jnp.where(member, logits, NEGATIVE)
    weights = jnp.where(member, jnp.exp(shown - jnp.max(shown, axis=1, keepdims=True)), 0.0)
    return weights / jnp.sum(weights, axis=1, keepdims=True)


def logits_grad(gates, grad_gates):
    return gates * (grad_gates - jnp.sum(gates * grad_gates, axis=1, keepdims=True))


def per_device(
    tokens, segment_ids, attention_routes, expert_routes, attention_gain, attention_kv,
    attention_query, attention_out, attention_router, feedforward_gain, feedforward_router,
    expert_gate_up, expert_down, output_grad,
):
    groups = lax.axis_size("t")
    grid_count = lax.axis_size("grid")
    group = lax.axis_index("t")
    plane = lax.axis_index("z")
    place = plane * HALVES + lax.axis_index("x")
    column = lax.axis_index("grid")
    rows, features = tokens.shape
    width_all = features * grid_count
    token_count = BLOCKS * rows
    own_rows = attention_gain.shape[0]
    head_width = attention_kv.shape[3]
    head_pair = attention_kv.shape[1] // HALVES
    span = head_pair * head_width
    hidden_units = expert_gate_up.shape[3] // HALVES

    def mine(array, axis=0):
        return lax.dynamic_slice_in_dim(array, column * features, features, axis)

    def own(array):
        return lax.dynamic_slice_in_dim(array, place * rows, rows, 0)

    query_pieces = attention_query.reshape(PLANES, own_rows, HALVES, span).transpose(0, 2, 1, 3)
    kv_pieces = attention_kv.reshape(own_rows, HALVES, head_pair, 2, head_width)
    kv_pieces = kv_pieces.transpose(1, 0, 3, 2, 4).reshape(1, HALVES, own_rows, 2 * span)
    kv_pieces = jnp.broadcast_to(kv_pieces, (PLANES,) + kv_pieces.shape[1:])
    qkv_pieces = jnp.concatenate([query_pieces, kv_pieces], axis=-1)
    qkv_weight = spread_weights(qkv_pieces.reshape(BLOCKS, own_rows, 3 * span))
    qkv_weight = qkv_weight.reshape(width_all, 3 * span)
    out_pieces = attention_out.reshape(BLOCKS, span, own_rows)
    out_weight = spread_weights(out_pieces).transpose(2, 0, 1, 3).reshape(span, width_all)
    up_pieces = expert_gate_up.reshape(PLANES, own_rows, 2, HALVES, hidden_units)
    up_pieces = up_pieces.transpose(0, 3, 1, 2, 4).reshape(BLOCKS, own_rows, 2 * hidden_units)
    up_weight = spread_weights(up_pieces).reshape(width_all, 2 * hidden_units)
    down_pieces = expert_down.reshape(BLOCKS, hidden_units, own_rows)
    down_weight = spread_weights(down_pieces).transpose(2, 0, 1, 3).reshape(hidden_units, width_all)

    small = jnp.concatenate(
        [attention_gain[:, None], feedforward_gain[:, None], attention_router, feedforward_router],
        axis=1,
    )
    small = lax.all_gather(small.T, ("t", "z", "x"), axis=1, tiled=True)
    gain_first, gain_second = small[0].astype(F32), small[1].astype(F32)
    router_first, router_second = small[2:6].T, small[6:10].T

    own_routes = jnp.concatenate([attention_routes, expert_routes], axis=1)
    all_routes = lax.all_gather(own_routes, PLACES, axis=0, tiled=True)
    member_first = jnp.any(routed(all_routes[:, :2]), axis=2)
    member_second = jnp.any(routed(all_routes[:, 2:]), axis=2)

    def plane_rank(member):
        shown = lax.dynamic_index_in_dim(member, plane, 1, keepdims=False)
        return ranks(shown.reshape(BLOCKS, rows))

    rank_first, rank_second = plane_rank(member_first), plane_rank(member_second)
    own_member_first, own_member_second = own(member_first), own(member_second)
    own_pick_first = picks(ranks(own_member_first.T)).astype(BF16)
    own_pick_second = picks(ranks(own_member_second.T)).astype(BF16)

    def to_slots(values, pick):
        return jnp.einsum("est,tf->esf", pick, values, preferred_element_type=F32).astype(BF16)

    def to_tokens(slots, pick):
        return jnp.einsum("est,esf->etf", pick, slots, preferred_element_type=F32)

    grad_out = output_grad.astype(F32)
    grad_slots_second = to_plane(to_slots(output_grad, own_pick_second))

    inputs = lax.all_gather(tokens, "grid", axis=1, tiled=True)
    inputs = lax.all_gather(inputs, PLACES, axis=0, tiled=True).astype(F32)
    inverse_first = lax.rsqrt(jnp.mean(inputs * inputs, axis=-1, keepdims=True) + EPSILON)
    hidden_first = (inputs * inverse_first * gain_first).astype(BF16)
    gates_first = route_gates(dot(hidden_first, router_first), member_first)
    position = jnp.arange(token_count, dtype=jnp.int32)
    cosine, sine_table = rope_tables(position, head_width)
    cosine, sine_table = cosine[:, None, :], sine_table[:, None, :]
    qkv = dot(hidden_first, qkv_weight)

    def turned(values, sine):
        split = values.reshape(values.shape[0], -1, head_width)
        return rotate(split, cosine, sine).reshape(values.shape).astype(BF16)

    queries = turned(qkv[:, :span], sine_table)
    keys = turned(qkv[:, span : 2 * span], sine_table)
    values = qkv[:, 2 * span :].astype(BF16)
    segment = lax.dynamic_slice_in_dim(segment_ids, group * token_count, token_count, 0)
    opens = jnp.concatenate([jnp.ones((1,), jnp.bool_), segment[1:] != segment[:-1]])
    document_start = lax.cummax(jnp.where(opens, position, 0))
    begin = document_start.reshape(BLOCKS, rows)[:, 0] // rows
    slot_pick = picks(rank_first)

    def slot_values(per_token):
        shown = jnp.where(slot_pick, per_token.reshape(BLOCKS, 1, rows), 0)
        return jnp.sum(shown, axis=-1).reshape(-1, 1)

    block_first = jnp.repeat(jnp.arange(BLOCKS, dtype=jnp.int32) * rows, CAP)[:, None]
    filled = slot_values(jnp.ones((token_count,), jnp.int32)) > 0
    low_bound = jnp.where(filled, slot_values(document_start), block_first)
    high_bound = jnp.where(filled, slot_values(position), block_first)
    attention_args = (begin, queries, keys, values, rank_first[:, None, :], low_bound, high_bound)
    attended, lse = attention_forward(*attention_args, head_width)
    gate_first = lax.dynamic_index_in_dim(gates_first, plane, 1, keepdims=False)
    gate_slots_first = slot_values(gate_first)
    branch_slots = from_plane(dot(attended, out_weight).astype(BF16), grid_count)
    branch_first = to_tokens(branch_slots, own_pick_first)
    own_gates_first = own(gates_first)
    residual = tokens.astype(F32) + jnp.sum(own_gates_first.T[:, :, None] * branch_first, axis=0)

    square = grid_sum(jnp.sum(residual * residual, axis=1))
    inverse_second = lax.rsqrt(square / width_all + EPSILON)[:, None]
    normed_second = residual * inverse_second
    hidden_second = (normed_second * mine(gain_second)).astype(BF16)
    slots_second = to_plane(to_slots(hidden_second, own_pick_second))
    plane_gates = dot(slots_second, router_second)
    slot_member = jnp.stack(
        [slot_values(member_second[:, e].astype(jnp.int32))[:, 0] for e in range(PLANES)], axis=1
    )
    rank_pick = picks(rank_second)

    def slot_values_second(per_token):
        shown = jnp.where(rank_pick, per_token.reshape(BLOCKS, 1, rows), 0)
        return jnp.sum(shown, axis=-1).reshape(-1)

    slot_member = jnp.stack(
        [slot_values_second(member_second[:, e].astype(jnp.int32)) for e in range(PLANES)], axis=1
    )
    filled_second = slot_values_second(jnp.ones((token_count,), jnp.int32))[:, None] > 0
    slot_gates = route_gates(plane_gates, (slot_member > 0) | ~filled_second)
    gate_slots_second = lax.dynamic_index_in_dim(slot_gates, plane, 1, keepdims=True)
    gate_up = dot(slots_second, up_weight)
    gate_pre, up_pre = gate_up[:, :hidden_units], gate_up[:, hidden_units:]
    sigmoid_gate = jax.nn.sigmoid(gate_pre)
    silu_gate = gate_pre * sigmoid_gate
    inner = silu_gate * up_pre
    result_slots = from_plane(dot(inner.astype(BF16), down_weight).astype(BF16), grid_count)
    own_logits = grid_sum(dot(hidden_second, mine(router_second)))
    own_gates_second = route_gates(own_logits, own_member_second)
    branch_second = to_tokens(result_slots, own_pick_second)
    layer_output = residual + jnp.sum(own_gates_second.T[:, :, None] * branch_second, axis=0)
    layer_output = layer_output.astype(BF16)

    grad_inner = gate_slots_second * contract_last(grad_slots_second, down_weight)
    grad_gate = grad_inner * up_pre * sigmoid_gate * (1.0 + gate_pre * (1.0 - sigmoid_gate))
    grad_gate_up = jnp.concatenate([grad_gate, grad_inner * silu_gate], axis=1).astype(BF16)
    grad_rows = from_plane(contract_last(grad_gate_up, up_weight).astype(BF16), grid_count)
    grad_up_weight = contract_first(slots_second, grad_gate_up).astype(BF16)
    grad_up_weight = return_gradients(
        grad_up_weight.reshape(groups, BLOCKS, own_rows, 2 * hidden_units)
    )
    grad_down = contract_first((gate_slots_second * inner).astype(BF16), grad_slots_second)
    grad_down = grad_down.astype(BF16).reshape(hidden_units, groups, BLOCKS, own_rows)
    grad_down = return_gradients(grad_down.transpose(1, 2, 0, 3))
    expert_gate_up_grad = grad_up_weight.reshape(PLANES, HALVES, own_rows, 2, hidden_units)
    expert_gate_up_grad = expert_gate_up_grad.transpose(0, 2, 3, 1, 4).reshape(expert_gate_up.shape)
    expert_down_grad = grad_down.reshape(expert_down.shape)

    grad_gates_second = grid_sum(jnp.sum(branch_second * grad_out[None], axis=2).T)
    grad_logits_second = logits_grad(own_gates_second, grad_gates_second)
    grad_hidden_second = jnp.sum(to_tokens(grad_rows, own_pick_second), axis=0)
    grad_hidden_second = grad_hidden_second + exact(
        grad_logits_second, mine(router_second).astype(F32).T
    )
    grad_router_second = exact(hidden_second.astype(F32).T, grad_logits_second)
    grad_gain_second = jnp.sum(grad_hidden_second * normed_second, axis=0)
    grad_normed = grad_hidden_second * mine(gain_second)
    inner_mean = grid_sum(jnp.sum(grad_normed * normed_second, axis=1))[:, None] / width_all
    grad_residual = grad_out + inverse_second * (grad_normed - normed_second * inner_mean)

    grad_slots_first = to_plane(to_slots(grad_residual.astype(BF16), own_pick_first))
    grad_attended = gate_slots_first * contract_last(grad_slots_first, out_weight)
    grad_attended = grad_attended.astype(BF16)
    grad_out_weight = contract_first(
        (gate_slots_first * attended.astype(F32)).astype(BF16), grad_slots_first
    )
    grad_out_weight = grad_out_weight.astype(BF16).reshape(span, groups, BLOCKS, own_rows)
    grad_out_weight = return_gradients(grad_out_weight.transpose(1, 2, 0, 3))
    attention_out_grad = grad_out_weight.reshape(attention_out.shape)
    grad_query, grad_keys, grad_values = attention_backward(
        *attention_args, attended, lse, grad_attended, head_width
    )
    grad_query = jnp.einsum(
        "bst,bsf->btf",
        slot_pick.astype(BF16),
        turned_slots(grad_query, high_bound, head_width).reshape(BLOCKS, CAP, span),
        preferred_element_type=F32,
    )
    grad_qkv = jnp.concatenate(
        [
            grad_query.reshape(token_count, span).astype(BF16),
            turned(grad_keys, -sine_table),
            grad_values.astype(BF16),
        ],
        axis=1,
    )
    grad_hidden = contract_last(grad_qkv, qkv_weight).astype(BF16)
    grad_hidden = lax.psum_scatter(grad_hidden, "grid", scatter_dimension=1, tiled=True)
    grad_hidden = lax.psum_scatter(grad_hidden, PLACES, scatter_dimension=0, tiled=True)
    grad_qkv_weight = contract_first(hidden_first, grad_qkv).astype(BF16)
    grad_qkv_weight = return_gradients(
        grad_qkv_weight.reshape(groups, BLOCKS, own_rows, 3 * span)
    ).astype(F32)
    attention_query_grad = grad_qkv_weight[..., :span].reshape(PLANES, HALVES, own_rows, span)
    attention_query_grad = attention_query_grad.transpose(0, 2, 1, 3).reshape(attention_query.shape)
    grad_kv_weight = grad_qkv_weight[..., span:].reshape(
        PLANES, HALVES, own_rows, 2, head_pair, head_width
    )
    attention_kv_grad = grad_kv_weight.sum(axis=0).transpose(1, 0, 3, 2, 4)
    attention_kv_grad = attention_kv_grad.reshape(attention_kv.shape)

    own_normed = tokens.astype(F32) * own(inverse_first)
    own_hidden = (own_normed * mine(gain_first)).astype(BF16)
    grad_gates_first = grid_sum(jnp.sum(branch_first * grad_residual[None], axis=2).T)
    grad_logits_first = logits_grad(own_gates_first, grad_gates_first)
    grad_hidden_first = grad_hidden.astype(F32) + exact(
        grad_logits_first, mine(router_first).astype(F32).T
    )
    grad_router_first = exact(own_hidden.astype(F32).T, grad_logits_first)
    grad_gain_first = jnp.sum(grad_hidden_first * own_normed, axis=0)
    grad_normed = grad_hidden_first * mine(gain_first)
    inner_mean = grid_sum(jnp.sum(grad_normed * own_normed, axis=1))[:, None] / width_all
    input_grad = grad_residual + own(inverse_first) * (grad_normed - own_normed * inner_mean)

    small_grads = jnp.concatenate(
        [grad_gain_first[None], grad_gain_second[None], grad_router_first.T, grad_router_second.T],
        axis=0,
    )
    small_grads = lax.all_gather(small_grads, "grid", axis=1, tiled=True)
    small_grads = small_grads.reshape(-1, groups * BLOCKS, own_rows).transpose(1, 0, 2)
    small_grads = lax.psum_scatter(
        small_grads, ("t",) + PLACES, scatter_dimension=0, tiled=False
    )
    return (
        layer_output,
        input_grad.astype(BF16),
        small_grads[0],
        attention_kv_grad,
        attention_query_grad,
        attention_out_grad.astype(F32),
        small_grads[2:6].T,
        small_grads[1],
        small_grads[6:10].T,
        expert_gate_up_grad.astype(F32),
        expert_down_grad.astype(F32),
    )


def turned_slots(values, positions, head_width):
    cosine, sine_table = rope_tables(positions[:, 0], head_width)
    split = values.reshape(values.shape[0], -1, head_width)
    turned = rotate(split, cosine[:, None, :], -sine_table[:, None, :])
    return turned.reshape(values.shape).astype(BF16)


def solution(mesh):
    groups = mesh.shape["wide"] // BLOCKS
    shape = (groups, PLANES, HALVES, mesh.shape["grid"])
    inner_mesh = Mesh(mesh.devices.reshape(shape), ("t", "z", "x", "grid"))
    wide = ("t", "z", "x")
    in_specs = (
        P(wide, "grid"),
        P(),
        P(wide, None),
        P(wide, None),
        P(wide),
        P(wide, "grid", None, None),
        P(None, wide, "grid", None),
        P(None, "grid", None, wide),
        P(wide, None),
        P(wide),
        P(wide, None),
        P(None, wide, None, "grid"),
        P(None, "grid", wide),
        P(wide, "grid"),
    )
    out_specs = (
        P(wide, "grid"),
        P(wide, "grid"),
        P(wide),
        P(wide, "grid", None, None),
        P(None, wide, "grid", None),
        P(None, "grid", None, wide),
        P(wide, None),
        P(wide),
        P(wide, None),
        P(None, wide, None, "grid"),
        P(None, "grid", wide),
    )
    return jax.shard_map(
        per_device, mesh=inner_mesh, in_specs=in_specs, out_specs=out_specs, check_vma=False
    )
```

time: 5030 us -> 2000 us (0.40)
  waiting for transfers between devices: 3540 us -> 750 us
  local copies, waits for them, and re-layouts: 497 us -> 345 us
  matrix products: 385 us -> 235 us
  Pallas kernels: 0 us -> 95.5 us
  other arithmetic: 210 us -> 128 us
    all_gather x21 -> x5, waiting for transfers between devices: 1890 us -> 114 us  [the longest x3 53.4 us: to_plane(): gathered = lax.all_gather(arrived, ('x', 'grid'), axis=0, tiled=False)]
    reduce_scatter x11 -> x6, waiting for transfers between devices: 1370 us -> 233 us  [the longest x3 153 us: from_plane(): lax.psum_scatter(pieces, ('x', 'grid'), scatter_dimension=0, tiled=False)]
    all_to_all x0 -> x11, waiting for transfers between devices: none -> 401 us  [the longest x8 364 us: exchanged(): return lax.all_to_all(pieces, PLACES, 0, 0, tiled=True)]
    unnamed x17 -> x11, waiting for transfers between devices: 153 us -> 1.36 us
    dot_general x45 -> x26, matrix products: 385 us -> 235 us  [the longest x7 83.5 us: dot(): return jnp.dot(left, right, preferred_element_type=F32)]
    gather x12 -> x0, local copies, waits for them, and re-layouts: 108 us -> none  [the longest x6 60.6 us: slot_pairs(): return slot_rows[slot_map[0]]]
    all_to_all x0 -> x3, blocking collectives: none -> 105 us  [to_plane(): arrived = lax.all_to_all(slots, 'z', 0, 0, tiled=True)]
    pallas_call x0 -> x2, Pallas kernels: none -> 95.5 us  [the longest x1 56.7 us: attention_backward(): pl.pallas_call(functools.partial(attention_backward_kernel, scaling=1.0 /...]
  transfers between devices with their start and end apart: 46 -> 22, of which waited for: 33 -> 15; matrix products, arithmetic and copies ran while one was open for 18% -> 23% of each run, Pallas kernels for 0% -> 0%
where the time goes in v1:
time: 2000 us; the launch traced here: 1990 us
  waiting for transfers between devices  750 us (38%)
  blocking collectives  373 us (19%)
  local copies, waits for them, and re-layouts  345 us (17%)
  matrix products  235 us (12%)
  other arithmetic  128 us (6%)
  Pallas kernels  95.5 us (5%)
  starting transfers between devices  49.8 us (2%)
    all_to_all x8, waiting for transfers between devices, exchanged(): return lax.all_to_all(pieces, PLACES, 0, 0, tiled=True)  364 us
    all_gather x1, blocking collectives, per_device(): small = lax.all_gather(small.T, ('t', 'z', 'x'), axis=1, tiled=True)  157 us
    reduce_scatter x3, waiting for transfers between devices, from_plane(): lax.psum_scatter(pieces, ('x', 'grid'), scatter_dimension=0, tiled=False)  153 us
    unnamed x139, local copies, waits for them, and re-layouts  115 us
    all_to_all x3, blocking collectives, to_plane(): arrived = lax.all_to_all(slots, 'z', 0, 0, tiled=True)  105 us
    dot_general x7, matrix products, dot(): return jnp.dot(left, right, preferred_element_type=F32)  83.5 us
    all_gather x1, blocking collectives, per_device(): all_routes = lax.all_gather(own_routes, PLACES, axis=0, tiled=True)  73.9 us
    dot_general x4, matrix products, contract_last(): lax.dot_general(left, right, (((1,), (1,)), ((), ())), preferred_element_...  66 us
  transfers between devices with their start and end apart: 22, of which 15 were waited for; matrix products, arithmetic and copies ran while one was open for 23% of the time, Pallas kernels for 0%

profile of v1, /device:TPU:0, one launch (start us, length us, event | category | flops | bytes accessed | tf_op | source)
XLA Modules:
  0.0 1991.7 jit_solution(7170087655874450028)
XLA Ops:
  8.0 26.9 %all-gather.9.cloned.1.call-done = bf16[512,2048]{1,0:T(8,128)(2,1)} async-done(((bf16[512,512]{1,0:T(8,128)(2,1)}), bf16[512,2048]{1,0:T(8,128)(2,1)}) %all-gather.9.cloned.1.call-update) | async-done | bytes 2097168 | tf_op jit(solution)/shard_map/all_gather | solution.py:330
  42.7 73.9 %all_gather.63 = s32[4096,4]{0,1:T(4,128)S(1)} all-gather(s32[512,4]{0,1:T(4,128)S(1)} %pad_add_fusion), channel_id=1, replica_groups=mesh['t'=1,'z'=4,'x'=2,'grid'=4] {'z','x'}, dimensions={0}, use_global_device_ids=true | all-gather | bytes 73728 | tf_op jit(solution)/shard_map/all_gather | solution.py:308
  135.0 157.0 %all_gather.66 = bf16[10,2048]{1,0:T(8,128)(2,1)S(1)} all-gather(bf16[10,256]{1,0:T(8,128)(2,1)S(1)} %maximum_bitcast_fusion), channel_id=1, replica_groups=mesh['t'=1,'z'=4,'x'=2,'grid'=4] {'t','z','x'}, dimensions={1}, use_global_device_ids=true | all-gather | bytes 46080 | tf_op jit(solution)/shard_map/all_gather | solution.py:303
  293.2 9.4 fusion.41
  304.9 33.6 %all-gather.11.cloned.1.call-done = bf16[4096,2048]{1,0:T(8,128)(2,1)} async-done(((bf16[512,2048]{1,0:T(8,128)(2,1)}), bf16[4096,2048]{1,0:T(8,128)(2,1)}) %all-gather.11.cloned.1.call-update) | async-done | bytes 16777232 | tf_op jit(solution)/shard_map/all_gather | solution.py:331
  338.5 7.2 fusion
  345.7 20.9 %fusion.84 = f32[4096,768]{0,1:T(8,128)} fusion(bf16[2048,768]{1,0:T(8,128)(2,1)} %bitcast.12, bf16[4096,2048]{1,0:T(8,128)(2,1)} %all-gather.11.cloned.1.call-done, f32[2048]{0:T(1024)S(1)} %bitcast.293, f32[4096]{0:T(1024)S(1)} %add_rsqrt_fusion), kind=kOutput, calls=%fused_computation.219 | convolution fusion | flops 12918456320 | bytes 32530432 | tf_op jit(solution)/shard_map/dot_general | solution.py:42
  370.4 7.9 fusion.90
  389.6 6.2 copy.298
  395.7 6.2 copy.296
  401.9 6.2 copy.297
  408.0 6.2 copy.295
  414.2 11.0 subtract_convert_fusion.1
  425.2 11.4 pad_maximum_fusion.7
  439.8 38.8 %attention_forward.1 = (bf16[2560,256]{1,0:T(8,128)(2,1)}, f32[2,2560,1]{2,1,0:T(8,128)}) custom-call(s32[8]{0:T(128)} %and_select_fusion.begin_ref, bf16[4096,256]{1,0:T(8,128)(2,1)} %bitcast.269, bf16[4096,256]{1,0:T(8,128)(2,1)} %bitcast.271, bf16[4096,256]{1,0:T(8,128)(2,1)} %copy.299.v_ref, s32[8,1,512]{2,1,0:T(1,128)} %subtract_select_fusion.rank_ref, ...), custom_call_target="tpu_custom_call" | custom-call | flops 10000000000 | bytes 8000000 | tf_op jit(solution)/shard_map/attention_forward/pallas_call | solution.py:154
  478.6 7.0 convolution_convert_fusion.3
  485.6 17.8 reshape.698
  503.4 10.5 copy.260
  517.5 76.4 %reduce-scatter.7.cloned.1.call-done = bf16[1,4,320,512]{3,2,1,0:T(8,128)(2,1)} async-done(((bf16[8,4,320,512]{3,2,1,0:T(8,128)(2,1)}), bf16[1,4,320,512]{3,2,1,0:T(8,128)(2,1)}) %reduce-scatter.7.cloned.1.call-update) | async-done | bytes 1310736 | tf_op jit(solution)/shard_map/reduce_scatter | solution.py:225
  598.5 8.3 fusion.97
  607.0 22.8 %all-to-all-done.2 = bf16[4,320,512]{2,1,0:T(8,128)(2,1)S(1)} async-done(((bf16[4,320,512]{2,1,0:T(8,128)(2,1)}), bf16[4,320,512]{2,1,0:T(8,128)(2,1)S(1)}, u32[]{:S(2)}, u32[]{:S(2)}) %all-to-all-start.2) | async-done | bytes 1310752 | tf_op jit(solution)/shard_map/all_to_all | solution.py:226
  643.1 35.3 %all_to_all.70 = bf16[4,320,512]{2,1,0:T(8,128)(2,1)} all-to-all(bf16[4,320,512]{2,1,0:T(8,128)(2,1)S(1)} %fusion.19), channel_id=1, replica_groups=mesh['t'=1,'z'=4,'x'=2,'grid'=4] {'z'}, dimensions={0} | all-to-all | bytes 2621440 | tf_op jit(solution)/shard_map/all_to_all | solution.py:215
  679.3 34.3 %all_to_all.71 = bf16[4,320,512]{2,1,0:T(8,128)(2,1)} all-to-all(bf16[4,320,512]{2,1,0:T(8,128)(2,1)S(1)} %fusion.20), channel_id=1, replica_groups=mesh['t'=1,'z'=4,'x'=2,'grid'=4] {'z'}, dimensions={0} | all-to-all | bytes 2621440 | tf_op jit(solution)/shard_map/all_to_all | solution.py:215
  717.8 14.7 copy.265
  738.2 43.5 %all-to-all-done.5 = bf16[8,704,256]{2,1,0:T(8,128)(2,1)S(1)} async-done(((bf16[8,704,256]{2,1,0:T(8,128)(2,1)}), bf16[8,704,256]{2,1,0:T(8,128)(2,1)S(1)}, u32[]{:S(2)}, u32[]{:S(2)}) %all-to-all-start.5) | async-done | bytes 2883616 | tf_op jit(solution)/shard_map/all_to_all | solution.py:203
  788.5 124.1 %all-to-all-done.4 = bf16[8,256,1408]{1,2,0:T(8,128)(2,1)} async-done(((bf16[8,256,1408]{1,2,0:T(8,128)(2,1)}), bf16[8,256,1408]{1,2,0:T(8,128)(2,1)}, u32[]{:S(2)}, u32[]{:S(2)}) %all-to-all-start.4) | async-done | bytes 5767200 | tf_op jit(solution)/shard_map/all_to_all | solution.py:203
  912.6 8.4 copy.267
  921.0 13.4 copy.264
  934.4 12.4 copy.304
  946.8 22.9 %fusion.99 = f32[2560,1408]{0,1:T(8,128)} fusion(bf16[2560,2048]{1,0:T(8,128)(2,1)} %bitcast.221, bf16[2048,1408]{1,0:T(8,128)(2,1)} %bitcast.252), kind=kOutput, calls=%fused_computation.232 | convolution fusion | flops 14763950080 | bytes 30670848 | tf_op jit(solution)/shard_map/dot_general | solution.py:42
  969.7 17.0 convolution_convert_fusion.2
  986.6 17.8 reshape.710
  1004.4 10.3 copy.269
  1021.1 13.6 copy.272
  1034.7 12.5 copy.306
  1047.2 7.2 fusion.98
  1054.6 15.0 multiply_convert_fusion.2
  1069.7 23.0 %convolution_convert_fusion.1 = bf16[2560,2048]{1,0:T(8,128)(2,1)} fusion(bf16[2048,1408]{1,0:T(8,128)(2,1)} %bitcast.253, bf16[2560,704]{0,1:T(8,128)(2,1)} %get-tuple-element.106, bf16[2560,704]{0,1:T(8,128)(2,1)} %get-tuple-element.105), kind=kOutput, calls=%fused_computation.7 | convolution fusion | flops 14783610880 | bytes 23461888 | tf_op jit(solution)/shard_map/dot_general | solution.py:50
  1092.7 18.2 reshape.716
  1110.9 10.5 copy.273
  1125.5 76.8 %reduce-scatter.11.cloned.1.call-done = bf16[1,4,320,512]{3,2,1,0:T(8,128)(2,1)} async-done(((bf16[8,4,320,512]{3,2,1,0:T(8,128)(2,1)}), bf16[1,4,320,512]{3,2,1,0:T(8,128)(2,1)}) %reduce-scatter.11.cloned.1.call-update) | async-done | bytes 1310736 | tf_op jit(solution)/shard_map/reduce_scatter | solution.py:225
  1224.9 14.5 all-to-all-done.8
  1252.6 35.3 %all_to_all.72 = bf16[4,320,512]{2,1,0:T(8,128)(2,1)} all-to-all(bf16[4,320,512]{2,1,0:T(8,128)(2,1)S(1)} %fusion.18), channel_id=1, replica_groups=mesh['t'=1,'z'=4,'x'=2,'grid'=4] {'z'}, dimensions={0} | all-to-all | bytes 2621440 | tf_op jit(solution)/shard_map/all_to_all | solution.py:215
  1288.1 6.4 multiply_cosine_fusion.1
  1296.1 53.4 %all-gather.17.cloned.1.call-done = bf16[32,320,512]{2,1,0:T(8,128)(2,1)} async-done(((bf16[4,320,512]{2,1,0:T(8,128)(2,1)}), bf16[32,320,512]{2,1,0:T(8,128)(2,1)}) %all-gather.17.cloned.1.call-update) | async-done | bytes 10485776 | tf_op jit(solution)/shard_map/all_gather | solution.py:216
  1349.5 13.4 copy.278
  1362.9 12.5 copy.307
  1375.3 8.0 fusion.5.grad_ref
  1383.3 56.7 %attention_backward.1 = (f32[2560,256]{1,0:T(8,128)}, f32[4096,256]{1,0:T(8,128)}, f32[4096,256]{1,0:T(8,128)}) custom-call(s32[8]{0:T(128)} %and_select_fusion.begin_ref, bf16[4096,256]{1,0:T(8,128)(2,1)} %bitcast.270, bf16[4096,256]{1,0:T(8,128)(2,1)} %bitcast.272, bf16[4096,256]{1,0:T(8,128)(2,1)} %copy.299.v_ref, ...), custom_call_target="tpu_custom_call" | custom-call | flops 20000000000 | bytes 16000000 | tf_op jit(solution)/shard_map/attention_backward/pallas_call | solution.py:178
  1463.5 19.6 subtract_convert_fusion
  1490.4 20.0 %convolution_convert_fusion = bf16[4096,2048]{1,0:T(8,128)(2,1)} fusion(bf16[2048,768]{1,0:T(8,128)(2,1)} %bitcast.12, bf16[4096,256]{1,0:T(8,128)(2,1)S(1)} %copy-done.19, bf16[4096,256]{1,0:T(8,128)(2,1)} %bitcast.273, bf16[4096,256]{1,0:T(8,128)(2,1)} %bitcast.309), kind=kOutput, calls=%fused_computation.5 | convolution fusion | flops 12912164864 | bytes 26214400 | tf_op jit(solution)/shard_map/dot_general | solution.py:50
  1511.2 14.8 fusion.9
  1534.9 22.3 %convolution_convert_fusion.4 = bf16[2048,1408]{1,0:T(8,128)(2,1)} fusion(bf16[2560,2048]{1,0:T(8,128)(2,1)} %bitcast.223, bf16[2560,704]{0,1:T(8,128)(2,1)} %get-tuple-element.106, bf16[2560,704]{0,1:T(8,128)(2,1)} %get-tuple-element.105), kind=kOutput, calls=%fused_computation.10 | convolution fusion | flops 14781251584 | bytes 23461888 | tf_op jit(solution)/shard_map/dot_general | solution.py:46
  1557.2 8.4 copy.289
  1565.6 34.8 %all-to-all-done.13 = bf16[8,704,256]{2,1,0:T(8,128)(2,1)S(1)} async-done(((bf16[8,704,256]{2,1,0:T(8,128)(2,1)}), bf16[8,704,256]{2,1,0:T(8,128)(2,1)S(1)}, u32[]{:S(2)}, u32[]{:S(2)}) %all-to-all-start.13) | async-done | bytes 2883616 | tf_op jit(solution)/shard_map/all_to_all | solution.py:203
  1606.8 7.7 convolution_convert_fusion.6
  1616.0 20.8 %reduce-scatter.13.cloned.1.call-done = bf16[4096,512]{1,0:T(8,128)(2,1)} async-done(((bf16[4096,2048]{1,0:T(8,128)(2,1)}), bf16[4096,512]{1,0:T(8,128)(2,1)}) %reduce-scatter.13.cloned.1.call-update) | async-done | bytes 4194320 | tf_op jit(solution)/shard_map/reduce_scatter | solution.py:457
  1636.8 130.3 %all-to-all-done.12 = bf16[8,256,1408]{1,2,0:T(8,128)(2,1)} async-done(((bf16[8,256,1408]{1,2,0:T(8,128)(2,1)}), bf16[8,256,1408]{1,2,0:T(8,128)(2,1)}, u32[]{:S(2)}, u32[]{:S(2)}) %all-to-all-start.12) | async-done | bytes 5767200 | tf_op jit(solution)/shard_map/all_to_all | solution.py:203
  1770.8 20.5 %convolution_convert_fusion.5 = bf16[2048,768]{1,0:T(8,128)(2,1)} fusion(bf16[4096,256]{1,0:T(8,128)(2,1)S(1)} %copy-done.20, bf16[4096,256]{1,0:T(8,128)(2,1)} %bitcast.274, bf16[4096,256]{1,0:T(8,128)(2,1)} %bitcast.310, bf16[4096,2048]{1,0:T(8,128)(2,1)} %all-gather.11.cloned.1.call-done, f32[2048]{0:T(1024)S(1)} %bitcast.295, f32[4096]{0:T(1024)S(1)} %copy-done.42), kind=kOutput, calls=%fused_computation.47 | convolution fusion | flops 12938903552 | bytes 26238976 | tf_op jit(solution)/shard_map/dot_general | solution.py:46
  1806.3 8.3 convert_bitcast_fusion
  1814.7 9.7 copy.290
  1824.4 17.6 copy.293
  1860.2 26.0 %all-to-all-done.10 = bf16[8,256,768]{2,1,0:T(8,128)(2,1)S(1)} async-done(((bf16[8,256,768]{2,1,0:T(8,128)(2,1)}), bf16[8,256,768]{2,1,0:T(8,128)(2,1)S(1)}, u32[]{:S(2)}, u32[]{:S(2)}) %all-to-all-start.10) | async-done | bytes 3145760 | tf_op jit(solution)/shard_map/all_to_all | solution.py:203
  1922.7 59.3 %reduce-scatter.17.cloned.1.call-done = f32[1,10,256]{2,1,0:T(8,128)} async-done(((f32[8,10,256]{2,1,0:T(8,128)}), f32[1,10,256]{2,1,0:T(8,128)}) %reduce-scatter.17.cloned.1.call-update) | async-done | bytes 10256 | tf_op jit(solution)/shard_map/reduce_scatter | solution.py:490
  (347 shorter events, 259.8 us)
Async XLA Ops:
  7.2 33.3 %copy-start.25 = (bf16[256,4,2,128]{3,2,1,0:T(2,128)(2,1)S(1)}, bf16[256,4,2,128]{3,2,1,0:T(2,128)(2,1)}, u32[]{:S(2)}) copy-start(bf16[256,4,2,128]{3,2,1,0:T(2,128)(2,1)} %param.19) | copy-start | bytes 1572868
  7.2 34.6 %copy-start.24 = (bf16[4,256,4,128]{3,2,1,0:T(4,128)(2,1)S(1)}, bf16[4,256,4,128]{3,2,1,0:T(4,128)(2,1)}, u32[]{:S(2)}) copy-start(bf16[4,256,4,128]{3,2,1,0:T(4,128)(2,1)} %param.20) | copy-start | bytes 3145732
  7.2 27.7 %all-gather.9.cloned.1.call-start = ((), (), s32[]{:S(2)}) async-start(), calls=%async_computation.20 | async-start | bytes 2621440 | tf_op jit(solution)/shard_map/all_gather | solution.py:330
  7.9 330.6 %all-gather.11.cloned.1.call-start = ((), (), s32[]{:S(2)}) async-start(), calls=%async_computation.21 | async-start | bytes 18874368 | tf_op jit(solution)/shard_map/all_gather | solution.py:331
  34.9 84.7 %all-to-all-start.1 = ((bf16[8,256,256]{2,1,0:T(8,128)(2,1)}), bf16[8,256,256]{2,1,0:T(8,128)(2,1)S(1)}, u32[]{:S(2)}, u32[]{:S(2)}) async-start(bf16[8,256,256]{2,1,0:T(8,128)(2,1)} %bitcast.280), calls=%async_computation.1 | async-start | bytes 2097152 | tf_op jit(solution)/shard_map/all_to_all | solution.py:203
  119.7 13.1 copy-start.17
  119.7 15.3 copy-start.54
  119.7 15.3 copy-start.55
  119.7 226.0 %all-to-all-start = ((bf16[8,256,768]{2,1,0:T(8,128)(2,1)}), bf16[8,256,768]{2,1,0:T(8,128)(2,1)}, u32[]{:S(2)}, u32[]{:S(2)}) async-start(bf16[8,256,768]{2,1,0:T(8,128)(2,1)} %bitcast.11), calls=%async_computation | async-start | bytes 6291456 | tf_op jit(solution)/shard_map/all_to_all | solution.py:203
  124.3 469.6 %reduce-scatter.7.cloned.1.call-start = ((), (), s32[]{:S(2)}) async-start(), calls=%async_computation.22 | async-start | bytes 11796480 | tf_op jit(solution)/shard_map/reduce_scatter | solution.py:225
  127.0 166.2 %copy-start.27 = (s32[8,512]{1,0:T(8,128)}, s32[8,512]{1,0:T(8,128)S(1)}, u32[]{:S(2)}) copy-start(s32[8,512]{1,0:T(8,128)S(1)} %get-tuple-element.101) | copy-start | bytes 49156
  292.0 12.8 copy-start.56
  293.2 305.3 %copy-start.45 = (f32[1,2048]{1,0:T(1,128)}, f32[1,2048]{1,0:T(1,128)S(1)}, u32[]{:S(2)}) copy-start(f32[1,2048]{1,0:T(1,128)S(1)} %get-tuple-element.128) | copy-start | bytes 24580
  302.6 111.5 %copy-start = (f32[4096,64]{1,0:T(8,128)}, f32[4096,64]{1,0:T(8,128)S(1)}, u32[]{:S(2)}) copy-start(f32[4096,64]{1,0:T(8,128)S(1)} %get-tuple-element.133) | copy-start | bytes 3145732
  304.8 173.8 %copy-start.13 = (bf16[256,1,8,256]{0,3,2,1:T(8,128)(2,1)}, bf16[256,1,8,256]{0,3,2,1:T(8,128)(2,1)S(1)}, u32[]{:S(2)}) copy-start(bf16[256,1,8,256]{0,3,2,1:T(8,128)(2,1)S(1)} %copy.259) | copy-start | bytes 3145732
  345.7 252.8 %copy-start.41 = (f32[4096]{0:T(1024)}, f32[4096]{0:T(1024)S(1)}, u32[]{:S(2)}) copy-start(f32[4096]{0:T(1024)S(1)} %add_rsqrt_fusion) | copy-start | bytes 49156
  517.3 124.0 %copy-start.35 = (f32[1,512]{1,0:T(1,128)}, f32[1,512]{1,0:T(1,128)S(1)}, u32[]{:S(2)}) copy-start(f32[1,512]{1,0:T(1,128)S(1)} %fusion.73) | copy-start | bytes 6148
  517.4 161.0 %copy-start.50 = (s32[4,512]{1,0:T(4,128)}, s32[4,512]{1,0:T(4,128)S(1)}, u32[]{:S(2)}) copy-start(s32[4,512]{1,0:T(4,128)S(1)} %fusion.62) | copy-start | bytes 24580
  517.5 112.3 %copy-start.39 = (s32[4,512]{1,0:T(4,128)}, s32[4,512]{1,0:T(4,128)S(1)}, u32[]{:S(2)}) copy-start(s32[4,512]{1,0:T(4,128)S(1)} %fusion.61) | copy-start | bytes 24580
  593.9 36.0 %all-to-all-start.2 = ((bf16[4,320,512]{2,1,0:T(8,128)(2,1)}), bf16[4,320,512]{2,1,0:T(8,128)(2,1)S(1)}, u32[]{:S(2)}, u32[]{:S(2)}) async-start(bf16[4,320,512]{2,1,0:T(8,128)(2,1)} %bitcast.278), calls=%async_computation.3 | async-start | bytes 2621440 | tf_op jit(solution)/shard_map/all_to_all | solution.py:226
  598.5 322.5 %all-gather.13.cloned.1.call-start = ((), (), s32[]{:S(2)}) async-start(), calls=%async_computation.28 | async-start | bytes 11796480 | tf_op jit(solution)/shard_map/all_gather | solution.py:216
  607.0 27.7 %copy-start.26 = (f32[4096,4]{0,1:T(4,128)}, f32[4096,4]{0,1:T(4,128)S(1)}, u32[]{:S(2)}) copy-start(f32[4096,4]{0,1:T(4,128)S(1)} %fusion.53) | copy-start | bytes 196612
  607.0 27.6 %copy-start.11 = (bf16[512,512]{1,0:T(8,128)(2,1)S(1)}, bf16[512,512]{1,0:T(8,128)(2,1)}, u32[]{:S(2)}) copy-start(bf16[512,512]{1,0:T(8,128)(2,1)} %param.14) | copy-start | bytes 1572868
  636.1 42.4 %copy-start.2 = (f32[512,512]{1,0:T(8,128)}, f32[512,512]{1,0:T(8,128)S(1)}, u32[]{:S(2)}) copy-start(f32[512,512]{1,0:T(8,128)S(1)} %get-tuple-element.100) | copy-start | bytes 3145732
  641.3 37.2 %copy-start.37 = (f32[512]{0:T(512)}, f32[512]{0:T(512)S(1)}, u32[]{:S(2)}) copy-start(f32[512]{0:T(512)S(1)} %rsqrt_bitcast_fusion) | copy-start | bytes 6148
  642.2 36.2 %copy-start.21 = (bf16[512,512]{1,0:T(8,128)(2,1)S(1)}, bf16[512,512]{1,0:T(8,128)(2,1)}, u32[]{:S(2)}) copy-start(bf16[512,512]{1,0:T(8,128)(2,1)} %param.27) | copy-start | bytes 1572868
  713.6 68.1 %all-to-all-start.5 = ((bf16[8,704,256]{2,1,0:T(8,128)(2,1)}), bf16[8,704,256]{2,1,0:T(8,128)(2,1)S(1)}, u32[]{:S(2)}, u32[]{:S(2)}) async-start(bf16[8,704,256]{2,1,0:T(8,128)(2,1)} %bitcast.265), calls=%async_computation.6 | async-start | bytes 5767168 | tf_op jit(solution)/shard_map/all_to_all | solution.py:203
  717.3 303.9 %all-gather.15.cloned.1.call-start = ((), (), s32[]{:S(2)}) async-start(), calls=%async_computation.29 | async-start | bytes 11796480 | tf_op jit(solution)/shard_map/all_gather | solution.py:216
  781.7 130.8 %all-to-all-start.4 = ((bf16[8,256,1408]{1,2,0:T(8,128)(2,1)}), bf16[8,256,1408]{1,2,0:T(8,128)(2,1)}, u32[]{:S(2)}, u32[]{:S(2)}) async-start(bf16[8,256,1408]{1,2,0:T(8,128)(2,1)} %bitcast.234), calls=%async_computation.5 | async-start | bytes 11534336 | tf_op jit(solution)/shard_map/all_to_all | solution.py:203
  786.4 335.1 %reduce-scatter.9.cloned.1.call-start = ((), (), s32[]{:S(2)}) async-start(), calls=%async_computation.23 | async-start | bytes 11796480 | tf_op jit(solution)/shard_map/reduce_scatter | solution.py:225
  946.8 22.9 %copy-start.18 = (bf16[88,8,8,256]{3,1,2,0:T(8,128)(2,1)S(1)}, bf16[88,8,8,256]{3,1,2,0:T(8,128)(2,1)}, u32[]{:S(2)}) copy-start(bf16[88,8,8,256]{3,1,2,0:T(8,128)(2,1)} %copy.305) | copy-start | bytes 8650756
  1014.8 187.6 %reduce-scatter.11.cloned.1.call-start = ((), (), s32[]{:S(2)}) async-start(), calls=%async_computation.24 | async-start | bytes 11796480 | tf_op jit(solution)/shard_map/reduce_scatter | solution.py:225
  1054.5 15.1 copy-start.47
  1121.5 86.5 %copy-start.22 = (bf16[512,512]{1,0:T(8,128)(2,1)S(1)}, bf16[512,512]{1,0:T(8,128)(2,1)}, u32[]{:S(2)}) copy-start(bf16[512,512]{1,0:T(8,128)(2,1)} %param.27) | copy-start | bytes 1572868
  1121.5 87.4 %copy-start.10 = (bf16[512,512]{1,0:T(8,128)(2,1)S(1)}, bf16[512,512]{1,0:T(8,128)(2,1)}, u32[]{:S(2)}) copy-start(bf16[512,512]{1,0:T(8,128)(2,1)} %copy-done.9) | copy-start | bytes 1572868
  1121.5 93.4 %copy-start.51 = (s32[4,512]{1,0:T(4,128)S(1)}, s32[4,512]{1,0:T(4,128)}, u32[]{:S(2)}) copy-start(s32[4,512]{1,0:T(4,128)} %copy-done.50) | copy-start | bytes 24580
  1121.5 80.8 %all-to-all-start.6 = ((bf16[4,320,512]{2,1,0:T(8,128)(2,1)}), bf16[4,320,512]{2,1,0:T(8,128)(2,1)S(1)}, u32[]{:S(2)}, u32[]{:S(2)}) async-start(bf16[4,320,512]{2,1,0:T(8,128)(2,1)} %bitcast.277), calls=%async_computation.8 | async-start | bytes 2621440 | tf_op jit(solution)/shard_map/all_to_all | solution.py:226
  1203.4 36.0 %all-to-all-start.8 = ((bf16[4,320,512]{2,1,0:T(8,128)(2,1)}), bf16[4,320,512]{2,1,0:T(8,128)(2,1)S(1)}, u32[]{:S(2)}, u32[]{:S(2)}) async-start(bf16[4,320,512]{2,1,0:T(8,128)(2,1)} %bitcast.279), calls=%async_computation.11 | async-start | bytes 2621440 | tf_op jit(solution)/shard_map/all_to_all | solution.py:226
  1208.0 141.5 %all-gather.17.cloned.1.call-start = ((), (), s32[]{:S(2)}) async-start(), calls=%async_computation.30 | async-start | bytes 11796480 | tf_op jit(solution)/shard_map/all_gather | solution.py:216
  1215.0 25.3 %copy-start.29 = (f32[512,4]{0,1:T(4,128)}, f32[512,4]{0,1:T(4,128)S(1)}, u32[]{:S(2)}) copy-start(f32[512,4]{0,1:T(4,128)S(1)} %fusion.63) | copy-start | bytes 24580
  1224.7 15.5 copy-start.3
  1224.7 15.5 copy-start.36
  1224.8 15.5 copy-start.38
  1224.9 16.8 copy-start.31
  1224.9 16.8 copy-start.43
  1241.7 10.0 copy-start.40
  1250.8 37.2 %copy-start.34 = (f32[8,320]{1,0:T(8,128)S(1)}, f32[8,320]{1,0:T(8,128)}, u32[]{:S(2)}) copy-start(f32[8,320]{1,0:T(8,128)} %get-tuple-element.94) | copy-start | bytes 30724
  1250.8 37.3 %copy-start.57 = (f32[64]{0:T(128)S(1)}, f32[64]{0:T(128)}, u32[]{:S(2)}) copy-start(f32[64]{0:T(128)} %copy-done.56) | copy-start | bytes 772
  1252.6 42.7 %copy-start.28 = (s32[8,512]{1,0:T(8,128)S(1)}, s32[8,512]{1,0:T(8,128)}, u32[]{:S(2)}) copy-start(s32[8,512]{1,0:T(8,128)} %copy-done.27) | copy-start | bytes 49156
  1287.9 348.8 %reduce-scatter.13.cloned.1.call-start = ((), (), s32[]{:S(2)}) async-start(), calls=%async_computation.25 | async-start | bytes 20971520 | tf_op jit(solution)/shard_map/reduce_scatter | solution.py:457
  1362.9 12.5 copy-start.14
  1529.3 71.1 %all-to-all-start.13 = ((bf16[8,704,256]{2,1,0:T(8,128)(2,1)}), bf16[8,704,256]{2,1,0:T(8,128)(2,1)S(1)}, u32[]{:S(2)}, u32[]{:S(2)}) async-start(bf16[8,704,256]{2,1,0:T(8,128)(2,1)} %bitcast.240), calls=%async_computation.19 | async-start | bytes 5767168 | tf_op jit(solution)/shard_map/all_to_all | solution.py:203
  1602.0 165.0 %all-to-all-start.12 = ((bf16[8,256,1408]{1,2,0:T(8,128)(2,1)}), bf16[8,256,1408]{1,2,0:T(8,128)(2,1)}, u32[]{:S(2)}, u32[]{:S(2)}) async-start(bf16[8,256,1408]{1,2,0:T(8,128)(2,1)} %copy.289), calls=%async_computation.18 | async-start | bytes 11534336 | tf_op jit(solution)/shard_map/all_to_all | solution.py:203
  1606.7 301.4 %reduce-scatter.15.cloned.1.call-start = ((), (), s32[]{:S(2)}) async-start(), calls=%async_computation.26 | async-start | bytes 4718592 | tf_op jit(solution)/shard_map/reduce_scatter | solution.py:458
  1614.8 156.1 %copy-start.20 = (bf16[4096,256]{1,0:T(8,128)(2,1)S(1)}, bf16[4096,256]{1,0:T(8,128)(2,1)}, u32[]{:S(2)}) copy-start(bf16[4096,256]{1,0:T(8,128)(2,1)} %convert_element_type.309) | copy-start | bytes 6291460
  1614.8 156.1 %copy-start.42 = (f32[4096]{0:T(1024)S(1)}, f32[4096]{0:T(1024)}, u32[]{:S(2)}) copy-start(f32[4096]{0:T(1024)} %copy-done.41) | copy-start | bytes 49156
  1614.8 156.1 %copy-start.46 = (f32[1,2048]{1,0:T(1,128)S(1)}, f32[1,2048]{1,0:T(1,128)}, u32[]{:S(2)}) copy-start(f32[1,2048]{1,0:T(1,128)} %copy-done.45) | copy-start | bytes 24580
  1767.0 29.7 %all-to-all-start.11 = ((bf16[8,256,256]{2,1,0:T(8,128)(2,1)}), bf16[8,256,256]{2,1,0:T(8,128)(2,1)S(1)}, u32[]{:S(2)}, u32[]{:S(2)}) async-start(bf16[8,256,256]{2,1,0:T(8,128)(2,1)} %bitcast.214), calls=%async_computation.17 | async-start | bytes 2097152 | tf_op jit(solution)/shard_map/all_to_all | solution.py:203
  1797.7 88.5 %all-to-all-start.10 = ((bf16[8,256,768]{2,1,0:T(8,128)(2,1)}), bf16[8,256,768]{2,1,0:T(8,128)(2,1)S(1)}, u32[]{:S(2)}, u32[]{:S(2)}) async-start(bf16[8,256,768]{2,1,0:T(8,128)(2,1)} %bitcast.264), calls=%async_computation.16 | async-start | bytes 6291456 | tf_op jit(solution)/shard_map/all_to_all | solution.py:203
  1801.3 180.7 %reduce-scatter.17.cloned.1.call-start = ((), (), s32[]{:S(2)}) async-start(), calls=%async_computation.27 | async-start | bytes 147456 | tf_op jit(solution)/shard_map/reduce_scatter | solution.py:490
  1844.5 11.5 copy-start.30
  1844.5 11.6 copy-start.32
  1844.5 11.6 copy-start.44
  1906.3 15.3 copy-start.8
  (18 other events, 69.8 us)
Sparse Core Ops, SparseCore 0:
  9.6 25.2 all-gather.8
  37.0 301.4 all-gather.10
  514.1 79.7 reduce-scatter.6
  678.5 91.7 all-gather.12
  772.1 123.6 all-gather.14
  1014.9 80.0 reduce-scatter.8
  1121.6 80.6 reduce-scatter.10
  1288.0 61.4 all-gather.16
  1510.6 126.0 reduce-scatter.12
  1640.6 197.6 reduce-scatter.14
  1921.7 60.2 reduce-scatter.16

commit v2 on v1

--- a/solution.py
+++ b/solution.py
@@ -18,6 +18,7 @@
 BF16 = jnp.bfloat16
 F32 = jnp.float32
 PLACES = ("z", "x")
+MESH = pl.DeviceIdType.MESH
 VMEM_BYTES = 56 * 1024 * 1024
 
 
@@ -211,19 +212,252 @@
     return exchanged(lax.psum_scatter(pieces, "t", scatter_dimension=0, tiled=False))
 
 
-def to_plane(slots):
-    arrived = lax.all_to_all(slots, "z", 0, 0, tiled=True)
-    gathered = lax.all_gather(arrived, ("x", "grid"), axis=0, tiled=False)
-    planes, cap, width = arrived.shape
-    gathered = gathered.reshape(HALVES, -1, planes, cap, width)
-    return gathered.transpose(2, 0, 3, 1, 4).reshape(BLOCKS * cap, -1)
-
-
-def from_plane(partial, grid_count):
-    pieces = partial.reshape(PLANES, HALVES, CAP, grid_count, -1).transpose(1, 3, 0, 2, 4)
-    pieces = pieces.reshape((HALVES * grid_count,) + pieces.shape[2:])
-    summed = lax.psum_scatter(pieces, ("x", "grid"), scatter_dimension=0, tiled=False)
-    return lax.all_to_all(summed, "z", 0, 0, tiled=True)
+def other_core(column):
+    return column + 1 - 2 * (column % 2)
+
+
+def meet(peers):
+    barrier = pltpu.get_barrier_semaphore()
+    for peer in peers:
+        pl.semaphore_signal(barrier, inc=1, device_id=peer, device_id_type=MESH)
+    pl.semaphore_wait(barrier, len(peers))
+
+
+def partners():
+    plane, half, column = lax.axis_index("z"), lax.axis_index("x"), lax.axis_index("grid")
+    planes = [{"z": (plane + j) % PLANES} for j in range(PLANES)]
+    along_x, along_y = {"x": 1 - half}, {"grid": (column + 2) % 4}
+    core = {"grid": other_core(column)}
+    return plane, half, column, planes, along_x, along_y, core
+
+
+def gather_kernel(slots_ref, out_ref, send, recv, local, *, same):
+    plane, half, column, planes, along_x, along_y, core = partners()
+    cap, width = slots_ref.shape[-2:]
+    middle = cap // 2
+    meet(planes[1:] + [along_x, along_y, core])
+
+    def piece(source, at_half, at_column, first=0, count=cap):
+        columns = pl.ds(pl.multiple_of(at_column * width, width), width)
+        return out_ref.at[source, at_half, pl.ds(first, count), columns]
+
+    def source_of(j):
+        return (plane - j + PLANES) % PLANES
+
+    def slots_for(j):
+        return slots_ref if same else slots_ref.at[(plane + j) % PLANES]
+
+    started = []
+
+    def copy(index, source, target, peer):
+        made = pltpu.make_async_remote_copy(
+            src_ref=source, dst_ref=target, send_sem=send.at[index], recv_sem=recv.at[index],
+            device_id=peer, device_id_type=MESH,
+        )
+        made.start()
+        started.append(made)
+
+    def arrived(index, target, peer):
+        pltpu.make_async_remote_copy(
+            src_ref=target, dst_ref=target, send_sem=send.at[index], recv_sem=recv.at[index],
+            device_id=peer, device_id_type=MESH,
+        ).wait_recv()
+
+    y_column, core_column = (column + 2) % 4, other_core(column)
+    core_y = (core_column + 2) % 4
+    for j in (2, 1, 3):
+        copy(j, slots_for(j), piece(plane, half, column), planes[j])
+    keep = pltpu.make_async_copy(slots_for(0), piece(plane, half, column), local)
+    keep.start()
+
+    def spread(j):
+        place = piece(source_of(j), half, column)
+        if j:
+            arrived(j, place, planes[(PLANES - j) % PLANES])
+        source = place if j else slots_for(0)
+        copy(4 + j, source, place, along_x)
+        copy(8 + j, source, place, along_y)
+        copy(12 + j, source, place, core)
+
+    def forward(j):
+        source = source_of(j)
+        from_x = piece(source, 1 - half, column)
+        arrived(4 + j, from_x, along_x)
+        part = piece(source, 1 - half, column, 0, middle)
+        copy(16 + j, part, part, along_y)
+        copy(20 + j, from_x, from_x, core)
+        from_y = piece(source, half, y_column)
+        arrived(8 + j, from_y, along_y)
+        part = piece(source, half, y_column, middle, cap - middle)
+        copy(24 + j, part, part, along_x)
+        copy(28 + j, from_y, from_y, core)
+
+    def cross(j):
+        source = source_of(j)
+        arrived(16 + j, piece(source, 1 - half, y_column, 0, middle), along_y)
+        arrived(24 + j, piece(source, 1 - half, y_column, middle, cap - middle), along_x)
+        place = piece(source, 1 - half, y_column)
+        copy(32 + j, place, place, core)
+
+    def from_core(j):
+        source = source_of(j)
+        arrived(12 + j, piece(source, half, core_column), core)
+        arrived(20 + j, piece(source, 1 - half, core_column), core)
+        arrived(28 + j, piece(source, half, core_y), core)
+        arrived(32 + j, piece(source, 1 - half, core_y), core)
+
+    order = (0, 1, 3, 2)
+    for step in range(len(order) + 2):
+        if step < len(order):
+            spread(order[step])
+        if 0 <= step - 1 < len(order):
+            forward(order[step - 1])
+        if 0 <= step - 2 < len(order):
+            cross(order[step - 2])
+    for j in order:
+        from_core(j)
+    for made in started:
+        made.wait_send()
+    keep.wait()
+
+
+def gathered(slots, collective_id):
+    rows, width = slots.shape[-2:]
+    out = pl.pallas_call(
+        functools.partial(gather_kernel, same=slots.ndim == 2),
+        out_shape=jax.ShapeDtypeStruct((PLANES, HALVES, rows, 4 * width), BF16),
+        in_specs=[pl.BlockSpec(memory_space=pl.ANY)],
+        out_specs=pl.BlockSpec(memory_space=pl.ANY),
+        scratch_shapes=[
+            pltpu.SemaphoreType.DMA((36,)),
+            pltpu.SemaphoreType.DMA((36,)),
+            pltpu.SemaphoreType.DMA,
+        ],
+        compiler_params=pltpu.CompilerParams(collective_id=collective_id, has_side_effects=True),
+        cost_estimate=pl.CostEstimate(flops=0, bytes_accessed=200_000_000, transcendentals=0),
+        name="gather_rows",
+    )(slots)
+    return out.reshape(BLOCKS * rows, 4 * width)
+
+
+def scatter_kernel(partial_ref, out_ref, own, other, crossing, side, send, recv, load):
+    plane, half, column, planes, along_x, along_y, core = partners()
+    cap, width = out_ref.shape[-2:]
+    middle = cap // 2
+    chunk = 32
+    meet(planes[1:] + [along_x, along_y, core])
+    y_column, core_column = (column + 2) % 4, other_core(column)
+    core_y = (core_column + 2) % 4
+    halves = (half, 1 - half, half, 1 - half)
+    own_columns = (column, column, y_column, y_column)
+    core_columns = (core_column, core_column, core_y, core_y)
+    started = []
+
+    def copy(index, source, target, peer):
+        made = pltpu.make_async_remote_copy(
+            src_ref=source, dst_ref=target, send_sem=send.at[index], recv_sem=recv.at[index],
+            device_id=peer, device_id_type=MESH,
+        )
+        made.start()
+        started.append(made)
+
+    def arrived(index, target, peer):
+        pltpu.make_async_remote_copy(
+            src_ref=target, dst_ref=target, send_sem=send.at[index], recv_sem=recv.at[index],
+            device_id=peer, device_id_type=MESH,
+        ).wait_recv()
+
+    def part(j, q, at_columns):
+        columns = pl.ds(pl.multiple_of(at_columns[q] * width, width), width)
+        return partial_ref.at[(plane + j) % PLANES, halves[q], :, columns]
+
+    def loading(j, q):
+        return pltpu.make_async_copy(part(j, q, own_columns), own.at[j, q], load.at[4 * j + q])
+
+    order = (2, 1, 3, 0)
+    for j in order:
+        for q in (3, 2, 1, 0):
+            copy(4 * j + q, part(j, q, core_columns), other.at[j, q], core)
+            loading(j, q).start()
+
+    def add(j, q, first, count, terms):
+        def step(i, nothing):
+            rows = pl.ds(pl.multiple_of(first + i * chunk, chunk), chunk)
+            total = own[j, q, rows, :].astype(F32)
+            for ref, index in terms:
+                total = total + ref[index + (rows, slice(None))].astype(F32)
+            own[j, q, rows, :] = total.astype(BF16)
+            return nothing
+
+        lax.fori_loop(0, count // chunk, step, 0)
+
+    def chip_sum(j, q):
+        arrived(4 * j + q, other.at[j, q], core)
+        loading(j, q).wait()
+        add(j, q, 0, cap, [(other, (j, q))])
+
+    def stage_one(j):
+        chip_sum(j, 3)
+        first, last = pl.ds(0, middle), pl.ds(middle, cap - middle)
+        copy(16 + j, own.at[j, 3, first], crossing.at[j, first], along_x)
+        copy(20 + j, own.at[j, 3, last], crossing.at[j, last], along_y)
+        chip_sum(j, 2)
+        chip_sum(j, 1)
+        chip_sum(j, 0)
+
+    def stage_two(j):
+        arrived(16 + j, crossing.at[j, pl.ds(0, middle)], along_x)
+        add(j, 2, 0, middle, [(crossing, (j,))])
+        copy(24 + j, own.at[j, 2], side.at[j, 1], along_y)
+        arrived(20 + j, crossing.at[j, pl.ds(middle, cap - middle)], along_y)
+        add(j, 1, middle, cap - middle, [(crossing, (j,))])
+        copy(28 + j, own.at[j, 1], side.at[j, 0], along_x)
+
+    def stage_three(j):
+        arrived(24 + j, side.at[j, 1], along_y)
+        arrived(28 + j, side.at[j, 0], along_x)
+        add(j, 0, 0, cap, [(side, (j, 0)), (side, (j, 1))])
+        if j:
+            copy(32 + j, own.at[j, 0], out_ref.at[plane], planes[j])
+
+    for step in range(len(order) + 2):
+        if step < len(order):
+            stage_one(order[step])
+        if 0 <= step - 1 < len(order):
+            stage_two(order[step - 1])
+        if 0 <= step - 2 < len(order):
+            stage_three(order[step - 2])
+    keep = pltpu.make_async_copy(own.at[0, 0], out_ref.at[plane], load.at[16])
+    keep.start()
+    for j in range(1, PLANES):
+        arrived(32 + j, out_ref.at[(plane - j + PLANES) % PLANES], planes[PLANES - j])
+    for made in started:
+        made.wait_send()
+    keep.wait()
+
+
+def scattered(partial, rows, collective_id):
+    width = partial.shape[1] // 4
+    return pl.pallas_call(
+        scatter_kernel,
+        out_shape=jax.ShapeDtypeStruct((PLANES, rows, width), BF16),
+        in_specs=[pl.BlockSpec(memory_space=pl.ANY)],
+        out_specs=pl.BlockSpec(memory_space=pl.ANY),
+        scratch_shapes=[
+            pltpu.VMEM((PLANES, 4, rows, width), BF16),
+            pltpu.VMEM((PLANES, 4, rows, width), BF16),
+            pltpu.VMEM((PLANES, rows, width), BF16),
+            pltpu.VMEM((PLANES, 2, rows, width), BF16),
+            pltpu.SemaphoreType.DMA((36,)),
+            pltpu.SemaphoreType.DMA((36,)),
+            pltpu.SemaphoreType.DMA((17,)),
+        ],
+        compiler_params=pltpu.CompilerParams(
+            collective_id=collective_id, has_side_effects=True, vmem_limit_bytes=VMEM_BYTES
+        ),
+        cost_estimate=pl.CostEstimate(flops=0, bytes_accessed=200_000_000, transcendentals=0),
+        name="scatter_rows",
+    )(partial.reshape(PLANES, HALVES, rows, 4 * width))
 
 
 def grid_sum(values):
@@ -286,15 +520,16 @@
     kv_pieces = kv_pieces.transpose(1, 0, 3, 2, 4).reshape(1, HALVES, own_rows, 2 * span)
     kv_pieces = jnp.broadcast_to(kv_pieces, (PLANES,) + kv_pieces.shape[1:])
     qkv_pieces = jnp.concatenate([query_pieces, kv_pieces], axis=-1)
-    qkv_weight = spread_weights(qkv_pieces.reshape(BLOCKS, own_rows, 3 * span))
-    qkv_weight = qkv_weight.reshape(width_all, 3 * span)
-    out_pieces = attention_out.reshape(BLOCKS, span, own_rows)
-    out_weight = spread_weights(out_pieces).transpose(2, 0, 1, 3).reshape(span, width_all)
+    out_pieces = attention_out.reshape(BLOCKS, span, own_rows).swapaxes(1, 2)
+    first_pieces = jnp.concatenate([qkv_pieces.reshape(BLOCKS, own_rows, 3 * span), out_pieces], axis=2)
+    first_weight = spread_weights(first_pieces).reshape(width_all, 4 * span)
+    qkv_weight, out_weight = first_weight[:, : 3 * span], first_weight[:, 3 * span :]
     up_pieces = expert_gate_up.reshape(PLANES, own_rows, 2, HALVES, hidden_units)
     up_pieces = up_pieces.transpose(0, 3, 1, 2, 4).reshape(BLOCKS, own_rows, 2 * hidden_units)
-    up_weight = spread_weights(up_pieces).reshape(width_all, 2 * hidden_units)
-    down_pieces = expert_down.reshape(BLOCKS, hidden_units, own_rows)
-    down_weight = spread_weights(down_pieces).transpose(2, 0, 1, 3).reshape(hidden_units, width_all)
+    down_pieces = expert_down.reshape(BLOCKS, hidden_units, own_rows).swapaxes(1, 2)
+    second_pieces = jnp.concatenate([up_pieces, down_pieces], axis=2)
+    second_weight = spread_weights(second_pieces).reshape(width_all, 3 * hidden_units)
+    up_weight, down_weight = second_weight[:, : 2 * hidden_units], second_weight[:, 2 * hidden_units :]
 
     small = jnp.concatenate(
         [attention_gain[:, None], feedforward_gain[:, None], attention_router, feedforward_router],
@@ -325,10 +560,9 @@
         return jnp.einsum("est,esf->etf", pick, slots, preferred_element_type=F32)
 
     grad_out = output_grad.astype(F32)
-    grad_slots_second = to_plane(to_slots(output_grad, own_pick_second))
-
-    inputs = lax.all_gather(tokens, "grid", axis=1, tiled=True)
-    inputs = lax.all_gather(inputs, PLACES, axis=0, tiled=True).astype(F32)
+    grad_slots_second = gathered(to_slots(output_grad, own_pick_second), 1)
+
+    inputs = gathered(tokens, 0).astype(F32)
     inverse_first = lax.rsqrt(jnp.mean(inputs * inputs, axis=-1, keepdims=True) + EPSILON)
     hidden_first = (inputs * inverse_first * gain_first).astype(BF16)
     gates_first = route_gates(dot(hidden_first, router_first), member_first)
@@ -362,7 +596,7 @@
     attended, lse = attention_forward(*attention_args, head_width)
     gate_first = lax.dynamic_index_in_dim(gates_first, plane, 1, keepdims=False)
     gate_slots_first = slot_values(gate_first)
-    branch_slots = from_plane(dot(attended, out_weight).astype(BF16), grid_count)
+    branch_slots = scattered(contract_last(attended, out_weight).astype(BF16), CAP, 2)
     branch_first = to_tokens(branch_slots, own_pick_first)
     own_gates_first = own(gates_first)
     residual = tokens.astype(F32) + jnp.sum(own_gates_first.T[:, :, None] * branch_first, axis=0)
@@ -371,11 +605,8 @@
     inverse_second = lax.rsqrt(square / width_all + EPSILON)[:, None]
     normed_second = residual * inverse_second
     hidden_second = (normed_second * mine(gain_second)).astype(BF16)
-    slots_second = to_plane(to_slots(hidden_second, own_pick_second))
+    slots_second = gathered(to_slots(hidden_second, own_pick_second), 1)
     plane_gates = dot(slots_second, router_second)
-    slot_member = jnp.stack(
-        [slot_values(member_second[:, e].astype(jnp.int32))[:, 0] for e in range(PLANES)], axis=1
-    )
     rank_pick = picks(rank_second)
 
     def slot_values_second(per_token):
@@ -393,27 +624,26 @@
     sigmoid_gate = jax.nn.sigmoid(gate_pre)
     silu_gate = gate_pre * sigmoid_gate
     inner = silu_gate * up_pre
-    result_slots = from_plane(dot(inner.astype(BF16), down_weight).astype(BF16), grid_count)
+    result_slots = scattered(contract_last(inner.astype(BF16), down_weight).astype(BF16), CAP, 2)
     own_logits = grid_sum(dot(hidden_second, mine(router_second)))
     own_gates_second = route_gates(own_logits, own_member_second)
     branch_second = to_tokens(result_slots, own_pick_second)
     layer_output = residual + jnp.sum(own_gates_second.T[:, :, None] * branch_second, axis=0)
     layer_output = layer_output.astype(BF16)
 
-    grad_inner = gate_slots_second * contract_last(grad_slots_second, down_weight)
+    grad_inner = gate_slots_second * dot(grad_slots_second, down_weight)
     grad_gate = grad_inner * up_pre * sigmoid_gate * (1.0 + gate_pre * (1.0 - sigmoid_gate))
     grad_gate_up = jnp.concatenate([grad_gate, grad_inner * silu_gate], axis=1).astype(BF16)
-    grad_rows = from_plane(contract_last(grad_gate_up, up_weight).astype(BF16), grid_count)
+    grad_rows = scattered(contract_last(grad_gate_up, up_weight).astype(BF16), CAP, 2)
     grad_up_weight = contract_first(slots_second, grad_gate_up).astype(BF16)
-    grad_up_weight = return_gradients(
-        grad_up_weight.reshape(groups, BLOCKS, own_rows, 2 * hidden_units)
-    )
-    grad_down = contract_first((gate_slots_second * inner).astype(BF16), grad_slots_second)
-    grad_down = grad_down.astype(BF16).reshape(hidden_units, groups, BLOCKS, own_rows)
-    grad_down = return_gradients(grad_down.transpose(1, 2, 0, 3))
-    expert_gate_up_grad = grad_up_weight.reshape(PLANES, HALVES, own_rows, 2, hidden_units)
+    grad_down = contract_first(grad_slots_second, (gate_slots_second * inner).astype(BF16))
+    grad_second = jnp.concatenate([grad_up_weight, grad_down.astype(BF16)], axis=1)
+    grad_second = return_gradients(grad_second.reshape(groups, BLOCKS, own_rows, 3 * hidden_units))
+    expert_gate_up_grad = grad_second[:, :, : 2 * hidden_units].reshape(
+        PLANES, HALVES, own_rows, 2, hidden_units
+    )
     expert_gate_up_grad = expert_gate_up_grad.transpose(0, 2, 3, 1, 4).reshape(expert_gate_up.shape)
-    expert_down_grad = grad_down.reshape(expert_down.shape)
+    expert_down_grad = grad_second[:, :, 2 * hidden_units :].swapaxes(1, 2).reshape(expert_down.shape)
 
     grad_gates_second = grid_sum(jnp.sum(branch_second * grad_out[None], axis=2).T)
     grad_logits_second = logits_grad(own_gates_second, grad_gates_second)
@@ -427,15 +657,16 @@
     inner_mean = grid_sum(jnp.sum(grad_normed * normed_second, axis=1))[:, None] / width_all
     grad_residual = grad_out + inverse_second * (grad_normed - normed_second * inner_mean)
 
-    grad_slots_first = to_plane(to_slots(grad_residual.astype(BF16), own_pick_first))
-    grad_attended = gate_slots_first * contract_last(grad_slots_first, out_weight)
+    grad_slots_first = gathered(to_slots(grad_residual.astype(BF16), own_pick_first), 1)
+    grad_attended = gate_slots_first * dot(grad_slots_first, out_weight)
     grad_attended = grad_attended.astype(BF16)
     grad_out_weight = contract_first(
-        (gate_slots_first * attended.astype(F32)).astype(BF16), grad_slots_first
-    )
-    grad_out_weight = grad_out_weight.astype(BF16).reshape(span, groups, BLOCKS, own_rows)
-    grad_out_weight = return_gradients(grad_out_weight.transpose(1, 2, 0, 3))
-    attention_out_grad = grad_out_weight.reshape(attention_out.shape)
+        grad_slots_first, (gate_slots_first * attended.astype(F32)).astype(BF16)
+    )
+    grad_out_weight = return_gradients(
+        grad_out_weight.astype(BF16).reshape(groups, BLOCKS, own_rows, span)
+    )
+    attention_out_grad = grad_out_weight.swapaxes(1, 2).reshape(attention_out.shape)
     grad_query, grad_keys, grad_values = attention_backward(
         *attention_args, attended, lse, grad_attended, head_width
     )
@@ -454,8 +685,7 @@
         axis=1,
     )
     grad_hidden = contract_last(grad_qkv, qkv_weight).astype(BF16)
-    grad_hidden = lax.psum_scatter(grad_hidden, "grid", scatter_dimension=1, tiled=True)
-    grad_hidden = lax.psum_scatter(grad_hidden, PLACES, scatter_dimension=0, tiled=True)
+    grad_hidden = jnp.sum(scattered(grad_hidden, rows, 3).astype(F32), axis=0)
     grad_qkv_weight = contract_first(hidden_first, grad_qkv).astype(BF16)
     grad_qkv_weight = return_gradients(
         grad_qkv_weight.reshape(groups, BLOCKS, own_rows, 3 * span)
@@ -472,7 +702,7 @@
     own_hidden = (own_normed * mine(gain_first)).astype(BF16)
     grad_gates_first = grid_sum(jnp.sum(branch_first * grad_residual[None], axis=2).T)
     grad_logits_first = logits_grad(own_gates_first, grad_gates_first)
-    grad_hidden_first = grad_hidden.astype(F32) + exact(
+    grad_hidden_first = grad_hidden + exact(
         grad_logits_first, mine(router_first).astype(F32).T
     )
     grad_router_first = exact(own_hidden.astype(F32).T, grad_logits_first)

time: 2000 us -> 1670 us (0.83)
  Pallas kernels: 95.5 us -> 760 us
  waiting for transfers between devices: 750 us -> 93 us
  blocking collectives: 373 us -> 180 us
  local copies, waits for them, and re-layouts: 345 us -> 175 us
    pallas_call x0 -> x8, Pallas kernels: none -> 671 us  [the longest x4 392 us: scattered(): pl.pallas_call(scatter_kernel, out_shape=jax.ShapeDtypeStruct((PLANES, ro...]
    all_to_all x8 -> x5, waiting for transfers between devices: 364 us -> 28.8 us  [exchanged(): return lax.all_to_all(pieces, PLACES, 0, 0, tiled=True)]
    reduce_scatter x5 -> x0, waiting for transfers between devices: 174 us -> none  [the longest x3 153 us: from_plane(): lax.psum_scatter(pieces, ('x', 'grid'), scatter_dimension=0, tiled=False)]
    all_gather x5 -> x0, waiting for transfers between devices: 114 us -> none  [the longest x3 53.4 us: to_plane(): gathered = lax.all_gather(arrived, ('x', 'grid'), axis=0, tiled=False)]
    all_to_all x3 -> x0, blocking collectives: 105 us -> none  [to_plane(): arrived = lax.all_to_all(slots, 'z', 0, 0, tiled=True)]
    reshape x9 -> x1, local copies, waits for them, and re-layouts: 97.7 us -> 0.01 us  [the longest x3 53.8 us: from_plane(): partial.reshape(PLANES, HALVES, CAP, grid_count, -1)]
    unnamed x139 -> x98, local copies, waits for them, and re-layouts: 115 us -> 69.9 us
    all_gather x1, blocking collectives: 157 us -> 112 us  [per_device(): small = lax.all_gather(small.T, ('t', 'z', 'x'), axis=1, tiled=True)]
  transfers between devices with their start and end apart: 22 -> 6, of which waited for: 15 -> 2; matrix products, arithmetic and copies ran while one was open for 23% -> 22% of each run, Pallas kernels for 0% -> 32%
where the time goes in v2:
time: 1670 us; the launch traced here: 1660 us
  Pallas kernels  760 us (46%)
  matrix products  237 us (14%)
  blocking collectives  180 us (11%)
  local copies, waits for them, and re-layouts  175 us (10%)
  other arithmetic  144 us (9%)
  waiting for transfers between devices  93 us (6%)
  starting transfers between devices  52.9 us (3%)
    pallas_call x4, Pallas kernels, scattered(): pl.pallas_call(scatter_kernel, out_shape=jax.ShapeDtypeStruct((PLANES, ro...  392 us
    pallas_call x4, Pallas kernels, gathered(): pl.pallas_call(functools.partial(gather_kernel, same=slots.ndim == 2), ou...  279 us
    all_gather x1, blocking collectives, per_device(): small = lax.all_gather(small.T, ('t', 'z', 'x'), axis=1, tiled=True)  112 us
    dot_general x7, matrix products, dot(): return jnp.dot(left, right, preferred_element_type=F32)  84.7 us
    unnamed x98, local copies, waits for them, and re-layouts  69.9 us
    dot_general x4, matrix products, contract_last(): lax.dot_general(left, right, (((1,), (1,)), ((), ())), preferred_element_...  67.8 us
    reduce_scatter x1, waiting for transfers between devices, per_device(): lax.psum_scatter(small_grads, ('t',) + PLACES, scatter_dimension=0, tiled...  64.2 us
    dot_general x4, matrix products, contract_first(): lax.dot_general(left, right, (((0,), (0,)), ((), ())), preferred_element_...  58 us
  transfers between devices with their start and end apart: 6, of which 2 were waited for; matrix products, arithmetic and copies ran while one was open for 22% of the time, Pallas kernels for 32%

profile of v2, /device:TPU:0, one launch (start us, length us, event | category | flops | bytes accessed | tf_op | source)
XLA Modules:
  0.0 1657.9 jit_solution(17504345326860788302)
XLA Ops:
  16.1 7.4 all-to-all-start
  24.5 112.3 %all_gather.32 = bf16[10,2048]{1,0:T(8,128)(2,1)S(1)} all-gather(bf16[10,256]{1,0:T(8,128)(2,1)S(1)} %maximum_bitcast_fusion), channel_id=1, replica_groups=mesh['t'=1,'z'=4,'x'=2,'grid'=4] {'t','z','x'}, dimensions={1}, use_global_device_ids=true | all-gather | bytes 46080 | tf_op jit(solution)/shard_map/all_gather | solution.py:538
  136.8 31.0 %all_gather.31 = s32[4096,4]{0,1:T(4,128)S(1)} all-gather(s32[512,4]{0,1:T(4,128)S(1)} %pad_add_fusion), channel_id=1, replica_groups=mesh['t'=1,'z'=4,'x'=2,'grid'=4] {'z','x'}, dimensions={0}, use_global_device_ids=true | all-gather | bytes 73728 | tf_op jit(solution)/shard_map/all_gather | solution.py:543
  178.4 85.5 %gather_rows.4 = bf16[4,2,512,2048]{3,2,1,0:T(8,128)(2,1)} custom-call(bf16[512,512]{1,0:T(8,128)(2,1)} %slots_ref.1), custom_call_target="tpu_custom_call" | custom-call | bytes 200000000 | tf_op jit(solution)/shard_map/gather_rows/pallas_call | solution.py:326
  263.9 7.5 multiply_reduce_fusion
  274.7 8.7 fusion.1
  289.9 14.8 copy.230
  304.7 5.7 copy.231
  312.3 75.8 %gather_rows.6 = bf16[4,2,320,2048]{3,2,1,0:T(8,128)(2,1)} custom-call(bf16[4,320,512]{2,1,0:T(8,128)(2,1)} %fusion.28.slots_ref), custom_call_target="tpu_custom_call" | custom-call | bytes 200000000 | tf_op jit(solution)/shard_map/gather_rows/pallas_call | solution.py:326
  388.1 10.4 fusion.100
  402.0 6.4 pad_maximum_fusion
  408.4 6.2 multiply_cosine_fusion.1
  414.6 9.4 fusion.51
  424.0 17.0 %all-to-all-start.1 = ((bf16[8,256,2112]{1,2,0:T(8,128)(2,1)}), bf16[8,256,2112]{1,2,0:T(8,128)(2,1)}, u32[]{:S(2)}, u32[]{:S(2)}) async-start(bf16[8,256,2112]{1,2,0:T(8,128)(2,1)} %pad_maximum_fusion), calls=%async_computation.1 | async-start | bytes 17301504 | tf_op jit(solution)/shard_map/all_to_all | solution.py:204
  441.0 20.4 %fusion.16 = f32[4096,768]{0,1:T(8,128)} fusion(bf16[4096,2048]{1,0:T(8,128)(2,1)} %fusion.1, bf16[2048,1024]{1,0:T(8,128)(2,1)} %bitcast.15), kind=kOutput, calls=%fused_computation.65 | convolution fusion | flops 12884901888 | bytes 32505856 | tf_op jit(solution)/shard_map/dot_general | solution.py:43
  469.3 6.2 fusion.93
  477.9 6.2 copy.257
  488.7 6.2 copy.255
  494.9 6.2 copy.256
  501.0 6.2 copy.254
  507.2 10.6 subtract_convert_fusion.1
  517.8 11.8 pad_maximum_fusion.10
  532.8 36.1 %attention_forward.1 = (bf16[2560,256]{1,0:T(8,128)(2,1)}, f32[2,2560,1]{2,1,0:T(8,128)}) custom-call(s32[8]{0:T(128)} %and_select_fusion.begin_ref, bf16[4096,256]{1,0:T(8,128)(2,1)} %bitcast.221, bf16[4096,256]{1,0:T(8,128)(2,1)} %bitcast.223, bf16[4096,256]{1,0:T(8,128)(2,1)} %copy.258.v_ref, s32[8,1,512]{2,1,0:T(1,128)} %subtract_select_fusion.rank_ref, ...), custom_call_target="tpu_custom_call" | custom-call | flops 10000000000 | bytes 8000000 | tf_op jit(solution)/shard_map/attention_forward/pallas_call | solution.py:155
  568.9 8.6 convolution_convert_fusion.3
  577.6 82.3 %scatter_rows.4 = bf16[4,320,512]{2,1,0:T(8,128)(2,1)} custom-call(bf16[4,2,320,2048]{3,2,1,0:T(8,128)(2,1)} %bitcast.184), custom_call_target="tpu_custom_call" | custom-call | bytes 200000000 | tf_op jit(solution)/shard_map/scatter_rows/pallas_call | solution.py:441
  665.3 5.2 all_gather.33
  671.1 5.4 all_gather.34
  678.7 58.7 %gather_rows.5 = bf16[4,2,320,2048]{3,2,1,0:T(8,128)(2,1)} custom-call(bf16[4,320,512]{2,1,0:T(8,128)(2,1)} %fusion.27.slots_ref), custom_call_target="tpu_custom_call" | custom-call | bytes 200000000 | tf_op jit(solution)/shard_map/gather_rows/pallas_call | solution.py:326
  737.6 6.8 fusion.101
  744.6 11.7 copy.232
  756.3 22.4 %fusion.5 = f32[2560,1408]{0,1:T(8,128)} fusion(bf16[2560,2048]{1,0:T(8,128)(2,1)} %bitcast.186, bf16[2048,2112]{1,0:T(8,128)(2,1)} %bitcast.206), kind=kOutput, calls=%fused_computation.34 | convolution fusion | flops 14763950080 | bytes 30670848 | tf_op jit(solution)/shard_map/dot_general | solution.py:43
  778.7 15.5 convolution_convert_fusion.2
  794.2 19.0 %multiply_convert_fusion.2 = (bf16[2560,704]{0,1:T(8,128)(2,1)}, bf16[2560,704]{0,1:T(8,128)(2,1)}) fusion(f32[2560,1408]{0,1:T(8,128)} %fusion.5, f32[2560]{0:T(1024)S(1)} %divide_reduce_fusion, bf16[2560,2048]{1,0:T(8,128)(2,1)} %bitcast.200, bf16[2048,2112]{1,0:T(8,128)(2,1)} %bitcast.208), kind=kOutput, calls=%fused_computation.16 | convolution fusion | flops 7407206400 | bytes 35268608 | tf_op jit(solution)/shard_map/dot_general | solution.py:43
  813.2 23.3 %convolution_convert_fusion.1 = bf16[2560,2048]{1,0:T(8,128)(2,1)} fusion(bf16[2048,2112]{1,0:T(8,128)(2,1)} %bitcast.209, bf16[2560,704]{0,1:T(8,128)(2,1)} %get-tuple-element.106, bf16[2560,704]{0,1:T(8,128)(2,1)} %get-tuple-element.105), kind=kOutput, calls=%fused_computation.6 | convolution fusion | flops 14783610880 | bytes 23461888 | tf_op jit(solution)/shard_map/dot_general | solution.py:51
  836.5 62.6 %scatter_rows.6 = bf16[4,320,512]{2,1,0:T(8,128)(2,1)} custom-call(bf16[4,2,320,2048]{3,2,1,0:T(8,128)(2,1)} %bitcast.205), custom_call_target="tpu_custom_call" | custom-call | bytes 200000000 | tf_op jit(solution)/shard_map/scatter_rows/pallas_call | solution.py:441
  901.3 51.8 %scatter_rows.5 = bf16[4,320,512]{2,1,0:T(8,128)(2,1)} custom-call(bf16[4,2,320,2048]{3,2,1,0:T(8,128)(2,1)} %bitcast.202), custom_call_target="tpu_custom_call" | custom-call | bytes 200000000 | tf_op jit(solution)/shard_map/scatter_rows/pallas_call | solution.py:441
  957.4 5.2 all_gather.35
  964.4 5.1 all_gather.36
  976.2 58.7 %gather_rows.7 = bf16[4,2,320,2048]{3,2,1,0:T(8,128)(2,1)} custom-call(bf16[4,320,512]{2,1,0:T(8,128)(2,1)} %fusion.26.slots_ref), custom_call_target="tpu_custom_call" | custom-call | bytes 200000000 | tf_op jit(solution)/shard_map/gather_rows/pallas_call | solution.py:326
  1035.0 8.6 convolution_convert_fusion.6
  1043.6 5.3 fusion.7.grad_ref
  1048.9 52.6 %attention_backward.1 = (f32[2560,256]{1,0:T(8,128)}, f32[4096,256]{1,0:T(8,128)}, f32[4096,256]{1,0:T(8,128)}) custom-call(s32[8]{0:T(128)} %and_select_fusion.begin_ref, bf16[4096,256]{1,0:T(8,128)(2,1)} %bitcast.222, bf16[4096,256]{1,0:T(8,128)(2,1)} %bitcast.224, bf16[4096,256]{1,0:T(8,128)(2,1)} %copy.258.v_ref, ...), custom_call_target="tpu_custom_call" | custom-call | flops 20000000000 | bytes 16000000 | tf_op jit(solution)/shard_map/attention_backward/pallas_call | solution.py:179
  1104.6 5.0 subtract_convert_fusion.3
  1115.0 17.0 %all-to-all-start.3 = ((bf16[8,256,256]{2,1,0:T(8,128)(2,1)}), bf16[8,256,256]{2,1,0:T(8,128)(2,1)S(1)}, u32[]{:S(2)}, u32[]{:S(2)}) async-start(bf16[8,256,256]{2,1,0:T(8,128)(2,1)} %bitcast.231), calls=%async_computation.4 | async-start | bytes 2097152 | tf_op jit(solution)/shard_map/all_to_all | solution.py:204
  1138.3 5.9 reshape.701
  1144.2 19.5 %subtract_convert_fusion = (bf16[4096,2,64]{2,1,0:T(2,128)(2,1)S(1)}, bf16[4096,2,64]{2,1,0:T(2,128)(2,1)S(1)}) fusion(f32[4096,2,128]{2,1,0:T(2,128)} %reshape.701, f32[4096,64]{1,0:T(8,128)} %get-tuple-element.131, f32[4096,64]{1,0:T(8,128)S(1)} %copy-done.2), kind=kLoop, calls=%fused_computation.41 | loop fusion | flops 4194304 | bytes 8388608 | tf_op jit(solution)/shard_map/convert.15
  1163.7 5.7 pad_maximum_fusion.12
  1171.1 18.8 %convolution_convert_fusion.5 = bf16[2048,768]{1,0:T(8,128)(2,1)} fusion(bf16[4096,2048]{1,0:T(8,128)(2,1)} %fusion.1, bf16[4096,256]{1,0:T(8,128)(2,1)S(1)} %copy-done.13, bf16[4096,256]{1,0:T(8,128)(2,1)S(1)} %bitcast.225, bf16[4096,256]{1,0:T(8,128)(2,1)S(1)} %bitcast.263), kind=kOutput, calls=%fused_computation.54 | convolution fusion | flops 12905349120 | bytes 26214400 | tf_op jit(solution)/shard_map/dot_general | solution.py:47
  1189.9 6.4 all-to-all-start.2
  1196.3 14.3 fusion.11
  1210.6 16.3 convolution_convert_fusion.4
  1231.0 7.3 copy.275
  1238.3 28.8 %all-to-all-done.2 = bf16[8,256,768]{2,1,0:T(8,128)(2,1)} async-done(((bf16[8,256,768]{2,1,0:T(8,128)(2,1)}), bf16[8,256,768]{2,1,0:T(8,128)(2,1)}, u32[]{:S(2)}, u32[]{:S(2)}) %all-to-all-start.2) | async-done | bytes 3145760 | tf_op jit(solution)/shard_map/all_to_all | solution.py:204
  1267.1 5.1 all-to-all-start.4
  1276.5 5.2 all_gather.37
  1282.0 20.4 %convolution_convert_fusion = bf16[4096,2048]{1,0:T(8,128)(2,1)} fusion(bf16[2048,1024]{1,0:T(8,128)(2,1)} %bitcast.15, bf16[4096,256]{1,0:T(8,128)(2,1)} %convert_element_type.323, bf16[4096,256]{1,0:T(8,128)(2,1)} %bitcast.226, bf16[4096,256]{1,0:T(8,128)(2,1)} %bitcast.262), kind=kOutput, calls=%fused_computation.4 | convolution fusion | flops 12912164864 | bytes 26214400 | tf_op jit(solution)/shard_map/dot_general | solution.py:51
  1302.4 195.8 %scatter_rows.7 = bf16[4,512,512]{2,1,0:T(8,128)(2,1)} custom-call(bf16[4,2,512,2048]{3,2,1,0:T(8,128)(2,1)} %bitcast.196), custom_call_target="tpu_custom_call" | custom-call | bytes 200000000 | tf_op jit(solution)/shard_map/scatter_rows/pallas_call | solution.py:441
  1503.6 5.1 all_gather.38
  1510.2 5.4 all_gather.39
  1518.8 64.2 %reduce-scatter.2.cloned.1.call-done = f32[1,10,256]{2,1,0:T(8,128)} async-done(((f32[8,10,256]{2,1,0:T(8,128)}), f32[1,10,256]{2,1,0:T(8,128)}) %reduce-scatter.2.cloned.1.call-update) | async-done | bytes 10256 | tf_op jit(solution)/shard_map/reduce_scatter | solution.py:720
  1598.2 5.9 reshape.705
  1613.2 5.7 convert_bitcast_fusion
  1618.9 9.5 copy.250
  1628.4 17.5 %copy.252 = f32[4,256,2,1408]{3,2,1,0:T(2,128)} copy(f32[4,256,2,1408]{1,3,2,0:T(8,128)} %bitcast.190) | data formatting | bytes 23068672
  (266 shorter events, 141.0 us)
Async XLA Ops:
  16.1 7.5 copy-start.25
  16.1 8.0 copy-start.35
  16.1 8.0 copy-start.36
  16.1 8.4 copy-start.33
  16.1 8.4 copy-start.34
  16.1 120.7 %copy-start.31 = (s32[512,2]{0,1:T(2,128)S(1)}, s32[512,2]{0,1:T(2,128)}, u32[]{:S(2)}) copy-start(s32[512,2]{0,1:T(2,128)} %param.17) | copy-start | bytes 12292
  16.1 120.7 %copy-start.32 = (s32[512,2]{0,1:T(2,128)S(1)}, s32[512,2]{0,1:T(2,128)}, u32[]{:S(2)}) copy-start(s32[512,2]{0,1:T(2,128)} %param.16) | copy-start | bytes 12292
  16.1 407.9 %all-to-all-start = ((bf16[8,256,1024]{2,1,0:T(8,128)(2,1)}), bf16[8,256,1024]{2,1,0:T(8,128)(2,1)}, u32[]{:S(2)}, u32[]{:S(2)}) async-start(bf16[8,256,1024]{2,1,0:T(8,128)(2,1)} %pad_maximum_fusion.6), calls=%async_computation | async-start | bytes 8388608 | tf_op jit(solution)/shard_map/all_to_all | solution.py:204
  136.8 137.9 %copy-start.26 = (f32[1,2048]{1,0:T(1,128)}, f32[1,2048]{1,0:T(1,128)S(1)}, u32[]{:S(2)}) copy-start(f32[1,2048]{1,0:T(1,128)S(1)} %get-tuple-element.128) | copy-start | bytes 24580
  263.9 10.8 copy-start
  272.1 126.7 %copy-start.18 = (s32[8,512]{1,0:T(8,128)}, s32[8,512]{1,0:T(8,128)S(1)}, u32[]{:S(2)}) copy-start(s32[8,512]{1,0:T(8,128)S(1)} %get-tuple-element.101) | copy-start | bytes 49156
  274.7 9.6 copy-start.15
  388.1 13.8 copy-start.11
  398.6 9.8 copy-start.17
  424.0 83.3 %copy-start.1 = (f32[4096,64]{1,0:T(8,128)}, f32[4096,64]{1,0:T(8,128)S(1)}, u32[]{:S(2)}) copy-start(f32[4096,64]{1,0:T(8,128)S(1)} %get-tuple-element.133) | copy-start | bytes 3145732
  424.0 320.6 %all-to-all-start.1 = ((bf16[8,256,2112]{1,2,0:T(8,128)(2,1)}), bf16[8,256,2112]{1,2,0:T(8,128)(2,1)}, u32[]{:S(2)}, u32[]{:S(2)}) async-start(bf16[8,256,2112]{1,2,0:T(8,128)(2,1)} %pad_maximum_fusion), calls=%async_computation.1 | async-start | bytes 17301504 | tf_op jit(solution)/shard_map/all_to_all | solution.py:204
  659.9 5.2 copy-start.6
  670.6 66.8 %copy-start.8 = (bf16[512,512]{1,0:T(8,128)(2,1)}, bf16[512,512]{1,0:T(8,128)(2,1)S(1)}, u32[]{:S(2)}) copy-start(bf16[512,512]{1,0:T(8,128)(2,1)S(1)} %multiply_convert_fusion.8) | copy-start | bytes 1572868
  744.5 218.4 %copy-start.20 = (f32[512,4]{0,1:T(4,128)}, f32[512,4]{0,1:T(4,128)S(1)}, u32[]{:S(2)}) copy-start(f32[512,4]{0,1:T(4,128)S(1)} %fusion.73) | copy-start | bytes 24580
  901.3 51.8 %copy-start.16 = (f32[512,512]{0,1:T(8,128)S(1)}, f32[512,512]{0,1:T(8,128)}, u32[]{:S(2)}) copy-start(f32[512,512]{0,1:T(8,128)} %copy.235) | copy-start | bytes 3145732
  962.9 10.4 copy-start.22
  963.0 10.3 copy-start.27
  973.3 1.0 copy-start.4
  976.2 58.8 %copy-start.12 = (bf16[2560,256]{1,0:T(8,128)(2,1)S(1)}, bf16[2560,256]{1,0:T(8,128)(2,1)}, u32[]{:S(2)}) copy-start(bf16[2560,256]{1,0:T(8,128)(2,1)} %get-tuple-element.16.out_ref) | copy-start | bytes 3932164
  976.2 58.8 %copy-start.29 = (f32[2560]{0:T(1024)S(1)}, f32[2560]{0:T(1024)}, u32[]{:S(2)}) copy-start(f32[2560]{0:T(1024)} %mul.523) | copy-start | bytes 30724
  1035.0 8.6 copy-start.3
  1109.7 22.4 %copy-start.19 = (s32[8,512]{1,0:T(8,128)S(1)}, s32[8,512]{1,0:T(8,128)}, u32[]{:S(2)}) copy-start(s32[8,512]{1,0:T(8,128)} %copy-done.18) | copy-start | bytes 49156
  1115.0 74.9 %all-to-all-start.3 = ((bf16[8,256,256]{2,1,0:T(8,128)(2,1)}), bf16[8,256,256]{2,1,0:T(8,128)(2,1)S(1)}, u32[]{:S(2)}, u32[]{:S(2)}) async-start(bf16[8,256,256]{2,1,0:T(8,128)(2,1)} %bitcast.231), calls=%async_computation.4 | async-start | bytes 2097152 | tf_op jit(solution)/shard_map/all_to_all | solution.py:204
  1132.0 4.8 copy-start.10
  1138.3 5.9 copy-start.2
  1163.7 7.4 copy-start.13
  1163.7 7.4 copy-start.37
  1169.8 1.3 copy-start.14
  1189.9 20.7 %slice-start = ((s8[10485760]{0:T(1024)(128)(4,1)}), s8[2097152]{0:T(1024)(128)(4,1)S(1)}, s32[]{:S(2)}) async-start(s8[10485760]{0:T(1024)(128)(4,1)} %bitcast.187), calls=%async_computation.7 | async-start | bytes 4194304
  1189.9 77.2 %all-to-all-start.2 = ((bf16[8,256,768]{2,1,0:T(8,128)(2,1)}), bf16[8,256,768]{2,1,0:T(8,128)(2,1)}, u32[]{:S(2)}, u32[]{:S(2)}) async-start(bf16[8,256,768]{2,1,0:T(8,128)(2,1)} %bitcast.219), calls=%async_computation.3 | async-start | bytes 6291456 | tf_op jit(solution)/shard_map/all_to_all | solution.py:204
  1196.3 14.3 slice-start.1
  1196.3 14.3 slice-start.2
  1196.3 14.3 copy-start.38
  1267.1 5.2 copy-start.24
  1267.1 5.9 copy-start.5
  1267.1 343.1 %all-to-all-start.4 = ((bf16[8,256,2112]{1,2,0:T(8,128)(2,1)}), bf16[8,256,2112]{1,2,0:T(8,128)(2,1)}, u32[]{:S(2)}, u32[]{:S(2)}) async-start(bf16[8,256,2112]{1,2,0:T(8,128)(2,1)} %bitcast.191), calls=%async_computation.5 | async-start | bytes 17301504 | tf_op jit(solution)/shard_map/all_to_all | solution.py:204
  1272.2 310.8 %reduce-scatter.2.cloned.1.call-start = ((), (), s32[]{:S(2)}) async-start(), calls=%async_computation.6 | async-start | bytes 147456 | tf_op jit(solution)/shard_map/reduce_scatter | solution.py:720
  1302.4 198.6 %copy-start.7 = (bf16[512,512]{1,0:T(8,128)(2,1)S(1)}, bf16[512,512]{1,0:T(8,128)(2,1)}, u32[]{:S(2)}) copy-start(bf16[512,512]{1,0:T(8,128)(2,1)} %slots_ref.1) | copy-start | bytes 1572868
  1498.2 11.7 copy-start.9
  1498.2 11.7 copy-start.21
  1498.2 11.7 copy-start.23
  1498.2 11.7 copy-start.28
  1498.2 12.0 copy-start.30
Sparse Core Ops, SparseCore 0:
  1516.5 66.4 reduce-scatter.1

commit v3 on v2

--- a/solution.py
+++ b/solution.py
@@ -3,6 +3,7 @@
 
 import jax
 import jax.numpy as jnp
+import numpy as np
 from jax import lax
 from jax.experimental import pallas as pl
 from jax.experimental.pallas import tpu as pltpu
@@ -22,21 +23,16 @@
 VMEM_BYTES = 56 * 1024 * 1024
 
 
-def rope_tables(positions, table_width):
-    half_width = table_width // 2
-    frequency = ROPE_BASE ** (-jnp.arange(half_width, dtype=F32) / half_width)
-    angles = positions.astype(F32)[:, None] * frequency[None, :]
-    return (jnp.cos(angles), jnp.sin(angles))
-
-
-def rotate(values, cosine, sine_table):
-    half_width = values.shape[-1] // 2
-    leading = values[..., :half_width]
-    trailing = values[..., half_width:]
-    return jnp.concatenate(
-        [leading * cosine - trailing * sine_table, trailing * cosine + leading * sine_table],
-        axis=-1,
-    )
+def rope_tables(token_count, width):
+    half = width // 2
+    frequency = np.float32(ROPE_BASE) ** (-np.arange(half, dtype=np.float32) / np.float32(half))
+    angles = np.arange(token_count, dtype=np.float32)[:, None] * frequency.astype(np.float32)[None, :]
+    cosine, sine = np.cos(angles).astype(np.float32), np.sin(angles).astype(np.float32)
+    return np.concatenate([cosine, cosine], axis=1), np.concatenate([-sine, sine], axis=1)
+
+
+def turned(values, cosine, sine):
+    return values * cosine + pltpu.roll(values, values.shape[1] // 2, 1) * sine
 
 
 def dot(left, right):
@@ -55,8 +51,64 @@
     return jnp.dot(left, right, precision=lax.Precision.HIGHEST)
 
 
-def first_of(position_ref, index):
-    return position_ref[index]
+def project_kernel(
+    tokens_ref, gain_ref, weight_ref, router_ref, cos_ref, sin_ref,
+    hidden_ref, q_ref, k_ref, v_ref, logits_ref, inverse_ref, *, head_width
+):
+    x = tokens_ref[0, 0].astype(F32)
+    inverse = lax.rsqrt(jnp.mean(x * x, axis=1, keepdims=True) + EPSILON)
+    inverse_ref[...] = inverse
+    hidden = (x * inverse * gain_ref[...]).astype(BF16)
+    hidden_ref[...] = hidden
+    logits_ref[...] = dot(hidden, router_ref[...])
+    made = dot(hidden, weight_ref[...])
+    span = q_ref.shape[1]
+    cosine, sine = cos_ref[...], sin_ref[...]
+    for head in range(span // head_width):
+        at = slice(head * head_width, (head + 1) * head_width)
+        q_ref[:, at] = turned(made[:, at], cosine, sine).astype(BF16)
+        k_ref[:, at] = turned(made[:, span:][:, at], cosine, sine).astype(BF16)
+    v_ref[...] = made[:, 2 * span :].astype(BF16)
+
+
+def project(tokens, rows, gain, weight, router, cosine, sine, span, head_width):
+    width = tokens.shape[-1]
+    token_count = BLOCKS * rows
+    whole = lambda b: (0, 0)
+    block = lambda b: (b, 0)
+    return pl.pallas_call(
+        functools.partial(project_kernel, head_width=head_width),
+        grid=(BLOCKS,),
+        in_specs=[
+            pl.BlockSpec((1, 1, rows, width), lambda b: (b // HALVES, b % HALVES, 0, 0)),
+            pl.BlockSpec((1, width), whole),
+            pl.BlockSpec((width, 3 * span), whole),
+            pl.BlockSpec((width, 128), whole),
+            pl.BlockSpec((rows, head_width), block),
+            pl.BlockSpec((rows, head_width), block),
+        ],
+        out_specs=[
+            pl.BlockSpec((rows, width), block),
+            pl.BlockSpec((rows, span), block),
+            pl.BlockSpec((rows, span), block),
+            pl.BlockSpec((rows, span), block),
+            pl.BlockSpec((rows, 128), block),
+            pl.BlockSpec((rows, 1), block),
+        ],
+        out_shape=[
+            jax.ShapeDtypeStruct((token_count, width), BF16),
+            jax.ShapeDtypeStruct((token_count, span), BF16),
+            jax.ShapeDtypeStruct((token_count, span), BF16),
+            jax.ShapeDtypeStruct((token_count, span), BF16),
+            jax.ShapeDtypeStruct((token_count, 128), F32),
+            jax.ShapeDtypeStruct((token_count, 1), F32),
+        ],
+        compiler_params=pltpu.CompilerParams(vmem_limit_bytes=VMEM_BYTES),
+        cost_estimate=pl.CostEstimate(
+            flops=20_000_000_000, bytes_accessed=50_000_000, transcendentals=0
+        ),
+        name="project",
+    )(tokens, gain, weight, router, cosine, sine)
 
 
 def attention_scores(q, k_ref, low_bound, high_bound, tile, tile_rows, scaling):
@@ -105,7 +157,7 @@
 
 def attention_backward_kernel(
     begin_ref, q_ref, k_ref, v_ref, rank_ref, low_ref, high_ref, out_ref, lse_ref, grad_ref,
-    dq_ref, dk_ref, dv_ref, *, scaling
+    cos_ref, sin_ref, dq_ref, dk_ref, dv_ref, dk_sum, dv_sum, *, scaling
 ):
     block = pl.program_id(1)
     cap, width = out_ref.shape
@@ -119,22 +171,36 @@
 
     @pl.when(block == 0)
     def _():
-        dk_ref[...] = jnp.zeros_like(dk_ref)
-        dv_ref[...] = jnp.zeros_like(dv_ref)
+        dk_sum[...] = jnp.zeros_like(dk_sum)
+        dv_sum[...] = jnp.zeros_like(dv_sum)
 
     def step(tile, dq):
         rows, keys, scores, allowed = attention_scores(
             q, k_ref, low_bound, high_bound, tile, tile_rows, scaling
         )
         chances = jnp.where(allowed, jnp.exp(scores - lse), 0.0)
-        dv_ref[rows, :] += contract_first(chances.astype(BF16), grad)
+        dv_sum[rows, :] += contract_first(chances.astype(BF16), grad)
         grad_chances = contract_last(grad, v_ref[rows, :])
         grad_scores = (chances * (grad_chances - delta)).astype(BF16)
-        dk_ref[rows, :] += contract_first(grad_scores, q) * scaling
+        dk_sum[rows, :] += contract_first(grad_scores, q) * scaling
         return dq + dot(grad_scores, keys)
 
-    dq = lax.fori_loop(begin_ref[block], block + 1, step, jnp.zeros((cap, width), F32))
-    dq_ref[...] = dq * scaling
+    dq = lax.fori_loop(begin_ref[block], block + 1, step, jnp.zeros((cap, width), F32)) * scaling
+    high = dq.astype(BF16)
+    rest = (dq - high.astype(F32)).astype(BF16)
+    dq_tokens = contract_first(pick, high) + contract_first(pick, rest)
+    own = pl.ds(pl.multiple_of(block * tile_rows, tile_rows), tile_rows)
+    dq_ref[...] = turned(dq_tokens, cos_ref[own, :], -sin_ref[own, :]).astype(BF16)
+
+    @pl.when(block == BLOCKS - 1)
+    def _():
+        def finish(tile, nothing):
+            rows = pl.ds(pl.multiple_of(tile * tile_rows, tile_rows), tile_rows)
+            dk_ref[rows, :] = turned(dk_sum[rows, :], cos_ref[rows, :], -sin_ref[rows, :]).astype(BF16)
+            dv_ref[rows, :] = dv_sum[rows, :].astype(BF16)
+            return nothing
+
+        lax.fori_loop(0, BLOCKS, finish, 0)
 
 
 def attention_specs(row_count, token_count, width):
@@ -144,6 +210,7 @@
         rank=pl.BlockSpec((1, 1, row_count), lambda h, b, s: (b, 0, 0)),
         bound=pl.BlockSpec((CAP, 1), lambda h, b, s: (b, 0)),
         slots=pl.BlockSpec((CAP, width), lambda h, b, s: (b, h)),
+        table=pl.BlockSpec((token_count, width), lambda h, b, s: (0, 0)),
         lse=pl.BlockSpec((1, CAP, 1), lambda h, b, s: (h, b, 0)),
     )
 
@@ -172,7 +239,7 @@
     )(begin, q, k, v, rank, low_bound, high_bound)
 
 
-def attention_backward(begin, q, k, v, rank, low_bound, high_bound, out, lse, grad, width):
+def attention_backward(begin, q, k, v, rank, low_bound, high_bound, out, lse, grad, cosine, sine, width):
     token_count, heads = q.shape[0], q.shape[1] // width
     row_count = token_count // BLOCKS
     s = attention_specs(row_count, token_count, width)
@@ -183,21 +250,22 @@
             grid=(heads, BLOCKS),
             in_specs=[
                 s["q"], s["k"], s["k"], s["rank"], s["bound"], s["bound"],
-                s["slots"], s["lse"], s["slots"],
+                s["slots"], s["lse"], s["slots"], s["table"], s["table"],
             ],
-            out_specs=[s["slots"], s["k"], s["k"]],
+            out_specs=[s["q"], s["k"], s["k"]],
+            scratch_shapes=[pltpu.VMEM((token_count, width), F32)] * 2,
         ),
         out_shape=[
-            jax.ShapeDtypeStruct((BLOCKS * CAP, heads * width), F32),
-            jax.ShapeDtypeStruct((token_count, heads * width), F32),
-            jax.ShapeDtypeStruct((token_count, heads * width), F32),
+            jax.ShapeDtypeStruct((token_count, heads * width), BF16),
+            jax.ShapeDtypeStruct((token_count, heads * width), BF16),
+            jax.ShapeDtypeStruct((token_count, heads * width), BF16),
         ],
         compiler_params=pltpu.CompilerParams(vmem_limit_bytes=VMEM_BYTES),
         cost_estimate=pl.CostEstimate(
             flops=20_000_000_000, bytes_accessed=16_000_000, transcendentals=8_000_000
         ),
         name="attention_backward",
-    )(begin, q, k, v, rank, low_bound, high_bound, out, lse, grad)
+    )(begin, q, k, v, rank, low_bound, high_bound, out, lse, grad, cosine, sine)
 
 
 def exchanged(pieces):
@@ -234,7 +302,7 @@
 def gather_kernel(slots_ref, out_ref, send, recv, local, *, same):
     plane, half, column, planes, along_x, along_y, core = partners()
     cap, width = slots_ref.shape[-2:]
-    middle = cap // 2
+    middle = cap // 32 * 16
     meet(planes[1:] + [along_x, along_y, core])
 
     def piece(source, at_half, at_column, first=0, count=cap):
@@ -337,7 +405,7 @@
         cost_estimate=pl.CostEstimate(flops=0, bytes_accessed=200_000_000, transcendentals=0),
         name="gather_rows",
     )(slots)
-    return out.reshape(BLOCKS * rows, 4 * width)
+    return out
 
 
 def scatter_kernel(partial_ref, out_ref, own, other, crossing, side, send, recv, load):
@@ -531,16 +599,25 @@
     second_weight = spread_weights(second_pieces).reshape(width_all, 3 * hidden_units)
     up_weight, down_weight = second_weight[:, : 2 * hidden_units], second_weight[:, 2 * hidden_units :]
 
+    own_routes = jnp.concatenate([attention_routes, expert_routes], axis=1)
     small = jnp.concatenate(
         [attention_gain[:, None], feedforward_gain[:, None], attention_router, feedforward_router],
         axis=1,
     )
-    small = lax.all_gather(small.T, ("t", "z", "x"), axis=1, tiled=True)
+    small = lax.all_gather(small, "t", axis=0).reshape(-1, small.shape[1])
+    small = small.T.reshape(small.shape[1], -1)
+    spare = jnp.zeros((small.shape[0], features - small.shape[1] % features), BF16)
+    small = jnp.concatenate([small, spare], axis=1).reshape(-1, features)
+    under = jnp.concatenate([own_routes.T.astype(BF16), small], axis=0)
+    under = jnp.pad(under, ((0, -under.shape[0] % 16), (0, 0)))
+    everything = gathered(jnp.concatenate([tokens, under], axis=0), 0)
+    under = everything[:, :, rows:, :features].reshape(BLOCKS, -1, features)
+    all_routes = under[:, :4].swapaxes(1, 2).reshape(token_count, 4).astype(jnp.int32)
+    small = under[:, 4 : 4 + 10].reshape(BLOCKS, 10, features)[:, :, : groups * own_rows]
+    small = small.reshape(BLOCKS, 10, groups, own_rows).transpose(1, 2, 0, 3).reshape(10, width_all)
     gain_first, gain_second = small[0].astype(F32), small[1].astype(F32)
     router_first, router_second = small[2:6].T, small[6:10].T
 
-    own_routes = jnp.concatenate([attention_routes, expert_routes], axis=1)
-    all_routes = lax.all_gather(own_routes, PLACES, axis=0, tiled=True)
     member_first = jnp.any(routed(all_routes[:, :2]), axis=2)
     member_second = jnp.any(routed(all_routes[:, 2:]), axis=2)
 
@@ -560,24 +637,16 @@
         return jnp.einsum("est,esf->etf", pick, slots, preferred_element_type=F32)
 
     grad_out = output_grad.astype(F32)
-    grad_slots_second = gathered(to_slots(output_grad, own_pick_second), 1)
-
-    inputs = gathered(tokens, 0).astype(F32)
-    inverse_first = lax.rsqrt(jnp.mean(inputs * inputs, axis=-1, keepdims=True) + EPSILON)
-    hidden_first = (inputs * inverse_first * gain_first).astype(BF16)
-    gates_first = route_gates(dot(hidden_first, router_first), member_first)
+    grad_slots_second = gathered(to_slots(output_grad, own_pick_second), 1).reshape(BLOCKS * CAP, -1)
+
+    cosine, sine = rope_tables(token_count, head_width)
+    cosine, sine = jnp.asarray(cosine), jnp.asarray(sine)
+    hidden_first, queries, keys, values, logits_first, inverse_first = project(
+        everything, rows, gain_first[None], first_weight, jnp.pad(router_first, ((0, 0), (0, 124))),
+        cosine, sine, span, head_width,
+    )
+    gates_first = route_gates(logits_first[:, :PLANES], member_first)
     position = jnp.arange(token_count, dtype=jnp.int32)
-    cosine, sine_table = rope_tables(position, head_width)
-    cosine, sine_table = cosine[:, None, :], sine_table[:, None, :]
-    qkv = dot(hidden_first, qkv_weight)
-
-    def turned(values, sine):
-        split = values.reshape(values.shape[0], -1, head_width)
-        return rotate(split, cosine, sine).reshape(values.shape).astype(BF16)
-
-    queries = turned(qkv[:, :span], sine_table)
-    keys = turned(qkv[:, span : 2 * span], sine_table)
-    values = qkv[:, 2 * span :].astype(BF16)
     segment = lax.dynamic_slice_in_dim(segment_ids, group * token_count, token_count, 0)
     opens = jnp.concatenate([jnp.ones((1,), jnp.bool_), segment[1:] != segment[:-1]])
     document_start = lax.cummax(jnp.where(opens, position, 0))
@@ -605,7 +674,7 @@
     inverse_second = lax.rsqrt(square / width_all + EPSILON)[:, None]
     normed_second = residual * inverse_second
     hidden_second = (normed_second * mine(gain_second)).astype(BF16)
-    slots_second = gathered(to_slots(hidden_second, own_pick_second), 1)
+    slots_second = gathered(to_slots(hidden_second, own_pick_second), 1).reshape(BLOCKS * CAP, -1)
     plane_gates = dot(slots_second, router_second)
     rank_pick = picks(rank_second)
 
@@ -634,10 +703,12 @@
     grad_inner = gate_slots_second * dot(grad_slots_second, down_weight)
     grad_gate = grad_inner * up_pre * sigmoid_gate * (1.0 + gate_pre * (1.0 - sigmoid_gate))
     grad_gate_up = jnp.concatenate([grad_gate, grad_inner * silu_gate], axis=1).astype(BF16)
-    grad_rows = scattered(contract_last(grad_gate_up, up_weight).astype(BF16), CAP, 2)
+    grad_rows = contract_last(grad_gate_up, up_weight).astype(BF16)
     grad_up_weight = contract_first(slots_second, grad_gate_up).astype(BF16)
     grad_down = contract_first(grad_slots_second, (gate_slots_second * inner).astype(BF16))
     grad_second = jnp.concatenate([grad_up_weight, grad_down.astype(BF16)], axis=1)
+    grad_rows, grad_second = lax.optimization_barrier((grad_rows, grad_second))
+    grad_rows = scattered(grad_rows, CAP, 2)
     grad_second = return_gradients(grad_second.reshape(groups, BLOCKS, own_rows, 3 * hidden_units))
     expert_gate_up_grad = grad_second[:, :, : 2 * hidden_units].reshape(
         PLANES, HALVES, own_rows, 2, hidden_units
@@ -657,42 +728,29 @@
     inner_mean = grid_sum(jnp.sum(grad_normed * normed_second, axis=1))[:, None] / width_all
     grad_residual = grad_out + inverse_second * (grad_normed - normed_second * inner_mean)
 
-    grad_slots_first = gathered(to_slots(grad_residual.astype(BF16), own_pick_first), 1)
+    grad_slots_first = gathered(to_slots(grad_residual.astype(BF16), own_pick_first), 1).reshape(BLOCKS * CAP, -1)
     grad_attended = gate_slots_first * dot(grad_slots_first, out_weight)
     grad_attended = grad_attended.astype(BF16)
     grad_out_weight = contract_first(
         grad_slots_first, (gate_slots_first * attended.astype(F32)).astype(BF16)
     )
-    grad_out_weight = return_gradients(
-        grad_out_weight.astype(BF16).reshape(groups, BLOCKS, own_rows, span)
-    )
-    attention_out_grad = grad_out_weight.swapaxes(1, 2).reshape(attention_out.shape)
-    grad_query, grad_keys, grad_values = attention_backward(
-        *attention_args, attended, lse, grad_attended, head_width
-    )
-    grad_query = jnp.einsum(
-        "bst,bsf->btf",
-        slot_pick.astype(BF16),
-        turned_slots(grad_query, high_bound, head_width).reshape(BLOCKS, CAP, span),
-        preferred_element_type=F32,
-    )
     grad_qkv = jnp.concatenate(
-        [
-            grad_query.reshape(token_count, span).astype(BF16),
-            turned(grad_keys, -sine_table),
-            grad_values.astype(BF16),
-        ],
+        attention_backward(
+            *attention_args, attended, lse, grad_attended, cosine, sine, head_width
+        ),
         axis=1,
     )
     grad_hidden = contract_last(grad_qkv, qkv_weight).astype(BF16)
+    grad_first = jnp.concatenate(
+        [contract_first(hidden_first, grad_qkv).astype(BF16), grad_out_weight.astype(BF16)], axis=1
+    )
+    grad_hidden, grad_first = lax.optimization_barrier((grad_hidden, grad_first))
     grad_hidden = jnp.sum(scattered(grad_hidden, rows, 3).astype(F32), axis=0)
-    grad_qkv_weight = contract_first(hidden_first, grad_qkv).astype(BF16)
-    grad_qkv_weight = return_gradients(
-        grad_qkv_weight.reshape(groups, BLOCKS, own_rows, 3 * span)
-    ).astype(F32)
-    attention_query_grad = grad_qkv_weight[..., :span].reshape(PLANES, HALVES, own_rows, span)
+    grad_first = return_gradients(grad_first.reshape(groups, BLOCKS, own_rows, 4 * span))
+    attention_out_grad = grad_first[..., 3 * span :].swapaxes(1, 2).reshape(attention_out.shape)
+    attention_query_grad = grad_first[..., :span].reshape(PLANES, HALVES, own_rows, span)
     attention_query_grad = attention_query_grad.transpose(0, 2, 1, 3).reshape(attention_query.shape)
-    grad_kv_weight = grad_qkv_weight[..., span:].reshape(
+    grad_kv_weight = grad_first[..., span : 3 * span].astype(F32).reshape(
         PLANES, HALVES, own_rows, 2, head_pair, head_width
     )
     attention_kv_grad = grad_kv_weight.sum(axis=0).transpose(1, 0, 3, 2, 4)
@@ -715,17 +773,17 @@
         [grad_gain_first[None], grad_gain_second[None], grad_router_first.T, grad_router_second.T],
         axis=0,
     )
+    small_grads = jnp.sum(lax.all_gather(small_grads, ("t",) + PLACES, axis=0), axis=0)
     small_grads = lax.all_gather(small_grads, "grid", axis=1, tiled=True)
-    small_grads = small_grads.reshape(-1, groups * BLOCKS, own_rows).transpose(1, 0, 2)
-    small_grads = lax.psum_scatter(
-        small_grads, ("t",) + PLACES, scatter_dimension=0, tiled=False
+    small_grads = lax.dynamic_slice_in_dim(
+        small_grads, (group * BLOCKS + place) * own_rows, own_rows, 1
     )
     return (
         layer_output,
         input_grad.astype(BF16),
         small_grads[0],
         attention_kv_grad,
-        attention_query_grad,
+        attention_query_grad.astype(F32),
         attention_out_grad.astype(F32),
         small_grads[2:6].T,
         small_grads[1],
@@ -733,13 +791,6 @@
         expert_gate_up_grad.astype(F32),
         expert_down_grad.astype(F32),
     )
-
-
-def turned_slots(values, positions, head_width):
-    cosine, sine_table = rope_tables(positions[:, 0], head_width)
-    split = values.reshape(values.shape[0], -1, head_width)
-    turned = rotate(split, cosine[:, None, :], -sine_table[:, None, :])
-    return turned.reshape(values.shape).astype(BF16)
 
 
 def solution(mesh):

time: 1670 us -> 1640 us (0.982)
  Pallas kernels: 760 us -> 1030 us
  blocking collectives: 180 us -> 72.2 us
  other arithmetic: 144 us -> 56.4 us
  local copies, waits for them, and re-layouts: 175 us -> 112 us
  matrix products: 237 us -> 203 us
  starting transfers between devices: 52.9 us -> 72.6 us
    pallas_call x4, Pallas kernels: 279 us -> 486 us  [gathered(): pl.pallas_call(functools.partial(gather_kernel, same=slots.ndim == 2), ou...]
    all_gather x2 -> x1, blocking collectives: 143 us -> 35 us  [per_device(): lax.all_gather(small_grads, ('t',) + PLACES, axis=0)]
    reduce_scatter x1 -> x0, waiting for transfers between devices: 64.2 us -> none  [per_device(): lax.psum_scatter(small_grads, ('t',) + PLACES, scatter_dimension=0, tiled...]
    all_to_all x5 -> x4, waiting for transfers between devices: 28.8 us -> 86.4 us  [exchanged(): return lax.all_to_all(pieces, PLACES, 0, 0, tiled=True)]
    another operation x13 -> x12, other arithmetic: 40.6 us -> 5.52 us
    dot_general x7 -> x5, matrix products: 84.7 us -> 54.2 us  [dot(): return jnp.dot(left, right, preferred_element_type=F32)]
    unnamed x98 -> x90, local copies, waits for them, and re-layouts: 69.9 us -> 42.1 us
    pallas_call x0 -> x1, Pallas kernels: none -> 27.6 us  [project(): pl.pallas_call(functools.partial(project_kernel, head_width=head_width),...]
  transfers between devices with their start and end apart: 6 -> 4, of which waited for: 2 -> 1; matrix products, arithmetic and copies ran while one was open for 22% -> 7% of each run, Pallas kernels for 32% -> 48%
where the time goes in v3:
time: 1640 us
  Pallas kernels  1030 us (63%)
  matrix products  203 us (12%)
  local copies, waits for them, and re-layouts  112 us (7%)
  waiting for transfers between devices  86.4 us (5%)
  starting transfers between devices  72.6 us (4%)
  blocking collectives  72.2 us (4%)
  other arithmetic  56.4 us (3%)
    pallas_call x4, Pallas kernels, gathered(): pl.pallas_call(functools.partial(gather_kernel, same=slots.ndim == 2), ou...  486 us
    pallas_call x4, Pallas kernels, scattered(): pl.pallas_call(scatter_kernel, out_shape=jax.ShapeDtypeStruct((PLANES, ro...  410 us
    all_to_all x4, waiting for transfers between devices, exchanged(): return lax.all_to_all(pieces, PLACES, 0, 0, tiled=True)  86.4 us
    all_to_all x4, starting transfers between devices, exchanged(): return lax.all_to_all(pieces, PLACES, 0, 0, tiled=True)  72.6 us
    pallas_call x1, Pallas kernels, attention_backward(): pl.pallas_call(functools.partial(attention_backward_kernel, scaling=1.0 /...  69.9 us
    dot_general x4, matrix products, contract_last(): lax.dot_general(left, right, (((1,), (1,)), ((), ())), preferred_element_...  66.9 us
    dot_general x4, matrix products, contract_first(): lax.dot_general(left, right, (((0,), (0,)), ((), ())), preferred_element_...  60.7 us
    dot_general x5, matrix products, dot(): return jnp.dot(left, right, preferred_element_type=F32)  54.2 us
  transfers between devices with their start and end apart: 4, of which 1 were waited for; matrix products, arithmetic and copies ran while one was open for 7% of the time, Pallas kernels for 48%

profile of v3, /device:TPU:0, one launch (start us, length us, event | category | flops | bytes accessed | tf_op | source)
XLA Modules:
  0.0 1639.1 jit_solution(11161117633552654675)
XLA Ops:
  2.2 2.7 reshape.484
  7.0 2.6 pad_maximum_fusion.5
  9.6 7.4 all-to-all-start
  18.6 161.5 %gather_rows.4.tokens_ref = bf16[4,2,528,2048]{3,2,1,0:T(8,128)(2,1)} custom-call(bf16[528,512]{1,0:T(8,128)(2,1)} %fusion.44.slots_ref), custom_call_target="tpu_custom_call" | custom-call | bytes 200000000 | tf_op jit(solution)/shard_map/gather_rows/pallas_call | solution.py:394
  182.8 14.6 copy.297
  197.4 3.2 copy.298
  200.9 3.7 pad_maximum_fusion
  204.7 43.3 %all-to-all-start.1 = ((bf16[8,256,2112]{1,2,0:T(8,128)(2,1)}), bf16[8,256,2112]{1,2,0:T(8,128)(2,1)}, u32[]{:S(2)}, u32[]{:S(2)}) async-start(bf16[8,256,2112]{1,2,0:T(8,128)(2,1)} %pad_maximum_fusion), calls=%async_computation.1 | async-start | bytes 17301504 | tf_op jit(solution)/shard_map/all_to_all | solution.py:272
  256.3 3.8 select_reduce_fusion.5
  260.9 2.5 select_reduce_fusion.6
  263.5 2.3 select_n.159.high_ref
  265.8 2.2 select_n.158.low_ref
  270.1 207.8 %gather_rows.6 = bf16[4,2,320,2048]{3,2,1,0:T(8,128)(2,1)} custom-call(bf16[4,320,512]{2,1,0:T(8,128)(2,1)} %fusion.21.slots_ref), custom_call_target="tpu_custom_call" | custom-call | bytes 200000000 | tf_op jit(solution)/shard_map/gather_rows/pallas_call | solution.py:394
  480.1 27.6 %project.1 = (bf16[4096,2048]{1,0:T(8,128)(2,1)}, bf16[4096,256]{1,0:T(8,128)(2,1)}, bf16[4096,256]{1,0:T(8,128)(2,1)}, bf16[4096,256]{1,0:T(8,128)(2,1)}, f32[4096,128]{1,0:T(8,128)}, /*index=5*/f32[4096,1]{1,0:T(8,128)}) custom-call(bf16[4,2,528,2048]{3,2,1,0:T(8,128)(2,1)} %gather_rows.4.tokens_ref, f32[1,2048]{1,0:T(1,128)} %bitcast.248, ...), custom_call_target="tpu_custom_call" | custom-call | flops 20000000000 | bytes 50000000 | tf_op jit(solution)/shard_map/project/pallas_call | solution.py:79
  507.7 2.2 copy.280
  510.1 2.0 copy.283
  516.6 40.2 %attention_forward.1 = (bf16[2560,256]{1,0:T(8,128)(2,1)}, f32[2,2560,1]{2,1,0:T(8,128)}) custom-call(s32[8]{0:T(128)} %and_select_fusion.begin_ref, bf16[4096,256]{1,0:T(8,128)(2,1)} %get-tuple-element.27.q_ref, bf16[4096,256]{1,0:T(8,128)(2,1)} %get-tuple-element.28.k_ref, bf16[4096,256]{1,0:T(8,128)(2,1)} %get-tuple-element.29.v_ref, ...), custom_call_target="tpu_custom_call" | custom-call | flops 10000000000 | bytes 8000000 | tf_op jit(solution)/shard_map/attention_forward/pallas_call | solution.py:222
  556.8 8.6 convolution_convert_fusion.3
  565.5 77.8 %scatter_rows.4 = bf16[4,320,512]{2,1,0:T(8,128)(2,1)} custom-call(bf16[4,2,320,2048]{3,2,1,0:T(8,128)(2,1)} %bitcast.187), custom_call_target="tpu_custom_call" | custom-call | bytes 200000000 | tf_op jit(solution)/shard_map/scatter_rows/pallas_call | solution.py:509
  643.3 4.9 multiply_reduce_fusion.3
  648.8 5.2 all_gather.33
  655.0 5.2 all_gather.34
  662.5 58.0 %gather_rows.5 = bf16[4,2,320,2048]{3,2,1,0:T(8,128)(2,1)} custom-call(bf16[4,320,512]{2,1,0:T(8,128)(2,1)} %fusion.20.slots_ref), custom_call_target="tpu_custom_call" | custom-call | bytes 200000000 | tf_op jit(solution)/shard_map/gather_rows/pallas_call | solution.py:394
  720.6 6.8 fusion.88
  728.1 11.8 copy.299
  739.9 22.7 %fusion.2 = f32[2560,1408]{0,1:T(8,128)} fusion(bf16[2560,2048]{1,0:T(8,128)(2,1)} %bitcast.189, bf16[2048,2112]{1,0:T(8,128)(2,1)} %bitcast.207), kind=kOutput, calls=%fused_computation.28 | convolution fusion | flops 14763950080 | bytes 30670848 | tf_op jit(solution)/shard_map/dot_general | solution.py:39
  762.6 15.2 fusion.8
  777.8 19.2 %multiply_convert_fusion.2 = (bf16[2560,704]{0,1:T(8,128)(2,1)}, bf16[2560,704]{0,1:T(8,128)(2,1)}) fusion(f32[2560,1408]{0,1:T(8,128)} %fusion.2, f32[2560]{0:T(1024)S(1)} %divide_reduce_fusion, bf16[2560,2048]{1,0:T(8,128)(2,1)} %bitcast.202, bf16[2048,2112]{1,0:T(8,128)(2,1)} %bitcast.208), kind=kOutput, calls=%fused_computation.12 | convolution fusion | flops 7407206400 | bytes 35268608 | tf_op jit(solution)/shard_map/dot_general | solution.py:39
  797.0 15.3 convolution_convert_fusion.2
  812.3 19.3 %convolution_convert_fusion.4 = bf16[2048,1408]{0,1:T(8,128)(2,1)} fusion(bf16[2560,2048]{1,0:T(8,128)(2,1)} %bitcast.190, bf16[2560,704]{0,1:T(8,128)(2,1)S(1)} %copy-done.37, bf16[2560,704]{0,1:T(8,128)(2,1)S(1)} %copy-done.36), kind=kOutput, calls=%fused_computation.8 | convolution fusion | flops 14781251584 | bytes 23461888 | tf_op jit(solution)/shard_map/dot_general | solution.py:43
  831.7 22.9 %convolution_convert_fusion.1 = bf16[2560,2048]{1,0:T(8,128)(2,1)} fusion(bf16[2048,2112]{1,0:T(8,128)(2,1)} %bitcast.210, bf16[2560,704]{0,1:T(8,128)(2,1)} %get-tuple-element.138, bf16[2560,704]{0,1:T(8,128)(2,1)} %get-tuple-element.137), kind=kOutput, calls=%fused_computation.2 | convolution fusion | flops 14783610880 | bytes 23461888 | tf_op jit(solution)/shard_map/dot_general | solution.py:47
  854.5 64.2 %scatter_rows.5 = bf16[4,320,512]{2,1,0:T(8,128)(2,1)} custom-call(bf16[4,2,320,2048]{3,2,1,0:T(8,128)(2,1)} %bitcast.203), custom_call_target="tpu_custom_call" | custom-call | bytes 200000000 | tf_op jit(solution)/shard_map/scatter_rows/pallas_call | solution.py:509
  918.7 6.0 pad_maximum_fusion.1
  924.8 51.5 %scatter_rows.6 = bf16[4,320,512]{2,1,0:T(8,128)(2,1)} custom-call(bf16[4,2,320,2048]{3,2,1,0:T(8,128)(2,1)} %bitcast.204), custom_call_target="tpu_custom_call" | custom-call | bytes 200000000 | tf_op jit(solution)/shard_map/scatter_rows/pallas_call | solution.py:509
  976.4 3.3 fusion.22
  981.8 5.2 all_gather.35
  987.4 2.1 multiply_reduce_fusion.4
  989.6 5.2 all_gather.36
  996.0 2.5 multiply_add_fusion
  1000.5 58.7 %gather_rows.7 = bf16[4,2,320,2048]{3,2,1,0:T(8,128)(2,1)} custom-call(bf16[4,320,512]{2,1,0:T(8,128)(2,1)} %fusion.19.slots_ref), custom_call_target="tpu_custom_call" | custom-call | bytes 200000000 | tf_op jit(solution)/shard_map/gather_rows/pallas_call | solution.py:394
  1059.2 7.1 convolution_convert_fusion.6
  1066.4 5.3 fusion.4.grad_ref
  1071.7 69.9 %attention_backward.1 = (bf16[4096,256]{1,0:T(8,128)(2,1)}, bf16[4096,256]{1,0:T(8,128)(2,1)}, bf16[4096,256]{1,0:T(8,128)(2,1)}) custom-call(s32[8]{0:T(128)} %and_select_fusion.begin_ref, bf16[4096,256]{1,0:T(8,128)(2,1)} %get-tuple-element.27.q_ref, bf16[4096,256]{1,0:T(8,128)(2,1)} %get-tuple-element.28.k_ref, ...), custom_call_target="tpu_custom_call" | custom-call | flops 20000000000 | bytes 16000000 | tf_op jit(solution)/shard_map/attention_backward/pallas_call | solution.py:246
  1141.7 3.2 constant_dynamic-update-slice_fusion.2
  1147.8 20.1 %convolution_convert_fusion = bf16[4096,2048]{1,0:T(8,128)(2,1)} fusion(bf16[4096,768]{1,0:T(8,128)(2,1)} %constant_dynamic-update-slice_fusion, bf16[2048,1024]{1,0:T(8,128)(2,1)} %bitcast.13.weight_ref), kind=kOutput, calls=%fused_computation | convolution fusion | flops 12893290496 | bytes 26214400 | tf_op jit(solution)/shard_map/dot_general | solution.py:47
  1167.8 19.1 %convolution_convert_fusion.5 = bf16[2048,768]{0,1:T(8,128)(2,1)S(1)} fusion(bf16[4096,2048]{1,0:T(8,128)(2,1)} %get-tuple-element.37, bf16[4096,768]{1,0:T(8,128)(2,1)} %constant_dynamic-update-slice_fusion), kind=kOutput, calls=%fused_computation.44 | convolution fusion | flops 12886474752 | bytes 26214400 | tf_op jit(solution)/shard_map/dot_general | solution.py:43
  1187.2 2.3 copy.342
  1189.5 16.7 %all-to-all-start.2 = ((bf16[8,256,1024]{1,2,0:T(8,128)(2,1)}), bf16[8,256,1024]{1,2,0:T(8,128)(2,1)}, u32[]{:S(2)}, u32[]{:S(2)}) async-start(bf16[8,256,1024]{1,2,0:T(8,128)(2,1)} %bitcast.198), calls=%async_computation.2 | async-start | bytes 8388608 | tf_op jit(solution)/shard_map/all_to_all | solution.py:272
  1206.2 7.5 copy.341
  1213.7 86.4 %all-to-all-done.2 = bf16[8,256,1024]{1,2,0:T(8,128)(2,1)} async-done(((bf16[8,256,1024]{1,2,0:T(8,128)(2,1)}), bf16[8,256,1024]{1,2,0:T(8,128)(2,1)}, u32[]{:S(2)}, u32[]{:S(2)}) %all-to-all-start.2) | async-done | bytes 4194336 | tf_op jit(solution)/shard_map/all_to_all | solution.py:272
  1300.1 5.1 all-to-all-start.3
  1306.8 2.8 multiply_reduce_fusion
  1310.0 5.2 all_gather.37
  1315.4 216.7 %scatter_rows.7 = bf16[4,512,512]{2,1,0:T(8,128)(2,1)} custom-call(bf16[4,2,512,2048]{3,2,1,0:T(8,128)(2,1)} %bitcast.197), custom_call_target="tpu_custom_call" | custom-call | bytes 200000000 | tf_op jit(solution)/shard_map/scatter_rows/pallas_call | solution.py:509
  1533.3 2.0 convert_reduce_fusion.1
  1537.3 5.7 all_gather.38
  1544.9 35.0 %all-gather.1 = f32[8,10,512]{2,1,0:T(8,128)S(1)} all-gather(f32[1,10,512]{2,1,0:T(8,128)S(1)} %maximum_bitcast_fusion), channel_id=2, replica_groups=mesh['t'=1,'z'=4,'x'=2,'grid'=4] {'t','z','x'}, dimensions={0}, use_global_device_ids=true | all-gather | bytes 184320 | tf_op jit(solution)/shard_map/all_gather | solution.py:776
  1579.9 5.5 all_gather.41
  1593.1 3.1 slice_convert_fusion.1
  1598.2 3.0 slice.209
  1601.2 5.7 convert_bitcast_fusion
  1606.9 9.6 copy.315
  1616.5 17.5 %copy.317 = f32[4,256,2,1408]{3,2,1,0:T(2,128)} copy(f32[4,256,2,1408]{1,3,2,0:T(8,128)} %bitcast.191) | data formatting | bytes 23068672
  1634.1 4.9 slice_convert_fusion
  (237 shorter events, 56.2 us)
Async XLA Ops:
  9.6 7.5 copy-start.19
  9.6 8.0 copy-start.34
  9.6 8.0 copy-start.35
  9.6 8.0 copy-start.30
  9.6 8.0 copy-start.31
  9.6 8.1 copy-start.32
  9.6 8.1 copy-start.33
  9.6 8.1 copy-start.4
  9.6 195.0 %all-to-all-start = ((bf16[8,256,1024]{2,1,0:T(8,128)(2,1)}), bf16[8,256,1024]{2,1,0:T(8,128)(2,1)}, u32[]{:S(2)}, u32[]{:S(2)}) async-start(bf16[8,256,1024]{2,1,0:T(8,128)(2,1)} %pad_maximum_fusion.5), calls=%async_computation | async-start | bytes 8388608 | tf_op jit(solution)/shard_map/all_to_all | solution.py:272
  18.6 163.1 %copy-start.14 = (bf16[512,512]{1,0:T(8,128)(2,1)S(1)}, bf16[512,512]{1,0:T(8,128)(2,1)}, u32[]{:S(2)}) copy-start(bf16[512,512]{1,0:T(8,128)(2,1)} %param.29) | copy-start | bytes 1572868
  197.4 3.5 copy-start.9
  204.7 523.5 %all-to-all-start.1 = ((bf16[8,256,2112]{1,2,0:T(8,128)(2,1)}), bf16[8,256,2112]{1,2,0:T(8,128)(2,1)}, u32[]{:S(2)}, u32[]{:S(2)}) async-start(bf16[8,256,2112]{1,2,0:T(8,128)(2,1)} %pad_maximum_fusion), calls=%async_computation.1 | async-start | bytes 17301504 | tf_op jit(solution)/shard_map/all_to_all | solution.py:272
  248.0 472.5 %copy-start.18 = (bf16[1,4,8,256]{3,1,2,0:T(4,128)(2,1)}, bf16[1,4,8,256]{3,1,2,0:T(4,128)(2,1)S(1)}, u32[]{:S(2)}) copy-start(bf16[1,4,8,256]{3,1,2,0:T(4,128)(2,1)S(1)} %copy.332) | copy-start | bytes 49156
  260.9 217.2 %copy-start.10 = (bf16[4,1,8,256]{0,3,2,1:T(8,128)(2,1)}, bf16[4,1,8,256]{0,3,2,1:T(8,128)(2,1)S(1)}, u32[]{:S(2)}) copy-start(bf16[4,1,8,256]{0,3,2,1:T(8,128)(2,1)S(1)} %copy.279) | copy-start | bytes 49156
  268.2 375.1 %copy-start.24 = (s32[4,512]{1,0:T(4,128)}, s32[4,512]{1,0:T(4,128)S(1)}, u32[]{:S(2)}) copy-start(s32[4,512]{1,0:T(4,128)S(1)} %get-tuple-element.162) | copy-start | bytes 24580
  268.2 392.4 %copy-start.28 = (s32[4,512]{1,0:T(4,128)}, s32[4,512]{1,0:T(4,128)S(1)}, u32[]{:S(2)}) copy-start(s32[4,512]{1,0:T(4,128)S(1)} %get-tuple-element.163) | copy-start | bytes 24580
  478.0 176.0 %copy-start.20 = (f32[512]{0:T(512)}, f32[512]{0:T(512)S(1)}, u32[]{:S(2)}) copy-start(f32[512]{0:T(512)S(1)} %dynamic_slice.47) | copy-start | bytes 6148
  514.0 42.9 %copy-start.2 = (f32[4096,4]{1,0:T(8,128)}, f32[4096,4]{1,0:T(8,128)S(1)}, u32[]{:S(2)}) copy-start(f32[4096,4]{1,0:T(8,128)S(1)} %broadcast_divide_fusion) | copy-start | bytes 196612
  648.8 71.7 %copy-start = (f32[512,512]{1,0:T(8,128)}, f32[512,512]{1,0:T(8,128)S(1)}, u32[]{:S(2)}) copy-start(f32[512,512]{1,0:T(8,128)S(1)} %get-tuple-element.128) | copy-start | bytes 3145732
  654.0 0.6 copy-start.22
  654.6 65.9 %copy-start.7 = (bf16[512,512]{1,0:T(8,128)(2,1)}, bf16[512,512]{1,0:T(8,128)(2,1)S(1)}, u32[]{:S(2)}) copy-start(bf16[512,512]{1,0:T(8,128)(2,1)S(1)} %multiply_convert_fusion.8) | copy-start | bytes 1572868
  797.0 15.3 copy-start.36
  797.0 15.3 copy-start.37
  854.5 64.2 %copy-start.6 = (bf16[2048,1408]{0,1:T(8,128)(2,1)S(1)}, bf16[2048,1408]{0,1:T(8,128)(2,1)}, u32[]{:S(2)}) copy-start(bf16[2048,1408]{0,1:T(8,128)(2,1)} %convolution_convert_fusion.4) | copy-start | bytes 17301508
  924.8 51.5 %copy-start.29 = (s32[4,512]{1,0:T(4,128)S(1)}, s32[4,512]{1,0:T(4,128)}, u32[]{:S(2)}) copy-start(s32[4,512]{1,0:T(4,128)} %copy-done.28) | copy-start | bytes 24580
  976.3 3.4 copy-start.15
  976.3 3.4 copy-start.16
  976.3 3.4 copy-start.17
  979.7 7.7 copy-start.1
  979.7 7.7 copy-start.21
  979.7 7.7 copy-start.23
  987.4 11.2 copy-start.25
  1000.5 58.7 %copy-start.11 = (bf16[2560,256]{1,0:T(8,128)(2,1)S(1)}, bf16[2560,256]{1,0:T(8,128)(2,1)}, u32[]{:S(2)}) copy-start(bf16[2560,256]{1,0:T(8,128)(2,1)} %get-tuple-element.30.out_ref) | copy-start | bytes 3932164
  1000.5 58.7 %copy-start.27 = (f32[2560]{0:T(1024)S(1)}, f32[2560]{0:T(1024)}, u32[]{:S(2)}) copy-start(f32[2560]{0:T(1024)} %mul.250) | copy-start | bytes 30724
  1059.2 7.1 copy-start.3
  1141.6 3.2 copy-start.13
  1141.6 4.7 copy-start.12
  1189.5 110.6 %all-to-all-start.2 = ((bf16[8,256,1024]{1,2,0:T(8,128)(2,1)}), bf16[8,256,1024]{1,2,0:T(8,128)(2,1)}, u32[]{:S(2)}, u32[]{:S(2)}) async-start(bf16[8,256,1024]{1,2,0:T(8,128)(2,1)} %bitcast.198), calls=%async_computation.2 | async-start | bytes 8388608 | tf_op jit(solution)/shard_map/all_to_all | solution.py:272
  1300.1 5.1 copy-start.26
  1300.1 298.0 %all-to-all-start.3 = ((bf16[8,256,2112]{1,2,0:T(8,128)(2,1)}), bf16[8,256,2112]{1,2,0:T(8,128)(2,1)}, u32[]{:S(2)}, u32[]{:S(2)}) async-start(bf16[8,256,2112]{1,2,0:T(8,128)(2,1)} %bitcast.192), calls=%async_computation.3 | async-start | bytes 17301504 | tf_op jit(solution)/shard_map/all_to_all | solution.py:272
  1315.4 219.9 %copy-start.5 = (bf16[512,512]{1,0:T(8,128)(2,1)S(1)}, bf16[512,512]{1,0:T(8,128)(2,1)}, u32[]{:S(2)}) copy-start(bf16[512,512]{1,0:T(8,128)(2,1)} %param.16) | copy-start | bytes 1572868
  1532.2 10.9 copy-start.8

commit v4 on v3

--- a/solution.py
+++ b/solution.py
@@ -104,9 +104,6 @@
             jax.ShapeDtypeStruct((token_count, 1), F32),
         ],
         compiler_params=pltpu.CompilerParams(vmem_limit_bytes=VMEM_BYTES),
-        cost_estimate=pl.CostEstimate(
-            flops=20_000_000_000, bytes_accessed=50_000_000, transcendentals=0
-        ),
         name="project",
     )(tokens, gain, weight, router, cosine, sine)
 
@@ -232,9 +229,6 @@
             jax.ShapeDtypeStruct((heads, BLOCKS * CAP, 1), F32),
         ],
         compiler_params=pltpu.CompilerParams(vmem_limit_bytes=VMEM_BYTES),
-        cost_estimate=pl.CostEstimate(
-            flops=10_000_000_000, bytes_accessed=8_000_000, transcendentals=8_000_000
-        ),
         name="attention_forward",
     )(begin, q, k, v, rank, low_bound, high_bound)
 
@@ -261,9 +255,6 @@
             jax.ShapeDtypeStruct((token_count, heads * width), BF16),
         ],
         compiler_params=pltpu.CompilerParams(vmem_limit_bytes=VMEM_BYTES),
-        cost_estimate=pl.CostEstimate(
-            flops=20_000_000_000, bytes_accessed=16_000_000, transcendentals=8_000_000
-        ),
         name="attention_backward",
     )(begin, q, k, v, rank, low_bound, high_bound, out, lse, grad, cosine, sine)
 
@@ -402,7 +393,6 @@
             pltpu.SemaphoreType.DMA,
         ],
         compiler_params=pltpu.CompilerParams(collective_id=collective_id, has_side_effects=True),
-        cost_estimate=pl.CostEstimate(flops=0, bytes_accessed=200_000_000, transcendentals=0),
         name="gather_rows",
     )(slots)
     return out
@@ -523,7 +513,6 @@
         compiler_params=pltpu.CompilerParams(
             collective_id=collective_id, has_side_effects=True, vmem_limit_bytes=VMEM_BYTES
         ),
-        cost_estimate=pl.CostEstimate(flops=0, bytes_accessed=200_000_000, transcendentals=0),
         name="scatter_rows",
     )(partial.reshape(PLANES, HALVES, rows, 4 * width))
 
@@ -596,9 +585,6 @@
     up_pieces = up_pieces.transpose(0, 3, 1, 2, 4).reshape(BLOCKS, own_rows, 2 * hidden_units)
     down_pieces = expert_down.reshape(BLOCKS, hidden_units, own_rows).swapaxes(1, 2)
     second_pieces = jnp.concatenate([up_pieces, down_pieces], axis=2)
-    second_weight = spread_weights(second_pieces).reshape(width_all, 3 * hidden_units)
-    up_weight, down_weight = second_weight[:, : 2 * hidden_units], second_weight[:, 2 * hidden_units :]
-
     own_routes = jnp.concatenate([attention_routes, expert_routes], axis=1)
     small = jnp.concatenate(
         [attention_gain[:, None], feedforward_gain[:, None], attention_router, feedforward_router],
@@ -610,7 +596,11 @@
     small = jnp.concatenate([small, spare], axis=1).reshape(-1, features)
     under = jnp.concatenate([own_routes.T.astype(BF16), small], axis=0)
     under = jnp.pad(under, ((0, -under.shape[0] % 16), (0, 0)))
+    under, second_pieces = lax.optimization_barrier((under, second_pieces))
     everything = gathered(jnp.concatenate([tokens, under], axis=0), 0)
+    second_pieces, everything = lax.optimization_barrier((second_pieces, everything))
+    second_weight = spread_weights(second_pieces).reshape(width_all, 3 * hidden_units)
+    up_weight, down_weight = second_weight[:, : 2 * hidden_units], second_weight[:, 2 * hidden_units :]
     under = everything[:, :, rows:, :features].reshape(BLOCKS, -1, features)
     all_routes = under[:, :4].swapaxes(1, 2).reshape(token_count, 4).astype(jnp.int32)
     small = under[:, 4 : 4 + 10].reshape(BLOCKS, 10, features)[:, :, : groups * own_rows]
@@ -637,8 +627,6 @@
         return jnp.einsum("est,esf->etf", pick, slots, preferred_element_type=F32)
 
     grad_out = output_grad.astype(F32)
-    grad_slots_second = gathered(to_slots(output_grad, own_pick_second), 1).reshape(BLOCKS * CAP, -1)
-
     cosine, sine = rope_tables(token_count, head_width)
     cosine, sine = jnp.asarray(cosine), jnp.asarray(sine)
     hidden_first, queries, keys, values, logits_first, inverse_first = project(
@@ -675,6 +663,10 @@
     normed_second = residual * inverse_second
     hidden_second = (normed_second * mine(gain_second)).astype(BF16)
     slots_second = gathered(to_slots(hidden_second, own_pick_second), 1).reshape(BLOCKS * CAP, -1)
+    slots_second, grad_slots = lax.optimization_barrier(
+        (slots_second, to_slots(output_grad, own_pick_second))
+    )
+    grad_slots_second = gathered(grad_slots, 1).reshape(BLOCKS * CAP, -1)
     plane_gates = dot(slots_second, router_second)
     rank_pick = picks(rank_second)
 
@@ -709,13 +701,6 @@
     grad_second = jnp.concatenate([grad_up_weight, grad_down.astype(BF16)], axis=1)
     grad_rows, grad_second = lax.optimization_barrier((grad_rows, grad_second))
     grad_rows = scattered(grad_rows, CAP, 2)
-    grad_second = return_gradients(grad_second.reshape(groups, BLOCKS, own_rows, 3 * hidden_units))
-    expert_gate_up_grad = grad_second[:, :, : 2 * hidden_units].reshape(
-        PLANES, HALVES, own_rows, 2, hidden_units
-    )
-    expert_gate_up_grad = expert_gate_up_grad.transpose(0, 2, 3, 1, 4).reshape(expert_gate_up.shape)
-    expert_down_grad = grad_second[:, :, 2 * hidden_units :].swapaxes(1, 2).reshape(expert_down.shape)
-
     grad_gates_second = grid_sum(jnp.sum(branch_second * grad_out[None], axis=2).T)
     grad_logits_second = logits_grad(own_gates_second, grad_gates_second)
     grad_hidden_second = jnp.sum(to_tokens(grad_rows, own_pick_second), axis=0)
@@ -729,6 +714,8 @@
     grad_residual = grad_out + inverse_second * (grad_normed - normed_second * inner_mean)
 
     grad_slots_first = gathered(to_slots(grad_residual.astype(BF16), own_pick_first), 1).reshape(BLOCKS * CAP, -1)
+    grad_second, grad_slots_first = lax.optimization_barrier((grad_second, grad_slots_first))
+    grad_second = return_gradients(grad_second.reshape(groups, BLOCKS, own_rows, 3 * hidden_units))
     grad_attended = gate_slots_first * dot(grad_slots_first, out_weight)
     grad_attended = grad_attended.astype(BF16)
     grad_out_weight = contract_first(
@@ -744,8 +731,16 @@
     grad_first = jnp.concatenate(
         [contract_first(hidden_first, grad_qkv).astype(BF16), grad_out_weight.astype(BF16)], axis=1
     )
-    grad_hidden, grad_first = lax.optimization_barrier((grad_hidden, grad_first))
-    grad_hidden = jnp.sum(scattered(grad_hidden, rows, 3).astype(F32), axis=0)
+    grad_hidden, grad_first, grad_second = lax.optimization_barrier(
+        (grad_hidden, grad_first, grad_second)
+    )
+    grad_hidden, grad_first = lax.optimization_barrier((scattered(grad_hidden, rows, 3), grad_first))
+    grad_hidden = jnp.sum(grad_hidden.astype(F32), axis=0)
+    expert_gate_up_grad = grad_second[:, :, : 2 * hidden_units].reshape(
+        PLANES, HALVES, own_rows, 2, hidden_units
+    )
+    expert_gate_up_grad = expert_gate_up_grad.transpose(0, 2, 3, 1, 4).reshape(expert_gate_up.shape)
+    expert_down_grad = grad_second[:, :, 2 * hidden_units :].swapaxes(1, 2).reshape(expert_down.shape)
     grad_first = return_gradients(grad_first.reshape(groups, BLOCKS, own_rows, 4 * span))
     attention_out_grad = grad_first[..., 3 * span :].swapaxes(1, 2).reshape(attention_out.shape)
     attention_query_grad = grad_first[..., :span].reshape(PLANES, HALVES, own_rows, span)

time: 1640 us -> 1410 us (0.86)
  Pallas kernels: 1030 us -> 759 us
  blocking collectives: 72.2 us -> 126 us
  waiting for transfers between devices: 86.4 us -> 62.7 us
    pallas_call x4, Pallas kernels: 486 us -> 327 us  [gathered(): pl.pallas_call(functools.partial(gather_kernel, same=slots.ndim == 2), ou...]
    pallas_call x4, Pallas kernels: 410 us -> 304 us  [scattered(): pl.pallas_call(scatter_kernel, out_shape=jax.ShapeDtypeStruct((PLANES, ro...]
    all_gather x1, blocking collectives: 35 us -> 89.2 us  [per_device(): lax.all_gather(small_grads, ('t',) + PLACES, axis=0)]
    all_to_all x4, waiting for transfers between devices: 86.4 us -> 62.7 us  [exchanged(): return lax.all_to_all(pieces, PLACES, 0, 0, tiled=True)]
    unnamed x90 -> x98, local copies, waits for them, and re-layouts: 42.1 us -> 41.7 us
  transfers between devices with their start and end apart: 4 -> 4, of which waited for: 1 -> 1; matrix products, arithmetic and copies ran while one was open for 7% -> 14% of each run, Pallas kernels for 48% -> 36%
where the time goes in v4:
time: 1410 us; the launch traced here: 1400 us
  Pallas kernels  759 us (54%)
  matrix products  211 us (15%)
  blocking collectives  126 us (9%)
  local copies, waits for them, and re-layouts  110 us (8%)
  starting transfers between devices  72.8 us (5%)
  waiting for transfers between devices  62.7 us (4%)
  other arithmetic  56.8 us (4%)
    pallas_call x4, Pallas kernels, gathered(): pl.pallas_call(functools.partial(gather_kernel, same=slots.ndim == 2), ou...  327 us
    pallas_call x4, Pallas kernels, scattered(): pl.pallas_call(scatter_kernel, out_shape=jax.ShapeDtypeStruct((PLANES, ro...  304 us
    all_gather x1, blocking collectives, per_device(): lax.all_gather(small_grads, ('t',) + PLACES, axis=0)  89.2 us
    all_to_all x4, starting transfers between devices, exchanged(): return lax.all_to_all(pieces, PLACES, 0, 0, tiled=True)  72.8 us
    dot_general x4, matrix products, contract_last(): lax.dot_general(left, right, (((1,), (1,)), ((), ())), preferred_element_...  67.2 us
    pallas_call x1, Pallas kernels, attention_backward(): pl.pallas_call(functools.partial(attention_backward_kernel, scaling=1.0 /...  63.3 us
    dot_general x4, matrix products, contract_first(): lax.dot_general(left, right, (((0,), (0,)), ((), ())), preferred_element_...  62.9 us
    all_to_all x4, waiting for transfers between devices, exchanged(): return lax.all_to_all(pieces, PLACES, 0, 0, tiled=True)  62.7 us
  transfers between devices with their start and end apart: 4, of which 1 were waited for; matrix products, arithmetic and copies ran while one was open for 14% of the time, Pallas kernels for 36%

profile of v4, /device:TPU:0, one launch (start us, length us, event | category | flops | bytes accessed | tf_op | source)
XLA Modules:
  0.0 1399.5 jit_solution(18373082023120048669)
XLA Ops:
  2.2 2.7 reshape.487
  7.0 2.6 pad_maximum_fusion.5
  9.6 7.4 all-to-all-start
  17.1 14.6 %copy.272 = bf16[4,256,2,1408]{1,3,2,0:T(8,128)(2,1)} copy(bf16[4,256,2,1408]{3,2,1,0:T(2,128)(2,1)} %param.27) | data formatting | bytes 11534336 | tf_op args[11]
  31.7 3.2 copy.273
  35.2 3.7 pad_maximum_fusion
  39.8 140.2 %gather_rows.4.tokens_ref = bf16[4,2,528,2048]{3,2,1,0:T(8,128)(2,1)} custom-call(bf16[528,512]{1,0:T(8,128)(2,1)} %pad_maximum_fusion.8.slots_ref), custom_call_target="tpu_custom_call" | custom-call | tf_op jit(solution)/shard_map/gather_rows/pallas_call | solution.py:385
  180.0 43.5 %all-to-all-start.1 = ((bf16[8,256,2112]{1,2,0:T(8,128)(2,1)}), bf16[8,256,2112]{1,2,0:T(8,128)(2,1)}, u32[]{:S(2)}, u32[]{:S(2)}) async-start(bf16[8,256,2112]{1,2,0:T(8,128)(2,1)} %pad_maximum_fusion), calls=%async_computation.1 | async-start | bytes 17301504 | tf_op jit(solution)/shard_map/all_to_all | solution.py:263
  235.2 3.8 select_reduce_fusion.5
  240.7 2.5 select_reduce_fusion.6
  243.3 2.3 select_n.159.high_ref
  245.7 2.2 select_n.158.low_ref
  251.2 27.7 %project.1 = (bf16[4096,2048]{1,0:T(8,128)(2,1)}, bf16[4096,256]{1,0:T(8,128)(2,1)}, bf16[4096,256]{1,0:T(8,128)(2,1)}, bf16[4096,256]{1,0:T(8,128)(2,1)}, f32[4096,128]{1,0:T(8,128)}, /*index=5*/f32[4096,1]{1,0:T(8,128)}) custom-call(bf16[4,2,528,2048]{3,2,1,0:T(8,128)(2,1)} %gather_rows.4.tokens_ref, f32[1,2048]{1,0:T(1,128)} %bitcast.241, ...), custom_call_target="tpu_custom_call" | custom-call | tf_op jit(solution)/shard_map/project/pallas_call | solution.py:79
  278.9 2.2 copy.282
  284.1 36.1 %attention_forward.1 = (bf16[2560,256]{1,0:T(8,128)(2,1)}, f32[2,2560,1]{2,1,0:T(8,128)}) custom-call(s32[8]{0:T(128)} %and_select_fusion.begin_ref, bf16[4096,256]{1,0:T(8,128)(2,1)} %get-tuple-element.41.q_ref, bf16[4096,256]{1,0:T(8,128)(2,1)} %get-tuple-element.42.k_ref, bf16[4096,256]{1,0:T(8,128)(2,1)} %get-tuple-element.43.v_ref, ...), custom_call_target="tpu_custom_call" | custom-call | tf_op jit(solution)/shard_map/attention_forward/pallas_call | solution.py:219
  320.2 8.6 convolution_convert_fusion.3
  328.8 113.7 %scatter_rows.4 = bf16[4,320,512]{2,1,0:T(8,128)(2,1)} custom-call(bf16[4,2,320,2048]{3,2,1,0:T(8,128)(2,1)} %bitcast.187), custom_call_target="tpu_custom_call" | custom-call | tf_op jit(solution)/shard_map/scatter_rows/pallas_call | solution.py:499
  442.6 4.9 multiply_reduce_fusion.3
  448.1 5.2 all_gather.33
  453.9 5.2 all_gather.34
  461.4 58.7 %gather_rows.5 = bf16[4,2,320,2048]{3,2,1,0:T(8,128)(2,1)} custom-call(bf16[4,320,512]{2,1,0:T(8,128)(2,1)} %fusion.20.slots_ref), custom_call_target="tpu_custom_call" | custom-call | tf_op jit(solution)/shard_map/gather_rows/pallas_call | solution.py:385
  520.1 69.4 %gather_rows.6 = bf16[4,2,320,2048]{3,2,1,0:T(8,128)(2,1)} custom-call(bf16[4,320,512]{2,1,0:T(8,128)(2,1)} %fusion.21.slots_ref), custom_call_target="tpu_custom_call" | custom-call | tf_op jit(solution)/shard_map/gather_rows/pallas_call | solution.py:385
  589.6 6.8 fusion.86
  597.2 11.8 copy.299
  609.0 22.7 %fusion.2 = f32[2560,1408]{0,1:T(8,128)} fusion(bf16[2560,2048]{1,0:T(8,128)(2,1)} %bitcast.189, bf16[2048,2112]{1,0:T(8,128)(2,1)} %bitcast.207), kind=kOutput, calls=%fused_computation.28 | convolution fusion | flops 14763950080 | bytes 30670848 | tf_op jit(solution)/shard_map/dot_general | solution.py:39
  631.6 15.2 %fusion.8 = bf16[2048,704]{0,1:T(8,128)(2,1)} fusion(bf16[2560,2048]{1,0:T(8,128)(2,1)} %bitcast.203, f32[2560]{0:T(1024)S(1)} %divide_reduce_fusion, f32[2560,1408]{0,1:T(8,128)} %fusion.2), kind=kOutput, calls=%fused_computation.46 | convolution fusion | flops 7396032512 | bytes 27797504 | tf_op jit(solution)/shard_map/dot_general | solution.py:43
  646.8 19.2 %multiply_convert_fusion.2 = (bf16[2560,704]{0,1:T(8,128)(2,1)}, bf16[2560,704]{0,1:T(8,128)(2,1)}) fusion(f32[2560,1408]{0,1:T(8,128)} %fusion.2, f32[2560]{0:T(1024)S(1)} %divide_reduce_fusion, bf16[2560,2048]{1,0:T(8,128)(2,1)} %bitcast.204, bf16[2048,2112]{1,0:T(8,128)(2,1)} %bitcast.208), kind=kOutput, calls=%fused_computation.12 | convolution fusion | flops 7407206400 | bytes 35268608 | tf_op jit(solution)/shard_map/dot_general | solution.py:39
  666.1 15.4 %convolution_convert_fusion.2 = bf16[2560,2048]{1,0:T(8,128)(2,1)} fusion(bf16[2048,2112]{1,0:T(8,128)(2,1)} %bitcast.209, f32[2560,1408]{0,1:T(8,128)} %fusion.2), kind=kOutput, calls=%fused_computation.3 | convolution fusion | flops 7398031360 | bytes 28049408 | tf_op jit(solution)/shard_map/dot_general | solution.py:47
  681.5 19.3 %convolution_convert_fusion.4 = bf16[2048,1408]{0,1:T(8,128)(2,1)} fusion(bf16[2560,2048]{1,0:T(8,128)(2,1)} %bitcast.190, bf16[2560,704]{0,1:T(8,128)(2,1)S(1)} %copy-done.41, bf16[2560,704]{0,1:T(8,128)(2,1)S(1)} %copy-done.40), kind=kOutput, calls=%fused_computation.8 | convolution fusion | flops 14781251584 | bytes 23461888 | tf_op jit(solution)/shard_map/dot_general | solution.py:43
  700.8 22.9 %convolution_convert_fusion.1 = bf16[2560,2048]{1,0:T(8,128)(2,1)} fusion(bf16[2048,2112]{1,0:T(8,128)(2,1)} %bitcast.210, bf16[2560,704]{0,1:T(8,128)(2,1)} %get-tuple-element.160, bf16[2560,704]{0,1:T(8,128)(2,1)} %get-tuple-element.159), kind=kOutput, calls=%fused_computation.2 | convolution fusion | flops 14783610880 | bytes 23461888 | tf_op jit(solution)/shard_map/dot_general | solution.py:47
  723.7 63.6 %scatter_rows.5 = bf16[4,320,512]{2,1,0:T(8,128)(2,1)} custom-call(bf16[4,2,320,2048]{3,2,1,0:T(8,128)(2,1)} %bitcast.205), custom_call_target="tpu_custom_call" | custom-call | tf_op jit(solution)/shard_map/scatter_rows/pallas_call | solution.py:499
  787.3 6.0 pad_maximum_fusion.1
  793.4 51.2 %scatter_rows.6 = bf16[4,320,512]{2,1,0:T(8,128)(2,1)} custom-call(bf16[4,2,320,2048]{3,2,1,0:T(8,128)(2,1)} %bitcast.206), custom_call_target="tpu_custom_call" | custom-call | tf_op jit(solution)/shard_map/scatter_rows/pallas_call | solution.py:499
  844.7 3.3 fusion.22
  850.1 5.2 all_gather.35
  855.7 2.1 multiply_reduce_fusion.4
  857.9 5.2 all_gather.36
  864.4 2.5 multiply_add_fusion
  868.8 59.0 %gather_rows.7 = bf16[4,2,320,2048]{3,2,1,0:T(8,128)(2,1)} custom-call(bf16[4,320,512]{2,1,0:T(8,128)(2,1)} %fusion.19.slots_ref), custom_call_target="tpu_custom_call" | custom-call | tf_op jit(solution)/shard_map/gather_rows/pallas_call | solution.py:385
  927.8 7.5 copy.341
  935.3 17.1 %all-to-all-start.2 = ((bf16[8,256,2112]{1,2,0:T(8,128)(2,1)}), bf16[8,256,2112]{1,2,0:T(8,128)(2,1)}, u32[]{:S(2)}, u32[]{:S(2)}) async-start(bf16[8,256,2112]{1,2,0:T(8,128)(2,1)} %bitcast.193), calls=%async_computation.2 | async-start | bytes 17301504 | tf_op jit(solution)/shard_map/all_to_all | solution.py:263
  954.4 8.2 fusion.4.grad_ref
  962.6 63.3 %attention_backward.1 = (bf16[4096,256]{1,0:T(8,128)(2,1)}, bf16[4096,256]{1,0:T(8,128)(2,1)}, bf16[4096,256]{1,0:T(8,128)(2,1)}) custom-call(s32[8]{0:T(128)} %and_select_fusion.begin_ref, bf16[4096,256]{1,0:T(8,128)(2,1)} %get-tuple-element.41.q_ref, bf16[4096,256]{1,0:T(8,128)(2,1)} %get-tuple-element.42.k_ref, ...), custom_call_target="tpu_custom_call" | custom-call | tf_op jit(solution)/shard_map/attention_backward/pallas_call | solution.py:240
  1029.4 9.2 convolution_convert_fusion.6
  1038.6 19.1 %convolution_convert_fusion.5 = bf16[2048,768]{0,1:T(8,128)(2,1)S(1)} fusion(bf16[4096,2048]{1,0:T(8,128)(2,1)} %get-tuple-element.56, bf16[4096,768]{1,0:T(8,128)(2,1)} %copy-done.19), kind=kOutput, calls=%fused_computation.44 | convolution fusion | flops 12886474752 | bytes 26214400 | tf_op jit(solution)/shard_map/dot_general | solution.py:43
  1057.7 2.6 pad_maximum_fusion.6
  1060.3 20.2 %convolution_convert_fusion = bf16[4096,2048]{1,0:T(8,128)(2,1)} fusion(bf16[4096,768]{1,0:T(8,128)(2,1)} %copy-done.19, bf16[2048,1024]{1,0:T(8,128)(2,1)} %bitcast.18.weight_ref), kind=kOutput, calls=%fused_computation | convolution fusion | flops 12893290496 | bytes 26214400 | tf_op jit(solution)/shard_map/dot_general | solution.py:47
  1080.5 62.7 %all-to-all-done.2 = bf16[8,256,2112]{1,2,0:T(8,128)(2,1)} async-done(((bf16[8,256,2112]{1,2,0:T(8,128)(2,1)}), bf16[8,256,2112]{1,2,0:T(8,128)(2,1)}, u32[]{:S(2)}, u32[]{:S(2)}) %all-to-all-start.2) | async-done | bytes 8650784 | tf_op jit(solution)/shard_map/all_to_all | solution.py:263
  1143.3 75.8 %scatter_rows.7 = bf16[4,512,512]{2,1,0:T(8,128)(2,1)} custom-call(bf16[4,2,512,2048]{3,2,1,0:T(8,128)(2,1)} %bitcast.197), custom_call_target="tpu_custom_call" | custom-call | tf_op jit(solution)/shard_map/scatter_rows/pallas_call | solution.py:499
  1219.1 2.2 copy.342
  1221.3 4.7 all-to-all-start.3
  1228.5 3.1 multiply_reduce_fusion
  1232.0 5.2 all_gather.37
  1240.6 2.0 convert_reduce_fusion.1
  1242.6 2.7 fusion.39
  1245.3 5.4 all_gather.38
  1250.7 89.2 %all-gather.1 = f32[8,10,512]{2,1,0:T(8,128)S(1)} all-gather(f32[1,10,512]{2,1,0:T(8,128)S(1)} %maximum_bitcast_fusion), channel_id=2, replica_groups=mesh['t'=1,'z'=4,'x'=2,'grid'=4] {'t','z','x'}, dimensions={0}, use_global_device_ids=true | all-gather | bytes 184320 | tf_op jit(solution)/shard_map/all_gather | solution.py:771
  1340.0 3.0 slice.179
  1343.0 5.7 convert_bitcast_fusion
  1348.7 9.6 copy.315
  1358.3 17.7 %copy.317 = f32[4,256,2,1408]{3,2,1,0:T(2,128)} copy(f32[4,256,2,1408]{1,3,2,0:T(8,128)} %bitcast.191) | data formatting | bytes 23068672
  1376.0 5.7 all_gather.41
  1384.1 4.9 slice_convert_fusion
  1394.1 3.1 slice_convert_fusion.1
  (246 shorter events, 55.4 us)
Async XLA Ops:
  9.6 7.4 copy-start.38
  9.6 7.4 copy-start.39
  9.6 7.4 copy-start.34
  9.6 7.5 copy-start.35
  9.6 170.4 %all-to-all-start = ((bf16[8,256,1024]{2,1,0:T(8,128)(2,1)}), bf16[8,256,1024]{2,1,0:T(8,128)(2,1)}, u32[]{:S(2)}, u32[]{:S(2)}) async-start(bf16[8,256,1024]{2,1,0:T(8,128)(2,1)} %pad_maximum_fusion.5), calls=%async_computation | async-start | bytes 8388608 | tf_op jit(solution)/shard_map/all_to_all | solution.py:263
  31.7 3.2 copy-start.36
  31.7 3.2 copy-start.37
  31.7 3.5 copy-start.12
  35.2 3.7 copy-start.5
  180.0 43.6 %copy-start.24 = (s32[4096]{0:T(1024)S(1)}, s32[4096]{0:T(1024)}, u32[]{:S(2)}) copy-start(s32[4096]{0:T(1024)} %param.17) | copy-start | bytes 49156
  180.0 45.7 %copy-start.16 = (bf16[512,512]{1,0:T(8,128)(2,1)S(1)}, bf16[512,512]{1,0:T(8,128)(2,1)}, u32[]{:S(2)}) copy-start(bf16[512,512]{1,0:T(8,128)(2,1)} %param.29) | copy-start | bytes 1572868
  180.0 417.2 %all-to-all-start.1 = ((bf16[8,256,2112]{1,2,0:T(8,128)(2,1)}), bf16[8,256,2112]{1,2,0:T(8,128)(2,1)}, u32[]{:S(2)}, u32[]{:S(2)}) async-start(bf16[8,256,2112]{1,2,0:T(8,128)(2,1)} %pad_maximum_fusion), calls=%async_computation.1 | async-start | bytes 17301504 | tf_op jit(solution)/shard_map/all_to_all | solution.py:263
  226.9 362.7 %copy-start.23 = (bf16[1,4,8,256]{3,1,2,0:T(4,128)(2,1)}, bf16[1,4,8,256]{3,1,2,0:T(4,128)(2,1)S(1)}, u32[]{:S(2)}) copy-start(bf16[1,4,8,256]{3,1,2,0:T(4,128)(2,1)S(1)} %copy.332) | copy-start | bytes 49156
  234.8 44.1 %copy-start.20 = (s32[8,512]{1,0:T(8,128)}, s32[8,512]{1,0:T(8,128)S(1)}, u32[]{:S(2)}) copy-start(s32[8,512]{1,0:T(8,128)S(1)} %get-tuple-element.155) | copy-start | bytes 49156
  239.8 39.1 %copy-start.13 = (bf16[4,1,8,256]{0,3,2,1:T(8,128)(2,1)}, bf16[4,1,8,256]{0,3,2,1:T(8,128)(2,1)S(1)}, u32[]{:S(2)}) copy-start(bf16[4,1,8,256]{0,3,2,1:T(8,128)(2,1)S(1)} %copy.281) | copy-start | bytes 49156
  247.9 205.3 %copy-start.25 = (f32[512]{0:T(512)}, f32[512]{0:T(512)S(1)}, u32[]{:S(2)}) copy-start(f32[512]{0:T(512)S(1)} %dynamic_slice.47) | copy-start | bytes 6148
  248.6 193.9 %copy-start.29 = (s32[4,512]{1,0:T(4,128)}, s32[4,512]{1,0:T(4,128)S(1)}, u32[]{:S(2)}) copy-start(s32[4,512]{1,0:T(4,128)S(1)} %get-tuple-element.184) | copy-start | bytes 24580
  248.6 210.8 %copy-start.32 = (s32[4,512]{1,0:T(4,128)}, s32[4,512]{1,0:T(4,128)S(1)}, u32[]{:S(2)}) copy-start(s32[4,512]{1,0:T(4,128)S(1)} %get-tuple-element.185) | copy-start | bytes 24580
  282.7 1.4 copy-start.3
  448.1 72.0 %copy-start.1 = (f32[512,512]{1,0:T(8,128)}, f32[512,512]{1,0:T(8,128)S(1)}, u32[]{:S(2)}) copy-start(f32[512,512]{1,0:T(8,128)S(1)} %get-tuple-element.150) | copy-start | bytes 3145732
  453.3 66.9 %copy-start.27 = (f32[512]{0:T(512)}, f32[512]{0:T(512)S(1)}, u32[]{:S(2)}) copy-start(f32[512]{0:T(512)S(1)} %rsqrt_bitcast_fusion) | copy-start | bytes 6148
  453.4 66.7 %copy-start.10 = (bf16[512,512]{1,0:T(8,128)(2,1)}, bf16[512,512]{1,0:T(8,128)(2,1)S(1)}, u32[]{:S(2)}) copy-start(bf16[512,512]{1,0:T(8,128)(2,1)S(1)} %multiply_convert_fusion.8) | copy-start | bytes 1572868
  666.1 15.4 %copy-start.40 = (bf16[2560,704]{0,1:T(8,128)(2,1)S(1)}, bf16[2560,704]{0,1:T(8,128)(2,1)}, u32[]{:S(2)}) copy-start(bf16[2560,704]{0,1:T(8,128)(2,1)} %get-tuple-element.159) | copy-start | bytes 10813444
  666.1 15.4 %copy-start.41 = (bf16[2560,704]{0,1:T(8,128)(2,1)S(1)}, bf16[2560,704]{0,1:T(8,128)(2,1)}, u32[]{:S(2)}) copy-start(bf16[2560,704]{0,1:T(8,128)(2,1)} %get-tuple-element.160) | copy-start | bytes 10813444
  723.7 63.6 %copy-start.9 = (bf16[2048,1408]{0,1:T(8,128)(2,1)S(1)}, bf16[2048,1408]{0,1:T(8,128)(2,1)}, u32[]{:S(2)}) copy-start(bf16[2048,1408]{0,1:T(8,128)(2,1)} %convolution_convert_fusion.4) | copy-start | bytes 17301508
  793.4 51.3 %copy-start.33 = (s32[4,512]{1,0:T(4,128)S(1)}, s32[4,512]{1,0:T(4,128)}, u32[]{:S(2)}) copy-start(s32[4,512]{1,0:T(4,128)} %copy-done.32) | copy-start | bytes 24580
  844.7 3.4 copy-start.17
  844.7 3.4 copy-start.18
  844.7 3.4 copy-start.22
  848.0 7.7 copy-start.2
  848.0 7.7 copy-start.26
  848.0 7.7 copy-start.28
  855.7 11.2 copy-start.30
  935.3 17.2 %copy-start.4 = (f32[4096,4]{1,0:T(8,128)S(1)}, f32[4096,4]{1,0:T(8,128)}, u32[]{:S(2)}) copy-start(f32[4096,4]{1,0:T(8,128)} %copy-done.3) | copy-start | bytes 196612
  935.3 18.4 %copy-start.21 = (s32[8,512]{1,0:T(8,128)S(1)}, s32[8,512]{1,0:T(8,128)}, u32[]{:S(2)}) copy-start(s32[8,512]{1,0:T(8,128)} %copy-done.20) | copy-start | bytes 49156
  935.3 208.0 %all-to-all-start.2 = ((bf16[8,256,2112]{1,2,0:T(8,128)(2,1)}), bf16[8,256,2112]{1,2,0:T(8,128)(2,1)}, u32[]{:S(2)}, u32[]{:S(2)}) async-start(bf16[8,256,2112]{1,2,0:T(8,128)(2,1)} %bitcast.193), calls=%async_computation.2 | async-start | bytes 17301504 | tf_op jit(solution)/shard_map/all_to_all | solution.py:263
  1025.9 2.2 copy-start.15
  1025.9 2.8 copy-start.14
  1027.8 1.5 copy-start.8
  1029.4 9.2 copy-start.19
  1143.3 75.8 %copy-start = (bf16[2048,1024]{0,1:T(8,128)(2,1)S(1)}, bf16[2048,1024]{0,1:T(8,128)(2,1)}, u32[]{:S(2)}) copy-start(bf16[2048,1024]{0,1:T(8,128)(2,1)} %pad_maximum_fusion.6) | copy-start | bytes 12582916
  1221.3 4.7 copy-start.31
  1221.3 167.6 %all-to-all-start.3 = ((bf16[8,256,1024]{1,2,0:T(8,128)(2,1)}), bf16[8,256,1024]{1,2,0:T(8,128)(2,1)}, u32[]{:S(2)}, u32[]{:S(2)}) async-start(bf16[8,256,1024]{1,2,0:T(8,128)(2,1)} %bitcast.198), calls=%async_computation.3 | async-start | bytes 8388608 | tf_op jit(solution)/shard_map/all_to_all | solution.py:263
  1237.5 5.1 copy-start.6
  1358.3 24.7 %copy-start.7 = (bf16[512,512]{1,0:T(8,128)(2,1)S(1)}, bf16[512,512]{1,0:T(8,128)(2,1)}, u32[]{:S(2)}) copy-start(bf16[512,512]{1,0:T(8,128)(2,1)} %param.16) | copy-start | bytes 1572868
  1358.3 24.7 %copy-start.11 = (f32[512,512]{1,0:T(8,128)S(1)}, f32[512,512]{1,0:T(8,128)}, u32[]{:S(2)}) copy-start(f32[512,512]{1,0:T(8,128)} %get-tuple-element.183) | copy-start | bytes 3145732

commit v5 on v4

v5 whole, which is shorter than its diff:
```python
import functools
import math

import jax
import jax.numpy as jnp
import numpy as np
from jax import lax
from jax.experimental import pallas as pl
from jax.experimental.pallas import tpu as pltpu
from jax.sharding import Mesh, PartitionSpec as P

CAP = 320
PLANES = 4
HALVES = 2
BLOCKS = PLANES * HALVES
EPSILON = 1e-05
ROPE_BASE = 10000.0
NEGATIVE = -1e30
BF16 = jnp.bfloat16
F32 = jnp.float32
PLACES = ("z", "x")
MESH = pl.DeviceIdType.MESH
VMEM_BYTES = 56 * 1024 * 1024


def rope_tables(token_count, width):
    half = width // 2
    frequency = np.float32(ROPE_BASE) ** (-np.arange(half, dtype=np.float32) / np.float32(half))
    angles = np.arange(token_count, dtype=np.float32)[:, None] * frequency.astype(np.float32)[None, :]
    cosine, sine = np.cos(angles).astype(np.float32), np.sin(angles).astype(np.float32)
    return np.concatenate([cosine, cosine], axis=1), np.concatenate([-sine, sine], axis=1)


def turned(values, cosine, sine):
    return values * cosine + pltpu.roll(values, values.shape[1] // 2, 1) * sine


def dot(left, right):
    return jnp.dot(left, right, preferred_element_type=F32)


def contract_first(left, right):
    return lax.dot_general(left, right, (((0,), (0,)), ((), ())), preferred_element_type=F32)


def contract_last(left, right):
    return lax.dot_general(left, right, (((1,), (1,)), ((), ())), preferred_element_type=F32)


def exact(left, right):
    return jnp.dot(left, right, precision=lax.Precision.HIGHEST)


def project_kernel(
    tokens_ref, small_ref, weight_ref, cos_ref, sin_ref,
    hidden_ref, q_ref, k_ref, v_ref, logits_ref, inverse_ref, *, head_width
):
    x = tokens_ref[0, 0].astype(F32)
    inverse = lax.rsqrt(jnp.mean(x * x, axis=1, keepdims=True) + EPSILON)
    inverse_ref[...] = inverse
    hidden = (x * inverse * small_ref[:1, :].astype(F32)).astype(BF16)
    hidden_ref[...] = hidden
    logits_ref[...] = contract_last(small_ref[...], hidden)
    made = dot(hidden, weight_ref[...])
    span = q_ref.shape[1]
    cosine, sine = cos_ref[...], sin_ref[...]
    for head in range(span // head_width):
        at = slice(head * head_width, (head + 1) * head_width)
        q_ref[:, at] = turned(made[:, at], cosine, sine).astype(BF16)
        k_ref[:, at] = turned(made[:, span:][:, at], cosine, sine).astype(BF16)
    v_ref[...] = made[:, 2 * span :].astype(BF16)


def project(tokens, rows, small, weight, cosine, sine, span, head_width):
    width = tokens.shape[-1]
    token_count = BLOCKS * rows
    whole = lambda b: (0, 0)
    block = lambda b: (b, 0)
    return pl.pallas_call(
        functools.partial(project_kernel, head_width=head_width),
        grid=(BLOCKS,),
        in_specs=[
            pl.BlockSpec((1, 1, rows, width), lambda b: (b // HALVES, b % HALVES, 0, 0)),
            pl.BlockSpec(small.shape, whole),
            pl.BlockSpec((width, 3 * span), whole),
            pl.BlockSpec((rows, head_width), block),
            pl.BlockSpec((rows, head_width), block),
        ],
        out_specs=[
            pl.BlockSpec((rows, width), block),
            pl.BlockSpec((rows, span), block),
            pl.BlockSpec((rows, span), block),
            pl.BlockSpec((rows, span), block),
            pl.BlockSpec((small.shape[0], rows), lambda b: (0, b)),
            pl.BlockSpec((rows, 1), block),
        ],
        out_shape=[
            jax.ShapeDtypeStruct((token_count, width), BF16),
            jax.ShapeDtypeStruct((token_count, span), BF16),
            jax.ShapeDtypeStruct((token_count, span), BF16),
            jax.ShapeDtypeStruct((token_count, span), BF16),
            jax.ShapeDtypeStruct((small.shape[0], token_count), F32),
            jax.ShapeDtypeStruct((token_count, 1), F32),
        ],
        compiler_params=pltpu.CompilerParams(vmem_limit_bytes=VMEM_BYTES),
        name="project",
    )(tokens, small, weight, cosine, sine)


def attention_scores(q, k_ref, low_bound, high_bound, tile, tile_rows, scaling):
    rows = pl.ds(pl.multiple_of(tile * tile_rows, tile_rows), tile_rows)
    keys = k_ref[rows, :]
    scores = contract_last(q, keys) * scaling
    column = tile * tile_rows + lax.broadcasted_iota(jnp.int32, scores.shape, 1)
    allowed = (column >= low_bound) & (column <= high_bound)
    return rows, keys, scores, allowed


def slots_of_block(rank_ref, table_ref, cap):
    rows = table_ref.shape[1]
    pick = (lax.broadcasted_iota(jnp.int32, (cap, rows), 0) == rank_ref[0]).astype(BF16)
    made = contract_last(pick, table_ref[...])
    base = pl.program_id(1) * rows
    filled = made[:, 4:5] > 0.5
    low = (64.0 * made[:, 2:3] + made[:, 3:4]).astype(jnp.int32)
    high = (64.0 * made[:, 0:1] + made[:, 1:2]).astype(jnp.int32)
    gate = made[:, 5:6] + made[:, 6:7] + made[:, 7:8]
    return pick, jnp.where(filled, low, base), jnp.where(filled, high, base), gate


def token_table(position, document_start, gate):
    first = gate.astype(BF16).astype(F32)
    second = (gate - first).astype(BF16).astype(F32)
    rows = [
        position // 64, position % 64, document_start // 64, document_start % 64,
        jnp.ones_like(gate), first, second, gate - first - second,
    ]
    return jnp.pad(jnp.stack([row.astype(BF16) for row in rows]), ((0, 8), (0, 0)))


def attention_forward_kernel(
    begin_ref, q_ref, k_ref, v_ref, rank_ref, table_ref, out_ref, gated_ref, gate_ref, lse_ref, *,
    scaling
):
    block = pl.program_id(1)
    cap, width = out_ref.shape
    tile_rows = q_ref.shape[0]
    pick, low_bound, high_bound, gate = slots_of_block(rank_ref, table_ref, cap)
    q = dot(pick, q_ref[...]).astype(BF16)

    def step(tile, carried):
        largest, total, summed = carried
        rows, _, scores, allowed = attention_scores(
            q, k_ref, low_bound, high_bound, tile, tile_rows, scaling
        )
        scores = jnp.where(allowed, scores, NEGATIVE)
        new_largest = jnp.maximum(largest, jnp.max(scores, axis=1, keepdims=True))
        weights = jnp.where(allowed, jnp.exp(scores - new_largest), 0.0)
        shrink = jnp.exp(largest - new_largest)
        return (
            new_largest,
            total * shrink + jnp.sum(weights, axis=1, keepdims=True),
            summed * shrink + dot(weights.astype(BF16), v_ref[rows, :]),
        )

    largest, total, summed = lax.fori_loop(
        begin_ref[block],
        block + 1,
        step,
        (jnp.full((cap, 1), NEGATIVE, F32), jnp.zeros((cap, 1), F32), jnp.zeros((cap, width), F32)),
    )
    attended = (summed / total).astype(BF16)
    out_ref[...] = attended
    gated_ref[...] = (gate * attended.astype(F32)).astype(BF16)
    gate_ref[...] = gate
    lse_ref[0] = largest + jnp.log(total)


def attention_backward_kernel(
    begin_ref, q_ref, k_ref, v_ref, rank_ref, table_ref, out_ref, lse_ref, grad_ref,
    cos_ref, sin_ref, dq_ref, dk_ref, dv_ref, dk_sum, dv_sum, *, scaling
):
    block = pl.program_id(1)
    cap, width = out_ref.shape
    tile_rows = q_ref.shape[0]
    pick, low_bound, high_bound, _ = slots_of_block(rank_ref, table_ref, cap)
    q = dot(pick, q_ref[...]).astype(BF16)
    grad = grad_ref[...]
    delta = jnp.sum(grad.astype(F32) * out_ref[...].astype(F32), axis=1, keepdims=True)
    lse = lse_ref[0]

    @pl.when(block == 0)
    def _():
        dk_sum[...] = jnp.zeros_like(dk_sum)
        dv_sum[...] = jnp.zeros_like(dv_sum)

    def step(tile, dq):
        rows, keys, scores, allowed = attention_scores(
            q, k_ref, low_bound, high_bound, tile, tile_rows, scaling
        )
        chances = jnp.where(allowed, jnp.exp(scores - lse), 0.0)
        dv_sum[rows, :] += contract_first(chances.astype(BF16), grad)
        grad_chances = contract_last(grad, v_ref[rows, :])
        grad_scores = (chances * (grad_chances - delta)).astype(BF16)
        dk_sum[rows, :] += contract_first(grad_scores, q) * scaling
        return dq + dot(grad_scores, keys)

    dq = lax.fori_loop(begin_ref[block], block + 1, step, jnp.zeros((cap, width), F32)) * scaling
    high = dq.astype(BF16)
    rest = (dq - high.astype(F32)).astype(BF16)
    dq_tokens = contract_first(pick, high) + contract_first(pick, rest)
    own = pl.ds(pl.multiple_of(block * tile_rows, tile_rows), tile_rows)
    dq_ref[...] = turned(dq_tokens, cos_ref[own, :], -sin_ref[own, :]).astype(BF16)

    @pl.when(block == BLOCKS - 1)
    def _():
        def finish(tile, nothing):
            rows = pl.ds(pl.multiple_of(tile * tile_rows, tile_rows), tile_rows)
            dk_ref[rows, :] = turned(dk_sum[rows, :], cos_ref[rows, :], -sin_ref[rows, :]).astype(BF16)
            dv_ref[rows, :] = dv_sum[rows, :].astype(BF16)
            return nothing

        lax.fori_loop(0, BLOCKS, finish, 0)


def attention_specs(row_count, token_count, width):
    return dict(
        q=pl.BlockSpec((row_count, width), lambda h, b, s: (b, h)),
        k=pl.BlockSpec((token_count, width), lambda h, b, s: (0, h)),
        rank=pl.BlockSpec((1, 1, row_count), lambda h, b, s: (b, 0, 0)),
        rows=pl.BlockSpec((16, row_count), lambda h, b, s: (0, b)),
        gate=pl.BlockSpec((CAP, 1), lambda h, b, s: (b, 0)),
        slots=pl.BlockSpec((CAP, width), lambda h, b, s: (b, h)),
        table=pl.BlockSpec((token_count, width), lambda h, b, s: (0, 0)),
        lse=pl.BlockSpec((1, CAP, 1), lambda h, b, s: (h, b, 0)),
    )


def attention_forward(begin, q, k, v, rank, table, width):
    token_count, heads = q.shape[0], q.shape[1] // width
    row_count = token_count // BLOCKS
    s = attention_specs(row_count, token_count, width)
    return pl.pallas_call(
        functools.partial(attention_forward_kernel, scaling=1.0 / math.sqrt(width)),
        grid_spec=pltpu.PrefetchScalarGridSpec(
            num_scalar_prefetch=1,
            grid=(heads, BLOCKS),
            in_specs=[s["q"], s["k"], s["k"], s["rank"], s["rows"]],
            out_specs=[s["slots"], s["slots"], s["gate"], s["lse"]],
        ),
        out_shape=[
            jax.ShapeDtypeStruct((BLOCKS * CAP, heads * width), BF16),
            jax.ShapeDtypeStruct((BLOCKS * CAP, heads * width), BF16),
            jax.ShapeDtypeStruct((BLOCKS * CAP, 1), F32),
            jax.ShapeDtypeStruct((heads, BLOCKS * CAP, 1), F32),
        ],
        compiler_params=pltpu.CompilerParams(vmem_limit_bytes=VMEM_BYTES),
        name="attention_forward",
    )(begin, q, k, v, rank, table)


def attention_backward(begin, q, k, v, rank, table, out, lse, grad, cosine, sine, width):
    token_count, heads = q.shape[0], q.shape[1] // width
    row_count = token_count // BLOCKS
    s = attention_specs(row_count, token_count, width)
    return pl.pallas_call(
        functools.partial(attention_backward_kernel, scaling=1.0 / math.sqrt(width)),
        grid_spec=pltpu.PrefetchScalarGridSpec(
            num_scalar_prefetch=1,
            grid=(heads, BLOCKS),
            in_specs=[
                s["q"], s["k"], s["k"], s["rank"], s["rows"],
                s["slots"], s["lse"], s["slots"], s["table"], s["table"],
            ],
            out_specs=[s["q"], s["k"], s["k"]],
            scratch_shapes=[pltpu.VMEM((token_count, width), F32)] * 2,
        ),
        out_shape=[
            jax.ShapeDtypeStruct((token_count, heads * width), BF16),
            jax.ShapeDtypeStruct((token_count, heads * width), BF16),
            jax.ShapeDtypeStruct((token_count, heads * width), BF16),
        ],
        compiler_params=pltpu.CompilerParams(vmem_limit_bytes=VMEM_BYTES),
        name="attention_backward",
    )(begin, q, k, v, rank, table, out, lse, grad, cosine, sine)


def exchanged(pieces):
    return lax.all_to_all(pieces, PLACES, 0, 0, tiled=True)


def over_groups(landed):
    return lax.all_gather(landed, "t", axis=0, tiled=False)


def group_sums(pieces):
    return lax.psum_scatter(pieces, "t", scatter_dimension=0, tiled=False)


def return_gradients(pieces):
    return exchanged(group_sums(pieces))


def other_core(column):
    return column + 1 - 2 * (column % 2)


def crossed(plane, j):
    return (plane, plane + 1 - 2 * (plane % 2), (plane + 2) % 4, 3 - plane)[j]


def meet(peers):
    barrier = pltpu.get_barrier_semaphore()
    for peer in peers:
        pl.semaphore_signal(barrier, inc=1, device_id=peer, device_id_type=MESH)
    pl.semaphore_wait(barrier, len(peers))


def partners():
    plane, half, column = lax.axis_index("z"), lax.axis_index("x"), lax.axis_index("grid")
    planes = [{"z": crossed(plane, j)} for j in range(PLANES)]
    along_x, along_y = {"x": 1 - half}, {"grid": (column + 2) % 4}
    core = {"grid": other_core(column)}
    return plane, half, column, planes, along_x, along_y, core


class Moves:
    def __init__(self, send, recv):
        self.send, self.recv, self.made = send, recv, {}

    def add(self, index, source, target, peer):
        self.made[index] = (source, target, peer)

    def copy(self, index, source, target, peer):
        return pltpu.make_async_remote_copy(
            src_ref=source, dst_ref=target, send_sem=self.send.at[index],
            recv_sem=self.recv.at[index], device_id=peer, device_id_type=MESH,
        )

    def start(self, index):
        self.copy(index, *self.made[index]).start()

    def arrived(self, index, target, peer):
        self.copy(index, target, target, peer).wait_recv()

    def all_sent(self):
        for index in self.made:
            self.copy(index, *self.made[index]).wait_send()


class Ride:
    def __init__(self, pieces_ref, landed_ref, send, recv, local):
        plane, half = lax.axis_index("z"), lax.axis_index("x")
        self.moves = Moves(send, recv)
        self.landings = {}
        own = plane * HALVES + half
        self.keep = pltpu.make_async_copy(pieces_ref.at[own], landed_ref.at[own], local)
        self.peers = []
        for dz in range(PLANES):
            for dx in range(HALVES):
                index = dz * HALVES + dx
                if index == 0:
                    continue
                at_half = 1 - half if dx else half
                peer = {"z": crossed(plane, dz), "x": at_half}
                other = crossed(plane, dz) * HALVES + at_half
                self.moves.add(index, pieces_ref.at[other], landed_ref.at[own], peer)
                self.landings[index] = (landed_ref.at[other], peer)
                if dz and dx:
                    self.peers.append(peer)

    def begin(self):
        self.keep.start()
        for index in (4, 6, 2):
            self.moves.start(index)

    def go_on(self, number):
        for index in ((5,), (7,), (3,), (1,))[number : number + 1]:
            self.moves.start(index[0])

    def finish(self):
        for index, (landing, peer) in self.landings.items():
            self.moves.arrived(index, landing, peer)
        self.moves.all_sent()
        self.keep.wait()


RIDE_SCRATCH = (
    pltpu.SemaphoreType.DMA((8,)),
    pltpu.SemaphoreType.DMA((8,)),
    pltpu.SemaphoreType.DMA,
)


def run_with_ride(steps, ride):
    steps[0]()
    if ride is not None:
        ride.begin()
    for number, step in enumerate(steps[1:-1]):
        step()
        if ride is not None:
            ride.go_on(number)
    steps[-1]()
    if ride is not None:
        ride.finish()


def gather_steps(slots_ref, out_ref, send, recv, local, same, share=2, more=()):
    plane, half, column, planes, along_x, along_y, core = partners()
    cap, width = slots_ref.shape[-2:]
    middle = cap * share // 64 * 16
    y_column, core_column = (column + 2) % 4, other_core(column)
    core_y = (core_column + 2) % 4
    sources = [crossed(plane, j) for j in range(PLANES)]
    moves = Moves(send, recv)

    def piece(source, at_half, at_column, first=0, count=cap):
        columns = pl.ds(pl.multiple_of(at_column * width, width), width)
        return out_ref.at[source, at_half, pl.ds(first, count), columns]

    def slots_for(j):
        return slots_ref if same else slots_ref.at[sources[j]]

    keep = pltpu.make_async_copy(slots_for(0), piece(plane, half, column), local)
    for j in range(PLANES):
        source = sources[j]
        place = piece(source, half, column)
        if j:
            moves.add(j, slots_for(j), piece(plane, half, column), planes[j])
        here = place if j else slots_for(0)
        moves.add(4 + j, here, place, along_x)
        moves.add(8 + j, here, place, along_y)
        moves.add(12 + j, here, place, core)
        from_x, from_y = piece(source, 1 - half, column), piece(source, half, y_column)
        first = piece(source, 1 - half, column, 0, middle)
        last = piece(source, half, y_column, middle, cap - middle)
        diagonal = piece(source, 1 - half, y_column)
        moves.add(16 + j, first, first, along_y)
        moves.add(20 + j, from_x, from_x, core)
        moves.add(24 + j, last, last, along_x)
        moves.add(28 + j, from_y, from_y, core)
        moves.add(32 + j, diagonal, diagonal, core)

    def begin():
        meet(planes[1:] + [along_x, along_y, core] + list(more))
        for j in (1, 3, 2):
            moves.start(j)
        keep.start()

    def spread(j):
        if j:
            moves.arrived(j, piece(sources[j], half, column), planes[j])
        for index in (4, 8, 12):
            moves.start(index + j)

    def forward(j):
        moves.arrived(4 + j, piece(sources[j], 1 - half, column), along_x)
        moves.start(16 + j)
        moves.start(20 + j)
        moves.arrived(8 + j, piece(sources[j], half, y_column), along_y)
        moves.start(24 + j)
        moves.start(28 + j)

    def cross(j):
        moves.arrived(16 + j, piece(sources[j], 1 - half, y_column, 0, middle), along_y)
        moves.arrived(24 + j, piece(sources[j], 1 - half, y_column, middle, cap - middle), along_x)
        moves.start(32 + j)

    def finish():
        for j in order:
            moves.arrived(12 + j, piece(sources[j], half, core_column), core)
            moves.arrived(20 + j, piece(sources[j], 1 - half, core_column), core)
            moves.arrived(28 + j, piece(sources[j], half, core_y), core)
            moves.arrived(32 + j, piece(sources[j], 1 - half, core_y), core)
        moves.all_sent()
        keep.wait()

    order = (0, 1, 3, 2)

    def step(number):
        if number < len(order):
            spread(order[number])
        if 0 <= number - 1 < len(order):
            forward(order[number - 1])
        if 0 <= number - 2 < len(order):
            cross(order[number - 2])

    return [begin] + [functools.partial(step, number) for number in range(len(order) + 2)] + [finish]


GATHER_SCRATCH = (
    pltpu.SemaphoreType.DMA((36,)),
    pltpu.SemaphoreType.DMA((36,)),
    pltpu.SemaphoreType.DMA,
)


def gather_kernel(*refs, same, share, rides):
    if rides:
        slots_ref, pieces_ref, out_ref, landed_ref = refs[:4]
        ride = Ride(pieces_ref, landed_ref, *refs[7:])
        scratch = refs[4:7]
    else:
        slots_ref, out_ref = refs[:2]
        ride, scratch = None, refs[2:]
    more = ride.peers if rides else ()
    run_with_ride(gather_steps(slots_ref, out_ref, *scratch, same, share, more), ride)


def gathered(slots, collective_id, ride=None, share=2):
    rows, width = slots.shape[-2:]
    rides = () if ride is None else (ride,)
    anywhere = pl.BlockSpec(memory_space=pl.ANY)
    out = pl.pallas_call(
        functools.partial(gather_kernel, same=slots.ndim == 2, share=share, rides=len(rides)),
        out_shape=[jax.ShapeDtypeStruct((PLANES, HALVES, rows, 4 * width), BF16)]
        + [jax.ShapeDtypeStruct(r.shape, BF16) for r in rides],
        in_specs=[anywhere] * (1 + len(rides)),
        out_specs=[anywhere] * (1 + len(rides)),
        scratch_shapes=list(GATHER_SCRATCH) + list(RIDE_SCRATCH) * len(rides),
        compiler_params=pltpu.CompilerParams(collective_id=collective_id, has_side_effects=True),
        name="gather_rows",
    )(slots, *rides)
    return out if rides else out[0]


def scatter_steps(
    partial_ref, out_ref, own, other, crossing, side, send, recv, load, share=2, more=()
):
    plane, half, column, planes, along_x, along_y, core = partners()
    cap, width = out_ref.shape[-2:]
    middle = cap * share // 64 * 16
    chunk = 32 if middle % 32 == 0 and cap % 32 == 0 else 16
    y_column, core_column = (column + 2) % 4, other_core(column)
    core_y = (core_column + 2) % 4
    halves = (half, 1 - half, half, 1 - half)
    own_columns = (column, column, y_column, y_column)
    core_columns = (core_column, core_column, core_y, core_y)
    moves = Moves(send, recv)
    first, last = pl.ds(0, middle), pl.ds(middle, cap - middle)

    def part(j, q, at_columns):
        columns = pl.ds(pl.multiple_of(at_columns[q] * width, width), width)
        return partial_ref.at[crossed(plane, j), halves[q], :, columns]

    def loading(j, q):
        return pltpu.make_async_copy(part(j, q, own_columns), own.at[j, q], load.at[4 * j + q])

    keep = pltpu.make_async_copy(own.at[0, 0], out_ref.at[plane], load.at[16])
    for j in range(PLANES):
        for q in range(4):
            moves.add(4 * j + q, part(j, q, core_columns), other.at[j, q], core)
        moves.add(16 + j, own.at[j, 3, first], crossing.at[j, first], along_x)
        moves.add(20 + j, own.at[j, 3, last], crossing.at[j, last], along_y)
        moves.add(24 + j, own.at[j, 2], side.at[j, 1], along_y)
        moves.add(28 + j, own.at[j, 1], side.at[j, 0], along_x)
        if j:
            moves.add(32 + j, own.at[j, 0], out_ref.at[plane], planes[j])

    def add(j, q, begin_row, count, terms):
        def step(i, nothing):
            rows = pl.ds(pl.multiple_of(begin_row + i * chunk, chunk), chunk)
            total = own[j, q, rows, :].astype(F32)
            for ref, index in terms:
                total = total + ref[index + (rows, slice(None))].astype(F32)
            own[j, q, rows, :] = total.astype(BF16)
            return nothing

        lax.fori_loop(0, count // chunk, step, 0)

    def chip_sum(j, q):
        moves.arrived(4 * j + q, other.at[j, q], core)
        loading(j, q).wait()
        add(j, q, 0, cap, [(other, (j, q))])

    def stage_one(j):
        chip_sum(j, 3)
        moves.start(16 + j)
        moves.start(20 + j)
        chip_sum(j, 2)
        chip_sum(j, 1)
        chip_sum(j, 0)

    def stage_two(j):
        moves.arrived(16 + j, crossing.at[j, first], along_x)
        add(j, 2, 0, middle, [(crossing, (j,))])
        moves.start(24 + j)
        moves.arrived(20 + j, crossing.at[j, last], along_y)
        add(j, 1, middle, cap - middle, [(crossing, (j,))])
        moves.start(28 + j)

    def stage_three(j):
        moves.arrived(24 + j, side.at[j, 1], along_y)
        moves.arrived(28 + j, side.at[j, 0], along_x)
        add(j, 0, 0, cap, [(side, (j, 0)), (side, (j, 1))])
        if j:
            moves.start(32 + j)
        else:
            keep.start()

    order = (2, 3, 1, 0)

    def begin():
        meet(planes[1:] + [along_x, along_y, core] + list(more))
        for j in order:
            for q in (3, 2, 1, 0):
                moves.start(4 * j + q)
                loading(j, q).start()

    def step(number):
        if number < len(order):
            stage_one(order[number])
        if 0 <= number - 1 < len(order):
            stage_two(order[number - 1])
        if 0 <= number - 2 < len(order):
            stage_three(order[number - 2])

    def finish():
        for j in range(1, PLANES):
            moves.arrived(32 + j, out_ref.at[crossed(plane, j)], planes[j])
        moves.all_sent()
        keep.wait()

    return [begin] + [functools.partial(step, number) for number in range(len(order) + 2)] + [finish]


def scatter_scratch(rows, width):
    return [
        pltpu.VMEM((PLANES, 4, rows, width), BF16),
        pltpu.VMEM((PLANES, 4, rows, width), BF16),
        pltpu.VMEM((PLANES, rows, width), BF16),
        pltpu.VMEM((PLANES, 2, rows, width), BF16),
        pltpu.SemaphoreType.DMA((36,)),
        pltpu.SemaphoreType.DMA((36,)),
        pltpu.SemaphoreType.DMA((17,)),
    ]


def scatter_kernel(*refs, share, rides):
    if rides:
        partial_ref, pieces_ref, out_ref, landed_ref = refs[:4]
        ride = Ride(pieces_ref, landed_ref, *refs[11:])
        scratch = refs[4:11]
    else:
        partial_ref, out_ref = refs[:2]
        ride, scratch = None, refs[2:]
    more = ride.peers if rides else ()
    run_with_ride(scatter_steps(partial_ref, out_ref, *scratch, share, more), ride)


def scattered(partial, rows, collective_id, ride=None, share=2):
    width = partial.shape[1] // 4
    rides = () if ride is None else (ride,)
    anywhere = pl.BlockSpec(memory_space=pl.ANY)
    out = pl.pallas_call(
        functools.partial(scatter_kernel, share=share, rides=len(rides)),
        out_shape=[jax.ShapeDtypeStruct((PLANES, rows, width), BF16)]
        + [jax.ShapeDtypeStruct(r.shape, BF16) for r in rides],
        in_specs=[anywhere] * (1 + len(rides)),
        out_specs=[anywhere] * (1 + len(rides)),
        scratch_shapes=scatter_scratch(rows, width) + list(RIDE_SCRATCH) * len(rides),
        compiler_params=pltpu.CompilerParams(
            collective_id=collective_id, has_side_effects=True, vmem_limit_bytes=VMEM_BYTES
        ),
        name="scatter_rows",
    )(partial.reshape(PLANES, HALVES, rows, 4 * width), *rides)
    return out if rides else out[0]


def carry(before, after, last, compute):
    number = pl.program_id(0)

    @pl.when(number == 0)
    def _():
        for step in before:
            step()

    compute()
    for place, step in enumerate(after):
        pl.when(number == place)(step)
    pl.when(number == BLOCKS - 1)(last)


def expert_forward_kernel(
    rows_ref, up_weight_ref, down_weight_ref, small_ref, rank_ref, member_ref, grad_ref,
    gate_ref, up_ref, result_ref, share_ref, grad_rows_ref, *scratch
):
    steps = gather_steps(grad_ref, grad_rows_ref, *scratch, False)
    units = gate_ref.shape[1]

    def compute():
        rows = rows_ref[0]
        made = dot(rows, up_weight_ref[...])
        gate, up = made[:, :units], made[:, units:]
        gate_ref[...] = gate
        up_ref[...] = up
        inner = (gate * jax.nn.sigmoid(gate) * up).astype(BF16)
        result_ref[0] = contract_last(inner, down_weight_ref[...]).astype(BF16)
        cap, count = rows.shape[0], rank_ref.shape[2]
        pick = (lax.broadcasted_iota(jnp.int32, (cap, count), 0) == rank_ref[0]).astype(BF16)
        member = contract_last(pick, member_ref[...]) > 0.5
        logits = jnp.where(member, contract_last(rows, small_ref[...]), NEGATIVE)
        largest = jnp.max(logits, axis=1, keepdims=True)
        weights = jnp.where(member, jnp.exp(logits - largest), 0.0)
        mine = lax.broadcasted_iota(jnp.int32, weights.shape, 1) == 6 + lax.axis_index("z")
        total = jnp.sum(weights, axis=1, keepdims=True)
        own = jnp.sum(jnp.where(mine, weights, 0.0), axis=1, keepdims=True)
        share_ref[...] = own / jnp.where(total > 0.0, total, 1.0)

    carry(steps[:2], steps[2:-1], steps[-1], compute)


def once(shape):
    return pl.BlockSpec(shape, lambda b: (0,) * len(shape), pipeline_mode=pl.Buffered(1))


def expert_forward(rows, up_weight, down_weight, small, rank, member, grad_slots, collective_id):
    _, cap, width = rows.shape
    units = down_weight.shape[1]
    count = BLOCKS * cap
    anywhere = pl.BlockSpec(memory_space=pl.ANY)
    block = lambda b: (b, 0)
    return pl.pallas_call(
        expert_forward_kernel,
        grid=(BLOCKS,),
        in_specs=[
            pl.BlockSpec((1, cap, width), lambda b: (b, 0, 0)),
            once(up_weight.shape),
            once(down_weight.shape),
            once(small.shape),
            pl.BlockSpec((1, 1, rank.shape[2]), lambda b: (b, 0, 0)),
            pl.BlockSpec((16, rank.shape[2]), lambda b: (0, b)),
            anywhere,
        ],
        out_specs=[
            pl.BlockSpec((cap, units), block),
            pl.BlockSpec((cap, units), block),
            pl.BlockSpec((1, cap, width), lambda b: (b, 0, 0)),
            pl.BlockSpec((cap, 1), block),
            anywhere,
        ],
        out_shape=[
            jax.ShapeDtypeStruct((count, units), F32),
            jax.ShapeDtypeStruct((count, units), F32),
            jax.ShapeDtypeStruct((BLOCKS, cap, width), BF16),
            jax.ShapeDtypeStruct((count, 1), F32),
            jax.ShapeDtypeStruct((PLANES, HALVES, cap, width), BF16),
        ],
        scratch_shapes=list(GATHER_SCRATCH),
        compiler_params=pltpu.CompilerParams(
            collective_id=collective_id, has_side_effects=True, vmem_limit_bytes=VMEM_BYTES
        ),
        name="expert_forward",
    )(rows, up_weight, down_weight, small, rank, member, grad_slots)


def expert_backward_kernel(
    gate_ref, up_ref, grad_ref, share_ref, up_weight_ref, down_weight_ref, result_ref,
    grad_rows_ref, grad_gate_up_ref, inner_ref, out_ref, *scratch
):
    steps = scatter_steps(result_ref, out_ref, *scratch)

    def compute():
        share = share_ref[...]
        grad_inner = dot(grad_ref[0], down_weight_ref[...]) * share
        gate, up = gate_ref[...], up_ref[...]
        sigmoid = jax.nn.sigmoid(gate)
        silu = gate * sigmoid
        inner_ref[...] = (share * silu * up).astype(BF16)
        grad_gate = grad_inner * up * sigmoid * (1.0 + gate * (1.0 - sigmoid))
        grad_gate_up = jnp.concatenate([grad_gate, grad_inner * silu], axis=1).astype(BF16)
        grad_gate_up_ref[...] = grad_gate_up
        grad_rows_ref[0] = contract_last(grad_gate_up, up_weight_ref[...]).astype(BF16)

    carry(steps[:1], steps[1:-1], steps[-1], compute)


def expert_backward(
    gate, up, grad_rows, share, up_weight, down_weight, result, collective_id
):
    _, cap, width = grad_rows.shape
    count, units = gate.shape
    anywhere = pl.BlockSpec(memory_space=pl.ANY)
    block = lambda b: (b, 0)
    rows = pl.BlockSpec((1, cap, width), lambda b: (b, 0, 0))
    return pl.pallas_call(
        expert_backward_kernel,
        grid=(BLOCKS,),
        in_specs=[
            pl.BlockSpec((cap, units), block),
            pl.BlockSpec((cap, units), block),
            rows,
            pl.BlockSpec((cap, 1), block),
            once(up_weight.shape),
            once(down_weight.shape),
            anywhere,
        ],
        out_specs=[
            rows,
            pl.BlockSpec((cap, 2 * units), block),
            pl.BlockSpec((cap, units), block),
            anywhere,
        ],
        out_shape=[
            jax.ShapeDtypeStruct((BLOCKS, cap, width), BF16),
            jax.ShapeDtypeStruct((count, 2 * units), BF16),
            jax.ShapeDtypeStruct((count, units), BF16),
            jax.ShapeDtypeStruct((PLANES, cap, width // 4), BF16),
        ],
        scratch_shapes=scatter_scratch(cap, width // 4),
        compiler_params=pltpu.CompilerParams(
            collective_id=collective_id, has_side_effects=True, vmem_limit_bytes=VMEM_BYTES
        ),
        name="expert_backward",
    )(gate, up, grad_rows, share, up_weight, down_weight, result.reshape(PLANES, HALVES, cap, width))


def expert_gradient_kernel(
    rows_ref, grad_ref, grad_gate_up_ref, inner_ref, partial_ref,
    up_grad_ref, down_first_ref, down_last_ref, out_ref, *scratch
):
    steps = scatter_steps(partial_ref, out_ref, *scratch)
    middle = down_first_ref.shape[1]

    def compute():
        up_grad_ref[...] = contract_first(rows_ref[...], grad_gate_up_ref[...]).astype(BF16)
        down_grad = contract_first(grad_ref[...], inner_ref[...]).astype(BF16)
        down_first_ref[0] = down_grad[:middle]
        down_last_ref[0] = down_grad[middle:]

    carry(steps[:1], steps[1:-1], steps[-1], compute)


def expert_gradient(rows, grad_rows, grad_gate_up, inner, partial, collective_id):
    count, width = rows.shape
    units = inner.shape[1]
    cap, tile = count // BLOCKS, width // BLOCKS
    anywhere = pl.BlockSpec(memory_space=pl.ANY)
    columns = pl.BlockSpec((count, tile), lambda b: (0, b))
    return pl.pallas_call(
        expert_gradient_kernel,
        grid=(BLOCKS,),
        in_specs=[columns, columns, once((count, 2 * units)), once((count, units)), anywhere],
        out_specs=[
            pl.BlockSpec((tile, 2 * units), lambda b: (b, 0)),
            pl.BlockSpec((1, tile // 2, units), lambda b: (b, 0, 0)),
            pl.BlockSpec((1, tile // 2, units), lambda b: (b, 0, 0)),
            anywhere,
        ],
        out_shape=[
            jax.ShapeDtypeStruct((width, 2 * units), BF16),
            jax.ShapeDtypeStruct((BLOCKS, tile // 2, units), BF16),
            jax.ShapeDtypeStruct((BLOCKS, tile // 2, units), BF16),
            jax.ShapeDtypeStruct((PLANES, cap, width // 4), BF16),
        ],
        scratch_shapes=scatter_scratch(cap, width // 4),
        compiler_params=pltpu.CompilerParams(
            collective_id=collective_id, has_side_effects=True, vmem_limit_bytes=VMEM_BYTES
        ),
        name="expert_gradient",
    )(rows, grad_rows, grad_gate_up, inner, partial.reshape(PLANES, HALVES, cap, width))


def grid_sum(values):
    shape = values.shape
    return lax.all_gather(values.reshape(-1, 128), "grid", axis=0).sum(axis=0).reshape(shape)


def prefix_ranks(member):
    counted = member.astype(BF16)
    width = member.shape[-1]
    before = jnp.arange(width)[:, None] < jnp.arange(width)[None, :]
    return jnp.where(member, dot(counted, before.astype(BF16)).astype(jnp.int32), -1)


def picks(rank):
    return (jnp.arange(CAP, dtype=jnp.int32)[:, None] == rank[..., None, :]).astype(BF16)


def members(first, second):
    names = jnp.arange(PLANES, dtype=first.dtype).reshape((PLANES,) + (1,) * first.ndim)
    return (first[None] == names) | (second[None] == names)


def route_gates(logits, member):
    shown = jnp.where(member, logits, NEGATIVE)
    weights = jnp.where(member, jnp.exp(shown - jnp.max(shown, axis=0, keepdims=True)), 0.0)
    return weights / jnp.sum(weights, axis=0, keepdims=True)


def logits_grad(gates, grad_gates):
    return gates * (grad_gates - jnp.sum(gates * grad_gates, axis=0, keepdims=True))


def exact_first(left, right):
    return lax.dot_general(
        left, right, (((0,), (0,)), ((), ())), precision=lax.Precision.HIGHEST
    )


def exact_last(left, right):
    return lax.dot_general(
        left, right, (((1,), (1,)), ((), ())), precision=lax.Precision.HIGHEST
    )


def norm_sums(grad_hidden, scaled, router, gates, grad_gates, width):
    parts = jnp.concatenate(
        [
            grad_gates,
            exact_last(router.astype(F32), scaled),
            jnp.sum(grad_hidden * scaled, axis=1)[None],
        ],
        axis=0,
    )
    parts = grid_sum(parts)
    grad_logits = logits_grad(gates, parts[:PLANES])
    inner = parts[2 * PLANES] + jnp.sum(grad_logits * parts[PLANES : 2 * PLANES], axis=0)
    return grad_logits, inner[:, None] / width


def per_device(
    tokens, segment_ids, attention_routes, expert_routes, attention_gain, attention_kv,
    attention_query, attention_out, attention_router, feedforward_gain, feedforward_router,
    expert_gate_up, expert_down, output_grad,
):
    groups = lax.axis_size("t")
    grid_count = lax.axis_size("grid")
    group = lax.axis_index("t")
    plane = lax.axis_index("z")
    place = plane * HALVES + lax.axis_index("x")
    column = lax.axis_index("grid")
    rows, features = tokens.shape
    width_all = features * grid_count
    token_count = BLOCKS * rows
    own_rows = attention_gain.shape[0]
    head_width = attention_kv.shape[3]
    head_pair = attention_kv.shape[1] // HALVES
    span = head_pair * head_width
    hidden_units = expert_gate_up.shape[3] // HALVES

    def mine(array, axis=0):
        return lax.dynamic_slice_in_dim(array, column * features, features, axis)

    def own(array, axis=0):
        return lax.dynamic_slice_in_dim(array, place * rows, rows, axis)

    query_pieces = attention_query.reshape(PLANES, own_rows, HALVES, span).transpose(0, 2, 1, 3)
    kv_pieces = attention_kv.reshape(own_rows, HALVES, head_pair, 2, head_width)
    kv_pieces = kv_pieces.transpose(1, 0, 3, 2, 4).reshape(1, HALVES, own_rows, 2 * span)
    kv_pieces = jnp.broadcast_to(kv_pieces, (PLANES,) + kv_pieces.shape[1:])
    qkv_pieces = jnp.concatenate([query_pieces, kv_pieces], axis=-1)
    out_pieces = attention_out.reshape(BLOCKS, span, own_rows).swapaxes(1, 2)
    first_pieces = jnp.concatenate([qkv_pieces.reshape(BLOCKS, own_rows, 3 * span), out_pieces], axis=2)
    up_pieces = expert_gate_up.reshape(PLANES, own_rows, 2, HALVES, hidden_units)
    up_pieces = up_pieces.transpose(0, 3, 1, 2, 4).reshape(BLOCKS, own_rows, 2 * hidden_units)
    down_pieces = expert_down.reshape(BLOCKS, hidden_units, own_rows).swapaxes(1, 2)
    down_halves = down_pieces[:, : own_rows // 2], down_pieces[:, own_rows // 2 :]

    own_routes = jnp.concatenate([attention_routes, expert_routes], axis=1)
    small = jnp.concatenate(
        [attention_gain[:, None], feedforward_gain[:, None], attention_router, feedforward_router],
        axis=1,
    )
    small = lax.all_gather(small, "t", axis=0).reshape(-1, small.shape[1])
    small = small.T.reshape(small.shape[1], -1)
    spare = jnp.zeros((small.shape[0], features - small.shape[1] % features), BF16)
    small = jnp.concatenate([small, spare], axis=1).reshape(-1, features)
    under = jnp.concatenate([own_routes.T.astype(BF16), small], axis=0)
    under = jnp.pad(under, ((0, -under.shape[0] % 16), (0, 0)))
    everything, first_weight = gathered(
        jnp.concatenate([tokens, under], axis=0), 0, ride=first_pieces, share=3
    )
    first_weight = over_groups(first_weight).reshape(width_all, 4 * span)
    qkv_weight, out_weight = first_weight[:, : 3 * span], first_weight[:, 3 * span :]
    up_pieces, everything = lax.optimization_barrier((up_pieces, everything))
    up_weight = over_groups(exchanged(up_pieces)).reshape(width_all, 2 * hidden_units)
    under = everything[:, :, rows:, :features].reshape(BLOCKS, -1, features).swapaxes(0, 1)
    small = under[4:, :, : groups * own_rows].reshape(-1, BLOCKS, groups, own_rows)
    small = jnp.pad(small.swapaxes(1, 2).reshape(-1, width_all), ((0, 4), (0, 0)))
    gain_first, gain_second = mine(small[0]).astype(F32), mine(small[1]).astype(F32)
    router_first, router_second = mine(small[2:6], 1), mine(small[6:10], 1)

    member_first, member_second = members(under[0], under[1]), members(under[2], under[3])
    own_member_first = lax.dynamic_index_in_dim(member_first, place, 1, keepdims=False)
    own_member_second = lax.dynamic_index_in_dim(member_second, place, 1, keepdims=False)
    rank = prefix_ranks(
        jnp.concatenate(
            [
                lax.dynamic_index_in_dim(member_first, plane, 0, keepdims=False),
                lax.dynamic_index_in_dim(member_second, plane, 0, keepdims=False),
                own_member_first,
                own_member_second,
            ],
            axis=0,
        )
    )
    rank_first, rank_second = rank[:BLOCKS, None], rank[BLOCKS : 2 * BLOCKS, None]
    own_pick_first = picks(rank[2 * BLOCKS : 2 * BLOCKS + PLANES])
    own_pick_second = picks(rank[2 * BLOCKS + PLANES :])
    member_first = member_first.reshape(PLANES, token_count)
    member_second = member_second.reshape(PLANES, token_count)

    def to_slots(values, pick):
        return jnp.einsum("est,tf->esf", pick, values, preferred_element_type=F32).astype(BF16)

    def to_tokens(slots, pick):
        return jnp.einsum("est,esf->etf", pick, slots, preferred_element_type=F32)

    grad_out = output_grad.astype(F32)
    cosine, sine = rope_tables(token_count, head_width)
    cosine, sine = jnp.asarray(cosine), jnp.asarray(sine)
    hidden_first, queries, keys, values, logits_first, inverse_first = project(
        everything, rows, small, first_weight, cosine, sine, span, head_width
    )
    gates_first = route_gates(logits_first[2 : 2 + PLANES], member_first)
    own_gates_first = own(gates_first, 1)
    position = jnp.arange(token_count, dtype=jnp.int32)
    segment = lax.dynamic_slice_in_dim(segment_ids, group * token_count, token_count, 0)
    opens = jnp.concatenate([jnp.ones((1,), jnp.bool_), segment[1:] != segment[:-1]])
    document_start = lax.cummax(jnp.where(opens, position, 0))
    begin = document_start.reshape(BLOCKS, rows)[:, 0] // rows
    table = token_table(
        position, document_start, lax.dynamic_index_in_dim(gates_first, plane, 0, keepdims=False)
    )
    attention_args = (begin, queries, keys, values, rank_first, table)
    attended, gated, gate_slots_first, lse = attention_forward(*attention_args, head_width)
    branch_slots, down_first = scattered(
        contract_last(attended, out_weight).astype(BF16), CAP, 2, ride=down_halves[0], share=1
    )
    branch_first = to_tokens(branch_slots, own_pick_first)
    residual = tokens.astype(F32) + jnp.sum(own_gates_first[:, :, None] * branch_first, axis=0)

    square = grid_sum(jnp.sum(residual * residual, axis=1))
    inverse_second = lax.rsqrt(square / width_all + EPSILON)[:, None]
    normed_second = residual * inverse_second
    hidden_second = (normed_second * gain_second).astype(BF16)
    slots_second, down_last = gathered(
        to_slots(hidden_second, own_pick_second), 1, ride=down_halves[1], share=3
    )
    down_weight = over_groups(jnp.concatenate([down_first, down_last], axis=1))
    down_weight = down_weight.reshape(width_all, hidden_units)
    slots_second = slots_second.reshape(BLOCKS, CAP, width_all)
    gate_pre, up_pre, result, gate_slots_second, grad_slots_second = expert_forward(
        slots_second,
        up_weight,
        down_weight,
        small,
        rank_second,
        jnp.pad(member_second.astype(BF16), ((6, 6), (0, 0))),
        to_slots(output_grad, own_pick_second),
        4,
    )
    grad_slots_second = grad_slots_second.reshape(BLOCKS, CAP, width_all)
    grad_rows, grad_gate_up, inner, result_slots = expert_backward(
        gate_pre, up_pre, grad_slots_second, gate_slots_second, up_weight, down_weight, result, 5
    )
    grad_up, grad_down_first, grad_down_last, grad_rows = expert_gradient(
        slots_second.reshape(-1, width_all), grad_slots_second.reshape(-1, width_all),
        grad_gate_up, inner, grad_rows, 6,
    )
    own_logits = grid_sum(contract_last(router_second, hidden_second))
    own_gates_second = route_gates(own_logits, own_member_second)
    branch_second = to_tokens(result_slots, own_pick_second)
    layer_output = residual + jnp.sum(own_gates_second[:, :, None] * branch_second, axis=0)
    layer_output = layer_output.astype(BF16)

    grad_hidden_second = jnp.sum(to_tokens(grad_rows, own_pick_second), axis=0)
    grad_logits_second, inner_mean = norm_sums(
        grad_hidden_second, normed_second * gain_second, router_second, own_gates_second,
        jnp.sum(branch_second * grad_out[None], axis=2), width_all,
    )
    grad_hidden_second = grad_hidden_second + exact_first(
        grad_logits_second, router_second.astype(F32)
    )
    grad_router_second = exact(grad_logits_second, hidden_second.astype(F32))
    grad_gain_second = jnp.sum(grad_hidden_second * normed_second, axis=0)
    grad_normed = grad_hidden_second * gain_second
    grad_residual = grad_out + inverse_second * (grad_normed - normed_second * inner_mean)

    if groups > 1:
        grad_down = jnp.concatenate([grad_down_first, grad_down_last], axis=1)
        grad_down = group_sums(grad_down.reshape(groups, BLOCKS, own_rows, hidden_units))
        grad_down_first, grad_down_last = jnp.split(grad_down, 2, axis=1)
    grad_slots_first, grad_down_first = gathered(
        to_slots(grad_residual.astype(BF16), own_pick_first), 1, ride=grad_down_first, share=3
    )
    grad_slots_first = grad_slots_first.reshape(BLOCKS * CAP, -1)
    grad_up, grad_slots_first = lax.optimization_barrier((grad_up, grad_slots_first))
    grad_up = return_gradients(grad_up.reshape(groups, BLOCKS, own_rows, 2 * hidden_units))
    grad_attended = gate_slots_first * dot(grad_slots_first, out_weight)
    grad_attended = grad_attended.astype(BF16)
    grad_out_weight = contract_first(
        grad_slots_first, gated
    )
    grad_qkv = jnp.concatenate(
        attention_backward(
            *attention_args, attended, lse, grad_attended, cosine, sine, head_width
        ),
        axis=1,
    )
    grad_hidden = contract_last(grad_qkv, qkv_weight).astype(BF16)
    grad_first = jnp.concatenate(
        [contract_first(hidden_first, grad_qkv).astype(BF16), grad_out_weight.astype(BF16)], axis=1
    )
    grad_hidden, grad_first, grad_up = lax.optimization_barrier((grad_hidden, grad_first, grad_up))
    grad_hidden, grad_down_last = scattered(grad_hidden, rows, 3, ride=grad_down_last, share=1)
    grad_hidden = jnp.sum(grad_hidden.astype(F32), axis=0)
    expert_gate_up_grad = grad_up.reshape(PLANES, HALVES, own_rows, 2, hidden_units)
    expert_gate_up_grad = expert_gate_up_grad.transpose(0, 2, 3, 1, 4).reshape(expert_gate_up.shape)
    expert_down_grad = jnp.concatenate([grad_down_first, grad_down_last], axis=1)
    expert_down_grad = expert_down_grad.swapaxes(1, 2).reshape(expert_down.shape)

    own_normed = tokens.astype(F32) * own(inverse_first)
    own_hidden = (own_normed * gain_first).astype(BF16)
    grad_logits_first, inner_mean = norm_sums(
        grad_hidden, own_normed * gain_first, router_first, own_gates_first,
        jnp.sum(branch_first * grad_residual[None], axis=2), width_all,
    )
    grad_hidden_first = grad_hidden + exact_first(grad_logits_first, router_first.astype(F32))
    grad_router_first = exact(grad_logits_first, own_hidden.astype(F32))
    grad_gain_first = jnp.sum(grad_hidden_first * own_normed, axis=0)
    grad_normed = grad_hidden_first * gain_first
    input_grad = grad_residual + own(inverse_first) * (grad_normed - own_normed * inner_mean)

    small_grads = jnp.concatenate(
        [grad_gain_first[None], grad_gain_second[None], grad_router_first, grad_router_second],
        axis=0,
    )
    small_grads = lax.all_gather(small_grads.astype(BF16), "grid", axis=1, tiled=True)
    small_grads = small_grads.reshape(-1, groups, BLOCKS, own_rows).transpose(1, 2, 0, 3)
    small_grads = jnp.pad(small_grads, ((0, 0), (0, 0), (0, 6), (0, 4 * span - own_rows)))
    grad_first = grad_first.reshape(groups, BLOCKS, own_rows, 4 * span)
    grad_first = return_gradients(jnp.concatenate([grad_first, small_grads], axis=2))
    small_grads = jnp.sum(grad_first[:, own_rows:, :own_rows].astype(F32), axis=0)
    grad_first = grad_first[:, :own_rows]
    attention_out_grad = grad_first[..., 3 * span :].swapaxes(1, 2).reshape(attention_out.shape)
    attention_query_grad = grad_first[..., :span].reshape(PLANES, HALVES, own_rows, span)
    attention_query_grad = attention_query_grad.transpose(0, 2, 1, 3).reshape(attention_query.shape)
    grad_kv_weight = grad_first[..., span : 3 * span].astype(F32).reshape(
        PLANES, HALVES, own_rows, 2, head_pair, head_width
    )
    attention_kv_grad = grad_kv_weight.sum(axis=0).transpose(1, 0, 3, 2, 4)
    attention_kv_grad = attention_kv_grad.reshape(attention_kv.shape)
    return (
        layer_output,
        input_grad.astype(BF16),
        small_grads[0],
        attention_kv_grad,
        attention_query_grad.astype(F32),
        attention_out_grad.astype(F32),
        small_grads[2:6].T,
        small_grads[1],
        small_grads[6:10].T,
        expert_gate_up_grad.astype(F32),
        expert_down_grad.astype(F32),
    )


def solution(mesh):
    groups = mesh.shape["wide"] // BLOCKS
    shape = (groups, PLANES, HALVES, mesh.shape["grid"])
    inner_mesh = Mesh(mesh.devices.reshape(shape), ("t", "z", "x", "grid"))
    wide = ("t", "z", "x")
    in_specs = (
        P(wide, "grid"),
        P(),
        P(wide, None),
        P(wide, None),
        P(wide),
        P(wide, "grid", None, None),
        P(None, wide, "grid", None),
        P(None, "grid", None, wide),
        P(wide, None),
        P(wide),
        P(wide, None),
        P(None, wide, None, "grid"),
        P(None, "grid", wide),
        P(wide, "grid"),
    )
    out_specs = (
        P(wide, "grid"),
        P(wide, "grid"),
        P(wide),
        P(wide, "grid", None, None),
        P(None, wide, "grid", None),
        P(None, "grid", None, wide),
        P(wide, None),
        P(wide),
        P(wide, None),
        P(None, wide, None, "grid"),
        P(None, "grid", wide),
    )
    return jax.shard_map(
        per_device, mesh=inner_mesh, in_specs=in_specs, out_specs=out_specs, check_vma=False
    )
```

time: 1410 us -> 1170 us (0.83)
  matrix products: 211 us -> 84.4 us
  blocking collectives: 126 us -> 26.4 us
  starting transfers between devices: 72.8 us -> 22.1 us
  Pallas kernels: 759 us -> 808 us
    all_gather x2 -> x1, blocking collectives: 94.9 us -> 5.25 us  [per_device(): lax.all_gather(small_grads.astype(BF16), 'grid', axis=1, tiled=True)]
    all_to_all x4 -> x3, starting transfers between devices: 72.8 us -> 22.1 us  [exchanged(): return lax.all_to_all(pieces, PLACES, 0, 0, tiled=True)]
    dot_general x5 -> x2, matrix products: 57.1 us -> 8.39 us  [dot(): return jnp.dot(left, right, preferred_element_type=F32)]
    pallas_call x8, Pallas kernels: 632 us -> 674 us  [the longest x3 287 us: gathered(): pl.pallas_call(functools.partial(gather_kernel, same=slots.ndim == 2, sha...]
    dot_general x4 -> x3, matrix products: 67.2 us -> 25.9 us  [contract_last(): lax.dot_general(left, right, (((1,), (1,)), ((), ())), preferred_element_...]
    dot_general x4 -> x2, matrix products: 62.9 us -> 26 us  [contract_first(): lax.dot_general(left, right, (((0,), (0,)), ((), ())), preferred_element_...]
    reshape x3 -> x6, local copies, waits for them, and re-layouts: 0.06 us -> 15.5 us  [the longest x1 6.4 us: per_device(): grad_first = grad_first.reshape(groups, BLOCKS, own_rows, 4 * span)]
    all_gather x6 -> x4, blocking collectives: 31.3 us -> 21.2 us  [grid_sum(): lax.all_gather(values.reshape(-1, 128), 'grid', axis=0).sum(axis=0)]
  transfers between devices with their start and end apart: 4 -> 3, of which waited for: 1 -> 2; matrix products, arithmetic and copies ran while one was open for 14% -> 12% of each run, Pallas kernels for 36% -> 26%
where the time goes in v5:
time: 1170 us
  Pallas kernels  808 us (69%)
  local copies, waits for them, and re-layouts  120 us (10%)
  matrix products  84.4 us (7%)
  waiting for transfers between devices  54.8 us (5%)
  other arithmetic  48.6 us (4%)
  blocking collectives  26.4 us (2%)
  starting transfers between devices  22.1 us (2%)
    pallas_call x3, Pallas kernels, gathered(): pl.pallas_call(functools.partial(gather_kernel, same=slots.ndim == 2, sha...  287 us
    pallas_call x2, Pallas kernels, scattered(): pl.pallas_call(functools.partial(scatter_kernel, share=share, rides=len(r...  185 us
    pallas_call x1, Pallas kernels, expert_forward(): pl.pallas_call(expert_forward_kernel, grid=(BLOCKS,), in_specs=[pl.BlockS...  70.7 us
    pallas_call x1, Pallas kernels, expert_backward(): pl.pallas_call(expert_backward_kernel, grid=(BLOCKS,), in_specs=[pl.Block...  67.3 us
    pallas_call x1, Pallas kernels, attention_backward(): pl.pallas_call(functools.partial(attention_backward_kernel, scaling=1.0 /...  66.9 us
    pallas_call x1, Pallas kernels, expert_gradient(): pl.pallas_call(expert_gradient_kernel, grid=(BLOCKS,), in_specs=[columns,...  63.4 us
    all_to_all x3, waiting for transfers between devices, exchanged(): return lax.all_to_all(pieces, PLACES, 0, 0, tiled=True)  54.8 us
    unnamed x66, local copies, waits for them, and re-layouts  41 us
  transfers between devices with their start and end apart: 3, of which 2 were waited for; matrix products, arithmetic and copies ran while one was open for 12% of the time, Pallas kernels for 26%

profile of v5, /device:TPU:0, one launch (start us, length us, event | category | flops | bytes accessed | tf_op | source)
XLA Modules:
  0.0 1166.2 jit_solution(15846757870150238649)
XLA Ops:
  3.3 1.1 copy.112
  4.9 2.7 reshape.407
  7.8 1.5 copy.115
  9.3 14.6 %copy.109 = bf16[4,256,2,1408]{1,3,2,0:T(8,128)(2,1)} copy(bf16[4,256,2,1408]{3,2,1,0:T(2,128)(2,1)} %param.27) | data formatting | bytes 11534336 | tf_op args[11]
  23.9 5.6 copy.110
  30.9 2.6 pad_maximum_fusion.refs_1_
  33.4 136.1 %gather_rows.3 = (bf16[4,2,528,2048]{3,2,1,0:T(8,128)(2,1)}, bf16[8,256,1024]{2,1,0:T(8,128)(2,1)}) custom-call(bf16[528,512]{1,0:T(8,128)(2,1)} %fusion.41.refs_0_, bf16[8,256,1024]{2,1,0:T(8,128)(2,1)} %pad_maximum_fusion.refs_1_), custom_call_target="tpu_custom_call" | custom-call | tf_op jit(solution)/shard_map/gather_rows/pallas_call | solution.py:514
  169.5 12.3 %all-to-all-start = ((bf16[8,256,1408]{1,2,0:T(8,128)(2,1)}), bf16[8,256,1408]{1,2,0:T(8,128)(2,1)}, u32[]{:S(2)}, u32[]{:S(2)}) async-start(bf16[8,256,1408]{1,2,0:T(8,128)(2,1)} %bitcast.190), calls=%async_computation | async-start | bytes 11534336 | tf_op jit(solution)/shard_map/all_to_all | solution.py:289
  184.0 1.2 copy.124
  185.3 3.1 copy.119
  189.2 27.2 %project.1 = (bf16[4096,2048]{1,0:T(8,128)(2,1)}, bf16[4096,256]{1,0:T(8,128)(2,1)}, bf16[4096,256]{1,0:T(8,128)(2,1)}, bf16[4096,256]{1,0:T(8,128)(2,1)}, f32[16,4096]{1,0:T(8,128)}, /*index=5*/f32[4096,1]{1,0:T(8,128)}) custom-call(bf16[4,2,528,2048]{3,2,1,0:T(8,128)(2,1)} %get-tuple-element.55.tokens_ref, bf16[16,2048]{1,0:T(8,128)(2,1)} %pad.24.small_ref, ...), custom_call_target="tpu_custom_call" | custom-call | tf_op jit(solution)/shard_map/project/pallas_call | solution.py:79
  222.6 40.7 %attention_forward.1 = (bf16[2560,256]{1,0:T(8,128)(2,1)}, bf16[2560,256]{1,0:T(8,128)(2,1)}, f32[2560,1]{1,0:T(8,128)}, f32[2,2560,1]{2,1,0:T(8,128)}) custom-call(s32[8]{0:T(128)} %and_select_fusion.4.begin_ref, bf16[4096,256]{1,0:T(8,128)(2,1)} %get-tuple-element.58.q_ref, bf16[4096,256]{1,0:T(8,128)(2,1)} %get-tuple-element.59.k_ref, ...), custom_call_target="tpu_custom_call" | custom-call | tf_op jit(solution)/shard_map/attention_forward/pallas_call | solution.py:243
  263.3 1.9 fusion.86
  265.2 6.9 convolution_convert_fusion.1
  272.0 94.7 %scatter_rows.2 = (bf16[4,320,512]{2,1,0:T(8,128)(2,1)}, bf16[8,128,704]{2,1,0:T(8,128)(2,1)}) custom-call(bf16[4,2,320,2048]{3,2,1,0:T(8,128)(2,1)} %bitcast.180, bf16[8,128,704]{2,1,0:T(8,128)(2,1)} %get-tuple-element.154.refs_1_), custom_call_target="tpu_custom_call" | custom-call | tf_op jit(solution)/shard_map/scatter_rows/pallas_call | solution.py:655
  366.8 4.9 multiply_reduce_fusion.3
  372.2 5.2 all_gather.10
  377.8 5.4 all_gather.11
  383.2 1.7 reduce.3
  384.9 1.9 fusion.12.refs_0_
  386.8 78.2 %gather_rows.4 = (bf16[4,2,320,2048]{3,2,1,0:T(8,128)(2,1)}, bf16[8,128,704]{2,1,0:T(8,128)(2,1)}) custom-call(bf16[4,320,512]{2,1,0:T(8,128)(2,1)} %fusion.12.refs_0_, bf16[8,128,704]{2,1,0:T(8,128)(2,1)} %get-tuple-element.153.refs_1_), custom_call_target="tpu_custom_call" | custom-call | tf_op jit(solution)/shard_map/gather_rows/pallas_call | solution.py:514
  466.2 4.0 pad_maximum_fusion.3
  471.7 2.0 fusion.13.grad_ref
  474.4 8.2 copy.121
  482.7 70.7 %expert_forward.1 = (f32[2560,704]{1,0:T(8,128)}, f32[2560,704]{1,0:T(8,128)}, bf16[8,320,2048]{2,1,0:T(8,128)(2,1)}, f32[2560,1]{1,0:T(8,128)}, bf16[4,2,320,2048]{3,2,1,0:T(8,128)(2,1)}) custom-call(bf16[8,320,2048]{2,1,0:T(8,128)(2,1)} %bitcast.184, bf16[2048,1408]{1,0:T(8,128)(2,1)} %bitcast.181, bf16[2048,704]{1,0:T(8,128)(2,1)} %bitcast.188, ...), custom_call_target="tpu_custom_call" | custom-call | tf_op jit(solution)/shard_map/expert_forward/pallas_call | solution.py:723
  553.4 67.3 %expert_backward.1 = (bf16[8,320,2048]{2,1,0:T(8,128)(2,1)}, bf16[2560,1408]{1,0:T(8,128)(2,1)}, bf16[2560,704]{1,0:T(8,128)(2,1)}, bf16[4,320,512]{2,1,0:T(8,128)(2,1)}) custom-call(f32[2560,704]{1,0:T(8,128)} %get-tuple-element.67.gate_ref, f32[2560,704]{1,0:T(8,128)} %get-tuple-element.68.up_ref, bf16[8,320,2048]{2,1,0:T(8,128)(2,1)} %bitcast.186, ...), custom_call_target="tpu_custom_call" | custom-call | tf_op jit(solution)/shard_map/expert_backward/pallas_call | solution.py:786
  620.7 63.4 %expert_gradient.1 = (bf16[2048,1408]{1,0:T(8,128)(2,1)}, bf16[8,128,704]{2,1,0:T(8,128)(2,1)}, bf16[8,128,704]{2,1,0:T(8,128)(2,1)}, bf16[4,320,512]{2,1,0:T(8,128)(2,1)}) custom-call(bf16[2560,2048]{1,0:T(8,128)(2,1)} %bitcast.185, bf16[2560,2048]{1,0:T(8,128)(2,1)} %bitcast.187, bf16[2560,1408]{1,0:T(8,128)(2,1)} %get-tuple-element.73.grad_gate_up_ref, ...), custom_call_target="tpu_custom_call" | custom-call | tf_op jit(solution)/shard_map/expert_gradient/pallas_call | solution.py:840
  684.1 3.4 multiply_reduce_fusion.5
  687.5 2.6 multiply_reduce_fusion.1
  690.1 5.3 all_gather.12
  695.5 2.6 copy.123
  698.1 3.5 multiply_reduce_fusion.4
  701.9 1.9 fusion.11.refs_0_
  703.8 72.7 %gather_rows.5 = (bf16[4,2,320,2048]{3,2,1,0:T(8,128)(2,1)}, bf16[8,128,704]{2,1,0:T(8,128)(2,1)}) custom-call(bf16[4,320,512]{2,1,0:T(8,128)(2,1)} %fusion.11.refs_0_, bf16[8,128,704]{2,1,0:T(8,128)(2,1)} %get-tuple-element.81.refs_1_), custom_call_target="tpu_custom_call" | custom-call | tf_op jit(solution)/shard_map/gather_rows/pallas_call | solution.py:514
  776.5 8.2 copy.125
  784.8 4.9 all-to-all-start.1
  789.7 8.2 fusion.3.grad_ref
  797.9 66.9 %attention_backward.1 = (bf16[4096,256]{1,0:T(8,128)(2,1)}, bf16[4096,256]{1,0:T(8,128)(2,1)}, bf16[4096,256]{1,0:T(8,128)(2,1)}) custom-call(s32[8]{0:T(128)} %and_select_fusion.4.begin_ref, bf16[4096,256]{1,0:T(8,128)(2,1)} %get-tuple-element.58.q_ref, bf16[4096,256]{1,0:T(8,128)(2,1)} %get-tuple-element.59.k_ref, ...), custom_call_target="tpu_custom_call" | custom-call | tf_op jit(solution)/shard_map/attention_backward/pallas_call | solution.py:266
  868.5 8.9 convolution_convert_fusion.3
  877.4 17.1 %convolution_convert_fusion.2 = bf16[2048,768]{0,1:T(8,128)(2,1)S(1)} fusion(bf16[4096,2048]{1,0:T(8,128)(2,1)} %get-tuple-element.87, bf16[4096,768]{1,0:T(8,128)(2,1)S(1)} %constant_dynamic-update-slice_fusion), kind=kOutput, calls=%fused_computation.17 | convolution fusion | flops 12886474752 | bytes 26214400 | tf_op jit(solution)/shard_map/dot_general | solution.py:43
  894.5 2.7 pad_maximum_fusion.1
  898.2 18.8 %convolution_convert_fusion = bf16[4096,2048]{1,0:T(8,128)(2,1)} fusion(bf16[4096,768]{1,0:T(8,128)(2,1)} %copy-done.13, bf16[2048,1024]{1,0:T(8,128)(2,1)S(1)} %bitcast.201), kind=kOutput, calls=%fused_computation | convolution fusion | flops 12893290496 | bytes 26214400 | tf_op jit(solution)/shard_map/dot_general | solution.py:47
  917.4 90.5 %scatter_rows.3 = (bf16[4,512,512]{2,1,0:T(8,128)(2,1)}, bf16[8,128,704]{2,1,0:T(8,128)(2,1)}) custom-call(bf16[4,2,512,2048]{3,2,1,0:T(8,128)(2,1)} %bitcast.192, bf16[8,128,704]{2,1,0:T(8,128)(2,1)} %get-tuple-element.91.refs_1_), custom_call_target="tpu_custom_call" | custom-call | tf_op jit(solution)/shard_map/scatter_rows/pallas_call | solution.py:655
  1008.0 2.0 convert_reduce_fusion
  1010.3 5.3 all_gather.26
  1016.2 1.8 fusion.35
  1018.0 5.2 all_gather.27
  1023.3 6.4 copy.140
  1029.7 3.9 fusion.2
  1033.5 4.8 all-to-all-start.2
  1038.4 3.3 convert_bitcast_fusion.1
  1041.7 6.4 copy.135
  1048.0 8.3 convert_bitcast_fusion
  1056.3 9.6 copy.134
  1066.0 17.5 %copy.139 = f32[4,256,2,1408]{3,2,1,0:T(2,128)} copy(f32[4,256,2,1408]{1,3,2,0:T(8,128)} %bitcast.183) | data formatting | bytes 23068672
  1083.5 54.4 %all-to-all-done.2 = bf16[8,272,1024]{2,1,0:T(8,128)(2,1)} async-done(((bf16[8,272,1024]{2,1,0:T(8,128)(2,1)}), bf16[8,272,1024]{2,1,0:T(8,128)(2,1)}, u32[]{:S(2)}, u32[]{:S(2)}) %all-to-all-start.2) | async-done | bytes 4456480 | tf_op jit(solution)/shard_map/all_to_all | solution.py:289
  1141.0 4.1 slice_convert_fusion
  1145.1 5.9 reshape.436
  1151.0 4.2 reduce_sum.223
  1155.3 1.8 copy.136
  1157.1 1.7 fusion.85
  1159.6 1.6 copy.132
  1161.2 3.0 reshape.437
  1164.2 1.5 convert_element_type.241
  (169 shorter events, 28.1 us)
Async XLA Ops:
  23.9 5.7 copy-start.15
  23.9 5.7 copy-start.16
  23.9 5.7 copy-start.1
  169.5 12.4 %copy-start.14 = (s32[4096]{0:T(1024)S(1)}, s32[4096]{0:T(1024)}, u32[]{:S(2)}) copy-start(s32[4096]{0:T(1024)} %param.17) | copy-start | bytes 49156
  169.5 14.5 %copy-start.8 = (bf16[512,512]{1,0:T(8,128)(2,1)S(1)}, bf16[512,512]{1,0:T(8,128)(2,1)}, u32[]{:S(2)}) copy-start(bf16[512,512]{1,0:T(8,128)(2,1)} %param.29) | copy-start | bytes 1572868
  169.5 304.9 %all-to-all-start = ((bf16[8,256,1408]{1,2,0:T(8,128)(2,1)}), bf16[8,256,1408]{1,2,0:T(8,128)(2,1)}, u32[]{:S(2)}, u32[]{:S(2)}) async-start(bf16[8,256,1408]{1,2,0:T(8,128)(2,1)} %bitcast.190), calls=%async_computation | async-start | bytes 11534336 | tf_op jit(solution)/shard_map/all_to_all | solution.py:289
  263.3 1.9 copy-start.3
  366.7 5.2 copy-start.2
  466.2 5.5 copy-start.9
  684.1 3.4 copy-start.12
  684.1 3.4 copy-start.18
  784.8 132.7 %all-to-all-start.1 = ((bf16[8,256,1408]{1,2,0:T(8,128)(2,1)}), bf16[8,256,1408]{1,2,0:T(8,128)(2,1)}, u32[]{:S(2)}, u32[]{:S(2)}) async-start(bf16[8,256,1408]{1,2,0:T(8,128)(2,1)} %copy.125), calls=%async_computation.1 | async-start | bytes 11534336 | tf_op jit(solution)/shard_map/all_to_all | solution.py:289
  797.9 67.2 %copy-start = (f32[4,512,512]{1,2,0:T(8,128)S(1)}, f32[4,512,512]{1,2,0:T(8,128)}, u32[]{:S(2)}) copy-start(f32[4,512,512]{1,2,0:T(8,128)} %get-tuple-element.187) | copy-start | bytes 12582916
  864.7 1.6 copy-start.7
  865.0 2.0 copy-start.6
  866.3 1.7 copy-start.5
  867.0 1.4 copy-start.17
  868.2 9.2 copy-start.13
  894.5 3.7 copy-start.4
  1033.5 4.8 copy-start.10
  1033.5 4.8 copy-start.11
  1033.5 104.4 %all-to-all-start.2 = ((bf16[8,272,1024]{2,1,0:T(8,128)(2,1)}), bf16[8,272,1024]{2,1,0:T(8,128)(2,1)}, u32[]{:S(2)}, u32[]{:S(2)}) async-start(bf16[8,272,1024]{2,1,0:T(8,128)(2,1)} %fusion.2), calls=%async_computation.2 | async-start | bytes 8912896 | tf_op jit(solution)/shard_map/all_to_all | solution.py:289

commit v6 on v5

--- a/solution.py
+++ b/solution.py
@@ -6,6 +6,7 @@
 import numpy as np
 from jax import lax
 from jax.experimental import pallas as pl
+from jax.experimental.layout import Layout, with_layout_constraint
 from jax.experimental.pallas import tpu as pltpu
 from jax.sharding import Mesh, PartitionSpec as P
 
@@ -52,7 +53,7 @@
 
 
 def project_kernel(
-    tokens_ref, small_ref, weight_ref, cos_ref, sin_ref,
+    tokens_ref, small_ref, query_weight_ref, shared_weight_ref, cos_ref, sin_ref,
     hidden_ref, q_ref, k_ref, v_ref, logits_ref, inverse_ref, *, head_width
 ):
     x = tokens_ref[0, 0].astype(F32)
@@ -61,14 +62,15 @@
     hidden = (x * inverse * small_ref[:1, :].astype(F32)).astype(BF16)
     hidden_ref[...] = hidden
     logits_ref[...] = contract_last(small_ref[...], hidden)
-    made = dot(hidden, weight_ref[...])
+    queries = dot(hidden, query_weight_ref[...])
+    shared = dot(hidden, shared_weight_ref[...])
     span = q_ref.shape[1]
     cosine, sine = cos_ref[...], sin_ref[...]
     for head in range(span // head_width):
         at = slice(head * head_width, (head + 1) * head_width)
-        q_ref[:, at] = turned(made[:, at], cosine, sine).astype(BF16)
-        k_ref[:, at] = turned(made[:, span:][:, at], cosine, sine).astype(BF16)
-    v_ref[...] = made[:, 2 * span :].astype(BF16)
+        q_ref[:, at] = turned(queries[:, at], cosine, sine).astype(BF16)
+        k_ref[:, at] = turned(shared[:, at], cosine, sine).astype(BF16)
+    v_ref[...] = shared[:, span:].astype(BF16)
 
 
 def project(tokens, rows, small, weight, cosine, sine, span, head_width):
@@ -82,7 +84,8 @@
         in_specs=[
             pl.BlockSpec((1, 1, rows, width), lambda b: (b // HALVES, b % HALVES, 0, 0)),
             pl.BlockSpec(small.shape, whole),
-            pl.BlockSpec((width, 3 * span), whole),
+            pl.BlockSpec((width, span), lambda b: (0, 1)),
+            pl.BlockSpec((width, 2 * span), lambda b: (0, 1)),
             pl.BlockSpec((rows, head_width), block),
             pl.BlockSpec((rows, head_width), block),
         ],
@@ -104,7 +107,7 @@
         ],
         compiler_params=pltpu.CompilerParams(vmem_limit_bytes=VMEM_BYTES),
         name="project",
-    )(tokens, small, weight, cosine, sine)
+    )(tokens, small, weight, weight, cosine, sine)
 
 
 def attention_scores(q, k_ref, low_bound, high_bound, tile, tile_rows, scaling):
@@ -285,8 +288,56 @@
     )(begin, q, k, v, rank, table, out, lse, grad, cosine, sine)
 
 
+def pack_up_kernel(weight_ref, pieces_ref):
+    units = pieces_ref.shape[2] // 2
+    both = weight_ref[0].astype(F32)
+    gate, up = both[:, 0, :], both[:, 1, :]
+    for half in range(HALVES):
+        at = slice(half * units, (half + 1) * units)
+        pieces_ref[half] = jnp.concatenate([gate[:, at], up[:, at]], axis=1).astype(BF16)
+
+
+def pack_up(weight):
+    experts, own_rows, _, units = weight.shape
+    tile = own_rows // 2
+    return pl.pallas_call(
+        pack_up_kernel,
+        grid=(experts, 2),
+        in_specs=[pl.BlockSpec((1, tile, 2, units), lambda e, r: (e, r, 0, 0))],
+        out_specs=pl.BlockSpec((HALVES, tile, units), lambda e, r: (e, r, 0)),
+        out_shape=jax.ShapeDtypeStruct((experts * HALVES, own_rows, units), BF16),
+        compiler_params=pltpu.CompilerParams(vmem_limit_bytes=VMEM_BYTES),
+        name="pack_up",
+    )(weight)
+
+
+def pack_down_kernel(weight_ref, first_ref, last_ref):
+    turned_rows = weight_ref[0].astype(F32).T.astype(BF16)
+    middle = first_ref.shape[1]
+    first_ref[0] = turned_rows[:middle]
+    last_ref[0] = turned_rows[middle:]
+
+
+def pack_down(weight):
+    places, units, own_rows = weight.shape
+    half = (places, own_rows // 2, units)
+    return pl.pallas_call(
+        pack_down_kernel,
+        grid=(places,),
+        in_specs=[pl.BlockSpec((1, units, own_rows), lambda p: (p, 0, 0))],
+        out_specs=[pl.BlockSpec((1,) + half[1:], lambda p: (p, 0, 0))] * 2,
+        out_shape=[jax.ShapeDtypeStruct(half, BF16)] * 2,
+        compiler_params=pltpu.CompilerParams(vmem_limit_bytes=VMEM_BYTES),
+        name="pack_down",
+    )(weight)
+
+
+def row_major(array):
+    return with_layout_constraint(array, Layout(major_to_minor=tuple(range(array.ndim))))
+
+
 def exchanged(pieces):
-    return lax.all_to_all(pieces, PLACES, 0, 0, tiled=True)
+    return row_major(lax.all_to_all(row_major(pieces), PLACES, 0, 0, tiled=True))
 
 
 def over_groups(landed):
@@ -349,7 +400,10 @@
 
 
 class Ride:
-    def __init__(self, pieces_ref, landed_ref, send, recv, local):
+    def __init__(self, pieces_ref, landed_ref, send, recv, local, columns=None):
+        if columns is None:
+            columns = pl.ds(0, pieces_ref.shape[2])
+        rows = pl.ds(0, pieces_ref.shape[1])
         plane, half = lax.axis_index("z"), lax.axis_index("x")
         self.moves = Moves(send, recv)
         self.landings = {}
@@ -364,8 +418,9 @@
                 at_half = 1 - half if dx else half
                 peer = {"z": crossed(plane, dz), "x": at_half}
                 other = crossed(plane, dz) * HALVES + at_half
-                self.moves.add(index, pieces_ref.at[other], landed_ref.at[own], peer)
-                self.landings[index] = (landed_ref.at[other], peer)
+                source = pieces_ref.at[other, rows, columns]
+                self.moves.add(index, source, landed_ref.at[own, rows, columns], peer)
+                self.landings[index] = (landed_ref.at[other, rows, columns], peer)
                 if dz and dx:
                     self.peers.append(peer)
 
@@ -405,7 +460,7 @@
         ride.finish()
 
 
-def gather_steps(slots_ref, out_ref, send, recv, local, same, share=2, more=()):
+def gather_parts(slots_ref, out_ref, send, recv, local, same, share=2, more=(), chain=None):
     plane, half, column, planes, along_x, along_y, core = partners()
     cap, width = slots_ref.shape[-2:]
     middle = cap * share // 64 * 16
@@ -425,7 +480,7 @@
     for j in range(PLANES):
         source = sources[j]
         place = piece(source, half, column)
-        if j:
+        if j and chain is None:
             moves.add(j, slots_for(j), piece(plane, half, column), planes[j])
         here = place if j else slots_for(0)
         moves.add(4 + j, here, place, along_x)
@@ -443,13 +498,18 @@
 
     def begin():
         meet(planes[1:] + [along_x, along_y, core] + list(more))
-        for j in (1, 3, 2):
-            moves.start(j)
+        if chain is None:
+            for j in (1, 3, 2):
+                moves.start(j)
+        else:
+            chain.begin()
         keep.start()
 
     def spread(j):
-        if j:
+        if j and chain is None:
             moves.arrived(j, piece(sources[j], half, column), planes[j])
+        elif j:
+            chain.arrived(j)
         for index in (4, 8, 12):
             moves.start(index + j)
 
@@ -476,6 +536,11 @@
         keep.wait()
 
     order = (0, 1, 3, 2)
+    return begin, spread, forward, cross, finish, order
+
+
+def gather_steps(*refs, **settings):
+    begin, spread, forward, cross, finish, order = gather_parts(*refs, **settings)
 
     def step(number):
         if number < len(order):
@@ -486,6 +551,145 @@
             cross(order[number - 2])
 
     return [begin] + [functools.partial(step, number) for number in range(len(order) + 2)] + [finish]
+
+
+class Chain:
+    def __init__(self, view, source, send, recv):
+        plane = lax.axis_index("z")
+        self.inner = (plane == 1) | (plane == 2)
+        near, far = {"z": crossed(plane, 1)}, {"z": crossed(plane, 3)}
+        self.views = [view(crossed(plane, j)) for j in range(PLANES)]
+        self.send, self.recv = send, recv
+        self.near_own = (0, 1, source, self.views[0], near)
+        self.far_own = (1, 3, source, self.views[0], far)
+        self.on_arrival = {
+            1: (2, 2, self.views[1], self.views[1], far),
+            3: (3, 2, self.views[3], self.views[3], near),
+            2: (4, 3, self.views[2], self.views[2], near),
+        }
+
+    def copy(self, at_send, at_recv, source, target, peer):
+        return pltpu.make_async_remote_copy(
+            src_ref=source, dst_ref=target, send_sem=self.send.at[at_send],
+            recv_sem=self.recv.at[at_recv], device_id=peer, device_id_type=MESH,
+        )
+
+    def begin(self):
+        self.copy(*self.near_own).start()
+
+        @pl.when(self.inner)
+        def _():
+            self.copy(*self.far_own).start()
+
+    def arrived(self, j):
+        place = self.views[j]
+        self.copy(0, j, place, place, self.near_own[-1]).wait_recv()
+
+        @pl.when(self.inner)
+        def _():
+            self.copy(*self.on_arrival[j]).start()
+
+    def finish(self):
+        self.copy(*self.near_own).wait_send()
+
+        @pl.when(self.inner)
+        def _():
+            self.copy(*self.far_own).wait_send()
+            for made in self.on_arrival.values():
+                self.copy(*made).wait_send()
+
+
+CHAIN_SCRATCH = (pltpu.SemaphoreType.DMA((5,)), pltpu.SemaphoreType.DMA((4,)))
+
+
+def opening_kernel(
+    tokens_ref, pieces_ref, out_ref, landed_ref, send, recv, local, ride_send, ride_recv,
+    ride_local, hop_send, hop_recv, *chain_sems, share
+):
+    plane, half, column = lax.axis_index("z"), lax.axis_index("x"), lax.axis_index("grid")
+    width = tokens_ref.shape[1]
+    middle = pieces_ref.shape[2] // 2
+    left, right = pl.ds(0, middle), pl.ds(middle, middle)
+    rows = pl.ds(0, pieces_ref.shape[1])
+    along_x = {"x": 1 - half}
+
+    def tokens_of(source):
+        columns = pl.ds(pl.multiple_of(column * width, width), width)
+        return out_ref.at[source, half, pl.ds(0, tokens_ref.shape[0]), columns]
+
+    def shared_of(at_half):
+        return lambda source: landed_ref.at[source * HALVES + at_half, rows, right]
+
+    own = plane * HALVES + half
+    tokens = Chain(tokens_of, tokens_ref, *chain_sems[:2])
+    here = Chain(shared_of(half), pieces_ref.at[own, rows, right], *chain_sems[2:4])
+    there = Chain(shared_of(1 - half), shared_of(1 - half)(plane), *chain_sems[4:])
+    ride = Ride(pieces_ref, landed_ref, ride_send, ride_recv, ride_local, left)
+    hop = pltpu.make_async_remote_copy(
+        src_ref=pieces_ref.at[plane * HALVES + 1 - half, rows, right],
+        dst_ref=landed_ref.at[own, rows, right],
+        send_sem=hop_send, recv_sem=hop_recv, device_id=along_x, device_id_type=MESH,
+    )
+    landing = shared_of(1 - half)(plane)
+    hop_here = pltpu.make_async_remote_copy(
+        src_ref=landing, dst_ref=landing, send_sem=hop_send, recv_sem=hop_recv,
+        device_id=along_x, device_id_type=MESH,
+    )
+    begin, spread, forward, cross, finish, _ = gather_parts(
+        tokens_ref, out_ref, send, recv, local, True, share, ride.peers, tokens
+    )
+    begin()
+    ride.keep.start()
+    spread(0)
+    hop.start()
+    here.begin()
+    spread(1)
+    forward(0)
+    ride.moves.start(2)
+    spread(3)
+    forward(1)
+    cross(0)
+    hop_here.wait_recv()
+    there.begin()
+    here.arrived(1)
+    spread(2)
+    forward(3)
+    cross(1)
+    ride.moves.start(6)
+    ride.moves.start(4)
+    here.arrived(3)
+    there.arrived(1)
+    forward(2)
+    cross(3)
+    for index in (3, 7, 5, 1):
+        ride.moves.start(index)
+    here.arrived(2)
+    there.arrived(3)
+    cross(2)
+    there.arrived(2)
+    finish()
+    ride.finish()
+    hop.wait_send()
+    for chain in (tokens, here, there):
+        chain.finish()
+
+
+def opened(tokens, pieces, collective_id, share):
+    rows, width = tokens.shape
+    anywhere = pl.BlockSpec(memory_space=pl.ANY)
+    return pl.pallas_call(
+        functools.partial(opening_kernel, share=share),
+        out_shape=[
+            jax.ShapeDtypeStruct((PLANES, HALVES, rows, 4 * width), BF16),
+            jax.ShapeDtypeStruct(pieces.shape, BF16),
+        ],
+        in_specs=[anywhere] * 2,
+        out_specs=[anywhere] * 2,
+        scratch_shapes=list(GATHER_SCRATCH) + list(RIDE_SCRATCH)
+        + [pltpu.SemaphoreType.DMA, pltpu.SemaphoreType.DMA] + list(CHAIN_SCRATCH) * 3,
+        compiler_params=pltpu.CompilerParams(collective_id=collective_id, has_side_effects=True),
+        name="open_rows",
+    )(tokens, pieces)
 
 
 GATHER_SCRATCH = (
@@ -667,7 +871,7 @@
     return out if rides else out[0]
 
 
-def carry(before, after, last, compute):
+def carry(before, after, places, compute):
     number = pl.program_id(0)
 
     @pl.when(number == 0)
@@ -676,9 +880,13 @@
             step()
 
     compute()
-    for place, step in enumerate(after):
-        pl.when(number == place)(step)
-    pl.when(number == BLOCKS - 1)(last)
+    for at in sorted(set(places)):
+
+        @pl.when(number == at)
+        def _(at=at):
+            for place, step in zip(places, after):
+                if place == at:
+                    step()
 
 
 def expert_forward_kernel(
@@ -707,7 +915,7 @@
         own = jnp.sum(jnp.where(mine, weights, 0.0), axis=1, keepdims=True)
         share_ref[...] = own / jnp.where(total > 0.0, total, 1.0)
 
-    carry(steps[:2], steps[2:-1], steps[-1], compute)
+    carry(steps[:2], steps[2:], (1, 3, 5, 6, 7, 7), compute)
 
 
 def once(shape):
@@ -772,7 +980,7 @@
         grad_gate_up_ref[...] = grad_gate_up
         grad_rows_ref[0] = contract_last(grad_gate_up, up_weight_ref[...]).astype(BF16)
 
-    carry(steps[:1], steps[1:-1], steps[-1], compute)
+    carry(steps[:1], steps[1:], (0, 1, 3, 4, 6, 7, 7), compute)
 
 
 def expert_backward(
@@ -828,7 +1036,7 @@
         down_first_ref[0] = down_grad[:middle]
         down_last_ref[0] = down_grad[middle:]
 
-    carry(steps[:1], steps[1:-1], steps[-1], compute)
+    carry(steps[:1], steps[1:], (0, 2, 4, 5, 6, 7, 7), compute)
 
 
 def expert_gradient(rows, grad_rows, grad_gate_up, inner, partial, collective_id):
@@ -866,6 +1074,110 @@
     return lax.all_gather(values.reshape(-1, 128), "grid", axis=0).sum(axis=0).reshape(shape)
 
 
+def closing_kernel(
+    hidden_ref, q_ref, k_ref, v_ref, rows_ref, gated_ref, partial_ref, pieces_ref,
+    grad_ref, out_ref, landed_ref, *scratch
+):
+    ride = Ride(pieces_ref, landed_ref, *scratch[7:])
+    steps = scatter_steps(partial_ref, out_ref, *scratch[:7], 1, ride.peers)
+    span = q_ref.shape[1]
+
+    def compute():
+        hidden = hidden_ref[...]
+        for place, ref in enumerate((q_ref, k_ref, v_ref)):
+            at = slice(place * span, (place + 1) * span)
+            grad_ref[:, at] = contract_first(hidden, ref[...]).astype(BF16)
+        grad_ref[:, 3 * span :] = contract_first(rows_ref[...], gated_ref[...]).astype(BF16)
+
+    def with_ride(number):
+        steps[1 + number]()
+        ride.go_on(number)
+
+    after = [functools.partial(with_ride, number) for number in range(6)]
+    carry([steps[0], ride.begin], after + [steps[-1], ride.finish], (1, 4, 7, 7, 7, 7, 7, 7), compute)
+
+
+def closing(hidden, q, k, v, rows, gated, partial, pieces, collective_id):
+    count, width = hidden.shape
+    slot_count, span = gated.shape
+    tile, own_rows = width // BLOCKS, count // BLOCKS
+    anywhere = pl.BlockSpec(memory_space=pl.ANY)
+    return pl.pallas_call(
+        closing_kernel,
+        grid=(BLOCKS,),
+        in_specs=[
+            pl.BlockSpec((count, tile), lambda b: (0, b)),
+            once((count, span)),
+            once((count, span)),
+            once((count, span)),
+            pl.BlockSpec((slot_count, tile), lambda b: (0, b)),
+            once((slot_count, span)),
+            anywhere,
+            anywhere,
+        ],
+        out_specs=[pl.BlockSpec((tile, 4 * span), lambda b: (b, 0)), anywhere, anywhere],
+        out_shape=[
+            jax.ShapeDtypeStruct((width, 4 * span), BF16),
+            jax.ShapeDtypeStruct((PLANES, own_rows, width // 4), BF16),
+            jax.ShapeDtypeStruct(pieces.shape, BF16),
+        ],
+        scratch_shapes=scatter_scratch(own_rows, width // 4) + list(RIDE_SCRATCH),
+        compiler_params=pltpu.CompilerParams(
+            collective_id=collective_id, has_side_effects=True, vmem_limit_bytes=VMEM_BYTES
+        ),
+        name="closing",
+    )(hidden, q, k, v, rows, gated, partial.reshape(PLANES, HALVES, own_rows, width), pieces)
+
+
+def finish_kernel(query_ref, all_ref, query_grad_ref, kv_grad_ref, out_grad_ref):
+    span = query_ref.shape[2] // 4
+    head_width = query_grad_ref.shape[3]
+    pair = span // head_width
+    own_rows = query_grad_ref.shape[1]
+    for half in range(HALVES):
+        landed = query_ref[half, :own_rows, :].astype(F32)
+        for head in range(pair):
+            at = half * pair + head
+            query_grad_ref[0, :, at, :] = landed[:, head * head_width : (head + 1) * head_width]
+        out_grad_ref[half] = landed[:, 3 * span :].T
+
+    @pl.when(pl.program_id(0) == 0)
+    def _():
+        for half in range(HALVES):
+            total = sum(
+                all_ref[z * HALVES + half, :own_rows, span : 3 * span].astype(F32)
+                for z in range(PLANES)
+            )
+            for kind in range(2):
+                for head in range(pair):
+                    first = kind * span + head * head_width
+                    kv_grad_ref[:, half * pair + head, kind, :] = total[:, first : first + head_width]
+
+
+def finish(landed, own_rows, span, heads, head_width):
+    places, height, width = landed.shape
+    return pl.pallas_call(
+        finish_kernel,
+        grid=(PLANES,),
+        in_specs=[
+            pl.BlockSpec((HALVES, height, width), lambda e: (e, 0, 0)),
+            pl.BlockSpec((places, height, width), lambda e: (0, 0, 0)),
+        ],
+        out_specs=[
+            pl.BlockSpec((1, own_rows, heads, head_width), lambda e: (e, 0, 0, 0)),
+            pl.BlockSpec((own_rows, heads, 2, head_width), lambda e: (0, 0, 0, 0)),
+            pl.BlockSpec((HALVES, span, own_rows), lambda e: (e, 0, 0)),
+        ],
+        out_shape=[
+            jax.ShapeDtypeStruct((PLANES, own_rows, heads, head_width), F32),
+            jax.ShapeDtypeStruct((own_rows, heads, 2, head_width), F32),
+            jax.ShapeDtypeStruct((places, span, own_rows), F32),
+        ],
+        compiler_params=pltpu.CompilerParams(vmem_limit_bytes=VMEM_BYTES),
+        name="attention_weight_gradients",
+    )(landed, landed)
+
+
 def prefix_ranks(member):
     counted = member.astype(BF16)
     width = member.shape[-1]
@@ -904,19 +1216,20 @@
     )
 
 
-def norm_sums(grad_hidden, scaled, router, gates, grad_gates, width):
-    parts = jnp.concatenate(
-        [
-            grad_gates,
-            exact_last(router.astype(F32), scaled),
-            jnp.sum(grad_hidden * scaled, axis=1)[None],
-        ],
-        axis=0,
-    )
-    parts = grid_sum(parts)
+def norm_sums(grad_hidden, scaled, router, grad_gates, width, gates=None, hidden=None, member=None):
+    parts = [
+        grad_gates,
+        exact_last(router.astype(F32), scaled),
+        jnp.sum(grad_hidden * scaled, axis=1)[None],
+    ]
+    if gates is None:
+        parts.append(contract_last(router, hidden))
+    parts = grid_sum(jnp.concatenate(parts, axis=0))
+    if gates is None:
+        gates = route_gates(parts[2 * PLANES + 1 :], member)
     grad_logits = logits_grad(gates, parts[:PLANES])
     inner = parts[2 * PLANES] + jnp.sum(grad_logits * parts[PLANES : 2 * PLANES], axis=0)
-    return grad_logits, inner[:, None] / width
+    return grad_logits, inner[:, None] / width, gates
 
 
 def per_device(
@@ -951,11 +1264,9 @@
     kv_pieces = jnp.broadcast_to(kv_pieces, (PLANES,) + kv_pieces.shape[1:])
     qkv_pieces = jnp.concatenate([query_pieces, kv_pieces], axis=-1)
     out_pieces = attention_out.reshape(BLOCKS, span, own_rows).swapaxes(1, 2)
-    first_pieces = jnp.concatenate([qkv_pieces.reshape(BLOCKS, own_rows, 3 * span), out_pieces], axis=2)
-    up_pieces = expert_gate_up.reshape(PLANES, own_rows, 2, HALVES, hidden_units)
-    up_pieces = up_pieces.transpose(0, 3, 1, 2, 4).reshape(BLOCKS, own_rows, 2 * hidden_units)
-    down_pieces = expert_down.reshape(BLOCKS, hidden_units, own_rows).swapaxes(1, 2)
-    down_halves = down_pieces[:, : own_rows // 2], down_pieces[:, own_rows // 2 :]
+    first_pieces = jnp.concatenate([out_pieces, qkv_pieces.reshape(BLOCKS, own_rows, 3 * span)], axis=2)
+    up_pieces = pack_up(expert_gate_up)
+    down_halves = pack_down(expert_down.reshape(BLOCKS, hidden_units, own_rows))
 
     own_routes = jnp.concatenate([attention_routes, expert_routes], axis=1)
     small = jnp.concatenate(
@@ -968,11 +1279,11 @@
     small = jnp.concatenate([small, spare], axis=1).reshape(-1, features)
     under = jnp.concatenate([own_routes.T.astype(BF16), small], axis=0)
     under = jnp.pad(under, ((0, -under.shape[0] % 16), (0, 0)))
-    everything, first_weight = gathered(
-        jnp.concatenate([tokens, under], axis=0), 0, ride=first_pieces, share=3
+    everything, first_weight = opened(
+        jnp.concatenate([tokens, under], axis=0), first_pieces, 0, 3
     )
     first_weight = over_groups(first_weight).reshape(width_all, 4 * span)
-    qkv_weight, out_weight = first_weight[:, : 3 * span], first_weight[:, 3 * span :]
+    out_weight, qkv_weight = first_weight[:, :span], first_weight[:, span:]
     up_pieces, everything = lax.optimization_barrier((up_pieces, everything))
     up_weight = over_groups(exchanged(up_pieces)).reshape(width_all, 2 * hidden_units)
     under = everything[:, :, rows:, :features].reshape(BLOCKS, -1, features).swapaxes(0, 1)
@@ -1059,17 +1370,16 @@
         slots_second.reshape(-1, width_all), grad_slots_second.reshape(-1, width_all),
         grad_gate_up, inner, grad_rows, 6,
     )
-    own_logits = grid_sum(contract_last(router_second, hidden_second))
-    own_gates_second = route_gates(own_logits, own_member_second)
     branch_second = to_tokens(result_slots, own_pick_second)
+
+    grad_hidden_second = jnp.sum(to_tokens(grad_rows, own_pick_second), axis=0)
+    grad_logits_second, inner_mean, own_gates_second = norm_sums(
+        grad_hidden_second, normed_second * gain_second, router_second,
+        jnp.sum(branch_second * grad_out[None], axis=2), width_all,
+        hidden=hidden_second, member=own_member_second,
+    )
     layer_output = residual + jnp.sum(own_gates_second[:, :, None] * branch_second, axis=0)
     layer_output = layer_output.astype(BF16)
-
-    grad_hidden_second = jnp.sum(to_tokens(grad_rows, own_pick_second), axis=0)
-    grad_logits_second, inner_mean = norm_sums(
-        grad_hidden_second, normed_second * gain_second, router_second, own_gates_second,
-        jnp.sum(branch_second * grad_out[None], axis=2), width_all,
-    )
     grad_hidden_second = grad_hidden_second + exact_first(
         grad_logits_second, router_second.astype(F32)
     )
@@ -1090,22 +1400,18 @@
     grad_up = return_gradients(grad_up.reshape(groups, BLOCKS, own_rows, 2 * hidden_units))
     grad_attended = gate_slots_first * dot(grad_slots_first, out_weight)
     grad_attended = grad_attended.astype(BF16)
-    grad_out_weight = contract_first(
-        grad_slots_first, gated
-    )
-    grad_qkv = jnp.concatenate(
-        attention_backward(
-            *attention_args, attended, lse, grad_attended, cosine, sine, head_width
-        ),
-        axis=1,
-    )
+    grad_query, grad_keys, grad_values = attention_backward(
+        *attention_args, attended, lse, grad_attended, cosine, sine, head_width
+    )
+    grad_qkv = jnp.concatenate([grad_query, grad_keys, grad_values], axis=1)
     grad_hidden = contract_last(grad_qkv, qkv_weight).astype(BF16)
-    grad_first = jnp.concatenate(
-        [contract_first(hidden_first, grad_qkv).astype(BF16), grad_out_weight.astype(BF16)], axis=1
-    )
-    grad_hidden, grad_first, grad_up = lax.optimization_barrier((grad_hidden, grad_first, grad_up))
-    grad_hidden, grad_down_last = scattered(grad_hidden, rows, 3, ride=grad_down_last, share=1)
+    grad_first, grad_hidden, grad_down_last = closing(
+        hidden_first, grad_query, grad_keys, grad_values, grad_slots_first, gated,
+        grad_hidden, grad_down_last, 3,
+    )
     grad_hidden = jnp.sum(grad_hidden.astype(F32), axis=0)
+    grad_first, grad_up = lax.optimization_barrier((grad_first, grad_up))
+    grad_first = return_gradients(grad_first.reshape(groups, BLOCKS, own_rows, 4 * span))
     expert_gate_up_grad = grad_up.reshape(PLANES, HALVES, own_rows, 2, hidden_units)
     expert_gate_up_grad = expert_gate_up_grad.transpose(0, 2, 3, 1, 4).reshape(expert_gate_up.shape)
     expert_down_grad = jnp.concatenate([grad_down_first, grad_down_last], axis=1)
@@ -1113,9 +1419,9 @@
 
     own_normed = tokens.astype(F32) * own(inverse_first)
     own_hidden = (own_normed * gain_first).astype(BF16)
-    grad_logits_first, inner_mean = norm_sums(
-        grad_hidden, own_normed * gain_first, router_first, own_gates_first,
-        jnp.sum(branch_first * grad_residual[None], axis=2), width_all,
+    grad_logits_first, inner_mean, _ = norm_sums(
+        grad_hidden, own_normed * gain_first, router_first,
+        jnp.sum(branch_first * grad_residual[None], axis=2), width_all, gates=own_gates_first,
     )
     grad_hidden_first = grad_hidden + exact_first(grad_logits_first, router_first.astype(F32))
     grad_router_first = exact(grad_logits_first, own_hidden.astype(F32))
@@ -1127,21 +1433,16 @@
         [grad_gain_first[None], grad_gain_second[None], grad_router_first, grad_router_second],
         axis=0,
     )
-    small_grads = lax.all_gather(small_grads.astype(BF16), "grid", axis=1, tiled=True)
-    small_grads = small_grads.reshape(-1, groups, BLOCKS, own_rows).transpose(1, 2, 0, 3)
-    small_grads = jnp.pad(small_grads, ((0, 0), (0, 0), (0, 6), (0, 4 * span - own_rows)))
-    grad_first = grad_first.reshape(groups, BLOCKS, own_rows, 4 * span)
-    grad_first = return_gradients(jnp.concatenate([grad_first, small_grads], axis=2))
-    small_grads = jnp.sum(grad_first[:, own_rows:, :own_rows].astype(F32), axis=0)
-    grad_first = grad_first[:, :own_rows]
-    attention_out_grad = grad_first[..., 3 * span :].swapaxes(1, 2).reshape(attention_out.shape)
-    attention_query_grad = grad_first[..., :span].reshape(PLANES, HALVES, own_rows, span)
-    attention_query_grad = attention_query_grad.transpose(0, 2, 1, 3).reshape(attention_query.shape)
-    grad_kv_weight = grad_first[..., span : 3 * span].astype(F32).reshape(
-        PLANES, HALVES, own_rows, 2, head_pair, head_width
-    )
-    attention_kv_grad = grad_kv_weight.sum(axis=0).transpose(1, 0, 3, 2, 4)
-    attention_kv_grad = attention_kv_grad.reshape(attention_kv.shape)
+    small_grads, grad_first = lax.optimization_barrier((small_grads, grad_first))
+    small_grads = jnp.sum(lax.all_gather(small_grads, ("t",) + PLACES, axis=0), axis=0)
+    small_grads = lax.all_gather(small_grads, "grid", axis=1, tiled=True)
+    small_grads = lax.dynamic_slice_in_dim(
+        small_grads, (group * BLOCKS + place) * own_rows, own_rows, 1
+    )
+    attention_query_grad, attention_kv_grad, attention_out_grad = finish(
+        grad_first, own_rows, span, attention_kv.shape[1], head_width
+    )
+    attention_out_grad = attention_out_grad.reshape(attention_out.shape)
     return (
         layer_output,
         input_grad.astype(BF16),

time: 1170 us -> 1070 us (0.915)
  local copies, waits for them, and re-layouts: 120 us -> 59.4 us
  blocking collectives: 26.4 us -> 52.2 us
  waiting for transfers between devices: 54.8 us -> 30.9 us
  matrix products: 84.4 us -> 62.2 us
  other arithmetic: 48.6 us -> 30 us
    pallas_call x0 -> x5, Pallas kernels: none -> 253 us  [the longest x1 120 us: opened(): pl.pallas_call(functools.partial(opening_kernel, share=share), out_shape=...]
    pallas_call x3 -> x2, Pallas kernels: 287 us -> 153 us  [gathered(): pl.pallas_call(functools.partial(gather_kernel, same=slots.ndim == 2, sha...]
    pallas_call x2 -> x1, Pallas kernels: 185 us -> 93.2 us  [scattered(): pl.pallas_call(functools.partial(scatter_kernel, share=share, rides=len(r...]
    all_gather x1 -> x2, blocking collectives: 5.25 us -> 36.2 us  [the longest x1 30.7 us: per_device(): lax.all_gather(small_grads, ('t',) + PLACES, axis=0)]
    dot_general x2 -> x0, matrix products: 26 us -> none  [contract_first(): lax.dot_general(left, right, (((0,), (0,)), ((), ())), preferred_element_...]
    all_to_all x3, waiting for transfers between devices: 54.8 us -> 30.9 us  [exchanged(): lax.all_to_all(row_major(pieces), PLACES, 0, 0, tiled=True)]
    unnamed x66 -> x36, local copies, waits for them, and re-layouts: 41 us -> 19.2 us
    reshape x6 -> x0, local copies, waits for them, and re-layouts: 15.4 us -> none  [the longest x1 6.4 us: per_device(): grad_first = grad_first.reshape(groups, BLOCKS, own_rows, 4 * span)]
  transfers between devices with their start and end apart: 3 -> 3, of which waited for: 2 -> 1; matrix products, arithmetic and copies ran while one was open for 12% -> 12% of each run, Pallas kernels for 26% -> 40%
where the time goes in v6:
time: 1070 us
  Pallas kernels  815 us (76%)
  matrix products  62.2 us (6%)
  local copies, waits for them, and re-layouts  59.4 us (6%)
  blocking collectives  52.2 us (5%)
  waiting for transfers between devices  30.9 us (3%)
  other arithmetic  30 us (3%)
  starting transfers between devices  15.9 us (1%)
    pallas_call x2, Pallas kernels, gathered(): pl.pallas_call(functools.partial(gather_kernel, same=slots.ndim == 2, sha...  153 us
    pallas_call x1, Pallas kernels, opened(): pl.pallas_call(functools.partial(opening_kernel, share=share), out_shape=...  120 us
    pallas_call x1, Pallas kernels, closing(): pl.pallas_call(closing_kernel, grid=(BLOCKS,), in_specs=[pl.BlockSpec((co...  109 us
    pallas_call x1, Pallas kernels, scattered(): pl.pallas_call(functools.partial(scatter_kernel, share=share, rides=len(r...  93.2 us
    pallas_call x1, Pallas kernels, attention_backward(): pl.pallas_call(functools.partial(attention_backward_kernel, scaling=1.0 /...  66.3 us
    pallas_call x1, Pallas kernels, expert_backward(): pl.pallas_call(expert_backward_kernel, grid=(BLOCKS,), in_specs=[pl.Block...  61.9 us
    pallas_call x1, Pallas kernels, expert_gradient(): pl.pallas_call(expert_gradient_kernel, grid=(BLOCKS,), in_specs=[columns,...  61.2 us
    pallas_call x1, Pallas kernels, expert_forward(): pl.pallas_call(expert_forward_kernel, grid=(BLOCKS,), in_specs=[pl.BlockS...  59 us
  transfers between devices with their start and end apart: 3, of which 1 were waited for; matrix products, arithmetic and copies ran while one was open for 12% of the time, Pallas kernels for 40%

profile of v6, /device:TPU:0, one launch (start us, length us, event | category | flops | bytes accessed | tf_op | source)
XLA Modules:
  0.0 1067.0 jit_solution(14581708647793617406)
XLA Ops:
  0.7 0.7 broadcast_in_dim.79
  2.1 0.7 convert.15
  2.7 0.7 convert.16
  3.4 1.1 copy.65
  5.0 0.7 reshape.379
  5.9 1.5 copy.63
  7.4 9.3 pack_up.1
  16.7 0.8 fusion.43.tokens_ref
  18.0 2.6 pad_maximum_fusion.pieces_ref
  20.5 120.0 %open_rows.1 = (bf16[4,2,528,2048]{3,2,1,0:T(8,128)(2,1)}, bf16[8,256,1024]{2,1,0:T(8,128)(2,1)}) custom-call(bf16[528,512]{1,0:T(8,128)(2,1)} %fusion.43.tokens_ref, bf16[8,256,1024]{2,1,0:T(8,128)(2,1)} %pad_maximum_fusion.pieces_ref), custom_call_target="tpu_custom_call" | custom-call | tf_op jit(solution)/shard_map/open_rows/pallas_call | solution.py:680
  140.6 5.0 all-to-all-start
  146.1 0.9 slice.137
  148.0 6.6 pack_down.1
  156.8 27.2 %project.1 = (bf16[4096,2048]{1,0:T(8,128)(2,1)}, bf16[4096,256]{1,0:T(8,128)(2,1)}, bf16[4096,256]{1,0:T(8,128)(2,1)}, bf16[4096,256]{1,0:T(8,128)(2,1)}, f32[16,4096]{1,0:T(8,128)}, /*index=5*/f32[4096,1]{1,0:T(8,128)}) custom-call(bf16[4,2,528,2048]{3,2,1,0:T(8,128)(2,1)} %get-tuple-element.62.tokens_ref, bf16[16,2048]{1,0:T(8,128)(2,1)} %pad.20.small_ref, ...), custom_call_target="tpu_custom_call" | custom-call | tf_op jit(solution)/shard_map/project/pallas_call | solution.py:81
  184.0 1.0 fusion.56
  185.0 1.0 fusion.70
  186.1 1.0 broadcast_divide_fusion
  188.8 40.7 %attention_forward.1 = (bf16[2560,256]{1,0:T(8,128)(2,1)}, bf16[2560,256]{1,0:T(8,128)(2,1)}, f32[2560,1]{1,0:T(8,128)}, f32[2,2560,1]{2,1,0:T(8,128)}) custom-call(s32[8]{0:T(128)} %and_select_fusion.4.begin_ref, bf16[4096,256]{1,0:T(8,128)(2,1)} %get-tuple-element.65.q_ref, bf16[4096,256]{1,0:T(8,128)(2,1)} %get-tuple-element.66.k_ref, ...), custom_call_target="tpu_custom_call" | custom-call | tf_op jit(solution)/shard_map/attention_forward/pallas_call | solution.py:246
  229.4 8.6 convolution_convert_fusion.1
  238.1 93.2 %scatter_rows.1 = (bf16[4,320,512]{2,1,0:T(8,128)(2,1)}, bf16[8,128,704]{2,1,0:T(8,128)(2,1)}) custom-call(bf16[4,2,320,2048]{3,2,1,0:T(8,128)(2,1)} %bitcast.154, bf16[8,128,704]{2,1,0:T(8,128)(2,1)} %get-tuple-element.69.refs_1_), custom_call_target="tpu_custom_call" | custom-call | tf_op jit(solution)/shard_map/scatter_rows/pallas_call | solution.py:859
  331.3 4.8 multiply_reduce_fusion.3
  336.1 1.3 copy.71
  337.4 1.4 multiply_reduce_fusion.6
  338.9 5.4 all_gather.12
  344.4 2.0 fusion.14.refs_0_
  346.4 79.9 %gather_rows.2 = (bf16[4,2,320,2048]{3,2,1,0:T(8,128)(2,1)}, bf16[8,128,704]{2,1,0:T(8,128)(2,1)}) custom-call(bf16[4,320,512]{2,1,0:T(8,128)(2,1)} %fusion.14.refs_0_, bf16[8,128,704]{2,1,0:T(8,128)(2,1)} %get-tuple-element.71.refs_1_), custom_call_target="tpu_custom_call" | custom-call | tf_op jit(solution)/shard_map/gather_rows/pallas_call | solution.py:718
  426.3 3.9 pad_maximum_fusion.2
  430.4 0.7 fusion.40
  431.2 2.0 fusion.15.grad_ref
  433.2 0.7 pad_convert_fusion.member_ref
  433.9 59.0 %expert_forward.1 = (f32[2560,704]{1,0:T(8,128)}, f32[2560,704]{1,0:T(8,128)}, bf16[8,320,2048]{2,1,0:T(8,128)(2,1)}, f32[2560,1]{1,0:T(8,128)}, bf16[4,2,320,2048]{3,2,1,0:T(8,128)(2,1)}) custom-call(bf16[8,320,2048]{2,1,0:T(8,128)(2,1)} %bitcast.157, bf16[2048,1408]{1,0:T(8,128)(2,1)} %bitcast.29.up_weight_ref, bf16[2048,704]{1,0:T(8,128)(2,1)} %bitcast.161, ...), custom_call_target="tpu_custom_call" | custom-call | tf_op jit(solution)/shard_map/expert_forward/pallas_call | solution.py:931
  492.9 61.9 %expert_backward.1 = (bf16[8,320,2048]{2,1,0:T(8,128)(2,1)}, bf16[2560,1408]{1,0:T(8,128)(2,1)}, bf16[2560,704]{1,0:T(8,128)(2,1)}, bf16[4,320,512]{2,1,0:T(8,128)(2,1)}) custom-call(f32[2560,704]{1,0:T(8,128)} %get-tuple-element.76.gate_ref, f32[2560,704]{1,0:T(8,128)} %get-tuple-element.77.up_ref, bf16[8,320,2048]{2,1,0:T(8,128)(2,1)} %bitcast.159, ...), custom_call_target="tpu_custom_call" | custom-call | tf_op jit(solution)/shard_map/expert_backward/pallas_call | solution.py:994
  554.8 61.2 %expert_gradient.1 = (bf16[2048,1408]{1,0:T(8,128)(2,1)}, bf16[8,128,704]{2,1,0:T(8,128)(2,1)}, bf16[8,128,704]{2,1,0:T(8,128)(2,1)}, bf16[4,320,512]{2,1,0:T(8,128)(2,1)}) custom-call(bf16[2560,2048]{1,0:T(8,128)(2,1)} %bitcast.158, bf16[2560,2048]{1,0:T(8,128)(2,1)} %bitcast.160, bf16[2560,1408]{1,0:T(8,128)(2,1)} %get-tuple-element.82.grad_gate_up_ref, ...), custom_call_target="tpu_custom_call" | custom-call | tf_op jit(solution)/shard_map/expert_gradient/pallas_call | solution.py:1048
  616.0 3.3 multiply_reduce_fusion.5
  619.3 3.4 multiply_reduce_fusion.2
  622.8 5.4 all_gather.13
  628.3 2.9 multiply_reduce_fusion.1
  631.2 1.3 copy.74
  632.5 3.5 multiply_reduce_fusion.4
  636.0 1.9 fusion.13.refs_0_
  637.9 72.7 %gather_rows.3 = (bf16[4,2,320,2048]{3,2,1,0:T(8,128)(2,1)}, bf16[8,128,704]{2,1,0:T(8,128)(2,1)}) custom-call(bf16[4,320,512]{2,1,0:T(8,128)(2,1)} %fusion.13.refs_0_, bf16[8,128,704]{2,1,0:T(8,128)(2,1)} %get-tuple-element.91.refs_1_), custom_call_target="tpu_custom_call" | custom-call | tf_op jit(solution)/shard_map/gather_rows/pallas_call | solution.py:718
  710.6 4.9 all-to-all-start.1
  715.5 1.7 reduce.4
  717.2 8.2 fusion.5.grad_ref
  725.4 66.3 %attention_backward.1 = (bf16[4096,256]{1,0:T(8,128)(2,1)}, bf16[4096,256]{1,0:T(8,128)(2,1)}, bf16[4096,256]{1,0:T(8,128)(2,1)}) custom-call(s32[8]{0:T(128)} %and_select_fusion.4.begin_ref, bf16[4096,256]{1,0:T(8,128)(2,1)} %get-tuple-element.65.q_ref, bf16[4096,256]{1,0:T(8,128)(2,1)} %get-tuple-element.66.k_ref, ...), custom_call_target="tpu_custom_call" | custom-call | tf_op jit(solution)/shard_map/attention_backward/pallas_call | solution.py:269
  791.8 20.2 %convolution_convert_fusion = bf16[4096,2048]{1,0:T(8,128)(2,1)} fusion(bf16[4096,256]{1,0:T(8,128)(2,1)} %get-tuple-element.96.v_ref, bf16[4096,256]{1,0:T(8,128)(2,1)} %get-tuple-element.95.k_ref, bf16[4096,256]{1,0:T(8,128)(2,1)} %get-tuple-element.94.q_ref, bf16[2048,1024]{1,0:T(8,128)(2,1)} %bitcast.167), kind=kOutput, calls=%fused_computation | convolution fusion | flops 12912164864 | bytes 26214400 | tf_op jit(solution)/shard_map/dot_general | solution.py:48
  811.9 108.7 %closing.1 = (bf16[2048,1024]{1,0:T(8,128)(2,1)}, bf16[4,512,512]{2,1,0:T(8,128)(2,1)}, bf16[8,128,704]{2,1,0:T(8,128)(2,1)}) custom-call(bf16[4096,2048]{1,0:T(8,128)(2,1)} %get-tuple-element.87.hidden_ref, bf16[4096,256]{1,0:T(8,128)(2,1)} %get-tuple-element.94.q_ref, bf16[4096,256]{1,0:T(8,128)(2,1)} %get-tuple-element.95.k_ref, ...), custom_call_target="tpu_custom_call" | custom-call | tf_op jit(solution)/shard_map/closing/pallas_call | solution.py:1105
  920.7 6.0 all-to-all-start.2
  926.7 1.1 dynamic-slice_reduce_fusion
  927.8 0.7 fusion.22
  928.6 1.3 copy.75
  929.9 2.2 convert_reduce_fusion
  932.7 1.9 multiply_reduce_fusion
  934.6 5.3 all_gather.28
  940.0 5.2 convert_bitcast_fusion
  945.1 6.4 copy.78
  952.3 1.8 fusion.37
  954.1 9.0 copy.76
  963.1 9.6 copy.77
  972.8 17.5 %copy.79 = f32[4,256,2,1408]{3,2,1,0:T(2,128)} copy(f32[4,256,2,1408]{1,3,2,0:T(8,128)} %bitcast.156) | data formatting | bytes 23068672
  990.3 30.9 %all-to-all-done.2.query_ref.all_ref = bf16[8,256,1024]{2,1,0:T(8,128)(2,1)} async-done(((bf16[8,256,1024]{2,1,0:T(8,128)(2,1)}), bf16[8,256,1024]{2,1,0:T(8,128)(2,1)}, u32[]{:S(2)}, u32[]{:S(2)}) %all-to-all-start.2) | async-done | bytes 4194336 | tf_op jit(solution)/shard_map/all_to_all | solution.py:340
  1021.2 30.7 %all-gather.1 = f32[8,10,512]{2,1,0:T(8,128)S(1)} all-gather(f32[1,10,512]{2,1,0:T(8,128)S(1)} %bitcast.199), channel_id=2, replica_groups=mesh['t'=1,'z'=4,'x'=2,'grid'=4] {'t','z','x'}, dimensions={0}, use_global_device_ids=true | all-gather | bytes 184320 | tf_op jit(solution)/shard_map/all_gather | solution.py:1437
  1051.9 5.4 all_gather.31
  1057.4 8.1 attention_weight_gradients.1
  (116 shorter events, 10.4 us)
Async XLA Ops:
  0.6 4.3 copy-start.5
  7.3 9.3 copy-start.7
  7.4 9.3 copy-start.8
  7.4 9.3 copy-start.1
  140.5 5.1 copy-start.6
  140.5 7.2 copy-start.2
  140.6 293.3 %all-to-all-start = ((bf16[8,256,1408]{2,1,0:T(8,128)(2,1)}), bf16[8,256,1408]{2,1,0:T(8,128)(2,1)}, u32[]{:S(2)}, u32[]{:S(2)}) async-start(bf16[8,256,1408]{2,1,0:T(8,128)(2,1)} %pack_up.1), calls=%async_computation | async-start | bytes 11534336 | tf_op jit(solution)/shard_map/all_to_all | solution.py:340
  426.3 4.9 copy-start.3
  616.0 3.3 copy-start.4
  710.6 210.0 %all-to-all-start.1 = ((bf16[8,256,1408]{2,1,0:T(8,128)(2,1)}), bf16[8,256,1408]{2,1,0:T(8,128)(2,1)}, u32[]{:S(2)}, u32[]{:S(2)}) async-start(bf16[8,256,1408]{2,1,0:T(8,128)(2,1)} %bitcast.174), calls=%async_computation.1 | async-start | bytes 11534336 | tf_op jit(solution)/shard_map/all_to_all | solution.py:340
  920.7 100.5 %all-to-all-start.2 = ((bf16[8,256,1024]{2,1,0:T(8,128)(2,1)}), bf16[8,256,1024]{2,1,0:T(8,128)(2,1)}, u32[]{:S(2)}, u32[]{:S(2)}) async-start(bf16[8,256,1024]{2,1,0:T(8,128)(2,1)} %bitcast.176), calls=%async_computation.2 | async-start | bytes 8388608 | tf_op jit(solution)/shard_map/all_to_all | solution.py:340
  929.9 2.8 copy-start

commit v7 on v6

--- a/solution.py
+++ b/solution.py
@@ -297,39 +297,11 @@
         pieces_ref[half] = jnp.concatenate([gate[:, at], up[:, at]], axis=1).astype(BF16)
 
 
-def pack_up(weight):
-    experts, own_rows, _, units = weight.shape
-    tile = own_rows // 2
-    return pl.pallas_call(
-        pack_up_kernel,
-        grid=(experts, 2),
-        in_specs=[pl.BlockSpec((1, tile, 2, units), lambda e, r: (e, r, 0, 0))],
-        out_specs=pl.BlockSpec((HALVES, tile, units), lambda e, r: (e, r, 0)),
-        out_shape=jax.ShapeDtypeStruct((experts * HALVES, own_rows, units), BF16),
-        compiler_params=pltpu.CompilerParams(vmem_limit_bytes=VMEM_BYTES),
-        name="pack_up",
-    )(weight)
-
-
 def pack_down_kernel(weight_ref, first_ref, last_ref):
     turned_rows = weight_ref[0].astype(F32).T.astype(BF16)
     middle = first_ref.shape[1]
     first_ref[0] = turned_rows[:middle]
     last_ref[0] = turned_rows[middle:]
-
-
-def pack_down(weight):
-    places, units, own_rows = weight.shape
-    half = (places, own_rows // 2, units)
-    return pl.pallas_call(
-        pack_down_kernel,
-        grid=(places,),
-        in_specs=[pl.BlockSpec((1, units, own_rows), lambda p: (p, 0, 0))],
-        out_specs=[pl.BlockSpec((1,) + half[1:], lambda p: (p, 0, 0))] * 2,
-        out_shape=[jax.ShapeDtypeStruct(half, BF16)] * 2,
-        compiler_params=pltpu.CompilerParams(vmem_limit_bytes=VMEM_BYTES),
-        name="pack_down",
-    )(weight)
 
 
 def row_major(array):
@@ -424,14 +396,14 @@
                 if dz and dx:
                     self.peers.append(peer)
 
-    def begin(self):
+    def begin(self, first=(4, 6, 2)):
         self.keep.start()
-        for index in (4, 6, 2):
+        for index in first:
             self.moves.start(index)
 
-    def go_on(self, number):
-        for index in ((5,), (7,), (3,), (1,))[number : number + 1]:
-            self.moves.start(index[0])
+    def go_on(self, number, plan=((5,), (7,), (3,), (1,))):
+        for index in plan[number] if number < len(plan) else ():
+            self.moves.start(index)
 
     def finish(self):
         for index, (landing, peer) in self.landings.items():
@@ -603,7 +575,8 @@
 
 
 def opening_kernel(
-    tokens_ref, pieces_ref, out_ref, landed_ref, send, recv, local, ride_send, ride_recv,
+    tokens_ref, pieces_ref, up_ref, down_ref, out_ref, landed_ref, up_pieces_ref, first_ref,
+    last_ref, send, recv, local, ride_send, ride_recv,
     ride_local, hop_send, hop_recv, *chain_sems, share
 ):
     plane, half, column = lax.axis_index("z"), lax.axis_index("x"), lax.axis_index("grid")
@@ -638,58 +611,96 @@
     begin, spread, forward, cross, finish, _ = gather_parts(
         tokens_ref, out_ref, send, recv, local, True, share, ride.peers, tokens
     )
-    begin()
-    ride.keep.start()
-    spread(0)
-    hop.start()
-    here.begin()
-    spread(1)
-    forward(0)
-    ride.moves.start(2)
-    spread(3)
-    forward(1)
-    cross(0)
-    hop_here.wait_recv()
-    there.begin()
-    here.arrived(1)
-    spread(2)
-    forward(3)
-    cross(1)
-    ride.moves.start(6)
-    ride.moves.start(4)
-    here.arrived(3)
-    there.arrived(1)
-    forward(2)
-    cross(3)
-    for index in (3, 7, 5, 1):
-        ride.moves.start(index)
-    here.arrived(2)
-    there.arrived(3)
-    cross(2)
-    there.arrived(2)
-    finish()
-    ride.finish()
-    hop.wait_send()
-    for chain in (tokens, here, there):
-        chain.finish()
-
-
-def opened(tokens, pieces, collective_id, share):
+
+    def first():
+        begin()
+        ride.keep.start()
+        spread(0)
+        hop.start()
+        here.begin()
+
+    def second():
+        spread(1)
+        forward(0)
+        ride.moves.start(2)
+
+    def third():
+        spread(3)
+        forward(1)
+        cross(0)
+        hop_here.wait_recv()
+        there.begin()
+        here.arrived(1)
+
+    def fourth():
+        spread(2)
+        forward(3)
+        cross(1)
+        ride.moves.start(6)
+        ride.moves.start(4)
+        here.arrived(3)
+        there.arrived(1)
+
+    def fifth():
+        forward(2)
+        cross(3)
+        for index in (3, 7, 5, 1):
+            ride.moves.start(index)
+        here.arrived(2)
+        there.arrived(3)
+        cross(2)
+        there.arrived(2)
+        finish()
+        ride.finish()
+        hop.wait_send()
+        for chain in (tokens, here, there):
+            chain.finish()
+
+    def compute():
+        pack_up_kernel(up_ref, up_pieces_ref)
+        pack_down_kernel(down_ref, first_ref, last_ref)
+
+    carry([first], [second, third, fourth, fifth], (3, 6, 7, 7), compute)
+
+
+def opened(tokens, pieces, up, down, collective_id, share):
     rows, width = tokens.shape
+    experts, own_rows, _, units = up.shape
+    places = experts * HALVES
+    tile = own_rows // 2
+    down_half = (places, own_rows // 2, units // HALVES)
     anywhere = pl.BlockSpec(memory_space=pl.ANY)
+    half = pl.BlockSpec((1,) + down_half[1:], lambda p: (p, 0, 0))
     return pl.pallas_call(
         functools.partial(opening_kernel, share=share),
+        grid=(places,),
+        in_specs=[
+            anywhere,
+            anywhere,
+            pl.BlockSpec((1, tile, 2, units), lambda p: (p // 2, p % 2, 0, 0)),
+            pl.BlockSpec((1,) + down.shape[1:], lambda p: (p, 0, 0)),
+        ],
+        out_specs=[
+            anywhere,
+            anywhere,
+            pl.BlockSpec((HALVES, tile, units), lambda p: (p // 2, p % 2, 0)),
+            half,
+            half,
+        ],
         out_shape=[
             jax.ShapeDtypeStruct((PLANES, HALVES, rows, 4 * width), BF16),
             jax.ShapeDtypeStruct(pieces.shape, BF16),
-        ],
-        in_specs=[anywhere] * 2,
-        out_specs=[anywhere] * 2,
+            jax.ShapeDtypeStruct((places, own_rows, units), BF16),
+            jax.ShapeDtypeStruct(down_half, BF16),
+            jax.ShapeDtypeStruct(down_half, BF16),
+        ],
         scratch_shapes=list(GATHER_SCRATCH) + list(RIDE_SCRATCH)
         + [pltpu.SemaphoreType.DMA, pltpu.SemaphoreType.DMA] + list(CHAIN_SCRATCH) * 3,
-        compiler_params=pltpu.CompilerParams(collective_id=collective_id, has_side_effects=True),
+        compiler_params=pltpu.CompilerParams(
+            collective_id=collective_id, has_side_effects=True, vmem_limit_bytes=VMEM_BYTES
+        ),
         name="open_rows",
-    )(tokens, pieces)
+    )(tokens, pieces, up, down)
 
 
 GATHER_SCRATCH = (
@@ -889,10 +900,21 @@
                     step()
 
 
+def join_halves(first_ref, last_ref, whole_ref):
+    count, height, _ = first_ref.shape
+
+    @pl.when(pl.program_id(0) == 0)
+    def _():
+        for place in range(count):
+            whole_ref[2 * place * height : (2 * place + 1) * height, :] = first_ref[place]
+            whole_ref[(2 * place + 1) * height : (2 * place + 2) * height, :] = last_ref[place]
+
+
 def expert_forward_kernel(
-    rows_ref, up_weight_ref, down_weight_ref, small_ref, rank_ref, member_ref, grad_ref,
-    gate_ref, up_ref, result_ref, share_ref, grad_rows_ref, *scratch
+    rows_ref, up_weight_ref, first_ref, last_ref, small_ref, rank_ref, member_ref, grad_ref,
+    gate_ref, up_ref, result_ref, share_ref, shared_ref, grad_rows_ref, down_weight_ref, *scratch
 ):
+    join_halves(first_ref, last_ref, down_weight_ref)
     steps = gather_steps(grad_ref, grad_rows_ref, *scratch, False)
     units = gate_ref.shape[1]
 
@@ -902,8 +924,8 @@
         gate, up = made[:, :units], made[:, units:]
         gate_ref[...] = gate
         up_ref[...] = up
-        inner = (gate * jax.nn.sigmoid(gate) * up).astype(BF16)
-        result_ref[0] = contract_last(inner, down_weight_ref[...]).astype(BF16)
+        inner = gate * jax.nn.sigmoid(gate) * up
+        result_ref[0] = contract_last(inner.astype(BF16), down_weight_ref[...]).astype(BF16)
         cap, count = rows.shape[0], rank_ref.shape[2]
         pick = (lax.broadcasted_iota(jnp.int32, (cap, count), 0) == rank_ref[0]).astype(BF16)
         member = contract_last(pick, member_ref[...]) > 0.5
@@ -913,7 +935,9 @@
         mine = lax.broadcasted_iota(jnp.int32, weights.shape, 1) == 6 + lax.axis_index("z")
         total = jnp.sum(weights, axis=1, keepdims=True)
         own = jnp.sum(jnp.where(mine, weights, 0.0), axis=1, keepdims=True)
-        share_ref[...] = own / jnp.where(total > 0.0, total, 1.0)
+        share = own / jnp.where(total > 0.0, total, 1.0)
+        share_ref[...] = share
+        shared_ref[...] = (share * inner).astype(BF16)
 
     carry(steps[:2], steps[2:], (1, 3, 5, 6, 7, 7), compute)
 
@@ -922,9 +946,9 @@
     return pl.BlockSpec(shape, lambda b: (0,) * len(shape), pipeline_mode=pl.Buffered(1))
 
 
-def expert_forward(rows, up_weight, down_weight, small, rank, member, grad_slots, collective_id):
+def expert_forward(rows, up_weight, down_halves, small, rank, member, grad_slots, collective_id):
     _, cap, width = rows.shape
-    units = down_weight.shape[1]
+    units = down_halves[0].shape[2]
     count = BLOCKS * cap
     anywhere = pl.BlockSpec(memory_space=pl.ANY)
     block = lambda b: (b, 0)
@@ -934,7 +958,8 @@
         in_specs=[
             pl.BlockSpec((1, cap, width), lambda b: (b, 0, 0)),
             once(up_weight.shape),
-            once(down_weight.shape),
+            once(down_halves[0].shape),
+            once(down_halves[1].shape),
             once(small.shape),
             pl.BlockSpec((1, 1, rank.shape[2]), lambda b: (b, 0, 0)),
             pl.BlockSpec((16, rank.shape[2]), lambda b: (0, b)),
@@ -945,6 +970,7 @@
             pl.BlockSpec((cap, units), block),
             pl.BlockSpec((1, cap, width), lambda b: (b, 0, 0)),
             pl.BlockSpec((cap, 1), block),
+            pl.BlockSpec((cap, units), block),
             anywhere,
         ],
         out_shape=[
@@ -952,45 +978,52 @@
             jax.ShapeDtypeStruct((count, units), F32),
             jax.ShapeDtypeStruct((BLOCKS, cap, width), BF16),
             jax.ShapeDtypeStruct((count, 1), F32),
+            jax.ShapeDtypeStruct((count, units), BF16),
             jax.ShapeDtypeStruct((PLANES, HALVES, cap, width), BF16),
         ],
-        scratch_shapes=list(GATHER_SCRATCH),
+        scratch_shapes=[pltpu.VMEM((width, units), BF16)] + list(GATHER_SCRATCH),
         compiler_params=pltpu.CompilerParams(
             collective_id=collective_id, has_side_effects=True, vmem_limit_bytes=VMEM_BYTES
         ),
         name="expert_forward",
-    )(rows, up_weight, down_weight, small, rank, member, grad_slots)
+    )(rows, up_weight, *down_halves, small, rank, member, grad_slots)
 
 
 def expert_backward_kernel(
-    gate_ref, up_ref, grad_ref, share_ref, up_weight_ref, down_weight_ref, result_ref,
-    grad_rows_ref, grad_gate_up_ref, inner_ref, out_ref, *scratch
+    gate_ref, up_ref, grad_ref, share_ref, up_weight_ref, first_ref, last_ref, columns_ref, inner_ref,
+    result_ref, grad_rows_ref, grad_gate_up_ref, down_first_ref, down_last_ref, out_ref,
+    down_weight_ref, *scratch
 ):
+    join_halves(first_ref, last_ref, down_weight_ref)
     steps = scatter_steps(result_ref, out_ref, *scratch)
+    middle = down_first_ref.shape[1]
 
     def compute():
-        share = share_ref[...]
-        grad_inner = dot(grad_ref[0], down_weight_ref[...]) * share
+        grad_inner = dot(grad_ref[0], down_weight_ref[...]) * share_ref[...]
         gate, up = gate_ref[...], up_ref[...]
         sigmoid = jax.nn.sigmoid(gate)
-        silu = gate * sigmoid
-        inner_ref[...] = (share * silu * up).astype(BF16)
         grad_gate = grad_inner * up * sigmoid * (1.0 + gate * (1.0 - sigmoid))
-        grad_gate_up = jnp.concatenate([grad_gate, grad_inner * silu], axis=1).astype(BF16)
+        grad_up = grad_inner * gate * sigmoid
+        grad_gate_up = jnp.concatenate([grad_gate, grad_up], axis=1).astype(BF16)
         grad_gate_up_ref[...] = grad_gate_up
         grad_rows_ref[0] = contract_last(grad_gate_up, up_weight_ref[...]).astype(BF16)
-
-    carry(steps[:1], steps[1:], (0, 1, 3, 4, 6, 7, 7), compute)
+        down_grad = contract_first(columns_ref[...], inner_ref[...]).astype(BF16)
+        down_first_ref[0] = down_grad[:middle]
+        down_last_ref[0] = down_grad[middle:]
+
+    carry(steps[:1], steps[1:], (0, 1, 2, 4, 5, 7, 7), compute)
 
 
 def expert_backward(
-    gate, up, grad_rows, share, up_weight, down_weight, result, collective_id
+    gate, up, grad_rows, share, up_weight, down_halves, inner, result, collective_id
 ):
     _, cap, width = grad_rows.shape
     count, units = gate.shape
+    tile = width // BLOCKS
     anywhere = pl.BlockSpec(memory_space=pl.ANY)
     block = lambda b: (b, 0)
     rows = pl.BlockSpec((1, cap, width), lambda b: (b, 0, 0))
+    half = pl.BlockSpec((1, tile // 2, units), lambda b: (b, 0, 0))
     return pl.pallas_call(
         expert_backward_kernel,
         grid=(BLOCKS,),
@@ -1000,86 +1033,80 @@
             rows,
             pl.BlockSpec((cap, 1), block),
             once(up_weight.shape),
-            once(down_weight.shape),
+            once(down_halves[0].shape),
+            once(down_halves[1].shape),
+            pl.BlockSpec((count, tile), lambda b: (0, b)),
+            once(inner.shape),
             anywhere,
         ],
-        out_specs=[
-            rows,
-            pl.BlockSpec((cap, 2 * units), block),
-            pl.BlockSpec((cap, units), block),
-            anywhere,
-        ],
+        out_specs=[rows, pl.BlockSpec((cap, 2 * units), block), half, half, anywhere],
         out_shape=[
             jax.ShapeDtypeStruct((BLOCKS, cap, width), BF16),
             jax.ShapeDtypeStruct((count, 2 * units), BF16),
-            jax.ShapeDtypeStruct((count, units), BF16),
+            jax.ShapeDtypeStruct((BLOCKS, tile // 2, units), BF16),
+            jax.ShapeDtypeStruct((BLOCKS, tile // 2, units), BF16),
             jax.ShapeDtypeStruct((PLANES, cap, width // 4), BF16),
         ],
-        scratch_shapes=scatter_scratch(cap, width // 4),
+        scratch_shapes=[pltpu.VMEM((width, units), BF16)] + scatter_scratch(cap, width // 4),
         compiler_params=pltpu.CompilerParams(
             collective_id=collective_id, has_side_effects=True, vmem_limit_bytes=VMEM_BYTES
         ),
         name="expert_backward",
-    )(gate, up, grad_rows, share, up_weight, down_weight, result.reshape(PLANES, HALVES, cap, width))
+    )(
+        gate, up, grad_rows, share, up_weight, *down_halves, grad_rows.reshape(count, width), inner,
+        result.reshape(PLANES, HALVES, cap, width),
+    )
 
 
 def expert_gradient_kernel(
-    rows_ref, grad_ref, grad_gate_up_ref, inner_ref, partial_ref,
-    up_grad_ref, down_first_ref, down_last_ref, out_ref, *scratch
+    rows_ref, grad_gate_up_ref, partial_ref, pieces_ref, up_grad_ref, out_ref, landed_ref, *scratch
 ):
-    steps = scatter_steps(partial_ref, out_ref, *scratch)
-    middle = down_first_ref.shape[1]
+    ride = Ride(pieces_ref, landed_ref, *scratch[7:])
+    steps = scatter_steps(partial_ref, out_ref, *scratch[:7], 1, ride.peers)
 
     def compute():
         up_grad_ref[...] = contract_first(rows_ref[...], grad_gate_up_ref[...]).astype(BF16)
-        down_grad = contract_first(grad_ref[...], inner_ref[...]).astype(BF16)
-        down_first_ref[0] = down_grad[:middle]
-        down_last_ref[0] = down_grad[middle:]
-
-    carry(steps[:1], steps[1:], (0, 2, 4, 5, 6, 7, 7), compute)
-
-
-def expert_gradient(rows, grad_rows, grad_gate_up, inner, partial, collective_id):
+
+    def with_ride(number):
+        steps[1 + number]()
+        ride.go_on(number)
+
+    after = [functools.partial(with_ride, number) for number in range(6)]
+    carry([steps[0], ride.begin], after + [steps[-1], ride.finish], (0, 2, 4, 6, 7, 7, 7, 7), compute)
+
+
+def expert_gradient(rows, grad_gate_up, partial, pieces, collective_id):
     count, width = rows.shape
-    units = inner.shape[1]
+    units = grad_gate_up.shape[1]
     cap, tile = count // BLOCKS, width // BLOCKS
     anywhere = pl.BlockSpec(memory_space=pl.ANY)
-    columns = pl.BlockSpec((count, tile), lambda b: (0, b))
     return pl.pallas_call(
         expert_gradient_kernel,
         grid=(BLOCKS,),
-        in_specs=[columns, columns, once((count, 2 * units)), once((count, units)), anywhere],
-        out_specs=[
-            pl.BlockSpec((tile, 2 * units), lambda b: (b, 0)),
-            pl.BlockSpec((1, tile // 2, units), lambda b: (b, 0, 0)),
-            pl.BlockSpec((1, tile // 2, units), lambda b: (b, 0, 0)),
+        in_specs=[
+            pl.BlockSpec((count, tile), lambda b: (0, b)),
+            once((count, units)),
             anywhere,
-        ],
+            anywhere,
+        ],
+        out_specs=[pl.BlockSpec((tile, units), lambda b: (b, 0)), anywhere, anywhere],
         out_shape=[
-            jax.ShapeDtypeStruct((width, 2 * units), BF16),
-            jax.ShapeDtypeStruct((BLOCKS, tile // 2, units), BF16),
-            jax.ShapeDtypeStruct((BLOCKS, tile // 2, units), BF16),
+            jax.ShapeDtypeStruct((width, units), BF16),
             jax.ShapeDtypeStruct((PLANES, cap, width // 4), BF16),
-        ],
-        scratch_shapes=scatter_scratch(cap, width // 4),
+            jax.ShapeDtypeStruct(pieces.shape, BF16),
+        ],
+        scratch_shapes=scatter_scratch(cap, width // 4) + list(RIDE_SCRATCH),
         compiler_params=pltpu.CompilerParams(
             collective_id=collective_id, has_side_effects=True, vmem_limit_bytes=VMEM_BYTES
         ),
         name="expert_gradient",
-    )(rows, grad_rows, grad_gate_up, inner, partial.reshape(PLANES, HALVES, cap, width))
-
-
-def grid_sum(values):
-    shape = values.shape
-    return lax.all_gather(values.reshape(-1, 128), "grid", axis=0).sum(axis=0).reshape(shape)
+    )(rows, grad_gate_up, partial.reshape(PLANES, HALVES, cap, width), pieces)
 
 
 def closing_kernel(
-    hidden_ref, q_ref, k_ref, v_ref, rows_ref, gated_ref, partial_ref, pieces_ref,
-    grad_ref, out_ref, landed_ref, *scratch
+    hidden_ref, q_ref, k_ref, v_ref, rows_ref, gated_ref, partial_ref, grad_ref, out_ref, *scratch
 ):
-    ride = Ride(pieces_ref, landed_ref, *scratch[7:])
-    steps = scatter_steps(partial_ref, out_ref, *scratch[:7], 1, ride.peers)
+    steps = scatter_steps(partial_ref, out_ref, *scratch)
     span = q_ref.shape[1]
 
     def compute():
@@ -1089,15 +1116,10 @@
             grad_ref[:, at] = contract_first(hidden, ref[...]).astype(BF16)
         grad_ref[:, 3 * span :] = contract_first(rows_ref[...], gated_ref[...]).astype(BF16)
 
-    def with_ride(number):
-        steps[1 + number]()
-        ride.go_on(number)
-
-    after = [functools.partial(with_ride, number) for number in range(6)]
-    carry([steps[0], ride.begin], after + [steps[-1], ride.finish], (1, 4, 7, 7, 7, 7, 7, 7), compute)
-
-
-def closing(hidden, q, k, v, rows, gated, partial, pieces, collective_id):
+    carry(steps[:1], steps[1:], (1, 4, 7, 7, 7, 7, 7), compute)
+
+
+def closing(hidden, q, k, v, rows, gated, partial, collective_id):
     count, width = hidden.shape
     slot_count, span = gated.shape
     tile, own_rows = width // BLOCKS, count // BLOCKS
@@ -1113,23 +1135,31 @@
             pl.BlockSpec((slot_count, tile), lambda b: (0, b)),
             once((slot_count, span)),
             anywhere,
-            anywhere,
-        ],
-        out_specs=[pl.BlockSpec((tile, 4 * span), lambda b: (b, 0)), anywhere, anywhere],
+        ],
+        out_specs=[pl.BlockSpec((tile, 4 * span), lambda b: (b, 0)), anywhere],
         out_shape=[
             jax.ShapeDtypeStruct((width, 4 * span), BF16),
             jax.ShapeDtypeStruct((PLANES, own_rows, width // 4), BF16),
-            jax.ShapeDtypeStruct(pieces.shape, BF16),
-        ],
-        scratch_shapes=scatter_scratch(own_rows, width // 4) + list(RIDE_SCRATCH),
+        ],
+        scratch_shapes=scatter_scratch(own_rows, width // 4),
         compiler_params=pltpu.CompilerParams(
             collective_id=collective_id, has_side_effects=True, vmem_limit_bytes=VMEM_BYTES
         ),
         name="closing",
-    )(hidden, q, k, v, rows, gated, partial.reshape(PLANES, HALVES, own_rows, width), pieces)
-
-
-def finish_kernel(query_ref, all_ref, query_grad_ref, kv_grad_ref, out_grad_ref):
+    )(hidden, q, k, v, rows, gated, partial.reshape(PLANES, HALVES, own_rows, width))
+
+
+def finish_kernel(
+    query_ref, all_ref, small_ref, query_grad_ref, kv_grad_ref, out_grad_ref, gains_ref,
+    router_first_ref, router_second_ref, landed_ref, *scratch
+):
+    ride = Ride(small_ref, landed_ref, *scratch)
+
+    @pl.when(pl.program_id(0) == 0)
+    def _():
+        meet([peer for _, _, peer in ride.moves.made.values()])
+        ride.begin(tuple(ride.moves.made))
+
     span = query_ref.shape[2] // 4
     head_width = query_grad_ref.shape[3]
     pair = span // head_width
@@ -1153,29 +1183,54 @@
                     first = kind * span + head * head_width
                     kv_grad_ref[:, half * pair + head, kind, :] = total[:, first : first + head_width]
 
-
-def finish(landed, own_rows, span, heads, head_width):
+    @pl.when(pl.program_id(0) == PLANES - 1)
+    def _():
+        ride.finish()
+        total = sum(landed_ref[place] for place in range(BLOCKS))
+        gains_ref[...] = total[:8]
+        spare = jnp.zeros((128 - total.shape[0], total.shape[1]), F32)
+        columns = jnp.concatenate([total, spare], axis=0).T
+        router_first_ref[...] = columns[:own_rows, 2 : 2 + PLANES]
+        router_second_ref[...] = columns[:own_rows, 2 + PLANES : 2 + 2 * PLANES]
+
+
+def finish(landed, small, own_rows, span, heads, head_width, collective_id):
     places, height, width = landed.shape
     return pl.pallas_call(
         finish_kernel,
         grid=(PLANES,),
         in_specs=[
             pl.BlockSpec((HALVES, height, width), lambda e: (e, 0, 0)),
-            pl.BlockSpec((places, height, width), lambda e: (0, 0, 0)),
+            once((places, height, width)),
+            once(small.shape),
         ],
         out_specs=[
             pl.BlockSpec((1, own_rows, heads, head_width), lambda e: (e, 0, 0, 0)),
             pl.BlockSpec((own_rows, heads, 2, head_width), lambda e: (0, 0, 0, 0)),
             pl.BlockSpec((HALVES, span, own_rows), lambda e: (e, 0, 0)),
+            pl.BlockSpec((8, small.shape[2]), lambda e: (0, 0)),
+            pl.BlockSpec((own_rows, PLANES), lambda e: (0, 0)),
+            pl.BlockSpec((own_rows, PLANES), lambda e: (0, 0)),
         ],
         out_shape=[
             jax.ShapeDtypeStruct((PLANES, own_rows, heads, head_width), F32),
             jax.ShapeDtypeStruct((own_rows, heads, 2, head_width), F32),
             jax.ShapeDtypeStruct((places, span, own_rows), F32),
-        ],
-        compiler_params=pltpu.CompilerParams(vmem_limit_bytes=VMEM_BYTES),
+            jax.ShapeDtypeStruct((8, small.shape[2]), F32),
+            jax.ShapeDtypeStruct((own_rows, PLANES), F32),
+            jax.ShapeDtypeStruct((own_rows, PLANES), F32),
+        ],
+        scratch_shapes=[pltpu.VMEM(small.shape, F32)] + list(RIDE_SCRATCH),
+        compiler_params=pltpu.CompilerParams(
+            collective_id=collective_id, has_side_effects=True, vmem_limit_bytes=VMEM_BYTES
+        ),
         name="attention_weight_gradients",
-    )(landed, landed)
+    )(landed, landed, small)
+
+
+def grid_sum(values):
+    shape = values.shape
+    return lax.all_gather(values.reshape(-1, 128), "grid", axis=0).sum(axis=0).reshape(shape)
 
 
 def prefix_ranks(member):
@@ -1265,9 +1320,6 @@
     qkv_pieces = jnp.concatenate([query_pieces, kv_pieces], axis=-1)
     out_pieces = attention_out.reshape(BLOCKS, span, own_rows).swapaxes(1, 2)
     first_pieces = jnp.concatenate([out_pieces, qkv_pieces.reshape(BLOCKS, own_rows, 3 * span)], axis=2)
-    up_pieces = pack_up(expert_gate_up)
-    down_halves = pack_down(expert_down.reshape(BLOCKS, hidden_units, own_rows))
-
     own_routes = jnp.concatenate([attention_routes, expert_routes], axis=1)
     small = jnp.concatenate(
         [attention_gain[:, None], feedforward_gain[:, None], attention_router, feedforward_router],
@@ -1279,12 +1331,12 @@
     small = jnp.concatenate([small, spare], axis=1).reshape(-1, features)
     under = jnp.concatenate([own_routes.T.astype(BF16), small], axis=0)
     under = jnp.pad(under, ((0, -under.shape[0] % 16), (0, 0)))
-    everything, first_weight = opened(
-        jnp.concatenate([tokens, under], axis=0), first_pieces, 0, 3
+    everything, first_weight, up_pieces, *down_halves = opened(
+        jnp.concatenate([tokens, under], axis=0), first_pieces, expert_gate_up,
+        expert_down.reshape(BLOCKS, hidden_units, own_rows), 0, 3,
     )
     first_weight = over_groups(first_weight).reshape(width_all, 4 * span)
     out_weight, qkv_weight = first_weight[:, :span], first_weight[:, span:]
-    up_pieces, everything = lax.optimization_barrier((up_pieces, everything))
     up_weight = over_groups(exchanged(up_pieces)).reshape(width_all, 2 * hidden_units)
     under = everything[:, :, rows:, :features].reshape(BLOCKS, -1, features).swapaxes(0, 1)
     small = under[4:, :, : groups * own_rows].reshape(-1, BLOCKS, groups, own_rows)
@@ -1336,8 +1388,11 @@
     )
     attention_args = (begin, queries, keys, values, rank_first, table)
     attended, gated, gate_slots_first, lse = attention_forward(*attention_args, head_width)
+    branch, grad_out_slots = lax.optimization_barrier(
+        (contract_last(attended, out_weight).astype(BF16), to_slots(output_grad, own_pick_second))
+    )
     branch_slots, down_first = scattered(
-        contract_last(attended, out_weight).astype(BF16), CAP, 2, ride=down_halves[0], share=1
+        branch, CAP, 2, ride=down_halves[0], share=1
     )
     branch_first = to_tokens(branch_slots, own_pick_first)
     residual = tokens.astype(F32) + jnp.sum(own_gates_first[:, :, None] * branch_first, axis=0)
@@ -1349,27 +1404,32 @@
     slots_second, down_last = gathered(
         to_slots(hidden_second, own_pick_second), 1, ride=down_halves[1], share=3
     )
-    down_weight = over_groups(jnp.concatenate([down_first, down_last], axis=1))
-    down_weight = down_weight.reshape(width_all, hidden_units)
+    down_weight = [
+        over_groups(half).reshape((groups * BLOCKS,) + half.shape[1:]) for half in (down_first, down_last)
+    ]
     slots_second = slots_second.reshape(BLOCKS, CAP, width_all)
-    gate_pre, up_pre, result, gate_slots_second, grad_slots_second = expert_forward(
+    gate_pre, up_pre, result, gate_slots_second, inner, grad_slots_second = expert_forward(
         slots_second,
         up_weight,
         down_weight,
         small,
         rank_second,
         jnp.pad(member_second.astype(BF16), ((6, 6), (0, 0))),
-        to_slots(output_grad, own_pick_second),
+        grad_out_slots,
         4,
     )
     grad_slots_second = grad_slots_second.reshape(BLOCKS, CAP, width_all)
-    grad_rows, grad_gate_up, inner, result_slots = expert_backward(
-        gate_pre, up_pre, grad_slots_second, gate_slots_second, up_weight, down_weight, result, 5
-    )
-    grad_up, grad_down_first, grad_down_last, grad_rows = expert_gradient(
-        slots_second.reshape(-1, width_all), grad_slots_second.reshape(-1, width_all),
-        grad_gate_up, inner, grad_rows, 6,
-    )
+    grad_rows, grad_gate_up, grad_down_first, grad_down_last, result_slots = expert_backward(
+        gate_pre, up_pre, grad_slots_second, gate_slots_second, up_weight, down_weight, inner, result, 5
+    )
+    if groups > 1:
+        grad_down = jnp.concatenate([grad_down_first, grad_down_last], axis=1)
+        grad_down = group_sums(grad_down.reshape(groups, BLOCKS, own_rows, hidden_units))
+        grad_down_first, grad_down_last = jnp.split(grad_down, 2, axis=1)
+    grad_up, grad_rows, grad_down_first = expert_gradient(
+        slots_second.reshape(-1, width_all), grad_gate_up, grad_rows, grad_down_first, 6
+    )
+    grad_rows, grad_down_last = lax.optimization_barrier((grad_rows, grad_down_last))
     branch_second = to_tokens(result_slots, own_pick_second)
 
     grad_hidden_second = jnp.sum(to_tokens(grad_rows, own_pick_second), axis=0)
@@ -1378,23 +1438,27 @@
         jnp.sum(branch_second * grad_out[None], axis=2), width_all,
         hidden=hidden_second, member=own_member_second,
     )
+    grad_hidden_second = grad_hidden_second + exact_first(
+        grad_logits_second, router_second.astype(F32)
+    )
+    grad_normed = grad_hidden_second * gain_second
+    grad_residual = grad_out + inverse_second * (grad_normed - normed_second * inner_mean)
+
+    grad_down_last = exchanged(grad_down_last)
+    grad_slots_first = gathered(to_slots(grad_residual.astype(BF16), own_pick_first), 8)
+    (
+        grad_slots_first, grad_down_last, residual, own_gates_second, branch_second, hidden_second,
+        grad_logits_second, grad_hidden_second, normed_second,
+    ) = lax.optimization_barrier(
+        (
+            grad_slots_first, grad_down_last, residual, own_gates_second, branch_second, hidden_second,
+            grad_logits_second, grad_hidden_second, normed_second,
+        )
+    )
     layer_output = residual + jnp.sum(own_gates_second[:, :, None] * branch_second, axis=0)
     layer_output = layer_output.astype(BF16)
-    grad_hidden_second = grad_hidden_second + exact_first(
-        grad_logits_second, router_second.astype(F32)
-    )
     grad_router_second = exact(grad_logits_second, hidden_second.astype(F32))
     grad_gain_second = jnp.sum(grad_hidden_second * normed_second, axis=0)
-    grad_normed = grad_hidden_second * gain_second
-    grad_residual = grad_out + inverse_second * (grad_normed - normed_second * inner_mean)
-
-    if groups > 1:
-        grad_down = jnp.concatenate([grad_down_first, grad_down_last], axis=1)
-        grad_down = group_sums(grad_down.reshape(groups, BLOCKS, own_rows, hidden_units))
-        grad_down_first, grad_down_last = jnp.split(grad_down, 2, axis=1)
-    grad_slots_first, grad_down_first = gathered(
-        to_slots(grad_residual.astype(BF16), own_pick_first), 1, ride=grad_down_first, share=3
-    )
     grad_slots_first = grad_slots_first.reshape(BLOCKS * CAP, -1)
     grad_up, grad_slots_first = lax.optimization_barrier((grad_up, grad_slots_first))
     grad_up = return_gradients(grad_up.reshape(groups, BLOCKS, own_rows, 2 * hidden_units))
@@ -1405,9 +1469,8 @@
     )
     grad_qkv = jnp.concatenate([grad_query, grad_keys, grad_values], axis=1)
     grad_hidden = contract_last(grad_qkv, qkv_weight).astype(BF16)
-    grad_first, grad_hidden, grad_down_last = closing(
-        hidden_first, grad_query, grad_keys, grad_values, grad_slots_first, gated,
-        grad_hidden, grad_down_last, 3,
+    grad_first, grad_hidden = closing(
+        hidden_first, grad_query, grad_keys, grad_values, grad_slots_first, gated, grad_hidden, 3
     )
     grad_hidden = jnp.sum(grad_hidden.astype(F32), axis=0)
     grad_first, grad_up = lax.optimization_barrier((grad_first, grad_up))
@@ -1433,26 +1496,27 @@
         [grad_gain_first[None], grad_gain_second[None], grad_router_first, grad_router_second],
         axis=0,
     )
-    small_grads, grad_first = lax.optimization_barrier((small_grads, grad_first))
-    small_grads = jnp.sum(lax.all_gather(small_grads, ("t",) + PLACES, axis=0), axis=0)
     small_grads = lax.all_gather(small_grads, "grid", axis=1, tiled=True)
-    small_grads = lax.dynamic_slice_in_dim(
-        small_grads, (group * BLOCKS + place) * own_rows, own_rows, 1
-    )
-    attention_query_grad, attention_kv_grad, attention_out_grad = finish(
-        grad_first, own_rows, span, attention_kv.shape[1], head_width
-    )
+    if groups > 1:
+        small_grads = lax.psum(small_grads, "t")
+    small_grads = small_grads.reshape(-1, groups, BLOCKS, own_rows)
+    small_grads = lax.dynamic_index_in_dim(small_grads, group, 1, keepdims=False).swapaxes(0, 1)
+    small_grads = jnp.pad(small_grads, ((0, 0), (0, 6), (0, -own_rows % 128)))
+    (
+        attention_query_grad, attention_kv_grad, attention_out_grad, gain_grads,
+        attention_router_grad, feedforward_router_grad,
+    ) = finish(grad_first, small_grads, own_rows, span, attention_kv.shape[1], head_width, 7)
     attention_out_grad = attention_out_grad.reshape(attention_out.shape)
     return (
         layer_output,
         input_grad.astype(BF16),
-        small_grads[0],
+        gain_grads[0, :own_rows],
         attention_kv_grad,
         attention_query_grad.astype(F32),
         attention_out_grad.astype(F32),
-        small_grads[2:6].T,
-        small_grads[1],
-        small_grads[6:10].T,
+        attention_router_grad,
+        gain_grads[1, :own_rows],
+        feedforward_router_grad,
         expert_gate_up_grad.astype(F32),
         expert_down_grad.astype(F32),
     )

time: 1070 us -> 1020 us (0.953)
  blocking collectives: 52.2 us -> 21.3 us
  waiting for transfers between devices: 30.9 us -> 11 us
  Pallas kernels: 815 us -> 798 us
  local copies, waits for them, and re-layouts: 59.4 us -> 74.9 us
    all_gather x1 -> x0, blocking collectives: 30.7 us -> none  [per_device(): lax.all_gather(small_grads, ('t',) + PLACES, axis=0)]
    pallas_call x1, Pallas kernels: 109 us -> 87.4 us  [closing(): pl.pallas_call(closing_kernel, grid=(BLOCKS,), in_specs=[pl.BlockSpec((co...]
    all_to_all x3 -> x4, waiting for transfers between devices: 30.9 us -> 11 us  [exchanged(): lax.all_to_all(row_major(pieces), PLACES, 0, 0, tiled=True)]
    unnamed x36 -> x60, local copies, waits for them, and re-layouts: 19.2 us -> 30.9 us
    pallas_call x4 -> x2, Pallas kernels: 197 us -> 192 us  [the longest x1 122 us: opened(): pl.pallas_call(functools.partial(opening_kernel, share=share), grid=(plac...]
  transfers between devices with their start and end apart: 3 -> 4, of which waited for: 1 -> 1; matrix products, arithmetic and copies ran while one was open for 12% -> 14% of each run, Pallas kernels for 40% -> 46%
where the time goes in v7:
time: 1020 us
  Pallas kernels  798 us (78%)
  local copies, waits for them, and re-layouts  74.9 us (7%)
  matrix products  62.8 us (6%)
  other arithmetic  28.8 us (3%)
  blocking collectives  21.3 us (2%)
  starting transfers between devices  19.2 us (2%)
  waiting for transfers between devices  11 us (1%)
    pallas_call x2, Pallas kernels, gathered(): pl.pallas_call(functools.partial(gather_kernel, same=slots.ndim == 2, sha...  145 us
    pallas_call x1, Pallas kernels, opened(): pl.pallas_call(functools.partial(opening_kernel, share=share), grid=(plac...  122 us
    pallas_call x1, Pallas kernels, scattered(): pl.pallas_call(functools.partial(scatter_kernel, share=share, rides=len(r...  95.1 us
    pallas_call x1, Pallas kernels, closing(): pl.pallas_call(closing_kernel, grid=(BLOCKS,), in_specs=[pl.BlockSpec((co...  87.4 us
    pallas_call x1, Pallas kernels, expert_gradient(): pl.pallas_call(expert_gradient_kernel, grid=(BLOCKS,), in_specs=[pl.Block...  70.2 us
    pallas_call x1, Pallas kernels, attention_backward(): pl.pallas_call(functools.partial(attention_backward_kernel, scaling=1.0 /...  68.5 us
    pallas_call x1, Pallas kernels, expert_backward(): pl.pallas_call(expert_backward_kernel, grid=(BLOCKS,), in_specs=[pl.Block...  67.5 us
    pallas_call x1, Pallas kernels, expert_forward(): pl.pallas_call(expert_forward_kernel, grid=(BLOCKS,), in_specs=[pl.BlockS...  60.6 us
  transfers between devices with their start and end apart: 4, of which 1 were waited for; matrix products, arithmetic and copies ran while one was open for 14% of the time, Pallas kernels for 46%

profile of v7, /device:TPU:0, one launch (start us, length us, event | category | flops | bytes accessed | tf_op | source)
XLA Modules:
  0.0 1017.5 jit_solution(16867008381364756913)
XLA Ops:
  3.4 1.1 copy.91
  5.9 1.5 copy.89
  8.7 2.6 pad_maximum_fusion.pieces_ref
  11.3 122.2 %open_rows.1 = (bf16[4,2,528,2048]{3,2,1,0:T(8,128)(2,1)}, bf16[8,256,1024]{2,1,0:T(8,128)(2,1)}, bf16[8,256,1408]{2,1,0:T(8,128)(2,1)}, bf16[8,128,704]{2,1,0:T(8,128)(2,1)}, bf16[8,128,704]{2,1,0:T(8,128)(2,1)}) custom-call(bf16[528,512]{1,0:T(8,128)(2,1)} %fusion.42.tokens_ref, bf16[8,256,1024]{2,1,0:T(8,128)(2,1)} %pad_maximum_fusion.pieces_ref, ...), custom_call_target="tpu_custom_call" | custom-call | tf_op jit(solution)/shard_map/open_rows/pallas_call | solution.py:674
  133.6 5.0 all-to-all-start
  139.4 1.1 slice.131
  141.4 1.1 convert_element_type.164
  144.7 27.2 %project.1 = (bf16[4096,2048]{1,0:T(8,128)(2,1)}, bf16[4096,256]{1,0:T(8,128)(2,1)}, bf16[4096,256]{1,0:T(8,128)(2,1)}, bf16[4096,256]{1,0:T(8,128)(2,1)}, f32[16,4096]{1,0:T(8,128)}, /*index=5*/f32[4096,1]{1,0:T(8,128)}) custom-call(bf16[4,2,528,2048]{3,2,1,0:T(8,128)(2,1)} %get-tuple-element.72.tokens_ref, bf16[16,2048]{1,0:T(8,128)(2,1)} %pad.24.small_ref, ...), custom_call_target="tpu_custom_call" | custom-call | tf_op jit(solution)/shard_map/project/pallas_call | solution.py:81
  171.9 1.0 fusion.54
  172.9 1.0 fusion.68
  176.7 42.0 %attention_forward.1 = (bf16[2560,256]{1,0:T(8,128)(2,1)}, bf16[2560,256]{1,0:T(8,128)(2,1)}, f32[2560,1]{1,0:T(8,128)}, f32[2,2560,1]{2,1,0:T(8,128)}) custom-call(s32[8]{0:T(128)} %and_select_fusion.4.begin_ref, bf16[4096,256]{1,0:T(8,128)(2,1)} %get-tuple-element.75.q_ref, bf16[4096,256]{1,0:T(8,128)(2,1)} %get-tuple-element.76.k_ref, ...), custom_call_target="tpu_custom_call" | custom-call | tf_op jit(solution)/shard_map/attention_forward/pallas_call | solution.py:246
  218.7 2.0 fusion.14.grad_ref
  220.7 6.9 convolution_convert_fusion.1
  227.6 95.1 %scatter_rows.1 = (bf16[4,320,512]{2,1,0:T(8,128)(2,1)}, bf16[8,128,704]{2,1,0:T(8,128)(2,1)}) custom-call(bf16[4,2,320,2048]{3,2,1,0:T(8,128)(2,1)} %bitcast.154, bf16[8,128,704]{2,1,0:T(8,128)(2,1)} %get-tuple-element.80.refs_1_), custom_call_target="tpu_custom_call" | custom-call | tf_op jit(solution)/shard_map/scatter_rows/pallas_call | solution.py:870
  322.8 4.8 multiply_reduce_fusion.3
  327.8 5.2 all_gather.8
  333.2 1.9 fusion.15.refs_0_
  335.1 79.7 %gather_rows.2 = (bf16[4,2,320,2048]{3,2,1,0:T(8,128)(2,1)}, bf16[8,128,704]{2,1,0:T(8,128)(2,1)}) custom-call(bf16[4,320,512]{2,1,0:T(8,128)(2,1)} %fusion.15.refs_0_, bf16[8,128,704]{2,1,0:T(8,128)(2,1)} %get-tuple-element.82.refs_1_), custom_call_target="tpu_custom_call" | custom-call | tf_op jit(solution)/shard_map/gather_rows/pallas_call | solution.py:729
  416.3 60.6 %expert_forward.1 = (f32[2560,704]{1,0:T(8,128)}, f32[2560,704]{1,0:T(8,128)}, bf16[8,320,2048]{2,1,0:T(8,128)(2,1)}, f32[2560,1]{1,0:T(8,128)}, bf16[2560,704]{...) custom-call(bf16[8,320,2048]{2,1,0:T(8,128)(2,1)} %bitcast.157, bf16[2048,1408]{1,0:T(8,128)(2,1)} %bitcast.31.up_weight_ref, ...), custom_call_target="tpu_custom_call" | custom-call | tf_op jit(solution)/shard_map/expert_forward/pallas_call | solution.py:955
  476.9 67.5 %expert_backward.1 = (bf16[8,320,2048]{2,1,0:T(8,128)(2,1)}, bf16[2560,1408]{1,0:T(8,128)(2,1)}, bf16[8,128,704]{2,1,0:T(8,128)(2,1)}, bf16[8,128,704]{2,1,0:T(8,128)(2,1)}, bf16[4,320,512]{2,1,0:T(8,128)(2,1)}) custom-call(f32[2560,704]{1,0:T(8,128)} %get-tuple-element.88.gate_ref, f32[2560,704]{1,0:T(8,128)} %get-tuple-element.89.up_ref, ...), custom_call_target="tpu_custom_call" | custom-call | tf_op jit(solution)/shard_map/expert_backward/pallas_call | solution.py:1027
  544.5 70.2 %expert_gradient.1 = (bf16[2048,1408]{1,0:T(8,128)(2,1)}, bf16[4,320,512]{2,1,0:T(8,128)(2,1)}, bf16[8,128,704]{2,1,0:T(8,128)(2,1)}) custom-call(bf16[2560,2048]{1,0:T(8,128)(2,1)} %bitcast.158, bf16[2560,1408]{1,0:T(8,128)(2,1)} %get-tuple-element.94.grad_gate_up_ref, bf16[4,2,320,2048]{3,2,1,0:T(8,128)(2,1)} %bitcast.170, ...), custom_call_target="tpu_custom_call" | custom-call | tf_op jit(solution)/shard_map/expert_gradient/pallas_call | solution.py:1083
  614.6 2.6 copy.103
  617.2 4.5 all-to-all-start.1
  621.7 3.4 multiply_reduce_fusion.5
  625.0 3.4 multiply_reduce_fusion.2
  628.5 5.4 all_gather.9
  634.1 3.2 multiply_add_fusion
  637.3 2.0 fusion.13.refs_0_
  639.2 65.3 %gather_rows.3 = bf16[4,2,320,2048]{3,2,1,0:T(8,128)(2,1)} custom-call(bf16[4,320,512]{2,1,0:T(8,128)(2,1)} %fusion.13.refs_0_), custom_call_target="tpu_custom_call" | custom-call | tf_op jit(solution)/shard_map/gather_rows/pallas_call | solution.py:729
  704.5 2.6 copy.104
  707.1 5.1 all-to-all-start.2
  712.2 1.7 reduce.3
  713.9 8.2 fusion.5.grad_ref
  722.2 68.5 %attention_backward.1 = (bf16[4096,256]{1,0:T(8,128)(2,1)}, bf16[4096,256]{1,0:T(8,128)(2,1)}, bf16[4096,256]{1,0:T(8,128)(2,1)}) custom-call(s32[8]{0:T(128)} %and_select_fusion.4.begin_ref, bf16[4096,256]{1,0:T(8,128)(2,1)} %get-tuple-element.75.q_ref, bf16[4096,256]{1,0:T(8,128)(2,1)} %get-tuple-element.76.k_ref, ...), custom_call_target="tpu_custom_call" | custom-call | tf_op jit(solution)/shard_map/attention_backward/pallas_call | solution.py:269
  790.7 20.2 %convolution_convert_fusion = bf16[4096,2048]{1,0:T(8,128)(2,1)} fusion(bf16[4096,256]{1,0:T(8,128)(2,1)} %get-tuple-element.114.v_ref, bf16[4096,256]{1,0:T(8,128)(2,1)} %get-tuple-element.113.k_ref, bf16[4096,256]{1,0:T(8,128)(2,1)} %get-tuple-element.112.q_ref, bf16[2048,1024]{1,0:T(8,128)(2,1)} %bitcast.167), kind=kOutput, calls=%fused_computation | convolution fusion | flops 12912164864 | bytes 26214400 | tf_op jit(solution)/shard_map/dot_general | solution.py:48
  810.9 87.4 %closing.1 = (bf16[2048,1024]{1,0:T(8,128)(2,1)}, bf16[4,512,512]{2,1,0:T(8,128)(2,1)}) custom-call(bf16[4096,2048]{1,0:T(8,128)(2,1)} %get-tuple-element.106.hidden_ref, bf16[4096,256]{1,0:T(8,128)(2,1)} %get-tuple-element.112.q_ref, bf16[4096,256]{1,0:T(8,128)(2,1)} %get-tuple-element.113.k_ref, bf16[4096,256]{1,0:T(8,128)(2,1)} %get-tuple-element.114.v_ref, ...), custom_call_target="tpu_custom_call" | custom-call | tf_op jit(solution)/shard_map/closing/pallas_call | solution.py:1127
  898.2 4.6 all-to-all-start.3
  902.8 1.1 dynamic-slice_reduce_fusion
  904.0 1.8 fusion.22
  905.7 2.8 multiply_reduce_fusion
  910.1 2.0 copy.112
  912.2 5.2 convert_bitcast_fusion
  917.3 6.4 copy.111
  923.7 3.0 convert_reduce_fusion
  926.7 1.6 copy.106
  928.2 1.2 fusion.32
  929.5 5.3 all_gather.10
  934.9 1.5 multiply_reduce_fusion.4
  936.4 1.5 fusion.92
  937.9 1.6 fusion.43
  939.6 1.0 fusion.37
  940.6 5.4 all_gather.11
  946.8 1.0 copy.113
  947.8 9.3 copy.109
  957.1 9.6 copy.110
  966.7 17.5 %copy.116 = f32[4,256,2,1408]{3,2,1,0:T(2,128)} copy(f32[4,256,2,1408]{1,3,2,0:T(8,128)} %bitcast.156) | data formatting | bytes 23068672
  984.3 11.0 %all-to-all-done.3.query_ref.all_ref = bf16[8,256,1024]{2,1,0:T(8,128)(2,1)} async-done(((bf16[8,256,1024]{2,1,0:T(8,128)(2,1)}), bf16[8,256,1024]{2,1,0:T(8,128)(2,1)}, u32[]{:S(2)}, u32[]{:S(2)}) %all-to-all-start.3) | async-done | bytes 4194336 | tf_op jit(solution)/shard_map/all_to_all | solution.py:312
  995.2 12.0 %attention_weight_gradients.1 = (f32[4,256,4,128]{3,2,1,0:T(4,128)}, f32[256,4,2,128]{3,2,1,0:T(2,128)}, f32[8,256,256]{2,1,0:T(8,128)}, f32[8,256]{1,0:T(8,128)}, f32[256,4]{1,0:T(8,128)}, /*index=5*/f32[256,4]{1,0:T(8,128)}) custom-call(bf16[8,256,1024]{2,1,0:T(8,128)(2,1)} %all-to-all-done.3.query_ref.all_ref, ...), custom_call_target="tpu_custom_call" | custom-call | tf_op jit(solution)/shard_map/attention_weight_gradients/pallas_call | solution.py:1199
  1007.3 1.4 fusion.91
  1008.7 1.6 copy.114
  1010.3 1.6 copy.115
  1011.9 2.7 copy.155
  1014.6 1.3 copy.156
  1015.9 1.3 copy.157
  (141 shorter events, 16.3 us)
Async XLA Ops:
  0.6 4.3 copy-start.11
  5.0 2.4 copy-start.14
  5.0 2.4 copy-start.15
  5.0 2.4 copy-start.9
  133.5 5.1 copy-start.13
  133.6 7.6 copy-start.12
  133.6 282.7 %all-to-all-start = ((bf16[8,256,1408]{2,1,0:T(8,128)(2,1)}), bf16[8,256,1408]{2,1,0:T(8,128)(2,1)}, u32[]{:S(2)}, u32[]{:S(2)}) async-start(bf16[8,256,1408]{2,1,0:T(8,128)(2,1)} %get-tuple-element.84), calls=%async_computation | async-start | bytes 11534336 | tf_op jit(solution)/shard_map/all_to_all | solution.py:312
  139.4 188.2 %copy-start.1 = (bf16[512,512]{0,1:T(8,128)(2,1)}, bf16[512,512]{0,1:T(8,128)(2,1)S(1)}, u32[]{:S(2)}) copy-start(bf16[512,512]{0,1:T(8,128)(2,1)S(1)} %copy.96) | copy-start | bytes 1572868
  141.4 30.6 %copy-start.4 = (bf16[512,512]{0,1:T(8,128)(2,1)}, bf16[512,512]{0,1:T(8,128)(2,1)S(1)}, u32[]{:S(2)}) copy-start(bf16[512,512]{0,1:T(8,128)(2,1)S(1)} %copy.95) | copy-start | bytes 1572868
  218.7 2.0 copy-start.3
  333.2 81.7 %copy-start.5 = (bf16[512,512]{0,1:T(8,128)(2,1)}, bf16[512,512]{0,1:T(8,128)(2,1)S(1)}, u32[]{:S(2)}) copy-start(bf16[512,512]{0,1:T(8,128)(2,1)S(1)} %get-tuple-element.123) | copy-start | bytes 1572868
  617.2 87.3 %all-to-all-start.1 = ((bf16[8,128,704]{1,2,0:T(8,128)(2,1)}), bf16[8,128,704]{1,2,0:T(8,128)(2,1)}, u32[]{:S(2)}, u32[]{:S(2)}) async-start(bf16[8,128,704]{1,2,0:T(8,128)(2,1)} %copy.103), calls=%async_computation.1 | async-start | bytes 2883584 | tf_op jit(solution)/shard_map/all_to_all | solution.py:312
  621.7 3.4 copy-start.6
  621.7 3.4 copy-start.10
  707.1 191.1 %all-to-all-start.2 = ((bf16[8,256,1408]{2,1,0:T(8,128)(2,1)}), bf16[8,256,1408]{2,1,0:T(8,128)(2,1)}, u32[]{:S(2)}, u32[]{:S(2)}) async-start(bf16[8,256,1408]{2,1,0:T(8,128)(2,1)} %bitcast.172), calls=%async_computation.2 | async-start | bytes 11534336 | tf_op jit(solution)/shard_map/all_to_all | solution.py:312
  898.2 97.0 %all-to-all-start.3 = ((bf16[8,256,1024]{2,1,0:T(8,128)(2,1)}), bf16[8,256,1024]{2,1,0:T(8,128)(2,1)}, u32[]{:S(2)}, u32[]{:S(2)}) async-start(bf16[8,256,1024]{2,1,0:T(8,128)(2,1)} %bitcast.174), calls=%async_computation.3 | async-start | bytes 8388608 | tf_op jit(solution)/shard_map/all_to_all | solution.py:312
  903.9 4.6 copy-start
  934.9 4.7 copy-start.2
  1007.3 7.3 copy-start.8
  1011.9 4.0 copy-start.7

commit v8 on v7

--- a/solution.py
+++ b/solution.py
@@ -912,19 +912,21 @@
 
 def expert_forward_kernel(
     rows_ref, up_weight_ref, first_ref, last_ref, small_ref, rank_ref, member_ref, grad_ref,
-    gate_ref, up_ref, result_ref, share_ref, shared_ref, grad_rows_ref, down_weight_ref, *scratch
+    slope_ref, silu_ref, result_ref, share_ref, shared_ref, grad_rows_ref, down_weight_ref, *scratch
 ):
     join_halves(first_ref, last_ref, down_weight_ref)
     steps = gather_steps(grad_ref, grad_rows_ref, *scratch, False)
-    units = gate_ref.shape[1]
+    units = slope_ref.shape[1]
 
     def compute():
         rows = rows_ref[0]
         made = dot(rows, up_weight_ref[...])
         gate, up = made[:, :units], made[:, units:]
-        gate_ref[...] = gate
-        up_ref[...] = up
-        inner = gate * jax.nn.sigmoid(gate) * up
+        sigmoid = jax.nn.sigmoid(gate)
+        silu = gate * sigmoid
+        slope_ref[...] = up * sigmoid * (1.0 + gate * (1.0 - sigmoid))
+        silu_ref[...] = silu
+        inner = silu * up
         result_ref[0] = contract_last(inner.astype(BF16), down_weight_ref[...]).astype(BF16)
         cap, count = rows.shape[0], rank_ref.shape[2]
         pick = (lax.broadcasted_iota(jnp.int32, (cap, count), 0) == rank_ref[0]).astype(BF16)
@@ -990,43 +992,59 @@
 
 
 def expert_backward_kernel(
-    gate_ref, up_ref, grad_ref, share_ref, up_weight_ref, first_ref, last_ref, columns_ref, inner_ref,
-    result_ref, grad_rows_ref, grad_gate_up_ref, down_first_ref, down_last_ref, out_ref,
-    down_weight_ref, *scratch
+    slope_ref, silu_ref, grad_ref, share_ref, up_weight_ref, first_ref, last_ref, columns_ref,
+    inner_ref, result_ref, *refs, rides
 ):
+    count = 6 if rides else 5
+    grad_rows_ref, grad_gate_up_ref, down_first_ref, down_last_ref, out_ref = refs[:5]
+    down_weight_ref, kept_ref, scratch = refs[count], refs[count + 1], refs[count + 2 :]
+    ride = Ride(kept_ref, refs[5], *scratch[7:]) if rides else None
+    steps = scatter_steps(result_ref, out_ref, *scratch[:7], 1, ride.peers if rides else ())
+    middle = down_first_ref.shape[1]
+    number = pl.program_id(0)
     join_halves(first_ref, last_ref, down_weight_ref)
-    steps = scatter_steps(result_ref, out_ref, *scratch)
-    middle = down_first_ref.shape[1]
-
-    def compute():
+
+    def down_gradient():
+        down_grad = contract_first(columns_ref[...], inner_ref[...]).astype(BF16)
+        kept_ref[number] = down_grad[:middle]
+        down_first_ref[0] = down_grad[:middle]
+        down_last_ref[0] = down_grad[middle:]
+
+    def rows_gradient():
         grad_inner = dot(grad_ref[0], down_weight_ref[...]) * share_ref[...]
-        gate, up = gate_ref[...], up_ref[...]
-        sigmoid = jax.nn.sigmoid(gate)
-        grad_gate = grad_inner * up * sigmoid * (1.0 + gate * (1.0 - sigmoid))
-        grad_up = grad_inner * gate * sigmoid
-        grad_gate_up = jnp.concatenate([grad_gate, grad_up], axis=1).astype(BF16)
+        grad_gate_up = jnp.concatenate(
+            [grad_inner * slope_ref[...], grad_inner * silu_ref[...]], axis=1
+        ).astype(BF16)
         grad_gate_up_ref[...] = grad_gate_up
         grad_rows_ref[0] = contract_last(grad_gate_up, up_weight_ref[...]).astype(BF16)
-        down_grad = contract_first(columns_ref[...], inner_ref[...]).astype(BF16)
-        down_first_ref[0] = down_grad[:middle]
-        down_last_ref[0] = down_grad[middle:]
-
-    carry(steps[:1], steps[1:], (0, 1, 2, 4, 5, 7, 7), compute)
+
+    def compute():
+        pl.when(number < BLOCKS)(down_gradient)
+        pl.when(number >= BLOCKS)(rows_gradient)
+
+    after, places = list(steps[1:]), [3, 7, 9, 11, 13, 15, 15]
+    if rides:
+        after += [ride.begin] + [functools.partial(ride.go_on, i) for i in range(4)] + [ride.finish]
+        places += [7, 8, 9, 10, 12, 15]
+    carry(steps[:1], after, places, compute)
 
 
 def expert_backward(
-    gate, up, grad_rows, share, up_weight, down_halves, inner, result, collective_id
+    slope, silu, grad_rows, share, up_weight, down_halves, inner, result, rides, collective_id
 ):
     _, cap, width = grad_rows.shape
-    count, units = gate.shape
+    count, units = slope.shape
     tile = width // BLOCKS
     anywhere = pl.BlockSpec(memory_space=pl.ANY)
-    block = lambda b: (b, 0)
-    rows = pl.BlockSpec((1, cap, width), lambda b: (b, 0, 0))
-    half = pl.BlockSpec((1, tile // 2, units), lambda b: (b, 0, 0))
+    at_row = lambda b: jnp.maximum(b - BLOCKS, 0)
+    at_tile = lambda b: jnp.minimum(b, BLOCKS - 1)
+    block = lambda b: (at_row(b), 0)
+    rows = pl.BlockSpec((1, cap, width), lambda b: (at_row(b), 0, 0))
+    half = pl.BlockSpec((1, tile // 2, units), lambda b: (at_tile(b), 0, 0))
+    half_shape = jax.ShapeDtypeStruct((BLOCKS, tile // 2, units), BF16)
     return pl.pallas_call(
-        expert_backward_kernel,
-        grid=(BLOCKS,),
+        functools.partial(expert_backward_kernel, rides=rides),
+        grid=(2 * BLOCKS,),
         in_specs=[
             pl.BlockSpec((cap, units), block),
             pl.BlockSpec((cap, units), block),
@@ -1035,25 +1053,32 @@
             once(up_weight.shape),
             once(down_halves[0].shape),
             once(down_halves[1].shape),
-            pl.BlockSpec((count, tile), lambda b: (0, b)),
+            pl.BlockSpec((count, tile), lambda b: (0, at_tile(b))),
             once(inner.shape),
             anywhere,
         ],
-        out_specs=[rows, pl.BlockSpec((cap, 2 * units), block), half, half, anywhere],
+        out_specs=[rows, pl.BlockSpec((cap, 2 * units), block), half, half, anywhere]
+        + [anywhere] * rides,
         out_shape=[
             jax.ShapeDtypeStruct((BLOCKS, cap, width), BF16),
             jax.ShapeDtypeStruct((count, 2 * units), BF16),
-            jax.ShapeDtypeStruct((BLOCKS, tile // 2, units), BF16),
-            jax.ShapeDtypeStruct((BLOCKS, tile // 2, units), BF16),
+            half_shape,
+            half_shape,
             jax.ShapeDtypeStruct((PLANES, cap, width // 4), BF16),
-        ],
-        scratch_shapes=[pltpu.VMEM((width, units), BF16)] + scatter_scratch(cap, width // 4),
+        ]
+        + [half_shape] * rides,
+        scratch_shapes=[
+            pltpu.VMEM((width, units), BF16),
+            pltpu.VMEM((BLOCKS, tile // 2, units), BF16),
+        ]
+        + scatter_scratch(cap, width // 4)
+        + list(RIDE_SCRATCH) * rides,
         compiler_params=pltpu.CompilerParams(
             collective_id=collective_id, has_side_effects=True, vmem_limit_bytes=VMEM_BYTES
         ),
         name="expert_backward",
     )(
-        gate, up, grad_rows, share, up_weight, *down_halves, grad_rows.reshape(count, width), inner,
+        slope, silu, grad_rows, share, up_weight, *down_halves, grad_rows.reshape(count, width), inner,
         result.reshape(PLANES, HALVES, cap, width),
     )
 
@@ -1150,16 +1175,9 @@
 
 
 def finish_kernel(
-    query_ref, all_ref, small_ref, query_grad_ref, kv_grad_ref, out_grad_ref, gains_ref,
-    router_first_ref, router_second_ref, landed_ref, *scratch
+    query_ref, all_ref, small_ref, query_grad_ref, kv_grad_ref, out_grad_ref, gain_first_ref,
+    gain_second_ref, router_first_ref, router_second_ref
 ):
-    ride = Ride(small_ref, landed_ref, *scratch)
-
-    @pl.when(pl.program_id(0) == 0)
-    def _():
-        meet([peer for _, _, peer in ride.moves.made.values()])
-        ride.begin(tuple(ride.moves.made))
-
     span = query_ref.shape[2] // 4
     head_width = query_grad_ref.shape[3]
     pair = span // head_width
@@ -1183,18 +1201,34 @@
                     first = kind * span + head * head_width
                     kv_grad_ref[:, half * pair + head, kind, :] = total[:, first : first + head_width]
 
-    @pl.when(pl.program_id(0) == PLANES - 1)
-    def _():
-        ride.finish()
-        total = sum(landed_ref[place] for place in range(BLOCKS))
-        gains_ref[...] = total[:8]
-        spare = jnp.zeros((128 - total.shape[0], total.shape[1]), F32)
-        columns = jnp.concatenate([total, spare], axis=0).T
-        router_first_ref[...] = columns[:own_rows, 2 : 2 + PLANES]
-        router_second_ref[...] = columns[:own_rows, 2 + PLANES : 2 + 2 * PLANES]
-
-
-def finish(landed, small, own_rows, span, heads, head_width, collective_id):
+        total = sum(small_ref[place] for place in range(BLOCKS))
+        gain_first_ref[...] = total[0:1]
+        gain_second_ref[...] = total[1:2]
+        router_first_ref[...] = total[2 : 2 + PLANES]
+        router_second_ref[...] = total[2 + PLANES : 2 + 2 * PLANES]
+
+
+def swap_kernel(pieces_ref, landed_ref, *scratch):
+    ride = Ride(pieces_ref, landed_ref, *scratch)
+    meet([peer for _, _, peer in ride.moves.made.values()])
+    ride.begin(tuple(ride.moves.made))
+    ride.finish()
+
+
+def swapped(pieces, collective_id):
+    whole = pl.BlockSpec(memory_space=pltpu.VMEM)
+    return pl.pallas_call(
+        swap_kernel,
+        out_shape=jax.ShapeDtypeStruct(pieces.shape, pieces.dtype),
+        in_specs=[whole],
+        out_specs=whole,
+        scratch_shapes=list(RIDE_SCRATCH),
+        compiler_params=pltpu.CompilerParams(collective_id=collective_id, has_side_effects=True),
+        name="swap_small",
+    )(pieces)
+
+
+def finish(landed, small, own_rows, span, heads, head_width):
     places, height, width = landed.shape
     return pl.pallas_call(
         finish_kernel,
@@ -1208,22 +1242,21 @@
             pl.BlockSpec((1, own_rows, heads, head_width), lambda e: (e, 0, 0, 0)),
             pl.BlockSpec((own_rows, heads, 2, head_width), lambda e: (0, 0, 0, 0)),
             pl.BlockSpec((HALVES, span, own_rows), lambda e: (e, 0, 0)),
-            pl.BlockSpec((8, small.shape[2]), lambda e: (0, 0)),
-            pl.BlockSpec((own_rows, PLANES), lambda e: (0, 0)),
-            pl.BlockSpec((own_rows, PLANES), lambda e: (0, 0)),
+            pl.BlockSpec((1, small.shape[2]), lambda e: (0, 0)),
+            pl.BlockSpec((1, small.shape[2]), lambda e: (0, 0)),
+            pl.BlockSpec((PLANES, small.shape[2]), lambda e: (0, 0)),
+            pl.BlockSpec((PLANES, small.shape[2]), lambda e: (0, 0)),
         ],
         out_shape=[
             jax.ShapeDtypeStruct((PLANES, own_rows, heads, head_width), F32),
             jax.ShapeDtypeStruct((own_rows, heads, 2, head_width), F32),
             jax.ShapeDtypeStruct((places, span, own_rows), F32),
-            jax.ShapeDtypeStruct((8, small.shape[2]), F32),
-            jax.ShapeDtypeStruct((own_rows, PLANES), F32),
-            jax.ShapeDtypeStruct((own_rows, PLANES), F32),
-        ],
-        scratch_shapes=[pltpu.VMEM(small.shape, F32)] + list(RIDE_SCRATCH),
-        compiler_params=pltpu.CompilerParams(
-            collective_id=collective_id, has_side_effects=True, vmem_limit_bytes=VMEM_BYTES
-        ),
+            jax.ShapeDtypeStruct((1, small.shape[2]), F32),
+            jax.ShapeDtypeStruct((1, small.shape[2]), F32),
+            jax.ShapeDtypeStruct((PLANES, small.shape[2]), F32),
+            jax.ShapeDtypeStruct((PLANES, small.shape[2]), F32),
+        ],
+        compiler_params=pltpu.CompilerParams(vmem_limit_bytes=VMEM_BYTES),
         name="attention_weight_gradients",
     )(landed, landed, small)
 
@@ -1419,17 +1452,19 @@
         4,
     )
     grad_slots_second = grad_slots_second.reshape(BLOCKS, CAP, width_all)
-    grad_rows, grad_gate_up, grad_down_first, grad_down_last, result_slots = expert_backward(
-        gate_pre, up_pre, grad_slots_second, gate_slots_second, up_weight, down_weight, inner, result, 5
+    grad_rows, grad_gate_up, grad_down_first, grad_down_last, result_slots, *landed = expert_backward(
+        gate_pre, up_pre, grad_slots_second, gate_slots_second, up_weight, down_weight, inner, result,
+        int(groups == 1), 5,
     )
     if groups > 1:
         grad_down = jnp.concatenate([grad_down_first, grad_down_last], axis=1)
         grad_down = group_sums(grad_down.reshape(groups, BLOCKS, own_rows, hidden_units))
         grad_down_first, grad_down_last = jnp.split(grad_down, 2, axis=1)
-    grad_up, grad_rows, grad_down_first = expert_gradient(
-        slots_second.reshape(-1, width_all), grad_gate_up, grad_rows, grad_down_first, 6
-    )
-    grad_rows, grad_down_last = lax.optimization_barrier((grad_rows, grad_down_last))
+        landed = [exchanged(grad_down_first)]
+    grad_down_first = landed[0]
+    grad_up, grad_rows, grad_down_last = expert_gradient(
+        slots_second.reshape(-1, width_all), grad_gate_up, grad_rows, grad_down_last, 6
+    )
     branch_second = to_tokens(result_slots, own_pick_second)
 
     grad_hidden_second = jnp.sum(to_tokens(grad_rows, own_pick_second), axis=0)
@@ -1444,14 +1479,13 @@
     grad_normed = grad_hidden_second * gain_second
     grad_residual = grad_out + inverse_second * (grad_normed - normed_second * inner_mean)
 
-    grad_down_last = exchanged(grad_down_last)
     grad_slots_first = gathered(to_slots(grad_residual.astype(BF16), own_pick_first), 8)
     (
-        grad_slots_first, grad_down_last, residual, own_gates_second, branch_second, hidden_second,
+        grad_slots_first, residual, own_gates_second, branch_second, hidden_second,
         grad_logits_second, grad_hidden_second, normed_second,
     ) = lax.optimization_barrier(
         (
-            grad_slots_first, grad_down_last, residual, own_gates_second, branch_second, hidden_second,
+            grad_slots_first, residual, own_gates_second, branch_second, hidden_second,
             grad_logits_second, grad_hidden_second, normed_second,
         )
     )
@@ -1502,21 +1536,24 @@
     small_grads = small_grads.reshape(-1, groups, BLOCKS, own_rows)
     small_grads = lax.dynamic_index_in_dim(small_grads, group, 1, keepdims=False).swapaxes(0, 1)
     small_grads = jnp.pad(small_grads, ((0, 0), (0, 6), (0, -own_rows % 128)))
+    small_grads, grad_first = lax.optimization_barrier((small_grads, grad_first))
     (
-        attention_query_grad, attention_kv_grad, attention_out_grad, gain_grads,
-        attention_router_grad, feedforward_router_grad,
-    ) = finish(grad_first, small_grads, own_rows, span, attention_kv.shape[1], head_width, 7)
+        attention_query_grad, attention_kv_grad, attention_out_grad, gain_grad_first,
+        gain_grad_second, router_grad_first, router_grad_second,
+    ) = finish(
+        grad_first, swapped(small_grads, 7), own_rows, span, attention_kv.shape[1], head_width
+    )
     attention_out_grad = attention_out_grad.reshape(attention_out.shape)
     return (
         layer_output,
         input_grad.astype(BF16),
-        gain_grads[0, :own_rows],
+        gain_grad_first[0, :own_rows],
         attention_kv_grad,
         attention_query_grad.astype(F32),
         attention_out_grad.astype(F32),
-        attention_router_grad,
-        gain_grads[1, :own_rows],
-        feedforward_router_grad,
+        router_grad_first[:, :own_rows].T,
+        gain_grad_second[0, :own_rows],
+        router_grad_second[:, :own_rows].T,
         expert_gate_up_grad.astype(F32),
         expert_down_grad.astype(F32),
     )

time: 1020 us -> 1020 us (level)
  Pallas kernels: 798 us -> 816 us
  local copies, waits for them, and re-layouts: 74.9 us -> 59.8 us
    pallas_call x1 -> x2, Pallas kernels: 67.5 us -> 94.1 us  [the longest x1 85 us: expert_backward(): pl.pallas_call(functools.partial(expert_backward_kernel, rides=rides), gr...]
    pallas_call x2, Pallas kernels: 145 us -> 131 us  [gathered(): pl.pallas_call(functools.partial(gather_kernel, same=slots.ndim == 2, sha...]
    unnamed x60 -> x49, local copies, waits for them, and re-layouts: 30.9 us -> 22.4 us
  transfers between devices with their start and end apart: 4 -> 3, of which waited for: 1 -> 1; matrix products, arithmetic and copies ran while one was open for 14% -> 13% of each run, Pallas kernels for 46% -> 40%
where the time goes in v8:
time: 1020 us
  Pallas kernels  816 us (80%)
  matrix products  62.5 us (6%)
  local copies, waits for them, and re-layouts  59.8 us (6%)
  other arithmetic  31.1 us (3%)
  blocking collectives  21.3 us (2%)
  starting transfers between devices  14.3 us (1%)
    pallas_call x2, Pallas kernels, gathered(): pl.pallas_call(functools.partial(gather_kernel, same=slots.ndim == 2, sha...  131 us
    pallas_call x1, Pallas kernels, opened(): pl.pallas_call(functools.partial(opening_kernel, share=share), grid=(plac...  122 us
    pallas_call x1, Pallas kernels, scattered(): pl.pallas_call(functools.partial(scatter_kernel, share=share, rides=len(r...  93.5 us
    pallas_call x1, Pallas kernels, closing(): pl.pallas_call(closing_kernel, grid=(BLOCKS,), in_specs=[pl.BlockSpec((co...  87.4 us
    pallas_call x1, Pallas kernels, expert_backward(): pl.pallas_call(functools.partial(expert_backward_kernel, rides=rides), gr...  85 us
    pallas_call x1, Pallas kernels, expert_gradient(): pl.pallas_call(expert_gradient_kernel, grid=(BLOCKS,), in_specs=[pl.Block...  74.5 us
    pallas_call x1, Pallas kernels, attention_backward(): pl.pallas_call(functools.partial(attention_backward_kernel, scaling=1.0 /...  72.9 us
    pallas_call x1, Pallas kernels, expert_forward(): pl.pallas_call(expert_forward_kernel, grid=(BLOCKS,), in_specs=[pl.BlockS...  59.9 us
  transfers between devices with their start and end apart: 3, of which 1 were waited for; matrix products, arithmetic and copies ran while one was open for 13% of the time, Pallas kernels for 40%

profile of v8, /device:TPU:0, one launch (start us, length us, event | category | flops | bytes accessed | tf_op | source)
XLA Modules:
  0.0 1015.6 jit_solution(15559603886192584385)
XLA Ops:
  0.7 0.7 broadcast_in_dim.79
  2.1 0.7 convert.15
  3.4 1.1 copy.85
  5.0 0.7 reshape.346
  5.9 1.5 copy.83
  7.5 0.8 fusion.42.tokens_ref
  8.7 2.6 pad_maximum_fusion.pieces_ref
  11.3 122.2 %open_rows.1 = (bf16[4,2,528,2048]{3,2,1,0:T(8,128)(2,1)}, bf16[8,256,1024]{2,1,0:T(8,128)(2,1)}, bf16[8,256,1408]{2,1,0:T(8,128)(2,1)}, bf16[8,128,704]{2,1,0:T(8,128)(2,1)}, bf16[8,128,704]{2,1,0:T(8,128)(2,1)}) custom-call(bf16[528,512]{1,0:T(8,128)(2,1)} %fusion.42.tokens_ref, bf16[8,256,1024]{2,1,0:T(8,128)(2,1)} %pad_maximum_fusion.pieces_ref, ...), custom_call_target="tpu_custom_call" | custom-call | tf_op jit(solution)/shard_map/open_rows/pallas_call | solution.py:674
  133.6 5.0 all-to-all-start
  139.4 1.1 slice.125
  141.4 1.1 convert_element_type.164
  144.7 27.2 %project.1 = (bf16[4096,2048]{1,0:T(8,128)(2,1)}, bf16[4096,256]{1,0:T(8,128)(2,1)}, bf16[4096,256]{1,0:T(8,128)(2,1)}, bf16[4096,256]{1,0:T(8,128)(2,1)}, f32[16,4096]{1,0:T(8,128)}, /*index=5*/f32[4096,1]{1,0:T(8,128)}) custom-call(bf16[4,2,528,2048]{3,2,1,0:T(8,128)(2,1)} %get-tuple-element.72.tokens_ref, bf16[16,2048]{1,0:T(8,128)(2,1)} %pad.24.small_ref, ...), custom_call_target="tpu_custom_call" | custom-call | tf_op jit(solution)/shard_map/project/pallas_call | solution.py:81
  171.9 1.0 fusion.54
  172.9 1.0 fusion.68
  174.0 1.0 broadcast_divide_fusion
  176.7 44.8 %attention_forward.1 = (bf16[2560,256]{1,0:T(8,128)(2,1)}, bf16[2560,256]{1,0:T(8,128)(2,1)}, f32[2560,1]{1,0:T(8,128)}, f32[2,2560,1]{2,1,0:T(8,128)}) custom-call(s32[8]{0:T(128)} %and_select_fusion.4.begin_ref, bf16[4096,256]{1,0:T(8,128)(2,1)} %get-tuple-element.75.q_ref, bf16[4096,256]{1,0:T(8,128)(2,1)} %get-tuple-element.76.k_ref, ...), custom_call_target="tpu_custom_call" | custom-call | tf_op jit(solution)/shard_map/attention_forward/pallas_call | solution.py:246
  221.4 1.9 fusion.14.grad_ref
  223.3 6.9 convolution_convert_fusion.1
  230.2 93.5 %scatter_rows.1 = (bf16[4,320,512]{2,1,0:T(8,128)(2,1)}, bf16[8,128,704]{2,1,0:T(8,128)(2,1)}) custom-call(bf16[4,2,320,2048]{3,2,1,0:T(8,128)(2,1)} %bitcast.156, bf16[8,128,704]{2,1,0:T(8,128)(2,1)} %get-tuple-element.80.refs_1_), custom_call_target="tpu_custom_call" | custom-call | tf_op jit(solution)/shard_map/scatter_rows/pallas_call | solution.py:870
  323.7 4.8 multiply_reduce_fusion.3
  328.7 5.2 all_gather.8
  334.1 1.9 fusion.15.refs_0_
  336.0 80.7 %gather_rows.2 = (bf16[4,2,320,2048]{3,2,1,0:T(8,128)(2,1)}, bf16[8,128,704]{2,1,0:T(8,128)(2,1)}) custom-call(bf16[4,320,512]{2,1,0:T(8,128)(2,1)} %fusion.15.refs_0_, bf16[8,128,704]{2,1,0:T(8,128)(2,1)} %get-tuple-element.82.refs_1_), custom_call_target="tpu_custom_call" | custom-call | tf_op jit(solution)/shard_map/gather_rows/pallas_call | solution.py:729
  417.5 0.7 pad_convert_fusion.member_ref
  418.2 59.9 %expert_forward.1 = (f32[2560,704]{1,0:T(8,128)}, f32[2560,704]{1,0:T(8,128)}, bf16[8,320,2048]{2,1,0:T(8,128)(2,1)}, f32[2560,1]{1,0:T(8,128)}, bf16[2560,704]{...) custom-call(bf16[8,320,2048]{2,1,0:T(8,128)(2,1)} %bitcast.159, bf16[2048,1408]{1,0:T(8,128)(2,1)} %bitcast.31.up_weight_ref, ...), custom_call_target="tpu_custom_call" | custom-call | tf_op jit(solution)/shard_map/expert_forward/pallas_call | solution.py:957
  478.2 85.0 %expert_backward.1 = (bf16[8,320,2048]{2,1,0:T(8,128)(2,1)}, bf16[2560,1408]{1,0:T(8,128)(2,1)}, bf16[8,128,704]{2,1,0:T(8,128)(2,1)}, bf16[8,128,704]{2,1,0:T(8...) custom-call(f32[2560,704]{1,0:T(8,128)} %get-tuple-element.88.slope_ref, ...), custom_call_target="tpu_custom_call" | custom-call | tf_op jit(solution)/shard_map/expert_backward/pallas_call | solution.py:1045
  563.2 74.5 %expert_gradient.1 = (bf16[2048,1408]{1,0:T(8,128)(2,1)}, bf16[4,320,512]{2,1,0:T(8,128)(2,1)}, bf16[8,128,704]{2,1,0:T(8,128)(2,1)}) custom-call(bf16[2560,2048]{1,0:T(8,128)(2,1)} %bitcast.160, bf16[2560,1408]{1,0:T(8,128)(2,1)} %get-tuple-element.94.grad_gate_up_ref, bf16[4,2,320,2048]{3,2,1,0:T(8,128)(2,1)} %bitcast.172, ...), custom_call_target="tpu_custom_call" | custom-call | tf_op jit(solution)/shard_map/expert_gradient/pallas_call | solution.py:1108
  637.8 3.4 multiply_reduce_fusion.5
  641.1 3.4 multiply_reduce_fusion.2
  644.5 5.4 all_gather.9
  650.1 3.2 multiply_add_fusion
  653.3 1.9 fusion.13.refs_0_
  655.2 50.5 %gather_rows.3 = bf16[4,2,320,2048]{3,2,1,0:T(8,128)(2,1)} custom-call(bf16[4,320,512]{2,1,0:T(8,128)(2,1)} %fusion.13.refs_0_), custom_call_target="tpu_custom_call" | custom-call | tf_op jit(solution)/shard_map/gather_rows/pallas_call | solution.py:729
  705.8 4.7 all-to-all-start.1
  710.5 1.7 reduce.3
  712.2 8.2 fusion.5.grad_ref
  720.4 72.9 %attention_backward.1 = (bf16[4096,256]{1,0:T(8,128)(2,1)}, bf16[4096,256]{1,0:T(8,128)(2,1)}, bf16[4096,256]{1,0:T(8,128)(2,1)}) custom-call(s32[8]{0:T(128)} %and_select_fusion.4.begin_ref, bf16[4096,256]{1,0:T(8,128)(2,1)} %get-tuple-element.75.q_ref, bf16[4096,256]{1,0:T(8,128)(2,1)} %get-tuple-element.76.k_ref, ...), custom_call_target="tpu_custom_call" | custom-call | tf_op jit(solution)/shard_map/attention_backward/pallas_call | solution.py:269
  793.3 20.2 %convolution_convert_fusion = bf16[4096,2048]{1,0:T(8,128)(2,1)} fusion(bf16[4096,256]{1,0:T(8,128)(2,1)} %get-tuple-element.111.v_ref, bf16[4096,256]{1,0:T(8,128)(2,1)} %get-tuple-element.110.k_ref, bf16[4096,256]{1,0:T(8,128)(2,1)} %get-tuple-element.109.q_ref, bf16[2048,1024]{1,0:T(8,128)(2,1)} %bitcast.169), kind=kOutput, calls=%fused_computation | convolution fusion | flops 12912164864 | bytes 26214400 | tf_op jit(solution)/shard_map/dot_general | solution.py:48
  813.4 87.4 %closing.1 = (bf16[2048,1024]{1,0:T(8,128)(2,1)}, bf16[4,512,512]{2,1,0:T(8,128)(2,1)}) custom-call(bf16[4096,2048]{1,0:T(8,128)(2,1)} %get-tuple-element.103.hidden_ref, bf16[4096,256]{1,0:T(8,128)(2,1)} %get-tuple-element.109.q_ref, bf16[4096,256]{1,0:T(8,128)(2,1)} %get-tuple-element.110.k_ref, bf16[4096,256]{1,0:T(8,128)(2,1)} %get-tuple-element.111.v_ref, ...), custom_call_target="tpu_custom_call" | custom-call | tf_op jit(solution)/shard_map/closing/pallas_call | solution.py:1152
  900.9 4.6 all-to-all-start.2
  905.5 1.1 dynamic-slice_reduce_fusion
  906.6 1.6 fusion.22
  908.2 5.2 convert_bitcast_fusion
  913.4 6.4 copy.103
  919.7 2.9 multiply_reduce_fusion.1
  922.6 1.0 add_convert_fusion
  923.6 2.0 copy.104
  925.6 3.0 convert_reduce_fusion
  928.6 1.6 copy.98
  930.1 1.2 fusion.32
  931.4 2.8 multiply_reduce_fusion
  934.3 5.3 all_gather.10
  939.6 1.5 multiply_reduce_fusion.4
  941.1 1.5 fusion.91
  942.7 1.6 fusion.43
  944.3 1.0 fusion.37
  945.4 5.4 all_gather.11
  951.6 1.0 copy.105
  952.6 9.3 copy.101
  961.8 9.6 copy.102
  971.5 17.5 %copy.106 = f32[4,256,2,1408]{3,2,1,0:T(2,128)} copy(f32[4,256,2,1408]{1,3,2,0:T(8,128)} %bitcast.158) | data formatting | bytes 23068672
  989.0 9.2 all-to-all-done.2.query_ref.all_ref
  998.2 9.0 swap_small.1.small_ref
  1007.3 8.0 attention_weight_gradients.1
  (126 shorter events, 10.1 us)
Async XLA Ops:
  0.6 4.3 copy-start.8
  5.0 2.4 copy-start.11
  5.0 2.4 copy-start.12
  5.0 2.4 copy-start.6
  133.5 5.1 copy-start.10
  133.5 7.6 copy-start.9
  133.6 284.7 %all-to-all-start = ((bf16[8,256,1408]{2,1,0:T(8,128)(2,1)}), bf16[8,256,1408]{2,1,0:T(8,128)(2,1)}, u32[]{:S(2)}, u32[]{:S(2)}) async-start(bf16[8,256,1408]{2,1,0:T(8,128)(2,1)} %get-tuple-element.84), calls=%async_computation | async-start | bytes 11534336 | tf_op jit(solution)/shard_map/all_to_all | solution.py:312
  139.3 189.2 %copy-start = (bf16[512,512]{0,1:T(8,128)(2,1)}, bf16[512,512]{0,1:T(8,128)(2,1)S(1)}, u32[]{:S(2)}) copy-start(bf16[512,512]{0,1:T(8,128)(2,1)S(1)} %copy.90) | copy-start | bytes 1572868
  141.3 30.6 %copy-start.3 = (bf16[512,512]{0,1:T(8,128)(2,1)}, bf16[512,512]{0,1:T(8,128)(2,1)S(1)}, u32[]{:S(2)}) copy-start(bf16[512,512]{0,1:T(8,128)(2,1)S(1)} %copy.89) | copy-start | bytes 1572868
  221.4 1.9 copy-start.2
  334.1 82.7 %copy-start.4 = (bf16[512,512]{0,1:T(8,128)(2,1)}, bf16[512,512]{0,1:T(8,128)(2,1)S(1)}, u32[]{:S(2)}) copy-start(bf16[512,512]{0,1:T(8,128)(2,1)S(1)} %get-tuple-element.117) | copy-start | bytes 1572868
  637.7 3.4 copy-start.5
  637.7 3.4 copy-start.7
  705.8 195.1 %all-to-all-start.1 = ((bf16[8,256,1408]{2,1,0:T(8,128)(2,1)}), bf16[8,256,1408]{2,1,0:T(8,128)(2,1)}, u32[]{:S(2)}, u32[]{:S(2)}) async-start(bf16[8,256,1408]{2,1,0:T(8,128)(2,1)} %bitcast.175), calls=%async_computation.1 | async-start | bytes 11534336 | tf_op jit(solution)/shard_map/all_to_all | solution.py:312
  900.9 97.4 %all-to-all-start.2 = ((bf16[8,256,1024]{2,1,0:T(8,128)(2,1)}), bf16[8,256,1024]{2,1,0:T(8,128)(2,1)}, u32[]{:S(2)}, u32[]{:S(2)}) async-start(bf16[8,256,1024]{2,1,0:T(8,128)(2,1)} %bitcast.176), calls=%async_computation.2 | async-start | bytes 8388608 | tf_op jit(solution)/shard_map/all_to_all | solution.py:312
  939.6 4.7 copy-start.1

commit v9 on v8

--- a/solution.py
+++ b/solution.py
@@ -22,6 +22,7 @@
 PLACES = ("z", "x")
 MESH = pl.DeviceIdType.MESH
 VMEM_BYTES = 56 * 1024 * 1024
+EARLY = 128
 
 
 def rope_tables(token_count, width):
@@ -119,16 +120,26 @@
     return rows, keys, scores, allowed
 
 
-def slots_of_block(rank_ref, table_ref, cap):
+def slots_of_block(rank_ref, table_ref, cap, block):
     rows = table_ref.shape[1]
     pick = (lax.broadcasted_iota(jnp.int32, (cap, rows), 0) == rank_ref[0]).astype(BF16)
     made = contract_last(pick, table_ref[...])
-    base = pl.program_id(1) * rows
+    base = block * rows
     filled = made[:, 4:5] > 0.5
     low = (64.0 * made[:, 2:3] + made[:, 3:4]).astype(jnp.int32)
     high = (64.0 * made[:, 0:1] + made[:, 1:2]).astype(jnp.int32)
     gate = made[:, 5:6] + made[:, 6:7] + made[:, 7:8]
     return pick, jnp.where(filled, low, base), jnp.where(filled, high, base), gate
+
+
+def rows_of_block(rank_ref, table_ref, cap, block):
+    rows = table_ref.shape[1]
+    pick = (lax.broadcasted_iota(jnp.int32, (cap, rows), 0) == rank_ref[0]).astype(BF16)
+    made = contract_last(table_ref[...], pick)
+    filled = made[4:5] > 0.5
+    low = (64.0 * made[2:3] + made[3:4]).astype(jnp.int32)
+    high = (64.0 * made[0:1] + made[1:2]).astype(jnp.int32)
+    return pick, jnp.where(filled, low, block * rows), jnp.where(filled, high, block * rows)
 
 
 def token_table(position, document_start, gate):
@@ -148,7 +159,7 @@
     block = pl.program_id(1)
     cap, width = out_ref.shape
     tile_rows = q_ref.shape[0]
-    pick, low_bound, high_bound, gate = slots_of_block(rank_ref, table_ref, cap)
+    pick, low_bound, high_bound, gate = slots_of_block(rank_ref, table_ref, cap, block)
     q = dot(pick, q_ref[...]).astype(BF16)
 
     def step(tile, carried):
@@ -181,16 +192,18 @@
 
 def attention_backward_kernel(
     begin_ref, q_ref, k_ref, v_ref, rank_ref, table_ref, out_ref, lse_ref, grad_ref,
-    cos_ref, sin_ref, dq_ref, dk_ref, dv_ref, dk_sum, dv_sum, *, scaling
+    cos_ref, sin_ref, dq_ref, dk_ref, dv_ref, dk_sum, dv_sum, *, scaling, width
 ):
-    block = pl.program_id(1)
-    cap, width = out_ref.shape
+    block = pl.program_id(0)
+    cap = out_ref.shape[0]
     tile_rows = q_ref.shape[0]
-    pick, low_bound, high_bound, _ = slots_of_block(rank_ref, table_ref, cap)
-    q = dot(pick, q_ref[...]).astype(BF16)
-    grad = grad_ref[...]
-    delta = jnp.sum(grad.astype(F32) * out_ref[...].astype(F32), axis=1, keepdims=True)
-    lse = lse_ref[0]
+    heads = [slice(h * width, (h + 1) * width) for h in range(out_ref.shape[1] // width)]
+    pick, low_bound, high_bound = rows_of_block(rank_ref, table_ref, cap, block)
+    queries = dot(pick, q_ref[...]).astype(BF16)
+    grads = grad_ref[...]
+    product = grads.astype(F32) * out_ref[...].astype(F32)
+    ones = jnp.ones((8, width), F32)
+    deltas = [exact_last(ones, product[:, at])[:1] for at in heads]
 
     @pl.when(block == 0)
     def _():
@@ -198,32 +211,43 @@
         dv_sum[...] = jnp.zeros_like(dv_sum)
 
     def step(tile, dq):
-        rows, keys, scores, allowed = attention_scores(
-            q, k_ref, low_bound, high_bound, tile, tile_rows, scaling
-        )
-        chances = jnp.where(allowed, jnp.exp(scores - lse), 0.0)
-        dv_sum[rows, :] += contract_first(chances.astype(BF16), grad)
-        grad_chances = contract_last(grad, v_ref[rows, :])
-        grad_scores = (chances * (grad_chances - delta)).astype(BF16)
-        dk_sum[rows, :] += contract_first(grad_scores, q) * scaling
-        return dq + dot(grad_scores, keys)
-
-    dq = lax.fori_loop(begin_ref[block], block + 1, step, jnp.zeros((cap, width), F32)) * scaling
-    high = dq.astype(BF16)
-    rest = (dq - high.astype(F32)).astype(BF16)
-    dq_tokens = contract_first(pick, high) + contract_first(pick, rest)
+        rows = pl.ds(pl.multiple_of(tile * tile_rows, tile_rows), tile_rows)
+        position = tile * tile_rows + lax.broadcasted_iota(jnp.int32, (tile_rows, cap), 0)
+        allowed = (position >= low_bound) & (position <= high_bound)
+        made = []
+        for h, at in enumerate(heads):
+            q, grad, keys = queries[:, at], grads[:, at], k_ref[rows, at]
+            scores = contract_last(keys, q) * scaling
+            chances = jnp.where(allowed, jnp.exp(scores - lse_ref[h, 0]), 0.0)
+            dv_sum[rows, at] += dot(chances.astype(BF16), grad)
+            grad_chances = contract_last(v_ref[rows, at], grad)
+            grad_scores = (chances * (grad_chances - deltas[h])).astype(BF16)
+            dk_sum[rows, at] += dot(grad_scores, q) * scaling
+            made.append(dq[h] + contract_first(grad_scores, keys))
+        return tuple(made)
+
+    zero = jnp.zeros((cap, width), F32)
+    dq = lax.fori_loop(begin_ref[block], block + 1, step, (zero,) * len(heads))
     own = pl.ds(pl.multiple_of(block * tile_rows, tile_rows), tile_rows)
-    dq_ref[...] = turned(dq_tokens, cos_ref[own, :], -sin_ref[own, :]).astype(BF16)
+    for h, at in enumerate(heads):
+        scaled = dq[h] * scaling
+        high = scaled.astype(BF16)
+        rest = (scaled - high.astype(F32)).astype(BF16)
+        dq_tokens = contract_first(pick, high) + contract_first(pick, rest)
+        dq_ref[:, at] = turned(dq_tokens, cos_ref[own, :], -sin_ref[own, :]).astype(BF16)
 
     @pl.when(block == BLOCKS - 1)
     def _():
-        def finish(tile, nothing):
+        def finish_tile(tile, nothing):
             rows = pl.ds(pl.multiple_of(tile * tile_rows, tile_rows), tile_rows)
-            dk_ref[rows, :] = turned(dk_sum[rows, :], cos_ref[rows, :], -sin_ref[rows, :]).astype(BF16)
+            for at in heads:
+                dk_ref[rows, at] = turned(
+                    dk_sum[rows, at], cos_ref[rows, :], -sin_ref[rows, :]
+                ).astype(BF16)
             dv_ref[rows, :] = dv_sum[rows, :].astype(BF16)
             return nothing
 
-        lax.fori_loop(0, BLOCKS, finish, 0)
+        lax.fori_loop(0, BLOCKS, finish_tile, 0)
 
 
 def attention_specs(row_count, token_count, width):
@@ -234,7 +258,6 @@
         rows=pl.BlockSpec((16, row_count), lambda h, b, s: (0, b)),
         gate=pl.BlockSpec((CAP, 1), lambda h, b, s: (b, 0)),
         slots=pl.BlockSpec((CAP, width), lambda h, b, s: (b, h)),
-        table=pl.BlockSpec((token_count, width), lambda h, b, s: (0, 0)),
         lse=pl.BlockSpec((1, CAP, 1), lambda h, b, s: (h, b, 0)),
     )
 
@@ -263,29 +286,34 @@
 
 
 def attention_backward(begin, q, k, v, rank, table, out, lse, grad, cosine, sine, width):
-    token_count, heads = q.shape[0], q.shape[1] // width
+    token_count, span = q.shape
     row_count = token_count // BLOCKS
-    s = attention_specs(row_count, token_count, width)
+    block = lambda b, s: (b, 0)
+    whole = lambda b, s: (0, 0)
+    tokens = pl.BlockSpec((row_count, span), block)
+    keys = pl.BlockSpec((token_count, span), whole)
+    slots = pl.BlockSpec((CAP, span), block)
+    angles = pl.BlockSpec((token_count, width), whole)
+    rows = [
+        pl.BlockSpec((1, 1, row_count), lambda b, s: (b, 0, 0)),
+        pl.BlockSpec((16, row_count), lambda b, s: (0, b)),
+    ]
+    sums = pl.BlockSpec((span // width, 1, 1, CAP), lambda b, s: (0, b, 0, 0))
     return pl.pallas_call(
-        functools.partial(attention_backward_kernel, scaling=1.0 / math.sqrt(width)),
+        functools.partial(
+            attention_backward_kernel, scaling=1.0 / math.sqrt(width), width=width
+        ),
         grid_spec=pltpu.PrefetchScalarGridSpec(
             num_scalar_prefetch=1,
-            grid=(heads, BLOCKS),
-            in_specs=[
-                s["q"], s["k"], s["k"], s["rank"], s["rows"],
-                s["slots"], s["lse"], s["slots"], s["table"], s["table"],
-            ],
-            out_specs=[s["q"], s["k"], s["k"]],
-            scratch_shapes=[pltpu.VMEM((token_count, width), F32)] * 2,
+            grid=(BLOCKS,),
+            in_specs=[tokens, keys, keys] + rows + [slots, sums, slots, angles, angles],
+            out_specs=[tokens, keys, keys],
+            scratch_shapes=[pltpu.VMEM((token_count, span), F32)] * 2,
         ),
-        out_shape=[
-            jax.ShapeDtypeStruct((token_count, heads * width), BF16),
-            jax.ShapeDtypeStruct((token_count, heads * width), BF16),
-            jax.ShapeDtypeStruct((token_count, heads * width), BF16),
-        ],
+        out_shape=[jax.ShapeDtypeStruct((token_count, span), BF16)] * 3,
         compiler_params=pltpu.CompilerParams(vmem_limit_bytes=VMEM_BYTES),
         name="attention_backward",
-    )(begin, q, k, v, rank, table, out, lse, grad, cosine, sine)
+    )(begin, q, k, v, rank, table, out, lse.reshape(-1, BLOCKS, 1, CAP), grad, cosine, sine)
 
 
 def pack_up_kernel(weight_ref, pieces_ref):
@@ -1084,13 +1112,16 @@
 
 
 def expert_gradient_kernel(
-    rows_ref, grad_gate_up_ref, partial_ref, pieces_ref, up_grad_ref, out_ref, landed_ref, *scratch
+    rows_ref, grad_gate_up_ref, partial_ref, pieces_ref, up_first_ref, up_last_ref, out_ref,
+    landed_ref, *scratch
 ):
     ride = Ride(pieces_ref, landed_ref, *scratch[7:])
     steps = scatter_steps(partial_ref, out_ref, *scratch[:7], 1, ride.peers)
 
     def compute():
-        up_grad_ref[...] = contract_first(rows_ref[...], grad_gate_up_ref[...]).astype(BF16)
+        up_grad = contract_first(rows_ref[...], grad_gate_up_ref[...]).astype(BF16)
+        up_first_ref[...] = up_grad[:, :EARLY]
+        up_last_ref[...] = up_grad[:, EARLY:]
 
     def with_ride(number):
         steps[1 + number]()
@@ -1114,9 +1145,15 @@
             anywhere,
             anywhere,
         ],
-        out_specs=[pl.BlockSpec((tile, units), lambda b: (b, 0)), anywhere, anywhere],
+        out_specs=[
+            pl.BlockSpec((tile, EARLY), lambda b: (b, 0)),
+            pl.BlockSpec((tile, units - EARLY), lambda b: (b, 0)),
+            anywhere,
+            anywhere,
+        ],
         out_shape=[
-            jax.ShapeDtypeStruct((width, units), BF16),
+            jax.ShapeDtypeStruct((width, EARLY), BF16),
+            jax.ShapeDtypeStruct((width, units - EARLY), BF16),
             jax.ShapeDtypeStruct((PLANES, cap, width // 4), BF16),
             jax.ShapeDtypeStruct(pieces.shape, BF16),
         ],
@@ -1141,7 +1178,7 @@
             grad_ref[:, at] = contract_first(hidden, ref[...]).astype(BF16)
         grad_ref[:, 3 * span :] = contract_first(rows_ref[...], gated_ref[...]).astype(BF16)
 
-    carry(steps[:1], steps[1:], (1, 4, 7, 7, 7, 7, 7), compute)
+    carry(steps[:1], steps[1:], (1, 3, 6, 7, 7, 7, 7), compute)
 
 
 def closing(hidden, q, k, v, rows, gated, partial, collective_id):
@@ -1206,6 +1243,34 @@
         gain_second_ref[...] = total[1:2]
         router_first_ref[...] = total[2 : 2 + PLANES]
         router_second_ref[...] = total[2 + PLANES : 2 + 2 * PLANES]
+
+
+def unpack_up_kernel(first_ref, last_ref, grad_ref):
+    units = grad_ref.shape[3] // HALVES
+    halves = [
+        jnp.concatenate([first_ref[half], last_ref[half]], axis=1).astype(F32) for half in range(HALVES)
+    ]
+    for kind in range(2):
+        at = slice(kind * units, (kind + 1) * units)
+        grad_ref[0, :, kind, :] = jnp.concatenate([half[:, at] for half in halves], axis=1)
+
+
+def unpack_up(first, last):
+    places, own_rows, early = first.shape
+    units = early + last.shape[2]
+    tile = own_rows // 2
+    return pl.pallas_call(
+        unpack_up_kernel,
+        grid=(places // HALVES, 2),
+        in_specs=[
+            pl.BlockSpec((HALVES, tile, early), lambda e, r: (e, r, 0)),
+            pl.BlockSpec((HALVES, tile, units - early), lambda e, r: (e, r, 0)),
+        ],
+        out_specs=pl.BlockSpec((1, tile, 2, units), lambda e, r: (e, r, 0, 0)),
+        out_shape=jax.ShapeDtypeStruct((places // HALVES, own_rows, 2, units), F32),
+        compiler_params=pltpu.CompilerParams(vmem_limit_bytes=VMEM_BYTES),
+        name="unpack_up",
+    )(first, last)
 
 
 def swap_kernel(pieces_ref, landed_ref, *scratch):
@@ -1462,7 +1527,7 @@
         grad_down_first, grad_down_last = jnp.split(grad_down, 2, axis=1)
         landed = [exchanged(grad_down_first)]
     grad_down_first = landed[0]
-    grad_up, grad_rows, grad_down_last = expert_gradient(
+    grad_up_first, grad_up, grad_rows, grad_down_last = expert_gradient(
         slots_second.reshape(-1, width_all), grad_gate_up, grad_rows, grad_down_last, 6
     )
     branch_second = to_tokens(result_slots, own_pick_second)
@@ -1479,13 +1544,14 @@
     grad_normed = grad_hidden_second * gain_second
     grad_residual = grad_out + inverse_second * (grad_normed - normed_second * inner_mean)
 
+    grad_up_first = return_gradients(grad_up_first.reshape(groups, BLOCKS, own_rows, EARLY))
     grad_slots_first = gathered(to_slots(grad_residual.astype(BF16), own_pick_first), 8)
     (
-        grad_slots_first, residual, own_gates_second, branch_second, hidden_second,
+        grad_slots_first, grad_up_first, residual, own_gates_second, branch_second, hidden_second,
         grad_logits_second, grad_hidden_second, normed_second,
     ) = lax.optimization_barrier(
         (
-            grad_slots_first, residual, own_gates_second, branch_second, hidden_second,
+            grad_slots_first, grad_up_first, residual, own_gates_second, branch_second, hidden_second,
             grad_logits_second, grad_hidden_second, normed_second,
         )
     )
@@ -1495,7 +1561,7 @@
     grad_gain_second = jnp.sum(grad_hidden_second * normed_second, axis=0)
     grad_slots_first = grad_slots_first.reshape(BLOCKS * CAP, -1)
     grad_up, grad_slots_first = lax.optimization_barrier((grad_up, grad_slots_first))
-    grad_up = return_gradients(grad_up.reshape(groups, BLOCKS, own_rows, 2 * hidden_units))
+    grad_up = return_gradients(grad_up.reshape(groups, BLOCKS, own_rows, 2 * hidden_units - EARLY))
     grad_attended = gate_slots_first * dot(grad_slots_first, out_weight)
     grad_attended = grad_attended.astype(BF16)
     grad_query, grad_keys, grad_values = attention_backward(
@@ -1509,8 +1575,7 @@
     grad_hidden = jnp.sum(grad_hidden.astype(F32), axis=0)
     grad_first, grad_up = lax.optimization_barrier((grad_first, grad_up))
     grad_first = return_gradients(grad_first.reshape(groups, BLOCKS, own_rows, 4 * span))
-    expert_gate_up_grad = grad_up.reshape(PLANES, HALVES, own_rows, 2, hidden_units)
-    expert_gate_up_grad = expert_gate_up_grad.transpose(0, 2, 3, 1, 4).reshape(expert_gate_up.shape)
+    expert_gate_up_grad = unpack_up(grad_up_first, grad_up)
     expert_down_grad = jnp.concatenate([grad_down_first, grad_down_last], axis=1)
     expert_down_grad = expert_down_grad.swapaxes(1, 2).reshape(expert_down.shape)
 
@@ -1554,7 +1619,7 @@
         router_grad_first[:, :own_rows].T,
         gain_grad_second[0, :own_rows],
         router_grad_second[:, :own_rows].T,
-        expert_gate_up_grad.astype(F32),
+        expert_gate_up_grad,
         expert_down_grad.astype(F32),
     )
 

time: 1020 us -> 1010 us (level)
  local copies, waits for them, and re-layouts: 59.8 us -> 24.5 us
  waiting for transfers between devices: 9.19 us -> 38 us
    all_to_all x3 -> x4, waiting for transfers between devices: 9.19 us -> 38 us  [exchanged(): lax.all_to_all(row_major(pieces), PLACES, 0, 0, tiled=True)]
    pallas_call x1, Pallas kernels: 72.9 us -> 53.2 us  [attention_backward(): pl.pallas_call(functools.partial(attention_backward_kernel, scaling=1.0 /...]
    convert_element_type x2 -> x0, local copies, waits for them, and re-layouts: 18.9 us -> none  [per_device(): expert_gate_up_grad.astype(F32)]
    unnamed x49 -> x48, local copies, waits for them, and re-layouts: 22.4 us -> 5.32 us
  transfers between devices with their start and end apart: 3 -> 4, of which waited for: 1 -> 1; matrix products, arithmetic and copies ran while one was open for 13% -> 10% of each run, Pallas kernels for 40% -> 45%
where the time goes in v9:
time: 1010 us
  Pallas kernels  809 us (80%)
  matrix products  63.9 us (6%)
  waiting for transfers between devices  38 us (4%)
  other arithmetic  31.5 us (3%)
  local copies, waits for them, and re-layouts  24.5 us (2%)
  blocking collectives  21.3 us (2%)
  starting transfers between devices  18.6 us (2%)
    pallas_call x2, Pallas kernels, gathered(): pl.pallas_call(functools.partial(gather_kernel, same=slots.ndim == 2, sha...  135 us
    pallas_call x1, Pallas kernels, opened(): pl.pallas_call(functools.partial(opening_kernel, share=share), grid=(plac...  122 us
    pallas_call x1, Pallas kernels, scattered(): pl.pallas_call(functools.partial(scatter_kernel, share=share, rides=len(r...  93.9 us
    pallas_call x1, Pallas kernels, closing(): pl.pallas_call(closing_kernel, grid=(BLOCKS,), in_specs=[pl.BlockSpec((co...  87.5 us
    pallas_call x1, Pallas kernels, expert_backward(): pl.pallas_call(functools.partial(expert_backward_kernel, rides=rides), gr...  85.1 us
    pallas_call x1, Pallas kernels, expert_gradient(): pl.pallas_call(expert_gradient_kernel, grid=(BLOCKS,), in_specs=[pl.Block...  74.5 us
    pallas_call x1, Pallas kernels, expert_forward(): pl.pallas_call(expert_forward_kernel, grid=(BLOCKS,), in_specs=[pl.BlockS...  59.9 us
    pallas_call x1, Pallas kernels, attention_backward(): pl.pallas_call(functools.partial(attention_backward_kernel, scaling=1.0 /...  53.2 us
  transfers between devices with their start and end apart: 4, of which 1 were waited for; matrix products, arithmetic and copies ran while one was open for 10% of the time, Pallas kernels for 45%

profile of v9, /device:TPU:0, one launch (start us, length us, event | category | flops | bytes accessed | tf_op | source)
XLA Modules:
  0.0 1008.6 jit_solution(14809149470531336451)
XLA Ops:
  0.7 0.7 broadcast_in_dim.79
  2.1 0.7 convert.12
  3.4 1.1 copy.80
  5.0 0.7 reshape.345
  5.9 1.5 copy.78
  7.5 0.8 fusion.42.tokens_ref
  8.7 2.6 pad_maximum_fusion.pieces_ref
  11.3 122.2 %open_rows.1 = (bf16[4,2,528,2048]{3,2,1,0:T(8,128)(2,1)}, bf16[8,256,1024]{2,1,0:T(8,128)(2,1)}, bf16[8,256,1408]{2,1,0:T(8,128)(2,1)}, bf16[8,128,704]{2,1,0:T(8,128)(2,1)}, bf16[8,128,704]{2,1,0:T(8,128)(2,1)}) custom-call(bf16[528,512]{1,0:T(8,128)(2,1)} %fusion.42.tokens_ref, bf16[8,256,1024]{2,1,0:T(8,128)(2,1)} %pad_maximum_fusion.pieces_ref, ...), custom_call_target="tpu_custom_call" | custom-call | tf_op jit(solution)/shard_map/open_rows/pallas_call | solution.py:702
  133.6 5.0 all-to-all-start
  139.4 1.1 slice.125
  141.4 1.1 convert_element_type.152
  144.7 27.2 %project.1 = (bf16[4096,2048]{1,0:T(8,128)(2,1)}, bf16[4096,256]{1,0:T(8,128)(2,1)}, bf16[4096,256]{1,0:T(8,128)(2,1)}, bf16[4096,256]{1,0:T(8,128)(2,1)}, f32[16,4096]{1,0:T(8,128)}, /*index=5*/f32[4096,1]{1,0:T(8,128)}) custom-call(bf16[4,2,528,2048]{3,2,1,0:T(8,128)(2,1)} %get-tuple-element.74.tokens_ref, bf16[16,2048]{1,0:T(8,128)(2,1)} %pad.24.small_ref, ...), custom_call_target="tpu_custom_call" | custom-call | tf_op jit(solution)/shard_map/project/pallas_call | solution.py:82
  171.9 1.0 fusion.54
  172.9 1.0 fusion.68
  174.0 1.0 broadcast_divide_fusion
  176.7 43.4 %attention_forward.1 = (bf16[2560,256]{1,0:T(8,128)(2,1)}, bf16[2560,256]{1,0:T(8,128)(2,1)}, f32[2560,1]{1,0:T(8,128)}, f32[2,2560,1]{2,1,0:T(8,128)}) custom-call(s32[8]{0:T(128)} %and_select_fusion.4.begin_ref, bf16[4096,256]{1,0:T(8,128)(2,1)} %get-tuple-element.77.q_ref, bf16[4096,256]{1,0:T(8,128)(2,1)} %get-tuple-element.78.k_ref, ...), custom_call_target="tpu_custom_call" | custom-call | tf_op jit(solution)/shard_map/attention_forward/pallas_call | solution.py:269
  220.1 1.9 fusion.14.grad_ref
  222.0 6.9 convolution_convert_fusion.1
  228.8 93.9 %scatter_rows.1 = (bf16[4,320,512]{2,1,0:T(8,128)(2,1)}, bf16[8,128,704]{2,1,0:T(8,128)(2,1)}) custom-call(bf16[4,2,320,2048]{3,2,1,0:T(8,128)(2,1)} %bitcast.153, bf16[8,128,704]{2,1,0:T(8,128)(2,1)} %get-tuple-element.82.refs_1_), custom_call_target="tpu_custom_call" | custom-call | tf_op jit(solution)/shard_map/scatter_rows/pallas_call | solution.py:898
  322.8 4.8 multiply_reduce_fusion.3
  327.8 5.2 all_gather.8
  333.1 1.9 fusion.15.refs_0_
  335.1 81.5 %gather_rows.2 = (bf16[4,2,320,2048]{3,2,1,0:T(8,128)(2,1)}, bf16[8,128,704]{2,1,0:T(8,128)(2,1)}) custom-call(bf16[4,320,512]{2,1,0:T(8,128)(2,1)} %fusion.15.refs_0_, bf16[8,128,704]{2,1,0:T(8,128)(2,1)} %get-tuple-element.84.refs_1_), custom_call_target="tpu_custom_call" | custom-call | tf_op jit(solution)/shard_map/gather_rows/pallas_call | solution.py:757
  417.4 0.7 pad_convert_fusion.member_ref
  418.1 59.9 %expert_forward.1 = (f32[2560,704]{1,0:T(8,128)}, f32[2560,704]{1,0:T(8,128)}, bf16[8,320,2048]{2,1,0:T(8,128)(2,1)}, f32[2560,1]{1,0:T(8,128)}, bf16[2560,704]{...) custom-call(bf16[8,320,2048]{2,1,0:T(8,128)(2,1)} %bitcast.154, bf16[2048,1408]{1,0:T(8,128)(2,1)} %bitcast.31.up_weight_ref, ...), custom_call_target="tpu_custom_call" | custom-call | tf_op jit(solution)/shard_map/expert_forward/pallas_call | solution.py:985
  478.0 85.1 %expert_backward.1 = (bf16[8,320,2048]{2,1,0:T(8,128)(2,1)}, bf16[2560,1408]{1,0:T(8,128)(2,1)}, bf16[8,128,704]{2,1,0:T(8,128)(2,1)}, bf16[8,128,704]{2,1,0:T(8...) custom-call(f32[2560,704]{1,0:T(8,128)} %get-tuple-element.90.slope_ref, ...), custom_call_target="tpu_custom_call" | custom-call | tf_op jit(solution)/shard_map/expert_backward/pallas_call | solution.py:1073
  563.1 74.5 %expert_gradient.1 = (bf16[2048,128]{1,0:T(8,128)(2,1)}, bf16[2048,1280]{1,0:T(8,128)(2,1)}, bf16[4,320,512]{2,1,0:T(8,128)(2,1)}, bf16[8,128,704]{2,1,0:T(8,128)(2,1)}) custom-call(bf16[2560,2048]{1,0:T(8,128)(2,1)} %bitcast.155, bf16[2560,1408]{1,0:T(8,128)(2,1)} %get-tuple-element.96.grad_gate_up_ref, bf16[4,2,320,2048]{3,2,1,0:T(8,128)(2,1)} %bitcast.167, ...), custom_call_target="tpu_custom_call" | custom-call | tf_op jit(solution)/shard_map/expert_gradient/pallas_call | solution.py:1139
  637.6 3.3 multiply_reduce_fusion.5
  640.9 4.2 all-to-all-start.1
  645.1 4.7 multiply_reduce_fusion.2
  649.8 5.4 all_gather.9
  655.4 3.2 multiply_add_fusion
  658.6 1.9 fusion.13.refs_0_
  660.5 54.0 %gather_rows.3 = bf16[4,2,320,2048]{3,2,1,0:T(8,128)(2,1)} custom-call(bf16[4,320,512]{2,1,0:T(8,128)(2,1)} %fusion.13.refs_0_), custom_call_target="tpu_custom_call" | custom-call | tf_op jit(solution)/shard_map/gather_rows/pallas_call | solution.py:757
  714.5 4.7 all-to-all-start.2
  719.1 2.5 reduce.3
  721.7 1.7 reduce.4
  723.4 0.7 reshape.372.lse_ref
  724.1 8.2 fusion.5.grad_ref
  732.3 53.2 %attention_backward.1 = (bf16[4096,256]{1,0:T(8,128)(2,1)}, bf16[4096,256]{1,0:T(8,128)(2,1)}, bf16[4096,256]{1,0:T(8,128)(2,1)}) custom-call(s32[8]{0:T(128)} %and_select_fusion.4.begin_ref, bf16[4096,256]{1,0:T(8,128)(2,1)} %get-tuple-element.77.q_ref, bf16[4096,256]{1,0:T(8,128)(2,1)} %get-tuple-element.78.k_ref, ...), custom_call_target="tpu_custom_call" | custom-call | tf_op jit(solution)/shard_map/attention_backward/pallas_call | solution.py:302
  785.5 20.4 %convolution_convert_fusion = bf16[4096,2048]{1,0:T(8,128)(2,1)} fusion(bf16[4096,256]{1,0:T(8,128)(2,1)} %get-tuple-element.114.v_ref, bf16[4096,256]{1,0:T(8,128)(2,1)} %get-tuple-element.113.k_ref, bf16[4096,256]{1,0:T(8,128)(2,1)} %get-tuple-element.112.q_ref, bf16[2048,1024]{1,0:T(8,128)(2,1)} %bitcast.164), kind=kOutput, calls=%fused_computation | convolution fusion | flops 12912164864 | bytes 26214400 | tf_op jit(solution)/shard_map/dot_general | solution.py:49
  805.8 87.5 %closing.1 = (bf16[2048,1024]{1,0:T(8,128)(2,1)}, bf16[4,512,512]{2,1,0:T(8,128)(2,1)}) custom-call(bf16[4096,2048]{1,0:T(8,128)(2,1)} %get-tuple-element.106.hidden_ref, bf16[4096,256]{1,0:T(8,128)(2,1)} %get-tuple-element.112.q_ref, bf16[4096,256]{1,0:T(8,128)(2,1)} %get-tuple-element.113.k_ref, bf16[4096,256]{1,0:T(8,128)(2,1)} %get-tuple-element.114.v_ref, ...), custom_call_target="tpu_custom_call" | custom-call | tf_op jit(solution)/shard_map/closing/pallas_call | solution.py:1189
  893.3 4.8 all-to-all-start.3
  898.2 1.1 dynamic-slice_reduce_fusion
  899.3 1.6 fusion.22
  901.0 5.2 convert_bitcast_fusion
  906.1 6.4 copy.97
  912.5 3.0 multiply_reduce_fusion
  916.5 1.0 add_convert_fusion
  917.5 2.0 copy.98
  919.5 3.0 convert_reduce_fusion
  922.5 1.6 copy.94
  924.0 1.2 fusion.32
  925.3 5.3 all_gather.10
  930.7 1.5 multiply_reduce_fusion.4
  932.2 1.5 fusion.91
  933.7 1.6 fusion.43
  935.4 1.0 fusion.37
  936.4 5.4 all_gather.11
  942.6 1.0 copy.99
  943.6 9.6 unpack_up.1
  953.2 38.0 %all-to-all-done.3.query_ref.all_ref = bf16[8,256,1024]{2,1,0:T(8,128)(2,1)} async-done(((bf16[8,256,1024]{2,1,0:T(8,128)(2,1)}), bf16[8,256,1024]{2,1,0:T(8,128)(2,1)}, u32[]{:S(2)}, u32[]{:S(2)}) %all-to-all-start.3) | async-done | bytes 4194336 | tf_op jit(solution)/shard_map/all_to_all | solution.py:340
  991.2 9.0 swap_small.1.small_ref
  1000.3 8.1 attention_weight_gradients.1
  (128 shorter events, 11.1 us)
Async XLA Ops:
  0.6 4.3 copy-start.8
  5.0 2.4 copy-start.11
  5.0 2.4 copy-start.12
  5.0 2.4 copy-start.7
  133.5 5.1 copy-start.10
  133.5 7.6 copy-start.9
  133.6 284.5 %all-to-all-start = ((bf16[8,256,1408]{2,1,0:T(8,128)(2,1)}), bf16[8,256,1408]{2,1,0:T(8,128)(2,1)}, u32[]{:S(2)}, u32[]{:S(2)}) async-start(bf16[8,256,1408]{2,1,0:T(8,128)(2,1)} %get-tuple-element.86), calls=%async_computation | async-start | bytes 11534336 | tf_op jit(solution)/shard_map/all_to_all | solution.py:340
  139.3 188.2 %copy-start.1 = (bf16[512,512]{0,1:T(8,128)(2,1)}, bf16[512,512]{0,1:T(8,128)(2,1)S(1)}, u32[]{:S(2)}) copy-start(bf16[512,512]{0,1:T(8,128)(2,1)S(1)} %copy.85) | copy-start | bytes 1572868
  141.3 30.6 %copy-start.4 = (bf16[512,512]{0,1:T(8,128)(2,1)}, bf16[512,512]{0,1:T(8,128)(2,1)S(1)}, u32[]{:S(2)}) copy-start(bf16[512,512]{0,1:T(8,128)(2,1)S(1)} %copy.84) | copy-start | bytes 1572868
  220.0 1.9 copy-start.3
  333.1 83.5 %copy-start.5 = (bf16[512,512]{0,1:T(8,128)(2,1)}, bf16[512,512]{0,1:T(8,128)(2,1)S(1)}, u32[]{:S(2)}) copy-start(bf16[512,512]{0,1:T(8,128)(2,1)S(1)} %get-tuple-element.120) | copy-start | bytes 1572868
  637.6 7.5 copy-start.6
  640.9 73.6 %all-to-all-start.1 = ((bf16[8,256,128]{2,1,0:T(8,128)(2,1)}), bf16[8,256,128]{2,1,0:T(8,128)(2,1)}, u32[]{:S(2)}, u32[]{:S(2)}) async-start(bf16[8,256,128]{2,1,0:T(8,128)(2,1)} %bitcast.179), calls=%async_computation.1 | async-start | bytes 1048576 | tf_op jit(solution)/shard_map/all_to_all | solution.py:340
  714.5 178.9 %all-to-all-start.2 = ((bf16[8,256,1280]{2,1,0:T(8,128)(2,1)}), bf16[8,256,1280]{2,1,0:T(8,128)(2,1)}, u32[]{:S(2)}, u32[]{:S(2)}) async-start(bf16[8,256,1280]{2,1,0:T(8,128)(2,1)} %bitcast.170), calls=%async_computation.2 | async-start | bytes 10485760 | tf_op jit(solution)/shard_map/all_to_all | solution.py:340
  893.3 97.9 %all-to-all-start.3 = ((bf16[8,256,1024]{2,1,0:T(8,128)(2,1)}), bf16[8,256,1024]{2,1,0:T(8,128)(2,1)}, u32[]{:S(2)}, u32[]{:S(2)}) async-start(bf16[8,256,1024]{2,1,0:T(8,128)(2,1)} %bitcast.171), calls=%async_computation.3 | async-start | bytes 8388608 | tf_op jit(solution)/shard_map/all_to_all | solution.py:340
  912.5 3.4 copy-start
  930.7 4.7 copy-start.2

commit v10 on v9

--- a/solution.py
+++ b/solution.py
@@ -313,7 +313,7 @@
         out_shape=[jax.ShapeDtypeStruct((token_count, span), BF16)] * 3,
         compiler_params=pltpu.CompilerParams(vmem_limit_bytes=VMEM_BYTES),
         name="attention_backward",
-    )(begin, q, k, v, rank, table, out, lse.reshape(-1, BLOCKS, 1, CAP), grad, cosine, sine)
+    )(begin, q, k, v, rank, table, out, lse, grad, cosine, sine)
 
 
 def pack_up_kernel(weight_ref, pieces_ref):
@@ -1128,7 +1128,7 @@
         ride.go_on(number)
 
     after = [functools.partial(with_ride, number) for number in range(6)]
-    carry([steps[0], ride.begin], after + [steps[-1], ride.finish], (0, 2, 4, 6, 7, 7, 7, 7), compute)
+    carry([steps[0], ride.begin], after + [steps[-1], ride.finish], (0, 1, 3, 5, 6, 7, 7, 7), compute)
 
 
 def expert_gradient(rows, grad_gate_up, partial, pieces, collective_id):
@@ -1486,8 +1486,12 @@
     )
     attention_args = (begin, queries, keys, values, rank_first, table)
     attended, gated, gate_slots_first, lse = attention_forward(*attention_args, head_width)
-    branch, grad_out_slots = lax.optimization_barrier(
-        (contract_last(attended, out_weight).astype(BF16), to_slots(output_grad, own_pick_second))
+    branch, grad_out_slots, lse = lax.optimization_barrier(
+        (
+            contract_last(attended, out_weight).astype(BF16),
+            to_slots(output_grad, own_pick_second),
+            lse.reshape(-1, BLOCKS, 1, CAP),
+        )
     )
     branch_slots, down_first = scattered(
         branch, CAP, 2, ride=down_halves[0], share=1
@@ -1577,7 +1581,7 @@
     grad_first = return_gradients(grad_first.reshape(groups, BLOCKS, own_rows, 4 * span))
     expert_gate_up_grad = unpack_up(grad_up_first, grad_up)
     expert_down_grad = jnp.concatenate([grad_down_first, grad_down_last], axis=1)
-    expert_down_grad = expert_down_grad.swapaxes(1, 2).reshape(expert_down.shape)
+    expert_down_grad = expert_down_grad.astype(F32).swapaxes(1, 2).reshape(expert_down.shape)
 
     own_normed = tokens.astype(F32) * own(inverse_first)
     own_hidden = (own_normed * gain_first).astype(BF16)
@@ -1601,7 +1605,9 @@
     small_grads = small_grads.reshape(-1, groups, BLOCKS, own_rows)
     small_grads = lax.dynamic_index_in_dim(small_grads, group, 1, keepdims=False).swapaxes(0, 1)
     small_grads = jnp.pad(small_grads, ((0, 0), (0, 6), (0, -own_rows % 128)))
-    small_grads, grad_first = lax.optimization_barrier((small_grads, grad_first))
+    small_grads, expert_gate_up_grad, expert_down_grad = lax.optimization_barrier(
+        (small_grads, expert_gate_up_grad, expert_down_grad)
+    )
     (
         attention_query_grad, attention_kv_grad, attention_out_grad, gain_grad_first,
         gain_grad_second, router_grad_first, router_grad_second,
@@ -1620,7 +1626,7 @@
         gain_grad_second[0, :own_rows],
         router_grad_second[:, :own_rows].T,
         expert_gate_up_grad,
-        expert_down_grad.astype(F32),
+        expert_down_grad,
     )
 
 

time: 1010 us -> 1010 us (level)
  waiting for transfers between devices: 38 us -> 0.01 us
  Pallas kernels: 809 us -> 837 us
    all_to_all x4, waiting for transfers between devices: 38 us -> 0.01 us  [exchanged(): lax.all_to_all(row_major(pieces), PLACES, 0, 0, tiled=True)]
    pallas_call x1, Pallas kernels: 9.04 us -> 42.2 us  [swapped(): pl.pallas_call(swap_kernel, out_shape=jax.ShapeDtypeStruct(pieces.shape,...]
  transfers between devices with their start and end apart: 4 -> 4, of which waited for: 1 -> 0; matrix products, arithmetic and copies ran while one was open for 10% -> 11% of each run, Pallas kernels for 45% -> 49%
where the time goes in v10:
time: 1010 us; the launch traced here: 1000 us
  Pallas kernels  837 us (83%)
  matrix products  63.9 us (6%)
  other arithmetic  31.6 us (3%)
  local copies, waits for them, and re-layouts  24.5 us (2%)
  blocking collectives  21.7 us (2%)
  starting transfers between devices  20 us (2%)
    pallas_call x2, Pallas kernels, gathered(): pl.pallas_call(functools.partial(gather_kernel, same=slots.ndim == 2, sha...  132 us
    pallas_call x1, Pallas kernels, opened(): pl.pallas_call(functools.partial(opening_kernel, share=share), grid=(plac...  122 us
    pallas_call x1, Pallas kernels, scattered(): pl.pallas_call(functools.partial(scatter_kernel, share=share, rides=len(r...  92.7 us
    pallas_call x1, Pallas kernels, closing(): pl.pallas_call(closing_kernel, grid=(BLOCKS,), in_specs=[pl.BlockSpec((co...  90.2 us
    pallas_call x1, Pallas kernels, expert_backward(): pl.pallas_call(functools.partial(expert_backward_kernel, rides=rides), gr...  85.1 us
    pallas_call x1, Pallas kernels, expert_gradient(): pl.pallas_call(expert_gradient_kernel, grid=(BLOCKS,), in_specs=[pl.Block...  72.1 us
    pallas_call x1, Pallas kernels, expert_forward(): pl.pallas_call(expert_forward_kernel, grid=(BLOCKS,), in_specs=[pl.BlockS...  59.5 us
    pallas_call x1, Pallas kernels, attention_backward(): pl.pallas_call(functools.partial(attention_backward_kernel, scaling=1.0 /...  53.2 us
  transfers between devices with their start and end apart: 4, of which 0 were waited for; matrix products, arithmetic and copies ran while one was open for 11% of the time, Pallas kernels for 49%

profile of v10, /device:TPU:0, one launch (start us, length us, event | category | flops | bytes accessed | tf_op | source)
XLA Modules:
  0.0 1000.4 jit_solution(4914570890271152329)
XLA Ops:
  0.7 0.7 broadcast_in_dim.79
  2.1 0.7 convert.12
  2.7 0.7 convert.13
  3.4 1.1 copy.80
  5.0 0.7 reshape.348
  5.9 1.5 copy.78
  7.5 0.8 fusion.42.tokens_ref
  8.7 2.6 pad_maximum_fusion.pieces_ref
  11.3 122.2 %open_rows.1 = (bf16[4,2,528,2048]{3,2,1,0:T(8,128)(2,1)}, bf16[8,256,1024]{2,1,0:T(8,128)(2,1)}, bf16[8,256,1408]{2,1,0:T(8,128)(2,1)}, bf16[8,128,704]{2,1,0:T(8,128)(2,1)}, bf16[8,128,704]{2,1,0:T(8,128)(2,1)}) custom-call(bf16[528,512]{1,0:T(8,128)(2,1)} %fusion.42.tokens_ref, bf16[8,256,1024]{2,1,0:T(8,128)(2,1)} %pad_maximum_fusion.pieces_ref, ...), custom_call_target="tpu_custom_call" | custom-call | tf_op jit(solution)/shard_map/open_rows/pallas_call | solution.py:702
  133.6 5.0 all-to-all-start
  139.4 1.1 slice.125
  141.4 1.1 convert_element_type.144
  144.7 27.2 %project.1 = (bf16[4096,2048]{1,0:T(8,128)(2,1)}, bf16[4096,256]{1,0:T(8,128)(2,1)}, bf16[4096,256]{1,0:T(8,128)(2,1)}, bf16[4096,256]{1,0:T(8,128)(2,1)}, f32[16,4096]{1,0:T(8,128)}, /*index=5*/f32[4096,1]{1,0:T(8,128)}) custom-call(bf16[4,2,528,2048]{3,2,1,0:T(8,128)(2,1)} %get-tuple-element.76.tokens_ref, bf16[16,2048]{1,0:T(8,128)(2,1)} %pad.24.small_ref, ...), custom_call_target="tpu_custom_call" | custom-call | tf_op jit(solution)/shard_map/project/pallas_call | solution.py:82
  171.9 1.0 fusion.54
  172.9 1.0 fusion.68
  174.0 1.0 broadcast_divide_fusion
  176.7 43.4 %attention_forward.1 = (bf16[2560,256]{1,0:T(8,128)(2,1)}, bf16[2560,256]{1,0:T(8,128)(2,1)}, f32[2560,1]{1,0:T(8,128)}, f32[2,2560,1]{2,1,0:T(8,128)}) custom-call(s32[8]{0:T(128)} %and_select_fusion.4.begin_ref, bf16[4096,256]{1,0:T(8,128)(2,1)} %get-tuple-element.79.q_ref, bf16[4096,256]{1,0:T(8,128)(2,1)} %get-tuple-element.80.k_ref, ...), custom_call_target="tpu_custom_call" | custom-call | tf_op jit(solution)/shard_map/attention_forward/pallas_call | solution.py:269
  220.1 2.6 reduce.2
  222.7 1.9 fusion.14.grad_ref
  224.7 6.9 convolution_convert_fusion.1
  231.5 92.7 %scatter_rows.1 = (bf16[4,320,512]{2,1,0:T(8,128)(2,1)}, bf16[8,128,704]{2,1,0:T(8,128)(2,1)}) custom-call(bf16[4,2,320,2048]{3,2,1,0:T(8,128)(2,1)} %bitcast.153, bf16[8,128,704]{2,1,0:T(8,128)(2,1)} %get-tuple-element.85.refs_1_), custom_call_target="tpu_custom_call" | custom-call | tf_op jit(solution)/shard_map/scatter_rows/pallas_call | solution.py:898
  324.3 4.8 multiply_reduce_fusion.3
  329.3 5.6 all_gather.8
  335.0 1.9 fusion.15.refs_0_
  337.0 79.4 %gather_rows.2 = (bf16[4,2,320,2048]{3,2,1,0:T(8,128)(2,1)}, bf16[8,128,704]{2,1,0:T(8,128)(2,1)}) custom-call(bf16[4,320,512]{2,1,0:T(8,128)(2,1)} %fusion.15.refs_0_, bf16[8,128,704]{2,1,0:T(8,128)(2,1)} %get-tuple-element.87.refs_1_), custom_call_target="tpu_custom_call" | custom-call | tf_op jit(solution)/shard_map/gather_rows/pallas_call | solution.py:757
  417.2 0.7 pad_convert_fusion.member_ref
  417.9 59.5 %expert_forward.1 = (f32[2560,704]{1,0:T(8,128)}, f32[2560,704]{1,0:T(8,128)}, bf16[8,320,2048]{2,1,0:T(8,128)(2,1)}, f32[2560,1]{1,0:T(8,128)}, bf16[2560,704]{...) custom-call(bf16[8,320,2048]{2,1,0:T(8,128)(2,1)} %bitcast.154, bf16[2048,1408]{1,0:T(8,128)(2,1)} %bitcast.31.up_weight_ref, ...), custom_call_target="tpu_custom_call" | custom-call | tf_op jit(solution)/shard_map/expert_forward/pallas_call | solution.py:985
  477.4 85.1 %expert_backward.1 = (bf16[8,320,2048]{2,1,0:T(8,128)(2,1)}, bf16[2560,1408]{1,0:T(8,128)(2,1)}, bf16[8,128,704]{2,1,0:T(8,128)(2,1)}, bf16[8,128,704]{2,1,0:T(8...) custom-call(f32[2560,704]{1,0:T(8,128)} %get-tuple-element.93.slope_ref, ...), custom_call_target="tpu_custom_call" | custom-call | tf_op jit(solution)/shard_map/expert_backward/pallas_call | solution.py:1073
  562.5 72.1 %expert_gradient.1 = (bf16[2048,128]{1,0:T(8,128)(2,1)}, bf16[2048,1280]{1,0:T(8,128)(2,1)}, bf16[4,320,512]{2,1,0:T(8,128)(2,1)}, bf16[8,128,704]{2,1,0:T(8,128)(2,1)}) custom-call(bf16[2560,2048]{1,0:T(8,128)(2,1)} %bitcast.155, bf16[2560,1408]{1,0:T(8,128)(2,1)} %get-tuple-element.99.grad_gate_up_ref, bf16[4,2,320,2048]{3,2,1,0:T(8,128)(2,1)} %bitcast.167, ...), custom_call_target="tpu_custom_call" | custom-call | tf_op jit(solution)/shard_map/expert_gradient/pallas_call | solution.py:1139
  634.6 3.3 multiply_reduce_fusion.5
  637.9 5.5 all-to-all-start.1
  643.4 4.7 multiply_reduce_fusion.2
  648.1 5.4 all_gather.9
  653.7 3.2 multiply_add_fusion
  656.8 1.9 fusion.13.refs_0_
  658.8 52.2 %gather_rows.3 = bf16[4,2,320,2048]{3,2,1,0:T(8,128)(2,1)} custom-call(bf16[4,320,512]{2,1,0:T(8,128)(2,1)} %fusion.13.refs_0_), custom_call_target="tpu_custom_call" | custom-call | tf_op jit(solution)/shard_map/gather_rows/pallas_call | solution.py:757
  711.0 4.7 all-to-all-start.2
  715.6 1.7 reduce.4
  718.0 8.2 fusion.5.grad_ref
  726.2 53.2 %attention_backward.1 = (bf16[4096,256]{1,0:T(8,128)(2,1)}, bf16[4096,256]{1,0:T(8,128)(2,1)}, bf16[4096,256]{1,0:T(8,128)(2,1)}) custom-call(s32[8]{0:T(128)} %and_select_fusion.4.begin_ref, bf16[4096,256]{1,0:T(8,128)(2,1)} %get-tuple-element.79.q_ref, bf16[4096,256]{1,0:T(8,128)(2,1)} %get-tuple-element.80.k_ref, ...), custom_call_target="tpu_custom_call" | custom-call | tf_op jit(solution)/shard_map/attention_backward/pallas_call | solution.py:302
  779.4 20.4 %convolution_convert_fusion = bf16[4096,2048]{1,0:T(8,128)(2,1)} fusion(bf16[4096,256]{1,0:T(8,128)(2,1)} %get-tuple-element.117.v_ref, bf16[4096,256]{1,0:T(8,128)(2,1)} %get-tuple-element.116.k_ref, bf16[4096,256]{1,0:T(8,128)(2,1)} %get-tuple-element.115.q_ref, bf16[2048,1024]{1,0:T(8,128)(2,1)} %bitcast.164), kind=kOutput, calls=%fused_computation | convolution fusion | flops 12912164864 | bytes 26214400 | tf_op jit(solution)/shard_map/dot_general | solution.py:49
  799.8 90.2 %closing.1 = (bf16[2048,1024]{1,0:T(8,128)(2,1)}, bf16[4,512,512]{2,1,0:T(8,128)(2,1)}) custom-call(bf16[4096,2048]{1,0:T(8,128)(2,1)} %get-tuple-element.109.hidden_ref, bf16[4096,256]{1,0:T(8,128)(2,1)} %get-tuple-element.115.q_ref, bf16[4096,256]{1,0:T(8,128)(2,1)} %get-tuple-element.116.k_ref, bf16[4096,256]{1,0:T(8,128)(2,1)} %get-tuple-element.117.v_ref, ...), custom_call_target="tpu_custom_call" | custom-call | tf_op jit(solution)/shard_map/closing/pallas_call | solution.py:1189
  890.0 4.8 all-to-all-start.3
  894.8 1.1 dynamic-slice_reduce_fusion
  895.9 1.6 fusion.22
  897.6 5.2 convert_bitcast_fusion
  902.7 6.4 copy.97
  909.1 3.0 multiply_reduce_fusion
  913.1 1.0 add_convert_fusion
  914.1 2.0 copy.98
  916.1 3.0 convert_reduce_fusion
  919.1 1.6 copy.94
  920.7 1.2 fusion.32
  921.9 5.3 all_gather.10
  927.3 1.5 multiply_reduce_fusion.4
  928.8 1.5 fusion.91
  930.4 1.6 fusion.43
  932.0 1.0 fusion.37
  933.0 5.4 all_gather.11
  938.6 0.7 pad.28.pieces_ref
  939.2 1.0 copy.99
  940.2 9.6 unpack_up.1
  949.8 42.2 %swap_small.1.small_ref = f32[8,16,256]{2,1,0:T(8,128)} custom-call(f32[8,16,256]{2,1,0:T(8,128)} %pad.28.pieces_ref), custom_call_target="tpu_custom_call" | custom-call | tf_op jit(solution)/shard_map/swap_small/pallas_call | solution.py:1285
  992.0 8.1 attention_weight_gradients.1
  (129 shorter events, 10.5 us)
Async XLA Ops:
  0.6 4.3 copy-start.8
  5.0 2.4 copy-start.11
  5.0 2.4 copy-start.12
  5.0 2.4 copy-start.7
  133.5 5.1 copy-start.10
  133.5 7.6 copy-start.9
  133.6 284.4 %all-to-all-start = ((bf16[8,256,1408]{2,1,0:T(8,128)(2,1)}), bf16[8,256,1408]{2,1,0:T(8,128)(2,1)}, u32[]{:S(2)}, u32[]{:S(2)}) async-start(bf16[8,256,1408]{2,1,0:T(8,128)(2,1)} %get-tuple-element.89), calls=%async_computation | async-start | bytes 11534336 | tf_op jit(solution)/shard_map/all_to_all | solution.py:340
  139.3 189.7 %copy-start.1 = (bf16[512,512]{0,1:T(8,128)(2,1)}, bf16[512,512]{0,1:T(8,128)(2,1)S(1)}, u32[]{:S(2)}) copy-start(bf16[512,512]{0,1:T(8,128)(2,1)S(1)} %copy.85) | copy-start | bytes 1572868
  141.3 30.6 %copy-start.4 = (bf16[512,512]{0,1:T(8,128)(2,1)}, bf16[512,512]{0,1:T(8,128)(2,1)S(1)}, u32[]{:S(2)}) copy-start(bf16[512,512]{0,1:T(8,128)(2,1)S(1)} %copy.84) | copy-start | bytes 1572868
  220.0 4.6 copy-start.3
  335.0 81.4 %copy-start.5 = (bf16[512,512]{0,1:T(8,128)(2,1)}, bf16[512,512]{0,1:T(8,128)(2,1)S(1)}, u32[]{:S(2)}) copy-start(bf16[512,512]{0,1:T(8,128)(2,1)S(1)} %get-tuple-element.126) | copy-start | bytes 1572868
  634.6 8.8 copy-start.6
  637.9 73.1 %all-to-all-start.1 = ((bf16[8,256,128]{2,1,0:T(8,128)(2,1)}), bf16[8,256,128]{2,1,0:T(8,128)(2,1)}, u32[]{:S(2)}, u32[]{:S(2)}) async-start(bf16[8,256,128]{2,1,0:T(8,128)(2,1)} %bitcast.179), calls=%async_computation.1 | async-start | bytes 1048576 | tf_op jit(solution)/shard_map/all_to_all | solution.py:340
  711.0 179.0 %all-to-all-start.2 = ((bf16[8,256,1280]{2,1,0:T(8,128)(2,1)}), bf16[8,256,1280]{2,1,0:T(8,128)(2,1)}, u32[]{:S(2)}, u32[]{:S(2)}) async-start(bf16[8,256,1280]{2,1,0:T(8,128)(2,1)} %bitcast.170), calls=%async_computation.2 | async-start | bytes 10485760 | tf_op jit(solution)/shard_map/all_to_all | solution.py:340
  890.0 102.1 %all-to-all-start.3 = ((bf16[8,256,1024]{2,1,0:T(8,128)(2,1)}), bf16[8,256,1024]{2,1,0:T(8,128)(2,1)}, u32[]{:S(2)}, u32[]{:S(2)}) async-start(bf16[8,256,1024]{2,1,0:T(8,128)(2,1)} %bitcast.171), calls=%async_computation.3 | async-start | bytes 8388608 | tf_op jit(solution)/shard_map/all_to_all | solution.py:340
  909.1 3.4 copy-start
  927.3 4.7 copy-start.2

commit v11 on v10

--- a/solution.py
+++ b/solution.py
@@ -111,15 +111,6 @@
     )(tokens, small, weight, weight, cosine, sine)
 
 
-def attention_scores(q, k_ref, low_bound, high_bound, tile, tile_rows, scaling):
-    rows = pl.ds(pl.multiple_of(tile * tile_rows, tile_rows), tile_rows)
-    keys = k_ref[rows, :]
-    scores = contract_last(q, keys) * scaling
-    column = tile * tile_rows + lax.broadcasted_iota(jnp.int32, scores.shape, 1)
-    allowed = (column >= low_bound) & (column <= high_bound)
-    return rows, keys, scores, allowed
-
-
 def slots_of_block(rank_ref, table_ref, cap, block):
     rows = table_ref.shape[1]
     pick = (lax.broadcasted_iota(jnp.int32, (cap, rows), 0) == rank_ref[0]).astype(BF16)
@@ -154,40 +145,45 @@
 
 def attention_forward_kernel(
     begin_ref, q_ref, k_ref, v_ref, rank_ref, table_ref, out_ref, gated_ref, gate_ref, lse_ref, *,
-    scaling
+    scaling, width
 ):
-    block = pl.program_id(1)
-    cap, width = out_ref.shape
+    block = pl.program_id(0)
+    cap = out_ref.shape[0]
     tile_rows = q_ref.shape[0]
+    heads = [slice(h * width, (h + 1) * width) for h in range(out_ref.shape[1] // width)]
     pick, low_bound, high_bound, gate = slots_of_block(rank_ref, table_ref, cap, block)
-    q = dot(pick, q_ref[...]).astype(BF16)
+    queries = dot(pick, q_ref[...]).astype(BF16)
 
     def step(tile, carried):
-        largest, total, summed = carried
-        rows, _, scores, allowed = attention_scores(
-            q, k_ref, low_bound, high_bound, tile, tile_rows, scaling
-        )
-        scores = jnp.where(allowed, scores, NEGATIVE)
-        new_largest = jnp.maximum(largest, jnp.max(scores, axis=1, keepdims=True))
-        weights = jnp.where(allowed, jnp.exp(scores - new_largest), 0.0)
-        shrink = jnp.exp(largest - new_largest)
-        return (
-            new_largest,
-            total * shrink + jnp.sum(weights, axis=1, keepdims=True),
-            summed * shrink + dot(weights.astype(BF16), v_ref[rows, :]),
-        )
-
-    largest, total, summed = lax.fori_loop(
-        begin_ref[block],
-        block + 1,
-        step,
-        (jnp.full((cap, 1), NEGATIVE, F32), jnp.zeros((cap, 1), F32), jnp.zeros((cap, width), F32)),
-    )
-    attended = (summed / total).astype(BF16)
-    out_ref[...] = attended
-    gated_ref[...] = (gate * attended.astype(F32)).astype(BF16)
+        rows = pl.ds(pl.multiple_of(tile * tile_rows, tile_rows), tile_rows)
+        column = tile * tile_rows + lax.broadcasted_iota(jnp.int32, (cap, tile_rows), 1)
+        allowed = (column >= low_bound) & (column <= high_bound)
+        made = []
+        for at, (largest, total, summed) in zip(heads, carried):
+            scores = contract_last(queries[:, at], k_ref[rows, at]) * scaling
+            scores = jnp.where(allowed, scores, NEGATIVE)
+            new_largest = jnp.maximum(largest, jnp.max(scores, axis=1, keepdims=True))
+            weights = jnp.where(allowed, jnp.exp(scores - new_largest), 0.0)
+            shrink = jnp.exp(largest - new_largest)
+            made.append(
+                (
+                    new_largest,
+                    total * shrink + jnp.sum(weights, axis=1, keepdims=True),
+                    summed * shrink + dot(weights.astype(BF16), v_ref[rows, at]),
+                )
+            )
+        return tuple(made)
+
+    start = (
+        jnp.full((cap, 1), NEGATIVE, F32), jnp.zeros((cap, 1), F32), jnp.zeros((cap, width), F32)
+    )
+    ended = lax.fori_loop(begin_ref[block], block + 1, step, (start,) * len(heads))
     gate_ref[...] = gate
-    lse_ref[0] = largest + jnp.log(total)
+    for h, (largest, total, summed) in enumerate(ended):
+        attended = (summed / total).astype(BF16)
+        out_ref[:, heads[h]] = attended
+        gated_ref[:, heads[h]] = (gate * attended.astype(F32)).astype(BF16)
+        lse_ref[h] = largest + jnp.log(total)
 
 
 def attention_backward_kernel(
@@ -250,33 +246,36 @@
         lax.fori_loop(0, BLOCKS, finish_tile, 0)
 
 
-def attention_specs(row_count, token_count, width):
-    return dict(
-        q=pl.BlockSpec((row_count, width), lambda h, b, s: (b, h)),
-        k=pl.BlockSpec((token_count, width), lambda h, b, s: (0, h)),
-        rank=pl.BlockSpec((1, 1, row_count), lambda h, b, s: (b, 0, 0)),
-        rows=pl.BlockSpec((16, row_count), lambda h, b, s: (0, b)),
-        gate=pl.BlockSpec((CAP, 1), lambda h, b, s: (b, 0)),
-        slots=pl.BlockSpec((CAP, width), lambda h, b, s: (b, h)),
-        lse=pl.BlockSpec((1, CAP, 1), lambda h, b, s: (h, b, 0)),
-    )
-
-
 def attention_forward(begin, q, k, v, rank, table, width):
-    token_count, heads = q.shape[0], q.shape[1] // width
+    token_count, span = q.shape
     row_count = token_count // BLOCKS
-    s = attention_specs(row_count, token_count, width)
+    heads = span // width
+    block = lambda b, s: (b, 0)
+    tokens = pl.BlockSpec((row_count, span), block)
+    keys = pl.BlockSpec((token_count, span), lambda b, s: (0, 0))
+    slots = pl.BlockSpec((CAP, span), block)
+    rows = [
+        pl.BlockSpec((1, 1, row_count), lambda b, s: (b, 0, 0)),
+        pl.BlockSpec((16, row_count), lambda b, s: (0, b)),
+    ]
     return pl.pallas_call(
-        functools.partial(attention_forward_kernel, scaling=1.0 / math.sqrt(width)),
+        functools.partial(
+            attention_forward_kernel, scaling=1.0 / math.sqrt(width), width=width
+        ),
         grid_spec=pltpu.PrefetchScalarGridSpec(
             num_scalar_prefetch=1,
-            grid=(heads, BLOCKS),
-            in_specs=[s["q"], s["k"], s["k"], s["rank"], s["rows"]],
-            out_specs=[s["slots"], s["slots"], s["gate"], s["lse"]],
+            grid=(BLOCKS,),
+            in_specs=[tokens, keys, keys] + rows,
+            out_specs=[
+                slots,
+                slots,
+                pl.BlockSpec((CAP, 1), block),
+                pl.BlockSpec((heads, CAP, 1), lambda b, s: (0, b, 0)),
+            ],
         ),
         out_shape=[
-            jax.ShapeDtypeStruct((BLOCKS * CAP, heads * width), BF16),
-            jax.ShapeDtypeStruct((BLOCKS * CAP, heads * width), BF16),
+            jax.ShapeDtypeStruct((BLOCKS * CAP, span), BF16),
+            jax.ShapeDtypeStruct((BLOCKS * CAP, span), BF16),
             jax.ShapeDtypeStruct((BLOCKS * CAP, 1), F32),
             jax.ShapeDtypeStruct((heads, BLOCKS * CAP, 1), F32),
         ],

time: 1010 us -> 1010 us (level)
    pallas_call x1, Pallas kernels: 43.4 us -> 31.8 us  [attention_forward(): pl.pallas_call(functools.partial(attention_forward_kernel, scaling=1.0 /...]
    pallas_call x1, Pallas kernels: 92.7 us -> 103 us  [scattered(): pl.pallas_call(functools.partial(scatter_kernel, share=share, rides=len(r...]
where the time goes in v11:
time: 1010 us; the launch traced here: 1000 us
  Pallas kernels  837 us (83%)
  matrix products  63.9 us (6%)
  other arithmetic  31.6 us (3%)
  local copies, waits for them, and re-layouts  24.5 us (2%)
  blocking collectives  21.3 us (2%)
  starting transfers between devices  20 us (2%)
    pallas_call x2, Pallas kernels, gathered(): pl.pallas_call(functools.partial(gather_kernel, same=slots.ndim == 2, sha...  133 us
    pallas_call x1, Pallas kernels, opened(): pl.pallas_call(functools.partial(opening_kernel, share=share), grid=(plac...  122 us
    pallas_call x1, Pallas kernels, scattered(): pl.pallas_call(functools.partial(scatter_kernel, share=share, rides=len(r...  103 us
    pallas_call x1, Pallas kernels, closing(): pl.pallas_call(closing_kernel, grid=(BLOCKS,), in_specs=[pl.BlockSpec((co...  93.2 us
    pallas_call x1, Pallas kernels, expert_backward(): pl.pallas_call(functools.partial(expert_backward_kernel, rides=rides), gr...  85.1 us
    pallas_call x1, Pallas kernels, expert_gradient(): pl.pallas_call(expert_gradient_kernel, grid=(BLOCKS,), in_specs=[pl.Block...  72 us
    pallas_call x1, Pallas kernels, expert_forward(): pl.pallas_call(expert_forward_kernel, grid=(BLOCKS,), in_specs=[pl.BlockS...  59.5 us
    pallas_call x1, Pallas kernels, attention_backward(): pl.pallas_call(functools.partial(attention_backward_kernel, scaling=1.0 /...  50.1 us
  transfers between devices with their start and end apart: 4, of which 0 were waited for; matrix products, arithmetic and copies ran while one was open for 11% of the time, Pallas kernels for 49%

profile of v11, /device:TPU:0, one launch (start us, length us, event | category | flops | bytes accessed | tf_op | source)
XLA Modules:
  0.0 999.9 jit_solution(14075361915682572192)
XLA Ops:
  0.7 0.7 broadcast_in_dim.79
  2.1 0.7 convert.12
  2.7 0.7 convert.13
  3.4 1.1 copy.80
  5.0 0.7 reshape.348
  5.9 1.5 copy.78
  7.5 0.8 fusion.42.tokens_ref
  8.7 2.6 pad_maximum_fusion.pieces_ref
  11.3 122.2 %open_rows.1 = (bf16[4,2,528,2048]{3,2,1,0:T(8,128)(2,1)}, bf16[8,256,1024]{2,1,0:T(8,128)(2,1)}, bf16[8,256,1408]{2,1,0:T(8,128)(2,1)}, bf16[8,128,704]{2,1,0:T(8,128)(2,1)}, bf16[8,128,704]{2,1,0:T(8,128)(2,1)}) custom-call(bf16[528,512]{1,0:T(8,128)(2,1)} %fusion.42.tokens_ref, bf16[8,256,1024]{2,1,0:T(8,128)(2,1)} %pad_maximum_fusion.pieces_ref, ...), custom_call_target="tpu_custom_call" | custom-call | tf_op jit(solution)/shard_map/open_rows/pallas_call | solution.py:701
  133.6 5.0 all-to-all-start
  139.4 1.1 slice.125
  141.4 1.1 convert_element_type.144
  144.7 27.2 %project.1 = (bf16[4096,2048]{1,0:T(8,128)(2,1)}, bf16[4096,256]{1,0:T(8,128)(2,1)}, bf16[4096,256]{1,0:T(8,128)(2,1)}, bf16[4096,256]{1,0:T(8,128)(2,1)}, f32[16,4096]{1,0:T(8,128)}, /*index=5*/f32[4096,1]{1,0:T(8,128)}) custom-call(bf16[4,2,528,2048]{3,2,1,0:T(8,128)(2,1)} %get-tuple-element.76.tokens_ref, bf16[16,2048]{1,0:T(8,128)(2,1)} %pad.24.small_ref, ...), custom_call_target="tpu_custom_call" | custom-call | tf_op jit(solution)/shard_map/project/pallas_call | solution.py:82
  171.9 1.0 fusion.54
  172.9 1.0 fusion.68
  174.0 1.0 broadcast_divide_fusion
  176.7 31.8 %attention_forward.1 = (bf16[2560,256]{1,0:T(8,128)(2,1)}, bf16[2560,256]{1,0:T(8,128)(2,1)}, f32[2560,1]{1,0:T(8,128)}, f32[2,2560,1]{2,1,0:T(8,128)}) custom-call(s32[8]{0:T(128)} %and_select_fusion.4.begin_ref, bf16[4096,256]{1,0:T(8,128)(2,1)} %get-tuple-element.79.q_ref, bf16[4096,256]{1,0:T(8,128)(2,1)} %get-tuple-element.80.k_ref, ...), custom_call_target="tpu_custom_call" | custom-call | tf_op jit(solution)/shard_map/attention_forward/pallas_call | solution.py:261
  208.5 2.6 reduce.2
  211.2 1.9 fusion.14.grad_ref
  213.1 6.9 convolution_convert_fusion.1
  219.9 102.9 %scatter_rows.1 = (bf16[4,320,512]{2,1,0:T(8,128)(2,1)}, bf16[8,128,704]{2,1,0:T(8,128)(2,1)}) custom-call(bf16[4,2,320,2048]{3,2,1,0:T(8,128)(2,1)} %bitcast.153, bf16[8,128,704]{2,1,0:T(8,128)(2,1)} %get-tuple-element.85.refs_1_), custom_call_target="tpu_custom_call" | custom-call | tf_op jit(solution)/shard_map/scatter_rows/pallas_call | solution.py:897
  322.8 4.8 multiply_reduce_fusion.3
  327.9 5.2 all_gather.8
  333.2 1.9 fusion.15.refs_0_
  335.2 80.8 %gather_rows.2 = (bf16[4,2,320,2048]{3,2,1,0:T(8,128)(2,1)}, bf16[8,128,704]{2,1,0:T(8,128)(2,1)}) custom-call(bf16[4,320,512]{2,1,0:T(8,128)(2,1)} %fusion.15.refs_0_, bf16[8,128,704]{2,1,0:T(8,128)(2,1)} %get-tuple-element.87.refs_1_), custom_call_target="tpu_custom_call" | custom-call | tf_op jit(solution)/shard_map/gather_rows/pallas_call | solution.py:756
  416.7 0.7 pad_convert_fusion.member_ref
  417.4 59.5 %expert_forward.1 = (f32[2560,704]{1,0:T(8,128)}, f32[2560,704]{1,0:T(8,128)}, bf16[8,320,2048]{2,1,0:T(8,128)(2,1)}, f32[2560,1]{1,0:T(8,128)}, bf16[2560,704]{...) custom-call(bf16[8,320,2048]{2,1,0:T(8,128)(2,1)} %bitcast.154, bf16[2048,1408]{1,0:T(8,128)(2,1)} %bitcast.31.up_weight_ref, ...), custom_call_target="tpu_custom_call" | custom-call | tf_op jit(solution)/shard_map/expert_forward/pallas_call | solution.py:984
  476.9 85.1 %expert_backward.1 = (bf16[8,320,2048]{2,1,0:T(8,128)(2,1)}, bf16[2560,1408]{1,0:T(8,128)(2,1)}, bf16[8,128,704]{2,1,0:T(8,128)(2,1)}, bf16[8,128,704]{2,1,0:T(8...) custom-call(f32[2560,704]{1,0:T(8,128)} %get-tuple-element.93.slope_ref, ...), custom_call_target="tpu_custom_call" | custom-call | tf_op jit(solution)/shard_map/expert_backward/pallas_call | solution.py:1072
  562.0 72.0 %expert_gradient.1 = (bf16[2048,128]{1,0:T(8,128)(2,1)}, bf16[2048,1280]{1,0:T(8,128)(2,1)}, bf16[4,320,512]{2,1,0:T(8,128)(2,1)}, bf16[8,128,704]{2,1,0:T(8,128)(2,1)}) custom-call(bf16[2560,2048]{1,0:T(8,128)(2,1)} %bitcast.155, bf16[2560,1408]{1,0:T(8,128)(2,1)} %get-tuple-element.99.grad_gate_up_ref, bf16[4,2,320,2048]{3,2,1,0:T(8,128)(2,1)} %bitcast.167, ...), custom_call_target="tpu_custom_call" | custom-call | tf_op jit(solution)/shard_map/expert_gradient/pallas_call | solution.py:1138
  634.1 3.3 multiply_reduce_fusion.5
  637.4 5.5 all-to-all-start.1
  642.9 4.7 multiply_reduce_fusion.2
  647.6 5.4 all_gather.9
  653.2 3.2 multiply_add_fusion
  656.4 1.9 fusion.13.refs_0_
  658.3 52.2 %gather_rows.3 = bf16[4,2,320,2048]{3,2,1,0:T(8,128)(2,1)} custom-call(bf16[4,320,512]{2,1,0:T(8,128)(2,1)} %fusion.13.refs_0_), custom_call_target="tpu_custom_call" | custom-call | tf_op jit(solution)/shard_map/gather_rows/pallas_call | solution.py:756
  710.5 4.7 all-to-all-start.2
  715.1 1.7 reduce.4
  717.5 8.2 fusion.5.grad_ref
  725.7 50.1 %attention_backward.1 = (bf16[4096,256]{1,0:T(8,128)(2,1)}, bf16[4096,256]{1,0:T(8,128)(2,1)}, bf16[4096,256]{1,0:T(8,128)(2,1)}) custom-call(s32[8]{0:T(128)} %and_select_fusion.4.begin_ref, bf16[4096,256]{1,0:T(8,128)(2,1)} %get-tuple-element.79.q_ref, bf16[4096,256]{1,0:T(8,128)(2,1)} %get-tuple-element.80.k_ref, ...), custom_call_target="tpu_custom_call" | custom-call | tf_op jit(solution)/shard_map/attention_backward/pallas_call | solution.py:301
  775.8 20.4 %convolution_convert_fusion = bf16[4096,2048]{1,0:T(8,128)(2,1)} fusion(bf16[4096,256]{1,0:T(8,128)(2,1)} %get-tuple-element.117.v_ref, bf16[4096,256]{1,0:T(8,128)(2,1)} %get-tuple-element.116.k_ref, bf16[4096,256]{1,0:T(8,128)(2,1)} %get-tuple-element.115.q_ref, bf16[2048,1024]{1,0:T(8,128)(2,1)} %bitcast.164), kind=kOutput, calls=%fused_computation | convolution fusion | flops 12912164864 | bytes 26214400 | tf_op jit(solution)/shard_map/dot_general | solution.py:49
  796.2 93.2 %closing.1 = (bf16[2048,1024]{1,0:T(8,128)(2,1)}, bf16[4,512,512]{2,1,0:T(8,128)(2,1)}) custom-call(bf16[4096,2048]{1,0:T(8,128)(2,1)} %get-tuple-element.109.hidden_ref, bf16[4096,256]{1,0:T(8,128)(2,1)} %get-tuple-element.115.q_ref, bf16[4096,256]{1,0:T(8,128)(2,1)} %get-tuple-element.116.k_ref, bf16[4096,256]{1,0:T(8,128)(2,1)} %get-tuple-element.117.v_ref, ...), custom_call_target="tpu_custom_call" | custom-call | tf_op jit(solution)/shard_map/closing/pallas_call | solution.py:1188
  889.5 4.8 all-to-all-start.3
  894.3 1.1 dynamic-slice_reduce_fusion
  895.4 1.6 fusion.22
  897.1 5.2 convert_bitcast_fusion
  902.2 6.4 copy.97
  908.6 3.0 multiply_reduce_fusion
  912.6 1.0 add_convert_fusion
  913.6 2.0 copy.98
  915.6 3.0 convert_reduce_fusion
  918.6 1.6 copy.94
  920.2 1.2 fusion.32
  921.4 5.3 all_gather.10
  926.8 1.5 multiply_reduce_fusion.4
  928.3 1.5 fusion.91
  929.9 1.6 fusion.43
  931.5 1.0 fusion.37
  932.5 5.4 all_gather.11
  938.1 0.7 pad.28.pieces_ref
  938.7 1.0 copy.99
  939.7 9.6 unpack_up.1
  949.3 42.2 %swap_small.1.small_ref = f32[8,16,256]{2,1,0:T(8,128)} custom-call(f32[8,16,256]{2,1,0:T(8,128)} %pad.28.pieces_ref), custom_call_target="tpu_custom_call" | custom-call | tf_op jit(solution)/shard_map/swap_small/pallas_call | solution.py:1284
  991.5 8.1 attention_weight_gradients.1
  (129 shorter events, 10.5 us)
Async XLA Ops:
  0.6 4.3 copy-start.8
  5.0 2.4 copy-start.11
  5.0 2.4 copy-start.12
  5.0 2.4 copy-start.7
  133.5 5.1 copy-start.10
  133.5 7.6 copy-start.9
  133.6 283.9 %all-to-all-start = ((bf16[8,256,1408]{2,1,0:T(8,128)(2,1)}), bf16[8,256,1408]{2,1,0:T(8,128)(2,1)}, u32[]{:S(2)}, u32[]{:S(2)}) async-start(bf16[8,256,1408]{2,1,0:T(8,128)(2,1)} %get-tuple-element.89), calls=%async_computation | async-start | bytes 11534336 | tf_op jit(solution)/shard_map/all_to_all | solution.py:339
  139.3 188.3 %copy-start.1 = (bf16[512,512]{0,1:T(8,128)(2,1)}, bf16[512,512]{0,1:T(8,128)(2,1)S(1)}, u32[]{:S(2)}) copy-start(bf16[512,512]{0,1:T(8,128)(2,1)S(1)} %copy.85) | copy-start | bytes 1572868
  141.3 30.6 %copy-start.4 = (bf16[512,512]{0,1:T(8,128)(2,1)}, bf16[512,512]{0,1:T(8,128)(2,1)S(1)}, u32[]{:S(2)}) copy-start(bf16[512,512]{0,1:T(8,128)(2,1)S(1)} %copy.84) | copy-start | bytes 1572868
  208.5 4.6 copy-start.3
  333.2 82.7 %copy-start.5 = (bf16[512,512]{0,1:T(8,128)(2,1)}, bf16[512,512]{0,1:T(8,128)(2,1)S(1)}, u32[]{:S(2)}) copy-start(bf16[512,512]{0,1:T(8,128)(2,1)S(1)} %get-tuple-element.126) | copy-start | bytes 1572868
  634.1 8.8 copy-start.6
  637.4 73.1 %all-to-all-start.1 = ((bf16[8,256,128]{2,1,0:T(8,128)(2,1)}), bf16[8,256,128]{2,1,0:T(8,128)(2,1)}, u32[]{:S(2)}, u32[]{:S(2)}) async-start(bf16[8,256,128]{2,1,0:T(8,128)(2,1)} %bitcast.179), calls=%async_computation.1 | async-start | bytes 1048576 | tf_op jit(solution)/shard_map/all_to_all | solution.py:339
  710.5 179.0 %all-to-all-start.2 = ((bf16[8,256,1280]{2,1,0:T(8,128)(2,1)}), bf16[8,256,1280]{2,1,0:T(8,128)(2,1)}, u32[]{:S(2)}, u32[]{:S(2)}) async-start(bf16[8,256,1280]{2,1,0:T(8,128)(2,1)} %bitcast.170), calls=%async_computation.2 | async-start | bytes 10485760 | tf_op jit(solution)/shard_map/all_to_all | solution.py:339
  889.5 102.1 %all-to-all-start.3 = ((bf16[8,256,1024]{2,1,0:T(8,128)(2,1)}), bf16[8,256,1024]{2,1,0:T(8,128)(2,1)}, u32[]{:S(2)}, u32[]{:S(2)}) async-start(bf16[8,256,1024]{2,1,0:T(8,128)(2,1)} %bitcast.171), calls=%async_computation.3 | async-start | bytes 8388608 | tf_op jit(solution)/shard_map/all_to_all | solution.py:339
  908.6 3.4 copy-start
  926.8 4.7 copy-start.2
